TPU v7x, 32 devices: a whole 2x2x4 slice. The times are simulated.
32 devices in a mesh: dp: 8 (over z, y), blk: 4 (over x, core).
Axes of the slice: x: 2, y: 2, z: 4, core: 2. Of those that a mesh axis runs over, the one named last changes fastest.
Arguments:
- tokens: bfloat16 [32, 512, 768], P('dp', 'blk'), may hold values from -6 to 6
- lengths: int32 [32, 8], P('dp'), may hold values from 1 to 385, 512 in all within a row
- w_qkv: bfloat16 [768, 2304], replicated, may hold values from -0.21875 to 0.21875
- bias_qv: float32 [1536], replicated, may hold values from -3 to 3
- w_out: bfloat16 [768, 768], replicated, may hold values from -0.875 to 0.875
- bias_out: float32 [768], replicated, may hold values from -3 to 3
- norm1_gain: float32 [768], replicated, may hold values from 0.25 to 1.75
- norm1_bias: float32 [768], replicated, may hold values from -3 to 3
- w_up: bfloat16 [768, 3072], replicated, may hold values from -0.21875 to 0.21875
- bias_up: float32 [3072], replicated, may hold values from -3 to 3
- w_down: bfloat16 [3072, 768], replicated, may hold values from -0.109375 to 0.109375
- bias_down: float32 [768], replicated, may hold values from -3 to 3
- norm2_gain: float32 [768], replicated, may hold values from 0.25 to 1.75
- norm2_bias: float32 [768], replicated, may hold values from -3 to 3
- cotangent: bfloat16 [32, 512, 768], P('dp', 'blk'), may hold values from -6 to 6
Outputs:
- outputs: bfloat16 [32, 512, 768], P('dp', 'blk')
- grad_tokens: bfloat16 [32, 512, 768], P('dp', 'blk')
- grad_w_qkv: float32 [768, 2304], P('dp')
- grad_bias_qv: float32 [1536], P('dp')
- grad_w_out: float32 [768, 768], P('dp')
- grad_bias_out: float32 [768], P('dp')
- grad_norm1_gain: float32 [768], P('dp')
- grad_norm1_bias: float32 [768], P('dp')
- grad_w_up: float32 [768, 3072], P('dp')
- grad_bias_up: float32 [3072], P('dp')
- grad_w_down: float32 [3072, 768], P('dp')
- grad_bias_down: float32 [768], P('dp')
- grad_norm2_gain: float32 [768], P('dp')
- grad_norm2_bias: float32 [768], P('dp')
Inputs may be any that keep to these rules, and one draw needn't show every extreme that they name: Each row's page lengths sum to 512; in each row the longest page has exactly the largest length.
All inputs are finite; a program needn't handle non-finite values.
Results may differ from a plain program's by a relative error of at most 0.019.
Values may be sent and summed in bfloat16 or wider, within the bound.
No kernel may reach another device: no remote copies, remote signals or barrier semaphores. Data moves between devices by JAX's collectives and lax.ppermute only.
A program may use at most 128 MiB of HBM per device.

v0:
```python
import math

import jax
import jax.numpy as jnp
from jax import lax
from jax.sharding import PartitionSpec as P

HEADS = 12


EPSILON = 1e-12
MASKED = -1e30


def from_behind(block, axis, distance):
    devices = range(lax.axis_size(axis))
    route = [((i - distance) % len(devices), i) for i in devices]
    return lax.ppermute(block, axis, route)


def page_numbers(lengths, total_slots):
    page_ends = jnp.cumsum(lengths, axis=1)
    slot_ids = jnp.arange(total_slots, dtype=jnp.int32)
    return jnp.sum((slot_ids[None, :, None] >= page_ends[:, None, :]).astype(jnp.int32), axis=2)


def contract_rows(left, right):
    return lax.dot_general(
        left, right, (((0,), (0,)), ((), ())), preferred_element_type=jnp.float32
    )


def times_transposed(left, right):
    return lax.dot_general(
        left, right, (((1,), (1,)), ((), ())), preferred_element_type=jnp.float32
    )


def normalize(inputs, gain_vec, shift_vec):
    centre = inputs - jnp.mean(inputs, axis=-1, keepdims=True)
    inverse = lax.rsqrt(jnp.mean(centre * centre, axis=-1, keepdims=True) + EPSILON)
    normed = centre * inverse
    return (normed * gain_vec + shift_vec, normed, inverse)


def normalize_back(upstream, normed, inverse, gain_vec):
    scaled = upstream * gain_vec
    inner = (
        scaled
        - jnp.mean(scaled, axis=-1, keepdims=True)
        - normed * jnp.mean(scaled * normed, axis=-1, keepdims=True)
    )
    return (inverse * inner, jnp.sum(upstream * normed, axis=0), jnp.sum(upstream, axis=0))


def block_scores(queries, key_rows, query_pages, key_pages):
    scaling = 1.0 / math.sqrt(queries.shape[-1])
    scores = (
        jnp.einsum("rqhd,rkhd->rhqk", queries, key_rows, preferred_element_type=jnp.float32)
        * scaling
    )
    same_page = (query_pages[:, :, None] == key_pages[:, None, :])[:, None]
    return (scores, same_page)


def absorb(carry_state, queries, query_pages, key_rows, value_rows, key_pages):
    running_max, total_mass, context_sum = carry_state
    scores, same_page = block_scores(queries, key_rows, query_pages, key_pages)
    block_max = jnp.max(jnp.where(same_page, scores, MASKED), axis=-1)
    new_max = jnp.maximum(running_max, block_max)
    decay = jnp.exp(running_max - new_max)
    weights = jnp.where(same_page, jnp.exp(scores - new_max[..., None]), 0.0)
    total_mass = total_mass * decay + jnp.sum(weights, axis=-1)
    context_sum = context_sum * decay[..., None] + jnp.einsum(
        "rhqk,rkhd->rhqd",
        weights.astype(jnp.bfloat16),
        value_rows,
        preferred_element_type=jnp.float32,
    )
    return (new_max, total_mass, context_sum)


def block_grads(
    queries, query_pages, grad_context, log_mass, balance, key_rows, value_rows, key_pages
):
    scores, same_page = block_scores(queries, key_rows, query_pages, key_pages)
    probs = jnp.where(same_page, jnp.exp(scores - log_mass[..., None]), 0.0)
    grad_value = jnp.einsum(
        "rhqk,rqhd->rkhd",
        probs.astype(jnp.bfloat16),
        grad_context,
        preferred_element_type=jnp.float32,
    )
    grad_weights = jnp.einsum(
        "rqhd,rkhd->rhqk", grad_context, value_rows, preferred_element_type=jnp.float32
    )
    grad_scores = (probs * (grad_weights - balance[..., None])).astype(jnp.bfloat16)
    scaling = 1.0 / math.sqrt(queries.shape[-1])
    grad_query = (
        jnp.einsum("rhqk,rkhd->rqhd", grad_scores, key_rows, preferred_element_type=jnp.float32)
        * scaling
    )
    grad_key = (
        jnp.einsum("rhqk,rqhd->rkhd", grad_scores, queries, preferred_element_type=jnp.float32)
        * scaling
    )
    return (grad_query, jnp.stack([grad_key, grad_value]))


def shards(
    tokens,
    lengths,
    w_qkv,
    bias_qv,
    w_out,
    bias_out,
    norm1_gain,
    norm1_bias,
    w_up,
    bias_up,
    w_down,
    bias_down,
    norm2_gain,
    norm2_bias,
    cotangent,
):
    row_count, slot_count, model_width = tokens.shape
    head_count = HEADS
    head_width = model_width // head_count
    axis_count = lax.axis_size("blk")
    position = lax.axis_index("blk")
    all_pages = page_numbers(lengths, slot_count * axis_count)

    def pages_from(first_slot, slot_total):
        return lax.dynamic_slice_in_dim(all_pages, first_slot, slot_total, 1)

    query_pages = pages_from(position * slot_count, slot_count)
    flat_tokens = tokens.reshape(row_count * slot_count, model_width)
    projected = jnp.dot(flat_tokens, w_qkv, preferred_element_type=jnp.float32)
    head_shape = (row_count, slot_count, head_count, head_width)
    queries = (
        (projected[:, :model_width] + bias_qv[:model_width])
        .astype(jnp.bfloat16)
        .reshape(head_shape)
    )
    key_rows = projected[:, model_width : 2 * model_width].astype(jnp.bfloat16).reshape(head_shape)
    value_rows = (
        (projected[:, 2 * model_width :] + bias_qv[model_width:])
        .astype(jnp.bfloat16)
        .reshape(head_shape)
    )
    key_values = jnp.stack([key_rows, value_rows])
    stat_shape = (row_count, head_count, slot_count)
    start_state = (
        jnp.full(stat_shape, MASKED, jnp.float32),
        jnp.zeros(stat_shape, jnp.float32),
        jnp.zeros((row_count, head_count, slot_count, head_width), jnp.float32),
    )
    carry_state = start_state
    visiting = key_values
    for turn_index in range(axis_count):
        if turn_index > 0:
            visiting = from_behind(visiting, "blk", 1)
        anchor = (position - turn_index) % axis_count
        carry_state = absorb(
            carry_state,
            queries,
            query_pages,
            visiting[0],
            visiting[1],
            pages_from(anchor * slot_count, slot_count),
        )
    running_max, total_mass, context_sum = carry_state
    log_mass = running_max + jnp.log(total_mass)
    context_heads = jnp.transpose(context_sum / total_mass[..., None], (0, 2, 1, 3))
    context_low = context_heads.reshape(row_count * slot_count, model_width).astype(jnp.bfloat16)
    attended = jnp.dot(context_low, w_out, preferred_element_type=jnp.float32) + bias_out
    first_norm, normed_one, inverse_one = normalize(
        flat_tokens.astype(jnp.float32) + attended, norm1_gain, norm1_bias
    )
    first_low = first_norm.astype(jnp.bfloat16)
    raised = jnp.dot(first_low, w_up, preferred_element_type=jnp.float32) + bias_up
    activated = jax.nn.gelu(raised, approximate=False).astype(jnp.bfloat16)
    lowered = jnp.dot(activated, w_down, preferred_element_type=jnp.float32) + bias_down
    outputs, normed_two, inverse_two = normalize(first_norm + lowered, norm2_gain, norm2_bias)
    upstream = cotangent.reshape(row_count * slot_count, model_width).astype(jnp.float32)
    grad_sum_two, grad_norm2_gain, grad_norm2_bias = normalize_back(
        upstream, normed_two, inverse_two, norm2_gain
    )
    grad_lowered = grad_sum_two.astype(jnp.bfloat16)
    grad_w_down = contract_rows(activated, grad_lowered)
    grad_bias_down = jnp.sum(grad_lowered.astype(jnp.float32), axis=0)
    cumulative = 0.5 * (1.0 + lax.erf(raised / math.sqrt(2.0)))
    slope = cumulative + raised * jnp.exp(-0.5 * raised * raised) / math.sqrt(2.0 * math.pi)
    grad_raised = (times_transposed(grad_lowered, w_down) * slope).astype(jnp.bfloat16)
    grad_w_up = contract_rows(first_low, grad_raised)
    grad_bias_up = jnp.sum(grad_raised.astype(jnp.float32), axis=0)
    grad_first = grad_sum_two + times_transposed(grad_raised, w_up)
    grad_sum_one, grad_norm1_gain, grad_norm1_bias = normalize_back(
        grad_first, normed_one, inverse_one, norm1_gain
    )
    grad_attended = grad_sum_one.astype(jnp.bfloat16)
    grad_w_out = contract_rows(context_low, grad_attended)
    grad_bias_out = jnp.sum(grad_attended.astype(jnp.float32), axis=0)
    grad_context = times_transposed(grad_attended, w_out).astype(jnp.bfloat16).reshape(head_shape)
    balance = jnp.transpose(
        jnp.sum(grad_context.astype(jnp.float32) * context_heads, axis=-1), (0, 2, 1)
    )
    zero_query = jnp.zeros(head_shape, jnp.float32)
    visiting = key_values
    grad_query = zero_query
    moving = jnp.zeros((2,) + head_shape, jnp.float32)
    for turn_index in range(axis_count):
        if turn_index > 0:
            visiting, moving = (
                from_behind(visiting, "blk", 1),
                from_behind(moving.astype(jnp.bfloat16), "blk", 1).astype(moving.dtype),
            )
        anchor = (position - turn_index) % axis_count
        extra_query, extra_pairs = block_grads(
            queries,
            query_pages,
            grad_context,
            log_mass,
            balance,
            visiting[0],
            visiting[1],
            pages_from(anchor * slot_count, slot_count),
        )
        grad_query = grad_query + extra_query
        moving = moving + extra_pairs
    own_pairs = from_behind(moving.astype(jnp.bfloat16), "blk", 1).astype(moving.dtype)
    flat_shape = (row_count * slot_count, model_width)
    grad_query_low = grad_query.astype(jnp.bfloat16).reshape(flat_shape)
    grad_key_low = own_pairs[0].astype(jnp.bfloat16).reshape(flat_shape)
    grad_value_low = own_pairs[1].astype(jnp.bfloat16).reshape(flat_shape)
    grad_projected = jnp.concatenate([grad_query_low, grad_key_low, grad_value_low], axis=1)
    grad_w_qkv = contract_rows(flat_tokens, grad_projected)
    grad_bias_qv = jnp.concatenate(
        [
            jnp.sum(grad_query_low.astype(jnp.float32), axis=0),
            jnp.sum(grad_value_low.astype(jnp.float32), axis=0),
        ]
    )
    grad_tokens = (grad_sum_one + times_transposed(grad_projected, w_qkv)).astype(jnp.bfloat16)
    (
        share_w_qkv,
        share_bias_qv,
        share_w_out,
        share_bias_out,
        share_norm1_gain,
        share_norm1_bias,
        share_w_up,
        share_bias_up,
        share_w_down,
        share_bias_down,
        share_norm2_gain,
        share_norm2_bias,
    ) = (
        lax.psum_scatter(grad_w_qkv, "dp", scatter_dimension=0, tiled=True),
        lax.psum_scatter(grad_bias_qv, "dp", scatter_dimension=0, tiled=True),
        lax.psum_scatter(grad_w_out, "dp", scatter_dimension=0, tiled=True),
        lax.psum_scatter(grad_bias_out, "dp", scatter_dimension=0, tiled=True),
        lax.psum_scatter(grad_norm1_gain, "dp", scatter_dimension=0, tiled=True),
        lax.psum_scatter(grad_norm1_bias, "dp", scatter_dimension=0, tiled=True),
        lax.psum_scatter(grad_w_up, "dp", scatter_dimension=0, tiled=True),
        lax.psum_scatter(grad_bias_up, "dp", scatter_dimension=0, tiled=True),
        lax.psum_scatter(grad_w_down, "dp", scatter_dimension=0, tiled=True),
        lax.psum_scatter(grad_bias_down, "dp", scatter_dimension=0, tiled=True),
        lax.psum_scatter(grad_norm2_gain, "dp", scatter_dimension=0, tiled=True),
        lax.psum_scatter(grad_norm2_bias, "dp", scatter_dimension=0, tiled=True),
    )
    (
        total_w_qkv,
        total_bias_qv,
        total_w_out,
        total_bias_out,
        total_norm1_gain,
        total_norm1_bias,
        total_w_up,
        total_bias_up,
        total_w_down,
        total_bias_down,
        total_norm2_gain,
        total_norm2_bias,
    ) = (
        lax.psum(share_w_qkv.astype(jnp.bfloat16), "blk").astype(jnp.float32),
        lax.psum(share_bias_qv.astype(jnp.bfloat16), "blk").astype(jnp.float32),
        lax.psum(share_w_out.astype(jnp.bfloat16), "blk").astype(jnp.float32),
        lax.psum(share_bias_out.astype(jnp.bfloat16), "blk").astype(jnp.float32),
        lax.psum(share_norm1_gain.astype(jnp.bfloat16), "blk").astype(jnp.float32),
        lax.psum(share_norm1_bias.astype(jnp.bfloat16), "blk").astype(jnp.float32),
        lax.psum(share_w_up.astype(jnp.bfloat16), "blk").astype(jnp.float32),
        lax.psum(share_bias_up.astype(jnp.bfloat16), "blk").astype(jnp.float32),
        lax.psum(share_w_down.astype(jnp.bfloat16), "blk").astype(jnp.float32),
        lax.psum(share_bias_down.astype(jnp.bfloat16), "blk").astype(jnp.float32),
        lax.psum(share_norm2_gain.astype(jnp.bfloat16), "blk").astype(jnp.float32),
        lax.psum(share_norm2_bias.astype(jnp.bfloat16), "blk").astype(jnp.float32),
    )
    token_shape = (row_count, slot_count, model_width)
    return (
        outputs.astype(jnp.bfloat16).reshape(token_shape),
        grad_tokens.reshape(token_shape),
        total_w_qkv,
        total_bias_qv,
        total_w_out,
        total_bias_out,
        total_norm1_gain,
        total_norm1_bias,
        total_w_up,
        total_bias_up,
        total_w_down,
        total_bias_down,
        total_norm2_gain,
        total_norm2_bias,
    )


def solution(mesh):
    in_specs = (
        P("dp", "blk", None),
        P("dp", None),
        P(),
        P(),
        P(),
        P(),
        P(),
        P(),
        P(),
        P(),
        P(),
        P(),
        P(),
        P(),
        P("dp", "blk", None),
    )
    out_specs = (
        P("dp", "blk", None),
        P("dp", "blk", None),
        P("dp", None),
        P("dp"),
        P("dp", None),
        P("dp"),
        P("dp"),
        P("dp"),
        P("dp", None),
        P("dp"),
        P("dp", None),
        P("dp"),
        P("dp"),
        P("dp"),
    )
    return jax.shard_map(shards, mesh=mesh, in_specs=in_specs, out_specs=out_specs, check_vma=False)
```

profile of v0, /device:TPU:0, one launch (start us, length us, event | category | flops | bytes accessed | tf_op | source)
XLA Modules:
  0.0 764.4 jit_solution(8118844731167546033)
XLA Ops:
  9.2 3.1 fusion.186
  15.5 2.3 copy.173
  17.8 3.3 fusion.48
  21.0 2.3 copy.176
  23.3 2.4 stack_reshape.7
  25.7 2.2 copy.182
  28.0 2.4 stack_reshape.6
  33.5 20.1 %collective-permute-done = bf16[2,4,128,12,64]{2,4,3,1,0:T(8,128)(2,1)} collective-permute-done((bf16[2,4,128,12,64]{2,4,3,1,0:T(8,128)(2,1)S(1)}, bf16[2,4,128,12,64]{2,4,3,1,0:T(8,128)(2,1)}, u32[]{:S(2)}, u32[]{:S(2)}) %collective-permute-start) | collective-permute-done | bytes 1572896 | tf_op jit(solution)/shard_map/ppermute | solution.py:18
  53.7 2.5 squeeze_stack_reshape.9
  56.1 2.4 squeeze_stack_reshape.8
  58.7 2.3 copy.172
  61.0 2.4 reshape.226
  65.7 8.1 %collective-permute-done.1 = bf16[2,4,128,12,64]{2,4,3,1,0:T(8,128)(2,1)} collective-permute-done((bf16[2,4,128,12,64]{2,4,3,1,0:T(8,128)(2,1)}, bf16[2,4,128,12,64]{2,4,3,1,0:T(8,128)(2,1)}, u32[]{:S(2)}, u32[]{:S(2)}) %collective-permute-start.1) | collective-permute-done | bytes 1572896 | tf_op jit(solution)/shard_map/ppermute | solution.py:18
  74.4 2.2 select_reduce_fusion.3
  76.7 2.5 select_reduce_fusion.2
  79.2 2.5 select_reduce_fusion.1
  81.7 12.3 %collective-permute-done.2 = bf16[2,4,128,12,64]{2,4,3,1,0:T(8,128)(2,1)S(1)} collective-permute-done((bf16[2,4,128,12,64]{2,4,3,1,0:T(8,128)(2,1)}, bf16[2,4,128,12,64]{2,4,3,1,0:T(8,128)(2,1)S(1)}, u32[]{:S(2)}, u32[]{:S(2)}) %collective-permute-start.2) | collective-permute-done | bytes 1572896 | tf_op jit(solution)/shard_map/ppermute | solution.py:18
  103.1 2.3 fusion.183
  107.7 16.2 %fusion.2 = (bf16[512,3072]{1,0:T(8,128)(2,1)S(1)}, f32[512,3072]{1,0:T(8,128)S(1)}) fusion(f32[3072]{0:T(1024)S(1)} %copy-done.51, bf16[768,3072]{1,0:T(8,128)(2,1)S(1)} %bitcast.262, f32[512,768]{1,0:T(8,128)S(1)} %get-tuple-element.138, f32[768]{0:T(1024)S(1)} %copy-done.54, f32[768]{0:T(1024)S(1)} %copy-done.46, f32[512]{0:T(512)S(1)} %add_rsqrt_fusion.1, ...), kind=kOutput, calls=%fused_computation.4 | convolution fusion | flops 2521694208 | bytes 15751168 | tf_op jit(solution)/shard_map/dot_general | solution.py:182
  123.9 2.8 fusion.185
  129.9 5.4 convert_reduce_fusion
  135.3 3.6 multiply_reduce_fusion
  141.2 2.2 fusion.112
  143.6 8.9 %fusion.173 = f32[768,3072]{1,0:T(8,128)} fusion(bf16[512,3072]{1,0:T(8,128)(2,1)} %copy-done.56, f32[512,768]{1,0:T(8,128)} %copy-done.14, f32[768]{0:T(1024)} %param.22, f32[768]{0:T(1024)S(1)} %copy-done.47, f32[512]{0:T(512)S(1)} %copy-done.45, f32[512]{0:T(512)S(1)} %broadcast_multiply_fusion.4), kind=kOutput, calls=%fused_computation.271 | convolution fusion | flops 2417885184 | bytes 14166016 | tf_op jit(solution)/shard_map/dot_general | solution.py:28
  152.5 8.7 %fusion.153 = f32[3072,768]{1,0:T(8,128)} fusion(bf16[512,3072]{1,0:T(8,128)(2,1)} %copy-done.19, f32[512,768]{1,0:T(8,128)} %copy-done.13), kind=kOutput, calls=%fused_computation.251 | convolution fusion | flops 2416312320 | bytes 14155776 | tf_op jit(solution)/shard_map/dot_general | solution.py:28
  161.3 3.5 convolution_convert_fusion
  164.8 2.3 copy.190
  167.1 2.6 reshape.228
  172.5 3.8 multiply_convert_fusion.3
  179.5 2.4 multiply_convert_fusion.2
  184.3 14.5 %collective-permute-done.3 = bf16[2,4,128,12,64]{2,4,3,1,0:T(8,128)(2,1)S(1)} collective-permute-done((bf16[2,4,128,12,64]{2,4,3,1,0:T(8,128)(2,1)S(1)}, bf16[2,4,128,12,64]{2,4,3,1,0:T(8,128)(2,1)S(1)}, u32[]{:S(2)}, u32[]{:S(2)}) %collective-permute-start.3) | collective-permute-done | bytes 1572896 | tf_op jit(solution)/shard_map/ppermute | solution.py:18
  199.5 2.4 multiply_convert_fusion.1
  204.3 15.0 %collective-permute-done.4 = bf16[2,4,128,12,64]{2,4,3,1,0:T(8,128)(2,1)S(1)} collective-permute-done((bf16[2,4,128,12,64]{2,4,3,1,0:T(8,128)(2,1)S(1)}, bf16[2,4,128,12,64]{2,4,3,1,0:T(8,128)(2,1)S(1)}, u32[]{:S(2)}, u32[]{:S(2)}) %collective-permute-start.4) | collective-permute-done | bytes 1572896 | tf_op jit(solution)/shard_map/ppermute | solution.py:18
  223.9 16.1 %collective-permute-done.5 = bf16[2,4,128,12,64]{2,4,3,1,0:T(8,128)(2,1)S(1)} collective-permute-done((bf16[2,4,128,12,64]{2,4,3,1,0:T(8,128)(2,1)S(1)}, bf16[2,4,128,12,64]{2,4,3,1,0:T(8,128)(2,1)S(1)}, u32[]{:S(2)}, u32[]{:S(2)}) %collective-permute-start.5) | collective-permute-done | bytes 1572896 | tf_op jit(solution)/shard_map/ppermute | solution.py:18
  246.2 14.2 %collective-permute-done.6 = bf16[2,4,128,12,64]{2,4,3,1,0:T(8,128)(2,1)S(1)} collective-permute-done((bf16[2,4,128,12,64]{2,4,3,1,0:T(8,128)(2,1)S(1)}, bf16[2,4,128,12,64]{2,4,3,1,0:T(8,128)(2,1)S(1)}, u32[]{:S(2)}, u32[]{:S(2)}) %collective-permute-start.6) | collective-permute-done | bytes 1572896 | tf_op jit(solution)/shard_map/ppermute | solution.py:18
  263.6 4.8 convolution_bitcast_fusion
  268.4 8.0 %copy.246 = f32[768,2304]{1,0:T(8,128)} copy(f32[768,2304]{0,1:T(8,128)} %convolution_bitcast_fusion) | data formatting | bytes 14155776
  281.9 99.1 %reduce-scatter.9.cloned.1.call-done = f32[96,3072]{1,0:T(8,128)} async-done(((f32[768,3072]{1,0:T(8,128)}), f32[96,3072]{1,0:T(8,128)}) %reduce-scatter.9.cloned.1.call-update) | async-done | bytes 1179664 | tf_op jit(solution)/shard_map/reduce_scatter | solution.py:266
  381.0 2.2 convert_element_type.266
  383.1 163.9 %reduce-scatter.11.cloned.1.call-done = f32[384,768]{1,0:T(8,128)} async-done(((f32[3072,768]{1,0:T(8,128)}), f32[384,768]{1,0:T(8,128)}) %reduce-scatter.11.cloned.1.call-update) | async-done | bytes 1179664 | tf_op jit(solution)/shard_map/reduce_scatter | solution.py:268
  549.2 129.6 %reduce-scatter.13.cloned.1.call-done = f32[96,2304]{1,0:T(8,128)} async-done(((f32[768,2304]{1,0:T(8,128)}), f32[96,2304]{1,0:T(8,128)}) %reduce-scatter.13.cloned.1.call-update) | async-done | bytes 884752
  678.7 2.2 copy.247
  683.7 36.8 %all-reduce.8 = (bf16[1536]{0:T(1024)(128)(2,1)}, bf16[768]{0:T(1024)(128)(2,1)}, bf16[768]{0:T(1024)(128)(2,1)}, bf16[768]{0:T(1024)(128)(2,1)}, bf16[3072]{0:T...) all-reduce(f32[1536]{0:T(1024)S(1)} %pad_maximum_fusion.2, ...), channel_id=3, replica_groups=mesh['dp'=8,'blk'=4] {'dp'}, use_global_device_ids=true, to_apply=%region_23.24.clone | all-reduce | flops 9216 | bytes 55296
  728.9 6.9 all-reduce.9
  744.5 5.0 add_convert_fusion
  749.6 2.2 copy.225
  753.4 2.2 convert_element_type.267
  755.6 2.2 convert_element_type.272
  (225 shorter events, 79.9 us)
Async XLA Ops:
  7.2 273.1 %reduce-scatter.7.cloned.1.call-start = ((), (), s32[]{:S(2)}) async-start(), calls=%async_computation.4 | async-start | bytes 2654208 | tf_op jit(solution)/shard_map/reduce_scatter | solution.py:262
  31.7 26.8 %copy-start.49 = (s32[4,8]{1,0:T(4,128)S(1)}, s32[4,8]{1,0:T(4,128)}, u32[]{:S(2)}) copy-start(s32[4,8]{1,0:T(4,128)} %param.16) | copy-start | bytes 388
  33.0 20.6 %collective-permute-start = (bf16[2,4,128,12,64]{2,4,3,1,0:T(8,128)(2,1)S(1)}, bf16[2,4,128,12,64]{2,4,3,1,0:T(8,128)(2,1)}, u32[]{:S(2)}, u32[]{:S(2)}) collective-permute-start(bf16[2,4,128,12,64]{2,4,3,1,0:T(8,128)(2,1)S(1)} %pad_maximum_fusion), channel_id=1, source_target_pairs={{3,0},{0,1},{1,2},{2,3},{7,4},{4,5},{5,6},{6,7},{11,8},{8,9},{9,10... | collective-permute-start | bytes 4718600 | tf_op jit(solution)/shard_map/ppermute | solution.py:18
  53.6 20.2 %collective-permute-start.1 = (bf16[2,4,128,12,64]{2,4,3,1,0:T(8,128)(2,1)}, bf16[2,4,128,12,64]{2,4,3,1,0:T(8,128)(2,1)}, u32[]{:S(2)}, u32[]{:S(2)}) collective-permute-start(bf16[2,4,128,12,64]{2,4,3,1,0:T(8,128)(2,1)} %collective-permute-done), channel_id=1, source_target_pairs={{3,0},{0,1},{1,2},{2,3},{7,4},{4,5},{5,6},{6,7},{11,8},{8,9},{9,10... | collective-permute-start | bytes 4718600 | tf_op jit(solution)/shard_map/ppermute | solution.py:18
  53.7 9.9 %copy-start.42 = (f32[768]{0:T(1024)S(1)}, f32[768]{0:T(1024)}, u32[]{:S(2)}) copy-start(f32[768]{0:T(1024)} %param.27) | copy-start | bytes 9220
  63.5 13.2 %copy-start.5 = (bf16[4,128,12,64]{1,0,3,2:T(4,128)(2,1)S(1)}, bf16[4,128,12,64]{1,0,3,2:T(4,128)(2,1)}, u32[]{:S(2)}) copy-start(bf16[4,128,12,64]{1,0,3,2:T(4,128)(2,1)} %reshape.226) | copy-start | bytes 2359300
  73.8 20.2 %collective-permute-start.2 = (bf16[2,4,128,12,64]{2,4,3,1,0:T(8,128)(2,1)}, bf16[2,4,128,12,64]{2,4,3,1,0:T(8,128)(2,1)S(1)}, u32[]{:S(2)}, u32[]{:S(2)}) collective-permute-start(bf16[2,4,128,12,64]{2,4,3,1,0:T(8,128)(2,1)} %collective-permute-done.1), channel_id=1, source_target_pairs={{3,0},{0,1},{1,2},{2,3},{7,4},{4,5},{5,6},{6,7},{11,8},{8,9},{9,10... | collective-permute-start | bytes 4718600 | tf_op jit(solution)/shard_map/ppermute | solution.py:18
  74.4 21.2 %copy-start.30 = (pred[4,128,128]{1,2,0:T(8,128)(4,1)}, pred[4,128,128]{1,2,0:T(8,128)(4,1)S(1)}, u32[]{:S(2)}) copy-start(pred[4,128,128]{1,2,0:T(8,128)(4,1)S(1)} %get-tuple-element.123) | copy-start | bytes 196612
  74.4 24.9 %copy-start.24 = (pred[4,128,128]{1,2,0:T(8,128)(4,1)}, pred[4,128,128]{1,2,0:T(8,128)(4,1)S(1)}, u32[]{:S(2)}) copy-start(pred[4,128,128]{1,2,0:T(8,128)(4,1)S(1)} %get-tuple-element.124) | copy-start | bytes 196612
  74.4 26.7 %copy-start.22 = (pred[4,128,128]{1,2,0:T(8,128)(4,1)}, pred[4,128,128]{1,2,0:T(8,128)(4,1)S(1)}, u32[]{:S(2)}) copy-start(pred[4,128,128]{1,2,0:T(8,128)(4,1)S(1)} %get-tuple-element.125) | copy-start | bytes 196612
  74.4 28.6 %copy-start.28 = (pred[4,128,128]{1,2,0:T(8,128)(4,1)}, pred[4,128,128]{1,2,0:T(8,128)(4,1)S(1)}, u32[]{:S(2)}) copy-start(pred[4,128,128]{1,2,0:T(8,128)(4,1)S(1)} %get-tuple-element.126) | copy-start | bytes 196612
  76.6 19.0 %copy-start.10 = (f32[4,12,128,128]{2,3,1,0:T(8,128)}, f32[4,12,128,128]{2,3,1,0:T(8,128)S(1)}, u32[]{:S(2)}) copy-start(f32[4,12,128,128]{2,3,1,0:T(8,128)S(1)} %get-tuple-element.134) | copy-start | bytes 9437188
  76.6 22.5 %copy-start.41 = (f32[4,12,128]{2,1,0:T(8,128)}, f32[4,12,128]{2,1,0:T(8,128)S(1)}, u32[]{:S(2)}) copy-start(f32[4,12,128]{2,1,0:T(8,128)S(1)} %get-tuple-element.133) | copy-start | bytes 73732
  79.2 20.1 %copy-start.3 = (f32[4,12,128,128]{2,3,1,0:T(8,128)}, f32[4,12,128,128]{2,3,1,0:T(8,128)S(1)}, u32[]{:S(2)}) copy-start(f32[4,12,128,128]{2,3,1,0:T(8,128)S(1)} %get-tuple-element.132) | copy-start | bytes 9437188
  81.7 19.3 %copy-start.1 = (f32[4,12,128,128]{2,3,1,0:T(8,128)}, f32[4,12,128,128]{2,3,1,0:T(8,128)S(1)}, u32[]{:S(2)}) copy-start(f32[4,12,128,128]{2,3,1,0:T(8,128)S(1)} %get-tuple-element.130) | copy-start | bytes 9437188
  81.7 13.2 %copy-start.21 = (bf16[4,128,12,64]{1,0,3,2:T(4,128)(2,1)S(1)}, bf16[4,128,12,64]{1,0,3,2:T(4,128)(2,1)}, u32[]{:S(2)}) copy-start(bf16[4,128,12,64]{1,0,3,2:T(4,128)(2,1)} %squeeze_stack_reshape.9) | copy-start | bytes 2359300
  94.0 9.0 %copy-start.34 = (bf16[2,4,128,12,64]{2,4,3,1,0:T(8,128)(2,1)}, bf16[2,4,128,12,64]{2,4,3,1,0:T(8,128)(2,1)S(1)}, u32[]{:S(2)}) copy-start(bf16[2,4,128,12,64]{2,4,3,1,0:T(8,128)(2,1)S(1)} %collective-permute-done.2) | copy-start | bytes 4718596
  94.8 8.2 %copy-start.8 = (f32[4,12,128,128]{2,3,1,0:T(8,128)}, f32[4,12,128,128]{2,3,1,0:T(8,128)S(1)}, u32[]{:S(2)}) copy-start(f32[4,12,128,128]{2,3,1,0:T(8,128)S(1)} %get-tuple-element.128) | copy-start | bytes 9437188
  94.8 4.4 copy-start.33
  94.9 6.2 copy-start.32
  94.9 8.2 %copy-start.36 = (f32[4,12,128]{2,1,0:T(8,128)}, f32[4,12,128]{2,1,0:T(8,128)S(1)}, u32[]{:S(2)}) copy-start(f32[4,12,128]{2,1,0:T(8,128)S(1)} %get-tuple-element.105) | copy-start | bytes 73732
  99.2 3.8 copy-start.39
  99.2 3.8 copy-start.40
  101.1 6.5 slice-start.2
  103.1 4.5 slice-start.3
  106.1 17.8 %slice-start = ((s8[4718592]{0:T(1024)(128)(4,1)}), s8[4194304]{0:T(1024)(128)(4,1)S(1)}, s32[]{:S(2)}) async-start(s8[4718592]{0:T(1024)(128)(4,1)} %bitcast.259), calls=%async_computation.9 | async-start | bytes 8388608
  107.0 32.0 %copy-start.14 = (f32[512,768]{1,0:T(8,128)}, f32[512,768]{1,0:T(8,128)S(1)}, u32[]{:S(2)}) copy-start(f32[512,768]{1,0:T(8,128)S(1)} %get-tuple-element.138) | copy-start | bytes 4718596
  107.6 31.4 %copy-start.44 = (f32[512]{0:T(512)}, f32[512]{0:T(512)S(1)}, u32[]{:S(2)}) copy-start(f32[512]{0:T(512)S(1)} %add_rsqrt_fusion.1) | copy-start | bytes 6148
  107.6 16.3 %slice-start.1 = ((s8[4718592]{0:T(1024)(128)(4,1)}), s8[524288]{0:T(1024)(128)(4,1)S(1)}, s32[]{:S(2)}) async-start(s8[4718592]{0:T(1024)(128)(4,1)} %bitcast.259), calls=%async_computation.10 | async-start | bytes 1048576
  107.6 16.3 %copy-start.53 = (f32[768]{0:T(1024)S(1)}, f32[768]{0:T(1024)}, u32[]{:S(2)}) copy-start(f32[768]{0:T(1024)} %param.26) | copy-start | bytes 9220
  129.9 5.4 copy-start.13
  143.5 237.5 %reduce-scatter.9.cloned.1.call-start = ((), (), s32[]{:S(2)}) async-start(), calls=%async_computation.5 | async-start | bytes 10616832 | tf_op jit(solution)/shard_map/reduce_scatter | solution.py:266
  152.5 394.6 %reduce-scatter.11.cloned.1.call-start = ((), (), s32[]{:S(2)}) async-start(), calls=%async_computation.6 | async-start | bytes 10616832 | tf_op jit(solution)/shard_map/reduce_scatter | solution.py:268
  161.2 517.5 %reduce-scatter.13.cloned.1.call-start = ((), (), s32[]{:S(2)}) async-start(), calls=%async_computation.7 | async-start | bytes 7962624
  172.5 3.8 copy-start.6
  172.5 5.0 copy-start.11
  178.9 19.9 %collective-permute-start.3 = (bf16[2,4,128,12,64]{2,4,3,1,0:T(8,128)(2,1)S(1)}, bf16[2,4,128,12,64]{2,4,3,1,0:T(8,128)(2,1)S(1)}, u32[]{:S(2)}, u32[]{:S(2)}) collective-permute-start(bf16[2,4,128,12,64]{2,4,3,1,0:T(8,128)(2,1)S(1)} %pad_maximum_fusion.1), channel_id=1, source_target_pairs={{3,0},{0,1},{1,2},{2,3},{7,4},{4,5},{5,6},{6,7},{11,8},{8,9},{9,10... | collective-permute-start | bytes 4718600 | tf_op jit(solution)/shard_map/ppermute | solution.py:18
  184.3 15.2 %copy-start.2 = (f32[4,12,128,128]{2,3,1,0:T(8,128)S(1)}, f32[4,12,128,128]{2,3,1,0:T(8,128)}, u32[]{:S(2)}) copy-start(f32[4,12,128,128]{2,3,1,0:T(8,128)} %copy-done.1) | copy-start | bytes 9437188
  184.3 15.2 %copy-start.23 = (pred[4,128,128]{1,2,0:T(8,128)(4,1)S(1)}, pred[4,128,128]{1,2,0:T(8,128)(4,1)}, u32[]{:S(2)}) copy-start(pred[4,128,128]{1,2,0:T(8,128)(4,1)} %copy-done.22) | copy-start | bytes 196612
  199.4 19.9 %collective-permute-start.4 = (bf16[2,4,128,12,64]{2,4,3,1,0:T(8,128)(2,1)S(1)}, bf16[2,4,128,12,64]{2,4,3,1,0:T(8,128)(2,1)S(1)}, u32[]{:S(2)}, u32[]{:S(2)}) collective-permute-start(bf16[2,4,128,12,64]{2,4,3,1,0:T(8,128)(2,1)S(1)} %fusion.16), channel_id=1, source_target_pairs={{3,0},{0,1},{1,2},{2,3},{7,4},{4,5},{5,6},{6,7},{11,8},{8,9},{9,10... | collective-permute-start | bytes 4718600 | tf_op jit(solution)/shard_map/ppermute | solution.py:18
  204.3 15.9 %copy-start.9 = (f32[4,12,128,128]{2,3,1,0:T(8,128)S(1)}, f32[4,12,128,128]{2,3,1,0:T(8,128)}, u32[]{:S(2)}) copy-start(f32[4,12,128,128]{2,3,1,0:T(8,128)} %copy-done.8) | copy-start | bytes 9437188
  204.3 15.9 %copy-start.29 = (pred[4,128,128]{1,2,0:T(8,128)(4,1)S(1)}, pred[4,128,128]{1,2,0:T(8,128)(4,1)}, u32[]{:S(2)}) copy-start(pred[4,128,128]{1,2,0:T(8,128)(4,1)} %copy-done.28) | copy-start | bytes 196612
  204.3 15.9 %copy-start.35 = (bf16[2,4,128,12,64]{2,4,3,1,0:T(8,128)(2,1)S(1)}, bf16[2,4,128,12,64]{2,4,3,1,0:T(8,128)(2,1)}, u32[]{:S(2)}) copy-start(bf16[2,4,128,12,64]{2,4,3,1,0:T(8,128)(2,1)} %copy-done.34) | copy-start | bytes 4718596
  219.9 20.1 %collective-permute-start.5 = (bf16[2,4,128,12,64]{2,4,3,1,0:T(8,128)(2,1)S(1)}, bf16[2,4,128,12,64]{2,4,3,1,0:T(8,128)(2,1)S(1)}, u32[]{:S(2)}, u32[]{:S(2)}) collective-permute-start(bf16[2,4,128,12,64]{2,4,3,1,0:T(8,128)(2,1)S(1)} %fusion.17), channel_id=1, source_target_pairs={{3,0},{0,1},{1,2},{2,3},{7,4},{4,5},{5,6},{6,7},{11,8},{8,9},{9,10... | collective-permute-start | bytes 4718600 | tf_op jit(solution)/shard_map/ppermute | solution.py:18
  223.9 16.7 %copy-start.20 = (bf16[4,128,12,64]{1,0,3,2:T(4,128)(2,1)S(1)}, bf16[4,128,12,64]{1,0,3,2:T(4,128)(2,1)}, u32[]{:S(2)}) copy-start(bf16[4,128,12,64]{1,0,3,2:T(4,128)(2,1)} %squeeze_stack_reshape.8) | copy-start | bytes 2359300
  240.6 19.9 %collective-permute-start.6 = (bf16[2,4,128,12,64]{2,4,3,1,0:T(8,128)(2,1)S(1)}, bf16[2,4,128,12,64]{2,4,3,1,0:T(8,128)(2,1)S(1)}, u32[]{:S(2)}, u32[]{:S(2)}) collective-permute-start(bf16[2,4,128,12,64]{2,4,3,1,0:T(8,128)(2,1)S(1)} %fusion.18), channel_id=1, source_target_pairs={{3,0},{0,1},{1,2},{2,3},{7,4},{4,5},{5,6},{6,7},{11,8},{8,9},{9,10... | collective-permute-start | bytes 4718600 | tf_op jit(solution)/shard_map/ppermute | solution.py:18
  276.5 473.1 %all-reduce.13.cloned.1.call-start = ((), (), s32[]{:S(2)}) async-start(), calls=%async_computation.8 | async-start | bytes 3833856 | tf_op jit(solution)/shard_map/psum | solution.py:287
  383.1 300.5 %copy-start.43 = (f32[768]{0:T(1024)S(1)}, f32[768]{0:T(1024)}, u32[]{:S(2)}) copy-start(f32[768]{0:T(1024)} %get-tuple-element.76) | copy-start | bytes 9220
  (25 other events, 50.4 us)
Sparse Core Ops, SparseCore 0:
  143.6 71.2 reduce-scatter.6
  218.5 162.4 reduce-scatter.8
  384.6 162.4 reduce-scatter.10
  550.6 128.1 reduce-scatter.12
  682.5 48.2 all-reduce.12
where the time goes:
time: 772 us; the launch traced here: 764 us
  waiting for transfers between devices  493 us (64%)
  matrix products  104 us (13%)
  local copies, waits for them, and re-layouts  62.5 us (8%)
  blocking collectives  43.7 us (6%)
  other arithmetic  42.6 us (6%)
  between operations  17 us (2%)
    reduce_scatter x1, waiting for transfers between devices, shards(): lax.psum_scatter(grad_w_down, 'dp', scatter_dimension=0, tiled=True)  164 us
    unnamed x6, waiting for transfers between devices  130 us
    ppermute x7, waiting for transfers between devices, from_behind(): return lax.ppermute(block, axis, route)  100 us
    reduce_scatter x1, waiting for transfers between devices, shards(): lax.psum_scatter(grad_w_up, 'dp', scatter_dimension=0, tiled=True)  99.1 us
    unnamed x1, blocking collectives  36.8 us
    unnamed x136, local copies, waits for them, and re-layouts  29 us
    dot_general x4, matrix products, contract_rows(): lax.dot_general(left, right, (((0,), (0,)), ((), ())), preferred_element_...  24.7 us
    dot_general x4, matrix products, times_transposed(): lax.dot_general(left, right, (((1,), (1,)), ((), ())), preferred_element_...  17.6 us
  transfers between devices with their start and end apart: 12, of which 10 were waited for; matrix products, arithmetic and copies ran while one was open for 16% of the time, Pallas kernels for 0%

commit v1 on v0

v1 whole, which is shorter than its diff:
```python
import functools
import math

import jax
import jax.numpy as jnp
from jax import lax
from jax.experimental import pallas as pl
from jax.experimental.pallas import tpu as pltpu
from jax.sharding import PartitionSpec as P

HEADS = 12
EPSILON = 1e-12
MASKED = -1e30
VMEM_BYTES = 56 * 2**20

f32 = jnp.float32
bf16 = jnp.bfloat16
NN = (((1,), (0,)), ((), ()))
NT = (((1,), (1,)), ((), ()))
TN = (((0,), (0,)), ((), ()))


def dot(left, right, dims=NN):
    return lax.dot_general(left, right, dims, preferred_element_type=f32)


def whole(shape):
    return pl.BlockSpec(shape, lambda i: (0,) * len(shape))


def params():
    return pltpu.CompilerParams(vmem_limit_bytes=VMEM_BYTES)


def cost(flops, bytes_accessed, transcendentals=0):
    return pl.CostEstimate(
        flops=flops, bytes_accessed=bytes_accessed, transcendentals=transcendentals
    )


def column_sum(values):
    return jnp.sum(values, axis=0, keepdims=True)


def row_mean(values):
    return jnp.mean(values, axis=-1, keepdims=True)


def normalize(inputs):
    centre = inputs - row_mean(inputs)
    inverse = lax.rsqrt(row_mean(centre * centre) + EPSILON)
    return centre * inverse, inverse


def normalize_back(scaled, normed, inverse):
    return inverse * (scaled - row_mean(scaled) - normed * row_mean(scaled * normed))


def attend_kernel(
    row_ref, x0, x1, x2, x3, wq, wk, wv, bq, bv, wo, bo,
    q_out, k_out, v_out, prob_out, context_out, normed_out, inverse_out,
    tokens, mask, total, *, steps, slots, pages, head_width,
):
    step = pl.program_id(0)
    count = tokens.shape[0]
    wide = wq.shape[1]

    @pl.when(step == 0)
    def _():
        for i, block in enumerate((x0, x1, x2, x3)):
            tokens[i * slots : (i + 1) * slots, :] = block[...]
        position = row_ref[pages]

        def page_of(dim):
            at = lax.broadcasted_iota(jnp.int32, (count, count), dim)
            slot = ((at // slots) ^ position) * slots + at % slots
            page = jnp.zeros((count, count), jnp.int32)
            end = 0
            for c in range(pages):
                end = end + row_ref[c]
                page = page + (slot >= end).astype(jnp.int32)
            return page

        mask[...] = jnp.where(page_of(0) == page_of(1), 0.0, MASKED)
        total[...] = jnp.zeros_like(total)

    x = tokens[...]
    q = (dot(x, wq[...]) + bq[...]).astype(bf16)
    k = dot(x, wk[...]).astype(bf16)
    v = (dot(x, wv[...]) + bv[...]).astype(bf16)
    q_out[...] = q
    k_out[...] = k
    v_out[...] = v
    scaled_q = q * jnp.asarray(1.0 / math.sqrt(head_width), bf16)
    head = lax.broadcasted_iota(jnp.int32, (count, wide), 1) // head_width
    none = jnp.zeros((count, wide), bf16)
    context = jnp.zeros((count, wide), f32)
    for h in range(wide // head_width):
        scores = dot(k, jnp.where(head == h, scaled_q, none), NT) + mask[...]
        powers = jnp.exp(scores - jnp.max(scores, axis=0, keepdims=True))
        probs = (powers * (1.0 / jnp.sum(powers, axis=0, keepdims=True))).astype(bf16)
        prob_out[h] = probs
        context = context + dot(probs, jnp.where(head == h, v, none), TN)
    context = context.astype(bf16)
    context_out[...] = context
    total[...] += dot(context, wo[...])

    @pl.when(step == steps - 1)
    def _():
        normed, inverse = normalize(tokens[...].astype(f32) + (total[...] + bo[...]))
        normed_out[...] = normed
        inverse_out[...] = inverse


def attend(row, blocks, w_qkv, bias_qv, w_out, bias_out):
    slots, width = blocks[0].shape
    count = slots * len(blocks)
    head_width = width // HEADS
    wide = 4 * head_width
    steps = width // wide

    def weight(part):
        return pl.BlockSpec((width, wide), lambda i: (0, part * steps + i))

    def shift(part):
        return pl.BlockSpec((1, wide), lambda i: (0, part * steps + i))

    columns = pl.BlockSpec((count, wide), lambda i: (0, i))
    narrow = jax.ShapeDtypeStruct((count, width), bf16)
    return pl.pallas_call(
        functools.partial(
            attend_kernel,
            steps=steps, slots=slots, pages=row.shape[0] - 1, head_width=head_width,
        ),
        grid=(steps,),
        in_specs=[pl.BlockSpec(memory_space=pltpu.SMEM)]
        + [whole((slots, width))] * 4
        + [weight(0), weight(1), weight(2), shift(0), shift(1)]
        + [pl.BlockSpec((wide, width), lambda i: (i, 0)), whole((1, width))],
        out_specs=[
            columns, columns, columns,
            pl.BlockSpec((4, count, count), lambda i: (i, 0, 0)),
            columns, whole((count, width)), whole((count, 1)),
        ],
        out_shape=[
            narrow, narrow, narrow,
            jax.ShapeDtypeStruct((HEADS, count, count), bf16),
            narrow,
            jax.ShapeDtypeStruct((count, width), f32),
            jax.ShapeDtypeStruct((count, 1), f32),
        ],
        scratch_shapes=[
            pltpu.VMEM((count, width), bf16),
            pltpu.VMEM((count, count), f32),
            pltpu.VMEM((count, width), f32),
        ],
        compiler_params=params(),
        cost_estimate=cost(8 * count * width * width, 40 * 2**20),
        name="attend",
    )(row, *blocks, w_qkv, w_qkv, w_qkv, bias_qv[None], bias_qv[None], w_out, bias_out[None])


def feed_kernel(
    normed_one, gain_one, shift_one, w_up, b_up, w_down, b_down, gain_two, shift_two, cotangent,
    active_out, slope_out, result_out, lowered_out, sum_out, first_out, vector_out,
    total, *, steps,
):
    step = pl.program_id(0)

    @pl.when(step == 0)
    def _():
        first_out[...] = (normed_one[...] * gain_one[...] + shift_one[...]).astype(bf16)
        total[...] = jnp.zeros_like(total)

    raised = dot(first_out[...], w_up[...]) + b_up[...]
    cumulative = 0.5 * (1.0 + lax.erf(raised * (1.0 / math.sqrt(2.0))))
    activated = (raised * cumulative).astype(bf16)
    active_out[...] = activated
    bell = jnp.exp(-0.5 * raised * raised) * (1.0 / math.sqrt(2.0 * math.pi))
    slope_out[...] = (cumulative + raised * bell).astype(bf16)
    total[...] += dot(activated, w_down[...])

    @pl.when(step == steps - 1)
    def _():
        first_norm = normed_one[...] * gain_one[...] + shift_one[...]
        normed, inverse = normalize(first_norm + (total[...] + b_down[...]))
        result_out[...] = (normed * gain_two[...] + shift_two[...]).astype(bf16)
        upstream = cotangent[...].astype(f32)
        grad_sum = normalize_back(upstream * gain_two[...], normed, inverse)
        lowered = grad_sum.astype(bf16)
        sum_out[...] = grad_sum
        lowered_out[...] = lowered
        vector_out[0:1, :] = column_sum(upstream * normed)
        vector_out[1:2, :] = column_sum(upstream)
        vector_out[2:3, :] = column_sum(lowered.astype(f32))


def feed(normed, gain_one, shift_one, w_up, b_up, w_down, b_down, gain_two, shift_two, cotangent):
    count, width = normed.shape
    hidden = w_up.shape[1]
    steps = 4
    wide = hidden // steps
    columns = pl.BlockSpec((count, wide), lambda i: (0, i))
    vector = whole((1, width))
    narrow = jax.ShapeDtypeStruct((count, width), bf16)
    return pl.pallas_call(
        functools.partial(feed_kernel, steps=steps),
        grid=(steps,),
        in_specs=[
            whole((count, width)), vector, vector,
            pl.BlockSpec((width, wide), lambda i: (0, i)),
            pl.BlockSpec((1, wide), lambda i: (0, i)),
            pl.BlockSpec((wide, width), lambda i: (i, 0)),
            vector, vector, vector, whole((count, width)),
        ],
        out_specs=[columns, columns] + [whole((count, width))] * 4 + [whole((8, width))],
        out_shape=[
            jax.ShapeDtypeStruct((count, hidden), bf16),
            jax.ShapeDtypeStruct((count, hidden), bf16),
            narrow, narrow,
            jax.ShapeDtypeStruct((count, width), f32),
            narrow,
            jax.ShapeDtypeStruct((8, width), f32),
        ],
        scratch_shapes=[pltpu.VMEM((count, width), f32)],
        compiler_params=params(),
        cost_estimate=cost(4 * count * width * hidden, 40 * 2**20),
        name="feed",
    )(
        normed, gain_one[None], shift_one[None], w_up, b_up[None], w_down, b_down[None],
        gain_two[None], shift_two[None], cotangent,
    )


def feed_back_kernel(
    lowered, active, slope, w_down, w_up, first, sum_two, normed_one, inverse_one, gain_one,
    down_out, up_out, bias_out, attended_out, sum_out, vector_out,
    turned, total, *, steps,
):
    step = pl.program_id(0)

    @pl.when(step == 0)
    def _():
        turned[...] = first[...].T
        total[...] = sum_two[...]

    down_out[...] = dot(active[...], lowered[...], TN).astype(bf16)
    raised = (dot(lowered[...], w_down[...], NT) * slope[...].astype(f32)).astype(bf16)
    bias_out[...] = column_sum(raised.astype(f32))
    up_out[...] = dot(turned[...], raised).astype(bf16)
    total[...] += dot(raised, w_up[...], NT)

    @pl.when(step == steps - 1)
    def _():
        upstream = total[...]
        normed = normed_one[...]
        grad_sum = normalize_back(upstream * gain_one[...], normed, inverse_one[...])
        attended = grad_sum.astype(bf16)
        sum_out[...] = grad_sum
        attended_out[...] = attended
        vector_out[0:1, :] = column_sum(upstream * normed)
        vector_out[1:2, :] = column_sum(upstream)
        vector_out[2:3, :] = column_sum(attended.astype(f32))


def feed_back(lowered, active, slope, w_down, w_up, first, sum_two, normed, inverse, gain_one):
    count, width = normed.shape
    hidden = w_up.shape[1]
    steps = 4
    wide = hidden // steps
    columns = pl.BlockSpec((count, wide), lambda i: (0, i))
    return pl.pallas_call(
        functools.partial(feed_back_kernel, steps=steps),
        grid=(steps,),
        in_specs=[
            whole((count, width)), columns, columns,
            pl.BlockSpec((wide, width), lambda i: (i, 0)),
            pl.BlockSpec((width, wide), lambda i: (0, i)),
            whole((count, width)), whole((count, width)), whole((count, width)),
            whole((count, 1)), whole((1, width)),
        ],
        out_specs=[
            pl.BlockSpec((wide, width), lambda i: (i, 0)),
            pl.BlockSpec((None, width, wide), lambda i: (i, 0, 0)),
            pl.BlockSpec((1, wide), lambda i: (0, i)),
            whole((count, width)), whole((count, width)), whole((8, width)),
        ],
        out_shape=[
            jax.ShapeDtypeStruct((hidden, width), bf16),
            jax.ShapeDtypeStruct((steps, width, wide), bf16),
            jax.ShapeDtypeStruct((1, hidden), f32),
            jax.ShapeDtypeStruct((count, width), bf16),
            jax.ShapeDtypeStruct((count, width), f32),
            jax.ShapeDtypeStruct((8, width), f32),
        ],
        scratch_shapes=[pltpu.VMEM((width, count), bf16), pltpu.VMEM((count, width), f32)],
        compiler_params=params(),
        cost_estimate=cost(8 * count * width * hidden, 50 * 2**20),
        name="feed_back",
    )(lowered, active, slope, w_down, w_up, first, sum_two, normed, inverse, gain_one[None])


def attend_back_kernel(
    x0, x1, x2, x3, attended, sum_one, context, prob, q_ref, k_ref, v_ref, wq, wk, wv, wo,
    pieces_out, tokens_out, bias_q, bias_v,
    turned, total, *, steps, slots, head_width,
):
    step = pl.program_id(0)
    count = attended.shape[0]
    wide = wq.shape[1]

    @pl.when(step == 0)
    def _():
        for i, block in enumerate((x0, x1, x2, x3)):
            turned[:, i * slots : (i + 1) * slots] = block[...].T
        total[...] = sum_one[...]

    grad_context = dot(attended[...], wo[...], NT).astype(bf16)
    grad_out = dot(context[...], attended[...], TN).astype(bf16)
    scaling = jnp.asarray(1.0 / math.sqrt(head_width), bf16)
    scaled_q = q_ref[...] * scaling
    scaled_k = k_ref[...] * scaling
    v = v_ref[...]
    head = lax.broadcasted_iota(jnp.int32, (count, wide), 1) // head_width
    none = jnp.zeros((count, wide), bf16)
    grad_q = jnp.zeros((count, wide), f32)
    grad_k = grad_q
    grad_v = grad_q
    for h in range(wide // head_width):
        mine = head == h
        probs = prob[h]
        wider = probs.astype(f32)
        upstream = jnp.where(mine, grad_context, none)
        weighted = wider * dot(v, upstream, NT)
        balance = jnp.sum(weighted, axis=0, keepdims=True)
        grad_scores = (weighted - wider * balance).astype(bf16)
        grad_v = grad_v + dot(probs, upstream)
        grad_k = grad_k + dot(grad_scores, jnp.where(mine, scaled_q, none))
        grad_q = grad_q + dot(grad_scores, jnp.where(mine, scaled_k, none), TN)
    grad_q = grad_q.astype(bf16)
    grad_k = grad_k.astype(bf16)
    grad_v = grad_v.astype(bf16)
    bias_q[...] = column_sum(grad_q.astype(f32))
    bias_v[...] = column_sum(grad_v.astype(f32))
    x_turned = turned[...]
    pieces = (
        dot(x_turned, grad_q).astype(bf16),
        dot(x_turned, grad_k).astype(bf16),
        dot(x_turned, grad_v).astype(bf16),
    )
    for s in range(steps):

        @pl.when(step == s)
        def _():
            for i, piece in enumerate(pieces):
                pieces_out[i, :, s * wide : (s + 1) * wide] = piece
            pieces_out[3, s * wide : (s + 1) * wide, :] = grad_out

    total[...] += (
        dot(grad_q, wq[...], NT) + dot(grad_k, wk[...], NT) + dot(grad_v, wv[...], NT)
    )

    @pl.when(step == steps - 1)
    def _():
        tokens_out[...] = total[...].astype(bf16)


def attend_back(blocks, attended, sum_one, context, prob, q, k, v, w_qkv, w_out):
    slots, width = blocks[0].shape
    count = slots * len(blocks)
    head_width = width // HEADS
    wide = 4 * head_width
    steps = width // wide

    def weight(part):
        return pl.BlockSpec((width, wide), lambda i: (0, part * steps + i))

    columns = pl.BlockSpec((count, wide), lambda i: (0, i))
    vector = pl.BlockSpec((1, wide), lambda i: (0, i))
    return pl.pallas_call(
        functools.partial(attend_back_kernel, steps=steps, slots=slots, head_width=head_width),
        grid=(steps,),
        in_specs=[whole((slots, width))] * 4
        + [
            whole((count, width)), whole((count, width)), columns,
            pl.BlockSpec((4, count, count), lambda i: (i, 0, 0)),
            columns, columns, columns, weight(0), weight(1), weight(2),
            pl.BlockSpec((wide, width), lambda i: (i, 0)),
        ],
        out_specs=[whole((4, width, width)), whole((count, width)), vector, vector],
        out_shape=[
            jax.ShapeDtypeStruct((4, width, width), bf16),
            jax.ShapeDtypeStruct((count, width), bf16),
            jax.ShapeDtypeStruct((1, width), f32),
            jax.ShapeDtypeStruct((1, width), f32),
        ],
        scratch_shapes=[pltpu.VMEM((width, count), bf16), pltpu.VMEM((count, width), f32)],
        compiler_params=params(),
        cost_estimate=cost(16 * count * width * width, 40 * 2**20),
        name="attend_back",
    )(*blocks, attended, sum_one, context, prob, q, k, v, w_qkv, w_qkv, w_qkv, w_out)


def swap(block, axis, bit):
    return lax.ppermute(block, axis, [(i, i ^ bit) for i in range(lax.axis_size(axis))])


def pick(block, index, dim=0):
    return lax.dynamic_index_in_dim(block, index, dim, keepdims=False)


def own_bit(axis, bit):
    return (lax.axis_index(axis) // bit) % 2


def added(terms):
    total = terms[0].astype(f32)
    for term in terms[1:]:
        total = total + term.astype(f32)
    return total


def reduce_pieces(piece, order):
    dims = [("blk", 2), ("blk", 1)] + [("dp", 1 << i) for i in reversed(range(dp_bits()))]
    terms = [piece]
    for stage in order:
        at = dims.index(stage)
        dims.pop(at)
        mine = own_bit(*stage)
        sent = added([pick(t, 1 - mine, at) for t in terms]).astype(bf16)
        terms = [pick(t, mine, at) for t in terms] + [swap(sent, *stage)]
    return added(terms).astype(bf16)


def dp_bits():
    return lax.axis_size("dp").bit_length() - 1


def spread(piece):
    position = lax.axis_index("blk")
    across = swap(piece, "blk", 2)
    pair = jnp.stack([piece, across])
    other = swap(pair, "blk", 1)
    every = jnp.stack([pair, other], axis=1)
    every = every.reshape((4,) + piece.shape)
    return [pick(every, position ^ i) for i in range(4)]


def shards(
    tokens, lengths, w_qkv, bias_qv, w_out, bias_out, norm1_gain, norm1_bias, w_up, bias_up,
    w_down, bias_down, norm2_gain, norm2_bias, cotangent,
):
    rows, slots, width = tokens.shape
    hidden = w_up.shape[1]
    shares = lax.axis_size("dp")
    position = lax.axis_index("blk")
    group = lax.axis_index("dp")

    def gather_row(array):
        return [pick(array, position)] + [
            swap(pick(array, position ^ i), "blk", i) for i in range(1, rows)
        ]

    def scatter_row(array):
        parts = array.reshape(rows, slots, width)
        parts = jnp.stack([parts[0]] + [swap(parts[i], "blk", i) for i in range(1, rows)])
        return jnp.stack([pick(parts, position ^ i) for i in range(rows)])

    row = jnp.concatenate([pick(lengths, position), position[None].astype(jnp.int32)])
    blocks = gather_row(tokens)
    cotangent_row = jnp.concatenate(gather_row(cotangent))
    q, k, v, prob, context, normed, inverse = attend(row, blocks, w_qkv, bias_qv, w_out, bias_out)
    active, slope, outputs, lowered, sum_two, first, vector_two = feed(
        normed, norm1_gain, norm1_bias, w_up, bias_up, w_down, bias_down,
        norm2_gain, norm2_bias, cotangent_row,
    )
    grad_down, grad_up, grad_bias_up, attended, sum_one, vector_one = feed_back(
        lowered, active, slope, w_down, w_up, first, sum_two, normed, inverse, norm1_gain
    )
    pieces, grad_tokens, grad_bias_q, grad_bias_v = attend_back(
        blocks, attended, sum_one, context, prob, q, k, v, w_qkv, w_out
    )

    bits = dp_bits()
    halves = (2,) * bits
    share = width // shares
    dp_dims = [("dp", 1 << i) for i in range(bits)]
    turns = [("blk", 2)] + dp_dims[:2]
    rest = dp_dims[2:]
    core = [("blk", 1)]

    def turned(first_turn):
        return core + turns[first_turn:] + turns[:first_turn] + rest

    down_piece = jnp.moveaxis(
        grad_down.reshape(shares, 4, hidden // shares // 4, width), 1, 0
    ).reshape((2, 2) + halves + (hidden // shares // 4, width))
    down = reduce_pieces(down_piece, turned(0))
    up = reduce_pieces(grad_up.reshape((2, 2) + halves + (share, hidden // 4)), turned(1))
    qkv = reduce_pieces(pieces.reshape((2, 2) + halves + (share, width)), turned(2))

    vectors = jnp.concatenate(
        [grad_bias_q, grad_bias_v, vector_one[:3], vector_two[:3], grad_bias_up.reshape(-1, width)]
    )
    for axis, bit in core + turns + rest:
        vectors = vectors + swap(vectors, axis, bit)

    def own_share(vector):
        flat = vector.reshape(-1)
        size = flat.shape[0] // shares
        return lax.dynamic_slice_in_dim(flat, group * size, size)

    down = jnp.concatenate(spread(down)).astype(f32)
    up = jnp.concatenate(spread(up), axis=1).astype(f32)
    grad_q, grad_k, grad_v, grad_out = spread(qkv)
    return (
        scatter_row(outputs),
        scatter_row(grad_tokens),
        jnp.concatenate([grad_q, grad_k, grad_v], axis=1).astype(f32),
        own_share(vectors[0:2]),
        grad_out.astype(f32),
        own_share(vectors[4]),
        own_share(vectors[2]),
        own_share(vectors[3]),
        up,
        own_share(vectors[8:]),
        down,
        own_share(vectors[7]),
        own_share(vectors[5]),
        own_share(vectors[6]),
    )


def solution(mesh):
    row_spec = P("dp", "blk", None)
    in_specs = (row_spec, P("dp", None)) + (P(),) * 12 + (row_spec,)
    wide, flat = P("dp", None), P("dp")
    out_specs = (
        row_spec, row_spec, wide, flat, wide, flat, flat, flat, wide, flat, wide, flat, flat, flat,
    )
    return jax.shard_map(shards, mesh=mesh, in_specs=in_specs, out_specs=out_specs, check_vma=False)
```

time: 772 us -> 232 us (0.30)
  waiting for transfers between devices: 493 us -> 56.4 us
  matrix products: 104 us -> 0 us
  Pallas kernels: 0 us -> 71.1 us
  blocking collectives: 43.7 us -> 0 us
  starting transfers between devices: 1.45 us -> 43.4 us
  local copies, waits for them, and re-layouts: 62.5 us -> 28.2 us
  between operations: 17 us -> 1.22 us
  other arithmetic: 42.6 us -> 31.1 us
    reduce_scatter x3 -> x0, waiting for transfers between devices: 263 us -> none  [the longest x1 164 us: shards(): lax.psum_scatter(grad_w_down, 'dp', scatter_dimension=0, tiled=True)]
    unnamed x6 -> x0, waiting for transfers between devices: 130 us -> none
    dot_general x36 -> x0, matrix products: 104 us -> none  [the longest x4 24.7 us: contract_rows(): lax.dot_general(left, right, (((0,), (0,)), ((), ())), preferred_element_...]
    pallas_call x0 -> x4, Pallas kernels: none -> 71.1 us  [the longest x1 23 us: attend_back(): pl.pallas_call(functools.partial(attend_back_kernel, steps=steps, slots=s...]
    ppermute x7 -> x38, waiting for transfers between devices: 100 us -> 56.4 us  [swap(): lax.ppermute(block, axis, [(i, i ^ bit) for i in range(lax.axis_size(axis...]
    ppermute x7 -> x38, starting transfers between devices: 1.25 us -> 43.4 us  [swap(): lax.ppermute(block, axis, [(i, i ^ bit) for i in range(lax.axis_size(axis...]
    unnamed x1 -> x0, blocking collectives: 36.8 us -> none
    unnamed x136 -> x54, local copies, waits for them, and re-layouts: 29 us -> 0.79 us
  transfers between devices with their start and end apart: 12 -> 38, of which waited for: 10 -> 16; matrix products, arithmetic and copies ran while one was open for 16% -> 21% of each run, Pallas kernels for 0% -> 10%
where the time goes in v1:
time: 232 us
  Pallas kernels  71.1 us (31%)
  waiting for transfers between devices  56.4 us (24%)
  starting transfers between devices  43.4 us (19%)
  other arithmetic  31.1 us (13%)
  local copies, waits for them, and re-layouts  28.2 us (12%)
    ppermute x38, waiting for transfers between devices, swap(): lax.ppermute(block, axis, [(i, i ^ bit) for i in range(lax.axis_size(axis...  56.4 us
    ppermute x38, starting transfers between devices, swap(): lax.ppermute(block, axis, [(i, i ^ bit) for i in range(lax.axis_size(axis...  43.4 us
    pallas_call x1, Pallas kernels, attend_back(): pl.pallas_call(functools.partial(attend_back_kernel, steps=steps, slots=s...  23 us
    pallas_call x1, Pallas kernels, feed_back(): pl.pallas_call(functools.partial(feed_back_kernel, steps=steps), grid=(st...  18.5 us
    convert_element_type x12, other arithmetic, reduce_pieces(): sent = added([pick(t, 1 - mine, at) for t in terms]).astype(bf16)  18 us
    pallas_call x1, Pallas kernels, attend(): pl.pallas_call(functools.partial(attend_kernel, steps=steps, slots=slots,...  14.8 us
    pallas_call x1, Pallas kernels, feed(): pl.pallas_call(functools.partial(feed_kernel, steps=steps), grid=(steps,)...  14.8 us
    squeeze x7, local copies, waits for them, and re-layouts, pick(): return lax.dynamic_index_in_dim(block, index, dim, keepdims=False)  10.4 us
  transfers between devices with their start and end apart: 38, of which 16 were waited for; matrix products, arithmetic and copies ran while one was open for 21% of the time, Pallas kernels for 10%

profile of v1, /device:TPU:0, one launch (start us, length us, event | category | flops | bytes accessed | tf_op | source)
XLA Modules:
  0.0 231.5 jit_solution(17955287101592632241)
XLA Ops:
  0.8 1.3 dynamic-slice_bitcast_fusion.4
  3.4 2.6 %collective-permute-start.2 = (bf16[128,768]{1,0:T(8,128)(2,1)S(1)}, bf16[128,768]{1,0:T(8,128)(2,1)S(1)}, u32[]{:S(2)}, u32[]{:S(2)}) collective-permute-start(bf16[128,768]{1,0:T(8,128)(2,1)S(1)} %get-tuple-element.82), channel_id=1, source_target_pairs={{0,3},{1,2},{2,1},{3,0},{4,7},{5,6},{6,5},{7,4},{8,11},{9,10},{10,... | collective-permute-start | bytes 589832 | tf_op jit(solution)/shard_map/ppermute | solution.py:405
  6.0 2.1 collective-permute-start.4
  12.9 2.5 %collective-permute-done.5 = bf16[128,768]{1,0:T(8,128)(2,1)S(1)} collective-permute-done((bf16[128,768]{1,0:T(8,128)(2,1)S(1)}, bf16[128,768]{1,0:T(8,128)(2,1)S(1)}, u32[]{:S(2)}, u32[]{:S(2)}) %collective-permute-start.5) | collective-permute-done | bytes 196640 | tf_op jit(solution)/shard_map/ppermute | solution.py:405
  15.4 4.6 %collective-permute-done.4 = bf16[128,768]{1,0:T(8,128)(2,1)S(1)} collective-permute-done((bf16[128,768]{1,0:T(8,128)(2,1)S(1)}, bf16[128,768]{1,0:T(8,128)(2,1)S(1)}, u32[]{:S(2)}, u32[]{:S(2)}) %collective-permute-start.4) | collective-permute-done | bytes 196640 | tf_op jit(solution)/shard_map/ppermute | solution.py:405
  21.0 3.1 %collective-permute-done.1.x2 = bf16[128,768]{1,0:T(8,128)(2,1)S(1)} collective-permute-done((bf16[128,768]{1,0:T(8,128)(2,1)S(1)}, bf16[128,768]{1,0:T(8,128)(2,1)S(1)}, u32[]{:S(2)}, u32[]{:S(2)}) %collective-permute-start.1) | collective-permute-done | bytes 196640 | tf_op jit(solution)/shard_map/ppermute | solution.py:405
  24.8 14.8 %attend.1 = (bf16[512,768]{1,0:T(8,128)(2,1)}, bf16[512,768]{1,0:T(8,128)(2,1)}, bf16[512,768]{1,0:T(8,128)(2,1)}, bf16[12,512,512]{2,1,0:T(8,128)(2,1)}, bf16[5...) custom-call(s32[9]{0:T(128)} %pad_add_fusion.row_ref, bf16[128,768]{1,0:T(8,128)(2,1)} %get-tuple-element.84.x0, ...), custom_call_target="tpu_custom_call" | custom-call | flops 2415919104 | bytes 41943040 | tf_op jit(solution)/shard_map/attend/pallas_call | solution.py:130
  39.6 14.8 %feed.1 = (bf16[512,3072]{1,0:T(8,128)(2,1)}, bf16[512,3072]{1,0:T(8,128)(2,1)}, bf16[512,768]{1,0:T(8,128)(2,1)}, bf16[512,768]{1,0:T(8,128)(2,1)}, f32[512,768...) custom-call(f32[512,768]{1,0:T(8,128)} %get-tuple-element.38.normed_one, f32[1,768]{1,0:T(1,128)} %broadcast_in_dim.32.gain_one, ...), custom_call_target="tpu_custom_call" | custom-call | flops 4831838208 | bytes 41943040 | tf_op jit(solution)/shard_map/feed/pallas_call | solution.py:206
  54.4 18.5 %feed_back.1 = (bf16[3072,768]{1,0:T(8,128)(2,1)}, bf16[4,768,768]{2,1,0:T(8,128)(2,1)}, f32[1,3072]{1,0:T(1,128)}, bf16[512,768]{1,0:T(8,128)(2,1)}, f32[512,768]{1,0:T(8,128)}, /*index=5*/f32[8,768]{1,0:T(8,128)}) custom-call(bf16[512,768]{1,0:T(8,128)(2,1)} %get-tuple-element.40.lowered, bf16[512,3072]{1,0:T(8,128)(2,1)} %get-tuple-element.41.active, ...), custom_call_target="tpu_custom_call" | custom-call | flops 9663676416 | bytes 52428800 | tf_op jit(solution)/shard_map/feed_back/pallas_call | solution.py:272
  72.9 3.4 %dynamic-slice_bitcast_fusion = bf16[2,2,2,2,96,768]{5,4,3,2,1,0:T(8,128)(2,1)} fusion(bf16[2,2,2,2,2,96,768]{6,5,4,3,2,1,0:T(8,128)(2,1)} %bitcast.311, s32[]{:T(128)S(6)} %select_n.278), kind=kLoop, calls=%fused_computation.8 | loop fusion | bytes 4718596 | tf_op jit(solution)/shard_map/jit(dynamic_index_in_dim)/squeeze | solution.py:409
  76.3 1.6 copy_bitcast_fusion
  78.4 23.0 %attend_back.1 = (bf16[4,768,768]{2,1,0:T(8,128)(2,1)}, bf16[512,768]{1,0:T(8,128)(2,1)}, f32[1,768]{1,0:T(1,128)}, f32[1,768]{1,0:T(1,128)}) custom-call(bf16[128,768]{1,0:T(8,128)(2,1)} %get-tuple-element.84.x0, bf16[128,768]{1,0:T(8,128)(2,1)} %copy-done.4, bf16[128,768]{1,0:T(8,128)(2,1)} %copy-done.5, bf16[128,768]{1,0:T(8,128)(2,1)} %copy-done.3, ...), custom_call_target="tpu_custom_call" | custom-call | flops 4831838208 | bytes 41943040 | tf_op jit(solution)/shard_map/attend_back/pallas_call | solution.py:380
  101.5 3.2 %copy_bitcast_fusion.1 = bf16[2,2,2,2,96,768]{5,4,1,3,2,0:T(8,128)(2,1)} fusion(bf16[2,2,2,2,2,96,768]{6,5,4,3,2,1,0:T(8,128)(2,1)} %bitcast.299, s32[]{:T(128)S(6)} %select_n.278), kind=kLoop, calls=%fused_computation.7 | loop fusion | bytes 4718596 | tf_op jit(solution)/shard_map/jit(dynamic_index_in_dim)/squeeze | solution.py:409
  106.6 2.7 %collective-permute-done.19 = f32[12,768]{1,0:T(8,128)S(1)} collective-permute-done((f32[12,768]{1,0:T(8,128)S(1)}, f32[12,768]{1,0:T(8,128)S(1)}, u32[]{:S(2)}, u32[]{:S(2)}) %collective-permute-start.19) | collective-permute-done | bytes 36896 | tf_op jit(solution)/shard_map/ppermute | solution.py:405
  109.3 1.7 collective-permute-start.20
  111.1 2.4 %collective-permute-done.20 = f32[12,768]{1,0:T(8,128)S(1)} collective-permute-done((f32[12,768]{1,0:T(8,128)S(1)}, f32[12,768]{1,0:T(8,128)S(1)}, u32[]{:S(2)}, u32[]{:S(2)}) %collective-permute-start.20) | collective-permute-done | bytes 36896 | tf_op jit(solution)/shard_map/ppermute | solution.py:405
  113.5 1.8 collective-permute-start.21
  115.2 2.4 %collective-permute-done.21 = f32[12,768]{1,0:T(8,128)S(1)} collective-permute-done((f32[12,768]{1,0:T(8,128)S(1)}, f32[12,768]{1,0:T(8,128)S(1)}, u32[]{:S(2)}, u32[]{:S(2)}) %collective-permute-start.21) | collective-permute-done | bytes 36896 | tf_op jit(solution)/shard_map/ppermute | solution.py:405
  117.7 1.8 collective-permute-start.22
  119.5 1.9 fusion
  122.5 1.5 collective-permute-start.32
  124.0 2.9 %fusion.1 = bf16[2,2,2,96,768]{4,3,2,1,0:T(8,128)(2,1)} fusion(bf16[2,2,2,2,96,768]{5,4,3,2,1,0:T(8,128)(2,1)} %collective-permute-done.24, s32[]{:T(128)S(6)} %select_n.283, bf16[2,2,2,2,2,96,768]{6,5,4,3,2,1,0:T(8,128)(2,1)} %bitcast.312, s32[]{:T(128)S(6)} %select_n.266, s32[]{:T(128)S(6)} %select_n.284), kind=kLoop, calls=%fused_computation.3 | loop fusion | flops 2359296 | bytes 3538956 | tf_op jit(solution)/shard_map/convert_element_type | solution.py:430
  126.9 1.5 collective-permute-start.25
  128.4 1.6 fusion.2
  132.5 2.7 %collective-permute-start.23 = (f32[12,768]{1,0:T(8,128)S(1)}, f32[12,768]{1,0:T(8,128)S(1)}, u32[]{:S(2)}, u32[]{:S(2)}) collective-permute-start(f32[12,768]{1,0:T(8,128)S(1)} %add.756), channel_id=1, source_target_pairs={{0,16},{4,20},{8,24},{12,28},{16,0},{20,4},{24,8},{28,12},{1,17},{... | collective-permute-start | bytes 110600 | tf_op jit(solution)/shard_map/ppermute | solution.py:405
  136.0 19.1 %collective-permute-done.23 = f32[12,768]{1,0:T(8,128)S(1)} collective-permute-done((f32[12,768]{1,0:T(8,128)S(1)}, f32[12,768]{1,0:T(8,128)S(1)}, u32[]{:S(2)}, u32[]{:S(2)}) %collective-permute-start.23) | collective-permute-done | bytes 36896 | tf_op jit(solution)/shard_map/ppermute | solution.py:405
  156.3 1.3 reshape.319
  158.2 1.4 dynamic_slice.385
  159.6 1.3 dynamic_slice.417
  163.8 1.6 fusion.3
  165.5 1.7 collective-permute-start.11
  167.7 1.6 fusion.4
  169.9 4.8 %collective-permute-start.26 = (bf16[2,2,96,768]{3,2,1,0:T(8,128)(2,1)S(1)}, bf16[2,2,96,768]{3,2,1,0:T(8,128)(2,1)S(1)}, u32[]{:S(2)}, u32[]{:S(2)}) collective-permute-start(bf16[2,2,96,768]{3,2,1,0:T(8,128)(2,1)S(1)} %fusion.4), channel_id=1, source_target_pairs={{0,8},{4,12},{8,0},{12,4},{16,24},{20,28},{24,16},{28,20},{1,9},{5... | collective-permute-start | bytes 1769480 | tf_op jit(solution)/shard_map/ppermute | solution.py:405
  174.7 1.3 fusion.5
  176.0 1.6 collective-permute-start.14
  179.0 3.4 %collective-permute-done.33 = bf16[2,2,96,768]{3,2,0,1:T(8,128)(2,1)S(1)} collective-permute-done((bf16[2,2,96,768]{3,2,0,1:T(8,128)(2,1)S(1)}, bf16[2,2,96,768]{3,2,0,1:T(8,128)(2,1)S(1)}, u32[]{:S(2)}, u32[]{:S(2)}) %collective-permute-start.33) | collective-permute-done | bytes 589856 | tf_op jit(solution)/shard_map/ppermute | solution.py:405
  182.4 1.3 fusion.6
  183.7 4.7 %collective-permute-start.34 = (bf16[2,96,768]{2,1,0:T(8,128)(2,1)S(1)}, bf16[2,96,768]{2,1,0:T(8,128)(2,1)S(1)}, u32[]{:S(2)}, u32[]{:S(2)}) collective-permute-start(bf16[2,96,768]{2,1,0:T(8,128)(2,1)S(1)} %fusion.6), channel_id=1, source_target_pairs={{0,8},{4,12},{8,0},{12,4},{16,24},{20,28},{24,16},{28,20},{1,9},{5... | collective-permute-start | bytes 884744 | tf_op jit(solution)/shard_map/ppermute | solution.py:405
  188.8 1.3 fusion.7
  190.1 1.7 collective-permute-start.27
  192.9 1.6 collective-permute-start.15
  197.4 1.4 collective-permute-done.27
  202.2 1.8 collective-permute-start.16
  204.0 9.0 %collective-permute-done.35 = bf16[96,768]{1,0:T(8,128)(2,1)S(1)} collective-permute-done((bf16[96,768]{1,0:T(8,128)(2,1)S(1)}, bf16[96,768]{1,0:T(8,128)(2,1)S(1)}, u32[]{:S(2)}, u32[]{:S(2)}) %collective-permute-start.35) | collective-permute-done | bytes 147488 | tf_op jit(solution)/shard_map/ppermute | solution.py:405
  214.2 1.7 collective-permute-start.36
  217.3 1.7 collective-permute-start.29
  221.1 3.0 %collective-permute-done.29 = bf16[96,768]{1,0:T(8,128)(2,1)S(1)} collective-permute-done((bf16[96,768]{1,0:T(8,128)(2,1)S(1)}, bf16[96,768]{1,0:T(8,128)(2,1)S(1)}, u32[]{:S(2)}, u32[]{:S(2)}) %collective-permute-start.29) | collective-permute-done | bytes 147488 | tf_op jit(solution)/shard_map/ppermute | solution.py:405
  226.1 1.3 collective-permute-done.18
  (160 shorter events, 40.3 us)
Async XLA Ops:
  0.6 11.6 %copy-start = (s32[4,8]{1,0:T(4,128)S(1)}, s32[4,8]{1,0:T(4,128)}, u32[]{:S(2)}) copy-start(s32[4,8]{1,0:T(4,128)} %param.16) | copy-start | bytes 388
  0.7 7.4 %copy-start.19 = (f32[768]{0:T(1024)S(1)}, f32[768]{0:T(1024)}, u32[]{:S(2)}) copy-start(f32[768]{0:T(1024)} %param.21) | copy-start | bytes 9220
  0.7 8.0 %copy-start.20 = (f32[768]{0:T(1024)S(1)}, f32[768]{0:T(1024)}, u32[]{:S(2)}) copy-start(f32[768]{0:T(1024)} %param.20) | copy-start | bytes 9220
  0.7 8.6 %copy-start.21 = (f32[768]{0:T(1024)S(1)}, f32[768]{0:T(1024)}, u32[]{:S(2)}) copy-start(f32[768]{0:T(1024)} %param.22) | copy-start | bytes 9220
  0.7 9.2 %copy-start.22 = (f32[768]{0:T(1024)S(1)}, f32[768]{0:T(1024)}, u32[]{:S(2)}) copy-start(f32[768]{0:T(1024)} %param.26) | copy-start | bytes 9220
  0.7 9.8 %copy-start.23 = (f32[768]{0:T(1024)S(1)}, f32[768]{0:T(1024)}, u32[]{:S(2)}) copy-start(f32[768]{0:T(1024)} %param.27) | copy-start | bytes 9220
  0.7 10.3 %copy-start.24 = (f32[768]{0:T(1024)S(1)}, f32[768]{0:T(1024)}, u32[]{:S(2)}) copy-start(f32[768]{0:T(1024)} %param.28) | copy-start | bytes 9220
  0.8 10.9 %copy-start.16 = (f32[1536]{0:T(1024)S(1)}, f32[1536]{0:T(1024)}, u32[]{:S(2)}) copy-start(f32[1536]{0:T(1024)} %param.18) | copy-start | bytes 18436
  2.1 10.2 %collective-permute-start.3 = (bf16[128,768]{1,0:T(8,128)(2,1)S(1)}, bf16[128,768]{1,0:T(8,128)(2,1)S(1)}, u32[]{:S(2)}, u32[]{:S(2)}) collective-permute-start(bf16[128,768]{1,0:T(8,128)(2,1)S(1)} %get-tuple-element.79), channel_id=1, source_target_pairs={{0,1},{1,0},{2,3},{3,2},{4,5},{5,4},{6,7},{7,6},{8,9},{9,8},{10,11... | collective-permute-start | bytes 589832 | tf_op jit(solution)/shard_map/ppermute | solution.py:405
  3.4 17.6 %collective-permute-start.2 = (bf16[128,768]{1,0:T(8,128)(2,1)S(1)}, bf16[128,768]{1,0:T(8,128)(2,1)S(1)}, u32[]{:S(2)}, u32[]{:S(2)}) collective-permute-start(bf16[128,768]{1,0:T(8,128)(2,1)S(1)} %get-tuple-element.82), channel_id=1, source_target_pairs={{0,3},{1,2},{2,1},{3,0},{4,7},{5,6},{6,5},{7,4},{8,11},{9,10},{10,... | collective-permute-start | bytes 589832 | tf_op jit(solution)/shard_map/ppermute | solution.py:405
  6.0 15.0 %collective-permute-start = (bf16[128,768]{1,0:T(8,128)(2,1)S(1)}, bf16[128,768]{1,0:T(8,128)(2,1)S(1)}, u32[]{:S(2)}, u32[]{:S(2)}) collective-permute-start(bf16[128,768]{1,0:T(8,128)(2,1)S(1)} %get-tuple-element.83), channel_id=1, source_target_pairs={{0,1},{1,0},{2,3},{3,2},{4,5},{5,4},{6,7},{7,6},{8,9},{9,8},{10,11... | collective-permute-start | bytes 589832 | tf_op jit(solution)/shard_map/ppermute | solution.py:405
  6.0 9.4 %collective-permute-start.5 = (bf16[128,768]{1,0:T(8,128)(2,1)S(1)}, bf16[128,768]{1,0:T(8,128)(2,1)S(1)}, u32[]{:S(2)}, u32[]{:S(2)}) collective-permute-start(bf16[128,768]{1,0:T(8,128)(2,1)S(1)} %get-tuple-element.80), channel_id=1, source_target_pairs={{0,3},{1,2},{2,1},{3,0},{4,7},{5,6},{6,5},{7,4},{8,11},{9,10},{10,... | collective-permute-start | bytes 589832 | tf_op jit(solution)/shard_map/ppermute | solution.py:405
  6.0 14.0 %collective-permute-start.4 = (bf16[128,768]{1,0:T(8,128)(2,1)S(1)}, bf16[128,768]{1,0:T(8,128)(2,1)S(1)}, u32[]{:S(2)}, u32[]{:S(2)}) collective-permute-start(bf16[128,768]{1,0:T(8,128)(2,1)S(1)} %get-tuple-element.81), channel_id=1, source_target_pairs={{0,2},{1,3},{2,0},{3,1},{4,6},{5,7},{6,4},{7,5},{8,10},{9,11},{10,... | collective-permute-start | bytes 589832 | tf_op jit(solution)/shard_map/ppermute | solution.py:405
  12.3 11.8 %collective-permute-start.1 = (bf16[128,768]{1,0:T(8,128)(2,1)S(1)}, bf16[128,768]{1,0:T(8,128)(2,1)S(1)}, u32[]{:S(2)}, u32[]{:S(2)}) collective-permute-start(bf16[128,768]{1,0:T(8,128)(2,1)S(1)} %get-tuple-element.85), channel_id=1, source_target_pairs={{0,2},{1,3},{2,0},{3,1},{4,6},{5,7},{6,4},{7,5},{8,10},{9,11},{10,... | collective-permute-start | bytes 589832 | tf_op jit(solution)/shard_map/ppermute | solution.py:405
  77.9 41.6 %collective-permute-start.31 = (bf16[2,2,2,2,96,768]{5,4,1,3,2,0:T(8,128)(2,1)}, bf16[2,2,2,2,96,768]{5,4,1,3,2,0:T(8,128)(2,1)}, u32[]{:S(2)}, u32[]{:S(2)}) collective-permute-start(bf16[2,2,2,2,96,768]{5,4,1,3,2,0:T(8,128)(2,1)} %copy_bitcast_fusion), channel_id=1, source_target_pairs={{0,1},{1,0},{2,3},{3,2},{4,5},{5,4},{6,7},{7,6},{8,9},{9,8},{10,11... | collective-permute-start | bytes 7077896 | tf_op jit(solution)/shard_map/ppermute | solution.py:405
  77.9 46.1 %collective-permute-start.24 = (bf16[2,2,2,2,96,768]{5,4,3,2,1,0:T(8,128)(2,1)}, bf16[2,2,2,2,96,768]{5,4,3,2,1,0:T(8,128)(2,1)}, u32[]{:S(2)}, u32[]{:S(2)}) collective-permute-start(bf16[2,2,2,2,96,768]{5,4,3,2,1,0:T(8,128)(2,1)} %dynamic-slice_bitcast_fusion), channel_id=1, source_target_pairs={{0,1},{1,0},{2,3},{3,2},{4,5},{5,4},{6,7},{7,6},{8,9},{9,8},{10,11... | collective-permute-start | bytes 7077896 | tf_op jit(solution)/shard_map/ppermute | solution.py:405
  104.7 23.7 %collective-permute-start.12 = (bf16[2,2,2,2,96,768]{5,4,1,3,2,0:T(8,128)(2,1)}, bf16[2,2,2,2,96,768]{5,4,1,3,2,0:T(8,128)(2,1)S(1)}, u32[]{:S(2)}, u32[]{:S(2)}) collective-permute-start(bf16[2,2,2,2,96,768]{5,4,1,3,2,0:T(8,128)(2,1)} %copy_bitcast_fusion.1), channel_id=1, source_target_pairs={{0,1},{1,0},{2,3},{3,2},{4,5},{5,4},{6,7},{7,6},{8,9},{9,8},{10,11... | collective-permute-start | bytes 7077896 | tf_op jit(solution)/shard_map/ppermute | solution.py:405
  106.0 3.3 %collective-permute-start.19 = (f32[12,768]{1,0:T(8,128)S(1)}, f32[12,768]{1,0:T(8,128)S(1)}, u32[]{:S(2)}, u32[]{:S(2)}) collective-permute-start(f32[12,768]{1,0:T(8,128)S(1)} %concatenate.21), channel_id=1, source_target_pairs={{0,1},{1,0},{2,3},{3,2},{4,5},{5,4},{6,7},{7,6},{8,9},{9,8},{10,11... | collective-permute-start | bytes 110600 | tf_op jit(solution)/shard_map/ppermute | solution.py:405
  109.3 4.1 %collective-permute-start.20 = (f32[12,768]{1,0:T(8,128)S(1)}, f32[12,768]{1,0:T(8,128)S(1)}, u32[]{:S(2)}, u32[]{:S(2)}) collective-permute-start(f32[12,768]{1,0:T(8,128)S(1)} %add.753), channel_id=1, source_target_pairs={{0,2},{1,3},{2,0},{3,1},{4,6},{5,7},{6,4},{7,5},{8,10},{9,11},{10,... | collective-permute-start | bytes 110600 | tf_op jit(solution)/shard_map/ppermute | solution.py:405
  113.5 4.2 %collective-permute-start.21 = (f32[12,768]{1,0:T(8,128)S(1)}, f32[12,768]{1,0:T(8,128)S(1)}, u32[]{:S(2)}, u32[]{:S(2)}) collective-permute-start(f32[12,768]{1,0:T(8,128)S(1)} %add.754), channel_id=1, source_target_pairs={{0,4},{4,0},{8,12},{12,8},{16,20},{20,16},{24,28},{28,24},{1,5},{5... | collective-permute-start | bytes 110600 | tf_op jit(solution)/shard_map/ppermute | solution.py:405
  117.7 14.8 %collective-permute-start.22 = (f32[12,768]{1,0:T(8,128)S(1)}, f32[12,768]{1,0:T(8,128)S(1)}, u32[]{:S(2)}, u32[]{:S(2)}) collective-permute-start(f32[12,768]{1,0:T(8,128)S(1)} %add.755), channel_id=1, source_target_pairs={{0,8},{4,12},{8,0},{12,4},{16,24},{20,28},{24,16},{28,20},{1,9},{5... | collective-permute-start | bytes 110600 | tf_op jit(solution)/shard_map/ppermute | solution.py:405
  122.5 41.3 %collective-permute-start.32 = (bf16[2,2,2,96,768]{4,3,2,1,0:T(8,128)(2,1)}, bf16[2,2,2,96,768]{4,3,2,1,0:T(8,128)(2,1)}, u32[]{:S(2)}, u32[]{:S(2)}) collective-permute-start(bf16[2,2,2,96,768]{4,3,2,1,0:T(8,128)(2,1)} %copy.87), channel_id=1, source_target_pairs={{0,2},{1,3},{2,0},{3,1},{4,6},{5,7},{6,4},{7,5},{8,10},{9,11},{10,... | collective-permute-start | bytes 3538952 | tf_op jit(solution)/shard_map/ppermute | solution.py:405
  126.9 40.3 %collective-permute-start.25 = (bf16[2,2,2,96,768]{4,3,2,1,0:T(8,128)(2,1)}, bf16[2,2,2,96,768]{4,3,2,1,0:T(8,128)(2,1)}, u32[]{:S(2)}, u32[]{:S(2)}) collective-permute-start(bf16[2,2,2,96,768]{4,3,2,1,0:T(8,128)(2,1)} %fusion.1), channel_id=1, source_target_pairs={{0,4},{4,0},{8,12},{12,8},{16,20},{20,16},{24,28},{28,24},{1,5},{5... | collective-permute-start | bytes 3538952 | tf_op jit(solution)/shard_map/ppermute | solution.py:405
  131.1 38.8 %collective-permute-start.13 = (bf16[2,2,2,96,768]{4,3,2,1,0:T(8,128)(2,1)}, bf16[2,2,2,96,768]{4,3,2,1,0:T(8,128)(2,1)S(1)}, u32[]{:S(2)}, u32[]{:S(2)}) collective-permute-start(bf16[2,2,2,96,768]{4,3,2,1,0:T(8,128)(2,1)} %copy.72), channel_id=1, source_target_pairs={{0,8},{4,12},{8,0},{12,4},{16,24},{20,28},{24,16},{28,20},{1,9},{5... | collective-permute-start | bytes 3538952 | tf_op jit(solution)/shard_map/ppermute | solution.py:405
  132.5 33.0 %collective-permute-start.8 = (bf16[128,768]{1,0:T(8,128)(2,1)}, bf16[128,768]{1,0:T(8,128)(2,1)}, u32[]{:S(2)}, u32[]{:S(2)}) collective-permute-start(bf16[128,768]{1,0:T(8,128)(2,1)} %get-tuple-element.75), channel_id=1, source_target_pairs={{0,3},{1,2},{2,1},{3,0},{4,7},{5,6},{6,5},{7,4},{8,11},{9,10},{10,... | collective-permute-start | bytes 589832 | tf_op jit(solution)/shard_map/ppermute | solution.py:405
  132.5 22.6 %collective-permute-start.23 = (f32[12,768]{1,0:T(8,128)S(1)}, f32[12,768]{1,0:T(8,128)S(1)}, u32[]{:S(2)}, u32[]{:S(2)}) collective-permute-start(f32[12,768]{1,0:T(8,128)S(1)} %add.756), channel_id=1, source_target_pairs={{0,16},{4,20},{8,24},{12,28},{16,0},{20,4},{24,8},{28,12},{1,17},{... | collective-permute-start | bytes 110600 | tf_op jit(solution)/shard_map/ppermute | solution.py:405
  155.1 14.2 %collective-permute-start.7 = (bf16[128,768]{1,0:T(8,128)(2,1)}, bf16[128,768]{1,0:T(8,128)(2,1)}, u32[]{:S(2)}, u32[]{:S(2)}) collective-permute-start(bf16[128,768]{1,0:T(8,128)(2,1)} %get-tuple-element.76), channel_id=1, source_target_pairs={{0,2},{1,3},{2,0},{3,1},{4,6},{5,7},{6,4},{7,5},{8,10},{9,11},{10,... | collective-permute-start | bytes 589832 | tf_op jit(solution)/shard_map/ppermute | solution.py:405
  163.8 6.0 %collective-permute-start.6 = (bf16[128,768]{1,0:T(8,128)(2,1)}, bf16[128,768]{1,0:T(8,128)(2,1)S(1)}, u32[]{:S(2)}, u32[]{:S(2)}) collective-permute-start(bf16[128,768]{1,0:T(8,128)(2,1)} %get-tuple-element.77), channel_id=1, source_target_pairs={{0,1},{1,0},{2,3},{3,2},{4,5},{5,4},{6,7},{7,6},{8,9},{9,8},{10,11... | collective-permute-start | bytes 589832 | tf_op jit(solution)/shard_map/ppermute | solution.py:405
  165.5 10.5 %collective-permute-start.11 = (bf16[128,768]{1,0:T(8,128)(2,1)S(1)}, bf16[128,768]{1,0:T(8,128)(2,1)S(1)}, u32[]{:S(2)}, u32[]{:S(2)}) collective-permute-start(bf16[128,768]{1,0:T(8,128)(2,1)S(1)} %copy-done.13), channel_id=1, source_target_pairs={{0,3},{1,2},{2,1},{3,0},{4,7},{5,6},{6,5},{7,4},{8,11},{9,10},{10,... | collective-permute-start | bytes 589832 | tf_op jit(solution)/shard_map/ppermute | solution.py:405
  167.2 15.2 %collective-permute-start.33 = (bf16[2,2,96,768]{3,2,0,1:T(8,128)(2,1)S(1)}, bf16[2,2,96,768]{3,2,0,1:T(8,128)(2,1)S(1)}, u32[]{:S(2)}, u32[]{:S(2)}) collective-permute-start(bf16[2,2,96,768]{3,2,0,1:T(8,128)(2,1)S(1)} %fusion.3), channel_id=1, source_target_pairs={{0,4},{4,0},{8,12},{12,8},{16,20},{20,16},{24,28},{28,24},{1,5},{5... | collective-permute-start | bytes 1769480 | tf_op jit(solution)/shard_map/ppermute | solution.py:405
  169.3 8.3 %copy-start.6 = (bf16[1,128,768]{2,1,0:T(8,128)(2,1)S(1)}, bf16[1,128,768]{2,1,0:T(8,128)(2,1)}, u32[]{:S(2)}) copy-start(bf16[1,128,768]{2,1,0:T(8,128)(2,1)} %get-tuple-element.74) | copy-start | bytes 589828
  169.3 9.4 %collective-permute-start.10 = (bf16[128,768]{1,0:T(8,128)(2,1)S(1)}, bf16[128,768]{1,0:T(8,128)(2,1)S(1)}, u32[]{:S(2)}, u32[]{:S(2)}) collective-permute-start(bf16[128,768]{1,0:T(8,128)(2,1)S(1)} %copy-done.12), channel_id=1, source_target_pairs={{0,2},{1,3},{2,0},{3,1},{4,6},{5,7},{6,4},{7,5},{8,10},{9,11},{10,... | collective-permute-start | bytes 589832 | tf_op jit(solution)/shard_map/ppermute | solution.py:405
  169.8 8.9 %copy-start.7 = (bf16[1,128,768]{2,1,0:T(8,128)(2,1)S(1)}, bf16[1,128,768]{2,1,0:T(8,128)(2,1)}, u32[]{:S(2)}) copy-start(bf16[1,128,768]{2,1,0:T(8,128)(2,1)} %get-tuple-element.66) | copy-start | bytes 589828
  169.8 8.9 %collective-permute-start.9 = (bf16[128,768]{1,0:T(8,128)(2,1)S(1)}, bf16[128,768]{1,0:T(8,128)(2,1)S(1)}, u32[]{:S(2)}, u32[]{:S(2)}) collective-permute-start(bf16[128,768]{1,0:T(8,128)(2,1)S(1)} %copy-done.11), channel_id=1, source_target_pairs={{0,1},{1,0},{2,3},{3,2},{4,5},{5,4},{6,7},{7,6},{8,9},{9,8},{10,11... | collective-permute-start | bytes 589832 | tf_op jit(solution)/shard_map/ppermute | solution.py:405
  169.9 18.9 %collective-permute-start.26 = (bf16[2,2,96,768]{3,2,1,0:T(8,128)(2,1)S(1)}, bf16[2,2,96,768]{3,2,1,0:T(8,128)(2,1)S(1)}, u32[]{:S(2)}, u32[]{:S(2)}) collective-permute-start(bf16[2,2,96,768]{3,2,1,0:T(8,128)(2,1)S(1)} %fusion.4), channel_id=1, source_target_pairs={{0,8},{4,12},{8,0},{12,4},{16,24},{20,28},{24,16},{28,20},{1,9},{5... | collective-permute-start | bytes 1769480 | tf_op jit(solution)/shard_map/ppermute | solution.py:405
  176.0 15.8 %collective-permute-start.14 = (bf16[2,2,96,768]{3,2,0,1:T(8,128)(2,1)S(1)}, bf16[2,2,96,768]{3,2,0,1:T(8,128)(2,1)S(1)}, u32[]{:S(2)}, u32[]{:S(2)}) collective-permute-start(bf16[2,2,96,768]{3,2,0,1:T(8,128)(2,1)S(1)} %fusion.5), channel_id=1, source_target_pairs={{0,2},{1,3},{2,0},{3,1},{4,6},{5,7},{6,4},{7,5},{8,10},{9,11},{10,... | collective-permute-start | bytes 1769480 | tf_op jit(solution)/shard_map/ppermute | solution.py:405
  183.7 11.7 %collective-permute-start.34 = (bf16[2,96,768]{2,1,0:T(8,128)(2,1)S(1)}, bf16[2,96,768]{2,1,0:T(8,128)(2,1)S(1)}, u32[]{:S(2)}, u32[]{:S(2)}) collective-permute-start(bf16[2,96,768]{2,1,0:T(8,128)(2,1)S(1)} %fusion.6), channel_id=1, source_target_pairs={{0,8},{4,12},{8,0},{12,4},{16,24},{20,28},{24,16},{28,20},{1,9},{5... | collective-permute-start | bytes 884744 | tf_op jit(solution)/shard_map/ppermute | solution.py:405
  190.1 8.7 %collective-permute-start.27 = (bf16[2,96,768]{2,1,0:T(8,128)(2,1)S(1)}, bf16[2,96,768]{2,1,0:T(8,128)(2,1)S(1)}, u32[]{:S(2)}, u32[]{:S(2)}) collective-permute-start(bf16[2,96,768]{2,1,0:T(8,128)(2,1)S(1)} %fusion.7), channel_id=1, source_target_pairs={{0,2},{1,3},{2,0},{3,1},{4,6},{5,7},{6,4},{7,5},{8,10},{9,11},{10,... | collective-permute-start | bytes 884744 | tf_op jit(solution)/shard_map/ppermute | solution.py:405
  192.9 8.3 %collective-permute-start.15 = (bf16[2,96,768]{2,1,0:T(8,128)(2,1)S(1)}, bf16[2,96,768]{2,1,0:T(8,128)(2,1)S(1)}, u32[]{:S(2)}, u32[]{:S(2)}) collective-permute-start(bf16[2,96,768]{2,1,0:T(8,128)(2,1)S(1)} %fusion.8), channel_id=1, source_target_pairs={{0,4},{4,0},{8,12},{12,8},{16,20},{20,16},{24,28},{28,24},{1,5},{5... | collective-permute-start | bytes 884744 | tf_op jit(solution)/shard_map/ppermute | solution.py:405
  196.6 16.4 %collective-permute-start.35 = (bf16[96,768]{1,0:T(8,128)(2,1)S(1)}, bf16[96,768]{1,0:T(8,128)(2,1)S(1)}, u32[]{:S(2)}, u32[]{:S(2)}) collective-permute-start(bf16[96,768]{1,0:T(8,128)(2,1)S(1)} %fusion.9), channel_id=1, source_target_pairs={{0,16},{4,20},{8,24},{12,28},{16,0},{20,4},{24,8},{28,12},{1,17},{... | collective-permute-start | bytes 442376 | tf_op jit(solution)/shard_map/ppermute | solution.py:405
  199.9 16.2 %collective-permute-start.28 = (bf16[96,768]{1,0:T(8,128)(2,1)S(1)}, bf16[96,768]{1,0:T(8,128)(2,1)S(1)}, u32[]{:S(2)}, u32[]{:S(2)}) collective-permute-start(bf16[96,768]{1,0:T(8,128)(2,1)S(1)} %fusion.12), channel_id=1, source_target_pairs={{0,16},{4,20},{8,24},{12,28},{16,0},{20,4},{24,8},{28,12},{1,17},{... | collective-permute-start | bytes 442376 | tf_op jit(solution)/shard_map/ppermute | solution.py:405
  202.2 16.8 %collective-permute-start.16 = (bf16[96,768]{1,0:T(8,128)(2,1)S(1)}, bf16[96,768]{1,0:T(8,128)(2,1)S(1)}, u32[]{:S(2)}, u32[]{:S(2)}) collective-permute-start(bf16[96,768]{1,0:T(8,128)(2,1)S(1)} %fusion.15), channel_id=1, source_target_pairs={{0,16},{4,20},{8,24},{12,28},{16,0},{20,4},{24,8},{28,12},{1,17},{... | collective-permute-start | bytes 442376 | tf_op jit(solution)/shard_map/ppermute | solution.py:405
  214.2 6.8 %collective-permute-start.36 = (bf16[96,768]{1,0:T(8,128)(2,1)S(1)}, bf16[96,768]{1,0:T(8,128)(2,1)S(1)}, u32[]{:S(2)}, u32[]{:S(2)}) collective-permute-start(bf16[96,768]{1,0:T(8,128)(2,1)S(1)} %fusion.11), channel_id=1, source_target_pairs={{0,2},{1,3},{2,0},{3,1},{4,6},{5,7},{6,4},{7,5},{8,10},{9,11},{10,... | collective-permute-start | bytes 442376 | tf_op jit(solution)/shard_map/ppermute | solution.py:405
  217.3 6.8 %collective-permute-start.29 = (bf16[96,768]{1,0:T(8,128)(2,1)S(1)}, bf16[96,768]{1,0:T(8,128)(2,1)S(1)}, u32[]{:S(2)}, u32[]{:S(2)}) collective-permute-start(bf16[96,768]{1,0:T(8,128)(2,1)S(1)} %fusion.14), channel_id=1, source_target_pairs={{0,2},{1,3},{2,0},{3,1},{4,6},{5,7},{6,4},{7,5},{8,10},{9,11},{10,... | collective-permute-start | bytes 442376 | tf_op jit(solution)/shard_map/ppermute | solution.py:405
  220.1 5.6 %collective-permute-start.17 = (bf16[96,768]{1,0:T(8,128)(2,1)S(1)}, bf16[96,768]{1,0:T(8,128)(2,1)S(1)}, u32[]{:S(2)}, u32[]{:S(2)}) collective-permute-start(bf16[96,768]{1,0:T(8,128)(2,1)S(1)} %fusion.17), channel_id=1, source_target_pairs={{0,2},{1,3},{2,0},{3,1},{4,6},{5,7},{6,4},{7,5},{8,10},{9,11},{10,... | collective-permute-start | bytes 442376 | tf_op jit(solution)/shard_map/ppermute | solution.py:405
  221.0 4.8 %collective-permute-start.37 = (bf16[2,96,768]{2,1,0:T(8,128)(2,1)S(1)}, bf16[2,96,768]{2,1,0:T(8,128)(2,1)S(1)}, u32[]{:S(2)}, u32[]{:S(2)}) collective-permute-start(bf16[2,96,768]{2,1,0:T(8,128)(2,1)S(1)} %get-tuple-element.99), channel_id=1, source_target_pairs={{0,1},{1,0},{2,3},{3,2},{4,5},{5,4},{6,7},{7,6},{8,9},{9,8},{10,11... | collective-permute-start | bytes 884744 | tf_op jit(solution)/shard_map/ppermute | solution.py:405
  224.2 1.8 collective-permute-start.30
  225.7 1.6 collective-permute-start.18
  (17 other events, 57.8 us)

commit v2 on v0

v2 whole, which is shorter than its diff:
```python
import functools
import math

import jax
import jax.numpy as jnp
from jax import lax
from jax.experimental import pallas as pl
from jax.experimental.pallas import tpu as pltpu
from jax.sharding import PartitionSpec as P

HEADS = 12
EPSILON = 1e-12
MASKED = -1e30
f32 = jnp.float32
bf16 = jnp.bfloat16
NN = (((1,), (0,)), ((), ()))
NT = (((1,), (1,)), ((), ()))
TN = (((0,), (0,)), ((), ()))
VMEM = pl.BlockSpec(memory_space=pltpu.VMEM)
SMEM = pl.BlockSpec(memory_space=pltpu.SMEM)
HBM = pl.BlockSpec(memory_space=pltpu.HBM)
ANY = pl.BlockSpec(memory_space=pl.ANY)


WEIGHTS = {
    "attend": 20 * 10**9, "feed": 20 * 10**9, "grad_down": 20 * 10**9, "grad_up": 10**7,
    "first_back": 20 * 10**9, "attend_back": 40 * 10**9, "grad_tokens": 10 * 10**9,
}


def dot(left, right, dims=NN):
    return lax.dot_general(left, right, dims, preferred_element_type=f32)


def call(
    kernel, name, scalars, arrays, outs, flops, scratch=(), far=(), far_outs=(), copies=0, room=8, after=()
):
    scratch = list(scratch)
    if copies:
        scratch.append(pltpu.SemaphoreType.DMA((copies,)))
    first, last = len(scalars) + len(arrays) + len(far), len(after)

    def body(*refs):
        kernel(*refs[:first], *refs[first + last :])

    return pl.pallas_call(
        body,
        in_specs=[SMEM] * len(scalars) + [VMEM] * len(arrays) + [HBM] * len(far) + [ANY] * last,
        out_specs=[VMEM] * len(outs) + [HBM] * len(far_outs),
        out_shape=[*outs, *[pltpu.HBM(a.shape, a.dtype) for a in far_outs]],
        scratch_shapes=scratch,
        compiler_params=pltpu.CompilerParams(vmem_limit_bytes=room * 2**20),
        cost_estimate=pl.CostEstimate(flops=WEIGHTS.get(name, 0), bytes_accessed=0, transcendentals=0),
        name=name,
    )(
        *scalars, *arrays, *[pltpu.with_memory_space_constraint(a, pltpu.HBM) for a in far], *after
    )


def shape(*dims, dtype=bf16):
    return jax.ShapeDtypeStruct(dims, dtype)


def cut(i, size):
    return pl.ds(pl.multiple_of(i * size, size), size)


def copy(source, target, semaphore):
    return pltpu.make_async_copy(source, target, semaphore)


def column_sum(values):
    return jnp.sum(values, axis=0, keepdims=True)


def row_mean(values):
    return jnp.mean(values, axis=-1, keepdims=True)


def normalize(inputs):
    centre = inputs - row_mean(inputs)
    inverse = lax.rsqrt(row_mean(centre * centre) + EPSILON)
    return centre * inverse, inverse


def normalize_back(scaled, normed, inverse):
    return inverse * (scaled - row_mean(scaled) - normed * row_mean(scaled * normed))


BIAS_Q, BIAS_V, BIAS_OUT, GAIN_ONE, SHIFT_ONE, BIAS_DOWN, GAIN_TWO, SHIFT_TWO, BIAS_UP = range(9)


def vector(ref, row):
    return ref[row : row + 1, :]


def attend_kernel(
    row_ref, x0, x1, x2, x3, vectors, w_qkv, w_out,
    normed_out, inverse_out, q_out, k_out, v_out, prob_out, context_out, tokens_out,
    weights, out_weights, tokens, mask, q_kept, k_kept, v_kept, context_kept, probs_kept, sems,
    *, pages, head_width,
):
    slots = x0.shape[0]
    count, width = tokens.shape
    wide = 4 * head_width
    groups = width // wide

    def load(i, part):
        here = cut(i + part * groups, wide)
        return copy(w_qkv.at[:, here], weights.at[i, part], sems.at[3 * i + part])

    def keep(i, number, source, target):
        return copy(source.at[:, cut(i, wide)], target.at[:, cut(i, wide)], sems.at[number * groups + i])

    def keep_probs(i):
        return copy(probs_kept.at[i], prob_out.at[pl.ds(4 * i, 4)], sems.at[7 * groups + i])

    kept = ((3, q_kept, q_out), (4, k_kept, k_out), (5, v_kept, v_out), (6, context_kept, context_out))
    for part in range(3):
        load(0, part).start()
    load_out = copy(w_out, out_weights, sems.at[8 * groups])
    for i, block in enumerate((x0, x1, x2, x3)):
        tokens[i * slots : (i + 1) * slots, :] = block[...]
    keep_tokens = copy(tokens, tokens_out, sems.at[8 * groups + 1])
    keep_tokens.start()
    position = row_ref[pages]

    def page_of(shape, dim):
        at = lax.broadcasted_iota(jnp.int32, shape, dim)
        slot = ((at // slots) ^ position) * slots + at % slots
        page = jnp.zeros(shape, jnp.int32)
        end = 0
        for c in range(pages):
            end = end + row_ref[c]
            page = page + (slot >= end).astype(jnp.int32)
        return page

    mask[...] = jnp.where(
        page_of((count, count), 0) == page_of((1, count), 1), 0.0, MASKED
    )
    head = lax.broadcasted_iota(jnp.int32, (count, wide), 1) // head_width
    none = jnp.zeros((count, wide), bf16)

    @pl.loop(0, groups)
    def _(i):
        here = cut(i, wide)

        @pl.when(i + 1 < groups)
        def _():
            for part in range(3):
                load(i + 1, part).start()

        @pl.when(i + 1 == groups)
        def _():
            load_out.start()

        for part in range(3):
            load(i, part).wait()
        x = tokens[...]
        q = (dot(x, weights[i, 0]) + vectors[BIAS_Q : BIAS_Q + 1, here]).astype(bf16)
        k = dot(x, weights[i, 1]).astype(bf16)
        v = (dot(x, weights[i, 2]) + vectors[BIAS_V : BIAS_V + 1, here]).astype(bf16)
        q_kept[:, here] = q
        k_kept[:, here] = k
        v_kept[:, here] = v
        scaled_q = q * jnp.asarray(1.0 / math.sqrt(head_width), bf16)
        context = jnp.zeros((count, wide), f32)
        for h in range(4):
            scores = dot(k, jnp.where(head == h, scaled_q, none), NT) + mask[...]
            powers = jnp.exp(scores - jnp.max(scores, axis=0, keepdims=True))
            probs = (powers * (1.0 / jnp.sum(powers, axis=0, keepdims=True))).astype(bf16)
            probs_kept[i, h] = probs
            context = context + dot(probs, jnp.where(head == h, v, none), TN)
        context_kept[:, here] = context.astype(bf16)
        for number, source, target in kept:
            keep(i, number, source, target).start()
        keep_probs(i).start()

    load_out.wait()
    attended = dot(context_kept[...], out_weights[...]) + vector(vectors, BIAS_OUT)
    normed, inverse = normalize(tokens[...].astype(f32) + attended)
    normed_out[...] = normed
    inverse_out[...] = inverse
    for i in range(groups):
        for number, source, target in kept:
            keep(i, number, source, target).wait()
        keep_probs(i).wait()
    keep_tokens.wait()


def attend(row, blocks, w_qkv, w_out, vectors):
    slots, width = blocks[0].shape
    count = slots * len(blocks)
    head_width = width // HEADS
    wide = 4 * head_width
    groups = width // wide
    narrow, full = shape(count, width), shape(count, width, dtype=f32)
    rows = pltpu.VMEM((count, width), bf16)
    return call(
        functools.partial(attend_kernel, pages=row.shape[0] - 1, head_width=head_width),
        "attend", [row], [*blocks, vectors],
        [full, shape(count, 1, dtype=f32)],
        8 * count * width * width + 16 * count * count * width,
        [
            pltpu.VMEM((groups, 3, width, wide), bf16), pltpu.VMEM((width, width), bf16), rows,
            pltpu.VMEM((count, count), f32), rows, rows, rows, rows,
            pltpu.VMEM((groups, 4, count, count), bf16),
        ],
        [w_qkv, w_out],
        [narrow, narrow, narrow, shape(HEADS, count, count), narrow, narrow],
        8 * groups + 2, 26,
    )


def feed_kernel(
    normed_one, vectors, c0, c1, c2, c3, w_up, w_down,
    active_out, slope_out, r0, r1, r2, r3, lowered_out, first_out, vector_out, sum_out, normed_far,
    total, sems,
):
    width = w_up.shape[0]
    steps = w_up.shape[1] // width

    keep_normed = copy(normed_one, normed_far, sems.at[0])
    keep_normed.start()
    first_norm = normed_one[...] * vector(vectors, GAIN_ONE) + vector(vectors, SHIFT_ONE)
    first_out[...] = first_norm.astype(bf16)
    total[...] = first_norm + vector(vectors, BIAS_DOWN)

    @pl.loop(0, steps)
    def _(i):
        here = cut(i, width)

        raised = dot(first_out[...], w_up[:, here]) + vectors[pl.ds(BIAS_UP + i, 1), :]
        cumulative = 0.5 * (1.0 + lax.erf(raised * (1.0 / math.sqrt(2.0))))
        activated = (raised * cumulative).astype(bf16)
        active_out[:, here] = activated
        bell = jnp.exp(-0.5 * raised * raised) * (1.0 / math.sqrt(2.0 * math.pi))
        slope_out[:, here] = (cumulative + raised * bell).astype(bf16)
        total[...] += dot(activated, w_down[here, :])

    normed, inverse = normalize(total[...])
    gain = vector(vectors, GAIN_TWO)
    result = (normed * gain + vector(vectors, SHIFT_TWO)).astype(bf16)
    slots = c0.shape[0]
    for i, block in enumerate((r0, r1, r2, r3)):
        block[...] = result[i * slots : (i + 1) * slots, :]
    upstream = jnp.concatenate([c0[...], c1[...], c2[...], c3[...]]).astype(f32)
    grad_sum = normalize_back(upstream * gain, normed, inverse)
    total[...] = grad_sum
    keep_sum = copy(total, sum_out, sems.at[1])
    keep_sum.start()
    lowered = grad_sum.astype(bf16)
    lowered_out[...] = lowered
    vector_out[0:1, :] = column_sum(upstream * normed)
    vector_out[1:2, :] = column_sum(upstream)
    vector_out[2:3, :] = column_sum(lowered.astype(f32))
    keep_sum.wait()
    keep_normed.wait()


def feed(normed, w_up, w_down, vectors, cotangents):
    count, width = normed.shape
    hidden = w_up.shape[1]
    narrow, full = shape(count, width), shape(count, width, dtype=f32)
    return call(
        feed_kernel, "feed", [], [normed, vectors, *cotangents, w_up, w_down],
        [shape(count, hidden)] * 2
        + [shape(*cotangents[0].shape)] * 4
        + [narrow, narrow, shape(8, width, dtype=f32)],
        4 * count * width * hidden,
        [pltpu.VMEM((count, width), f32)], [], [full, full], 2, 14,
    )


def grad_down_kernel(place, active, lowered, keep, send, *, shares):
    width = lowered.shape[1]
    hidden = active.shape[1]
    rows = hidden // shares // 4
    odd = place[0] == 1

    @pl.loop(0, hidden // width)
    def _(i):
        value = dot(active[:, cut(i, width)], lowered[...], TN).astype(bf16)
        count = width // rows // 4
        for d in range(count):
            for x in range(2):
                at = (d * 4 + x * 2) * rows
                first = value[at : at + rows, :]
                second = value[at + rows : at + 2 * rows, :]
                keep[x, i * count + d] = jnp.where(odd, second, first)
                send[x, i * count + d] = jnp.where(odd, first, second)


def grad_down_plain(active, lowered, down):
    width = lowered.shape[1]

    @pl.loop(0, active.shape[1] // width)
    def _(i):
        down[cut(i, width), :] = dot(active[:, cut(i, width)], lowered[...], TN).astype(bf16)


def grad_down(place, active, lowered, shares):
    count, width = lowered.shape
    hidden = active.shape[1]
    rows = hidden // shares // 4
    flops = 2 * count * width * hidden
    if rows % 16 or width % (4 * rows):
        (whole,) = call(
            grad_down_plain, "grad_down", [], [active, lowered], [shape(hidden, width)], flops,
            room=12,
        )
        parts = jnp.moveaxis(whole.reshape(shares, 2, 2, rows, width), 0, 2)
        parts = [parts[:, i] for i in range(2)]
        odd = place[0] == 1
        return jnp.where(odd, parts[1], parts[0]), jnp.where(odd, parts[0], parts[1])
    return call(
        functools.partial(grad_down_kernel, shares=shares), "grad_down",
        [place], [active, lowered], [shape(2, shares, rows, width)] * 2, flops, room=12,
    )


def grad_up_kernel(
    place, lowered, slope, first, w_down, raised_out, keep, send, bias_out, turned
):
    width = lowered.shape[1]
    turned[...] = first[...].T

    def work(b):
        here = cut(b, width)
        raised = dot(lowered[...], w_down[here, :], NT) * slope[:, here].astype(f32)
        raised = raised.astype(bf16)
        raised_out[:, here] = raised
        bias_out[pl.ds(b, 1), :] = column_sum(raised.astype(f32))
        return dot(turned[...], raised).astype(bf16)

    @pl.loop(0, 2)
    def _(x):
        send[x] = work(2 * x + 1 - place[0])
        keep[x] = work(2 * x + place[0])


def grad_up(place, lowered, slope, w_down, first):
    count, width = lowered.shape
    hidden = w_down.shape[0]
    return call(
        grad_up_kernel, "grad_up", [place], [lowered, slope, first, w_down],
        [shape(count, hidden)] + [shape(2, width, width)] * 2
        + [shape(hidden // width, width, dtype=f32)],
        4 * count * width * hidden,
        [pltpu.VMEM((width, count), bf16)], room=12,
    )


def first_back_kernel(
    raised, inverse_one, vectors, w_up, sum_two, normed_one,
    attended_out, vector_out, sum_out, total, sum_kept, normed, sems,
):
    load_sum = copy(sum_two, sum_kept, sems.at[0])
    load_sum.start()
    load_normed = copy(normed_one, normed, sems.at[1])
    load_normed.start()
    total[...] = dot(raised[...], w_up[...], NT)

    load_sum.wait()
    load_normed.wait()
    upstream = total[...] + sum_kept[...]
    grad_sum = normalize_back(
        upstream * vector(vectors, GAIN_ONE), normed[...], inverse_one[...]
    )
    total[...] = grad_sum
    keep_sum = copy(total, sum_out, sems.at[2])
    keep_sum.start()
    attended = grad_sum.astype(bf16)
    attended_out[...] = attended
    vector_out[0:1, :] = column_sum(upstream * normed[...])
    vector_out[1:2, :] = column_sum(upstream)
    vector_out[2:3, :] = column_sum(attended.astype(f32))
    keep_sum.wait()


def first_back(raised, w_up, sum_two, normed, inverse, vectors, after):
    count, width = normed.shape
    hidden = w_up.shape[1]
    full = shape(count, width, dtype=f32)
    rows = pltpu.VMEM((count, width), f32)
    return call(
        first_back_kernel, "first_back", [], [raised, inverse, vectors, w_up],
        [shape(count, width), shape(8, width, dtype=f32)],
        2 * count * width * hidden,
        [rows, rows, rows], [sum_two, normed], [full], 3, 14, after,
    )


def small_pieces(shares, width):
    q, v, gain_one, shift_one, out, gain_two, shift_two, down, up = range(9)
    share = width // shares

    def flat(row, first):
        return row + first // width, first % width

    def pieces(d):
        at = d * share
        return (
            (flat(q, 2 * at), flat(q, 2 * at + share), (out, at)),
            ((gain_one, at), (shift_one, at), (down, at)),
            ((gain_two, at), (shift_two, at), flat(up, 4 * at)),
            tuple(flat(up, 4 * at + j * share) for j in (1, 2, 3)),
        )

    return [pieces(d) for d in range(shares)]


def attend_back_kernel(
    place, attended, vector_one, vector_two, bias_up, tokens, context, prob, q_ref, k_ref, v_ref, w_out,
    keep_0, keep_1, keep_2, send_0, send_1, send_2, small_keep, small_send, grads_out,
    rows_kept, turned, turned_context, probs_kept, q_kept, k_kept, v_kept, weights, sums, small, sems,
    *, head_width,
):
    count, width = attended.shape
    wide = 4 * head_width
    groups = width // wide
    shares = small_keep.shape[1]

    def load(i):
        here = cut(i, wide)
        pairs = (
            (w_out.at[here, :], weights.at[here, :]),
            (v_ref.at[:, here], v_kept.at[:, here]),
            (prob.at[pl.ds(4 * i, 4)], probs_kept.at[i]),
            (q_ref.at[:, here], q_kept.at[:, here]),
            (k_ref.at[:, here], k_kept.at[:, here]),
        )
        return [copy(s, t, sems.at[5 * i + n]) for n, (s, t) in enumerate(pairs)]

    load_tokens = copy(tokens, rows_kept.at[0], sems.at[5 * groups])
    load_context = copy(context, rows_kept.at[1], sems.at[5 * groups + 1])
    load_tokens.start()
    load_context.start()
    for one in load(0):
        one.start()
    load_tokens.wait()
    turned[...] = rows_kept[0].T
    load_context.wait()
    turned_context[...] = rows_kept[1].T
    head = lax.broadcasted_iota(jnp.int32, (count, wide), 1) // head_width
    none = jnp.zeros((count, wide), bf16)
    odd = place[0] == 1

    @pl.loop(0, groups)
    def _(i):
        here = cut(i, wide)

        @pl.when(i + 1 < groups)
        def _():
            for one in load(i + 1):
                one.start()

        for one in load(i):
            one.wait()
        grad_context = dot(attended[...], weights[here, :], NT).astype(bf16)
        scaling = jnp.asarray(1.0 / math.sqrt(head_width), bf16)
        scaled_q = q_kept[:, here] * scaling
        scaled_k = k_kept[:, here] * scaling
        v = v_kept[:, here]
        grad_q = jnp.zeros((count, wide), f32)
        grad_k = grad_q
        grad_v = grad_q
        for h in range(4):
            mine = head == h
            probs = probs_kept[i, h]
            wider = probs.astype(f32)
            upstream = jnp.where(mine, grad_context, none)
            weighted = wider * dot(v, upstream, NT)
            balance = jnp.sum(weighted, axis=0, keepdims=True)
            grad_scores = (weighted - wider * balance).astype(bf16)
            grad_v = grad_v + dot(probs, upstream)
            grad_k = grad_k + dot(grad_scores, jnp.where(mine, scaled_q, none))
            grad_q = grad_q + dot(grad_scores, jnp.where(mine, scaled_k, none), TN)
        grad_q = grad_q.astype(bf16)
        grad_k = grad_k.astype(bf16)
        grad_v = grad_v.astype(bf16)
        grads_out[:, here] = grad_q
        grads_out[:, cut(i + groups, wide)] = grad_k
        grads_out[:, cut(i + 2 * groups, wide)] = grad_v
        sums[0:1, here] = column_sum(grad_q.astype(f32))
        sums[1:2, here] = column_sum(grad_v.astype(f32))
        pieces = (
            dot(turned[...], grad_q).astype(bf16),
            dot(turned[...], grad_k).astype(bf16),
            dot(turned[...], grad_v).astype(bf16),
            dot(turned_context[...], attended[:, here]).astype(bf16),
        )
        for s, (keep, send) in enumerate(((keep_0, send_0), (keep_1, send_1), (keep_2, send_2))):

            @pl.when(i == s)
            def _(keep=keep, send=send):
                for x in range(2):
                    keep[x] = jnp.where(odd, pieces[2 * x + 1], pieces[2 * x])
                    send[x] = jnp.where(odd, pieces[2 * x], pieces[2 * x + 1])

    sums[2:5, :] = vector_one[0:3, :]
    sums[5:8, :] = vector_two[0:3, :]
    sums[8:12, :] = bias_up[...]
    share = width // shares
    small[...] = jnp.zeros_like(small)
    for d, by_blk in enumerate(small_pieces(shares, width)):
        for b, three in enumerate(by_blk):
            for j, (row, column) in enumerate(three):
                small[b, d, j : j + 1, 0:share] = sums[row : row + 1, column : column + share]
    for x in range(2):
        even_part = small[2 * x].astype(bf16)
        odd_part = small[2 * x + 1].astype(bf16)
        small_keep[x] = jnp.where(odd, odd_part, even_part)
        small_send[x] = jnp.where(odd, even_part, odd_part)


def attend_back(place, attended, small, far, shares, after):
    count, width = attended.shape
    head_width = width // HEADS
    wide = 4 * head_width
    groups = width // wide
    rows, turned = pltpu.VMEM((count, width), bf16), pltpu.VMEM((width, count), bf16)
    keep_0, keep_1, keep_2, send_0, send_1, send_2, small_keep, small_send, grads = call(
        functools.partial(attend_back_kernel, head_width=head_width),
        "attend_back", [place], [attended, *small],
        [shape(2, width, wide)] * 6 + [shape(2, shares, 16, wide)] * 2 + [shape(count, 3 * width)],
        10 * count * width * width + 40 * count * count * width,
        [
            pltpu.VMEM((2, count, width), bf16), turned, turned,
            pltpu.VMEM((groups, 4, count, count), bf16), rows, rows, rows,
            pltpu.VMEM((width, width), bf16),
            pltpu.VMEM((16, width), f32), pltpu.VMEM((4, shares, 16, wide), f32),
        ],
        far, [], 5 * groups + 2, 28, after,
    )
    return [keep_0, keep_1, keep_2], [send_0, send_1, send_2], small_keep, small_send, grads


def grad_tokens_kernel(grads, sum_one, w_qkv, r0, r1, r2, r3, total, weights, sems):
    width = sum_one.shape[1]

    def load(i):
        return copy(w_qkv.at[:, cut(i, width)], weights.at[i], sems.at[i])

    load_sum = copy(sum_one, total, sems.at[3])
    load(0).start()
    load_sum.start()
    load(1).start()
    load_sum.wait()

    @pl.loop(0, 3)
    def _(i):
        @pl.when(i == 0)
        def _():
            load(2).start()

        load(i).wait()
        total[...] += dot(grads[:, cut(i, width)], weights[i], NT)

    result = total[...].astype(bf16)
    slots = r0.shape[0]
    for i, block in enumerate((r0, r1, r2, r3)):
        block[...] = result[i * slots : (i + 1) * slots, :]


def grad_tokens(sum_one, grads, w_qkv, slots, after):
    count, width = sum_one.shape
    return call(
        grad_tokens_kernel, "grad_tokens", [], [grads], [shape(slots, width)] * 4,
        6 * count * width * width,
        [pltpu.VMEM((count, width), f32), pltpu.VMEM((3, width, width), bf16)],
        [sum_one, w_qkv], [], 4, 12, after,
    )


def swap(block, axis, bit):
    return lax.ppermute(block, axis, [(i, i ^ bit) for i in range(lax.axis_size(axis))])


def pick(block, index, dim=0):
    return lax.dynamic_index_in_dim(block, index, dim, keepdims=False)


def every(count, work):
    if count <= 8:
        for number in range(count):
            work(number)
    else:
        pl.loop(0, count)(work)


def cut_units(bits, units, extra, orders, flip, after):
    parts, dims = len(orders), len(orders[0])
    arrays, numbers = [], {}
    for array in [a for unit in units for part in unit for a in part[:2]] + list(extra):
        if id(array) not in numbers:
            numbers[id(array)] = len(arrays)
            arrays.append(array)
    rows = arrays[0].shape[-2]
    size = sum({id(part[0]): part[0].shape[-1] for part in units[0]}.values()) // parts
    more = [extra[0].shape[-2] if extra and s == 0 else 0 for s in range(parts)]
    outs = [shape(2 ** (dims - 1), len(units) * rows + m, size) for m in more]

    def kernel(bits_ref, *refs):
        ins, results = refs[: len(arrays)], refs[len(arrays) :]

        def work(number):
            for s, order in enumerate(orders):
                index = [None] * dims
                index[order[0]] = bits_ref[order[0]] ^ flip
                for i, n in enumerate(order[1:]):
                    index[n] = (number >> (dims - 2 - i)) & 1
                for u, unit in enumerate(units):
                    kept, arrived, column = unit[s]
                    at = (*index, slice(None), slice(column * size, (column + 1) * size))
                    total = ins[numbers[id(kept)]][at] + ins[numbers[id(arrived)]][at]
                    results[s][number, u * rows : (u + 1) * rows] = total
                if more[s]:
                    kept, arrived = [ins[numbers[id(a)]] for a in extra]
                    at = tuple(index)
                    results[s][number, len(units) * rows :] = kept[at] + arrived[at]

        every(2 ** (dims - 1), work)

    return call(kernel, "cut_units", [bits], arrays, outs, 0, after=after)


def halve(bits, pairs, axes, join, after=()):
    taken = pairs[0][0].shape[0] // (2 if axes else 1)
    sizes = [a.shape[1] for a, _ in pairs]
    width = pairs[0][0].shape[2]
    flips = (1, 0) if axes else (0,)
    outs = [shape(taken, sum(sizes), width)] if join else [shape(taken, n, width) for n in sizes]
    arrays = [a for pair in pairs for a in pair]

    def kernel(bits_ref, *refs):
        ins, results = refs[: len(arrays)], refs[len(arrays) :]

        def work(number):
            for f, flip in enumerate(flips):
                for s in range(len(pairs)):
                    at = number + ((bits_ref[axes[s]] ^ flip) * taken if axes else 0)
                    total = ins[2 * s][at] + ins[2 * s + 1][at]
                    if join:
                        first = sum(sizes[:s])
                        results[f][number, first : first + sizes[s]] = total
                    else:
                        results[f * len(pairs) + s][number] = total

        every(taken, work)

    made = call(kernel, "halve", [bits], arrays, outs * len(flips), 0, after=after)
    return made[: len(outs)], made[len(outs) :]


class Group:
    def __init__(self, units, extra, bits, names):
        self.units, self.extra, self.bits, self.names = units, extra, bits, names
        size = len(names)
        turn = [0, size - 1, size - 2]
        rest = list(range(size - 3, 0, -1))
        self.orders = [turn[s:] + turn[:s] + rest for s in range(3)]
        self.stage = 0
        self.pairs = None

    def step(self, after=()):
        if self.stage == 0:
            sent = cut_units(self.bits, self.units, self.extra, self.orders, 1, after)
            keep = cut_units(self.bits, self.units, self.extra, self.orders, 0, [sent[0]])
        else:
            axes = [order[self.stage] for order in self.orders]
            sent, keep = halve(self.bits, self.pairs, axes, self.stage == 3, after)
        arrived = [
            swap(block, *self.names[order[self.stage]]) for block, order in zip(sent, self.orders)
        ]
        self.pairs = list(zip(keep, arrived))
        self.stage += 1
        return sent

    def finish(self, after=()):
        (own,), _ = halve(self.bits, self.pairs, None, False, after)
        across = swap(own, "blk", 2)
        return own, swap(own, "blk", 1), across, swap(across, "blk", 1)


def chosen(place, b, refs):
    relative = place[1] ^ b
    values = [ref[...] for ref in refs]
    return jnp.where(
        relative < 2,
        jnp.where(relative == 0, values[0], values[1]),
        jnp.where(relative == 2, values[2], values[3]),
    ).astype(f32)


def place_feed(place, pieces, rows, shares):
    size = pieces[0].shape[2]
    width = 3 * size

    def kernel(place_ref, p0, p1, p2, p3, down, up):
        for b in range(4):
            for s in range(3):
                at = 2 * s * rows
                columns = slice(s * size, (s + 1) * size)
                value = chosen(place_ref, b, [p.at[0, at : at + rows] for p in (p0, p1, p2, p3)])
                down[b * rows : (b + 1) * rows, columns] = value
                at = at + rows
                columns = slice(b * width + s * size, b * width + (s + 1) * size)
                value = chosen(place_ref, b, [p.at[0, at : at + rows] for p in (p0, p1, p2, p3)])
                up[:, columns] = value

    return call(
        kernel, "place_feed", [place], pieces,
        [shape(4 * rows, width, dtype=f32), shape(rows, 4 * width, dtype=f32)], 0,
    )


def place_own(place, pieces, rows, shares):
    size = pieces[0].shape[2]
    width = 3 * size
    share = width // shares
    extra = pieces[0].shape[1] - 3 * rows

    def kernel(place_ref, p0, p1, p2, p3, qkv, out, *small):
        refs = (p0, p1, p2, p3)
        bias_qv, bias_out, gain_one, shift_one, bias_up, bias_down, gain_two, shift_two = small
        for b in range(4):
            for s in range(3):
                at = s * rows + (extra if s else 0)
                value = chosen(place_ref, b, [p.at[0, at : at + rows] for p in refs])
                columns = slice(s * size, (s + 1) * size)
                if b == 3:
                    out[:, columns] = value
                else:
                    qkv[:, b * width + s * size : b * width + (s + 1) * size] = value
            value = chosen(place_ref, b, [p.at[0, rows : rows + extra] for p in refs])
            targets = (
                ((bias_qv, 0), (bias_qv, 1), (bias_out, 0)),
                ((gain_one, 0), (shift_one, 0), (bias_down, 0)),
                ((gain_two, 0), (shift_two, 0), (bias_up, 0)),
                ((bias_up, 1), (bias_up, 2), (bias_up, 3)),
            )[b]
            for j, (ref, part) in enumerate(targets):
                ref[:, part * share : (part + 1) * share] = value[j : j + 1, 0:share]

    vectors = [shape(1, n * share, dtype=f32) for n in (2, 1, 1, 1, 4, 1, 1, 1)]
    return call(
        kernel, "place_own", [place], pieces,
        [shape(rows, 3 * width, dtype=f32), shape(rows, width, dtype=f32), *vectors], 0,
    )


def place_rows(place, blocks, after):
    slots, width = blocks[0].shape

    def kernel(place_ref, *refs):
        for i in range(4):
            refs[4][place_ref[1] ^ i] = refs[i][...]

    return call(kernel, "place_rows", [place], blocks, [shape(4, slots, width)], 0, after=after)[0]


def shards(
    tokens, lengths, w_qkv, bias_qv, w_out, bias_out, norm1_gain, norm1_bias, w_up, bias_up,
    w_down, bias_down, norm2_gain, norm2_bias, cotangent,
):
    rows, slots, width = tokens.shape
    shares = lax.axis_size("dp")
    dp_bits = shares.bit_length() - 1
    position = lax.axis_index("blk").astype(jnp.int32)
    group = lax.axis_index("dp").astype(jnp.int32)
    place = jnp.stack([position % 2, position])
    names = [("blk", 2)] + [("dp", 1 << i) for i in reversed(range(dp_bits))]
    bits = jnp.stack([position // 2] + [(group >> i) % 2 for i in reversed(range(dp_bits))])

    def gather_row(array):
        return [pick(array, position)] + [
            swap(pick(array, position ^ i), "blk", i) for i in (2, 3, 1)
        ]

    def in_order(blocks):
        return [blocks[0], blocks[3], blocks[1], blocks[2]]

    def scatter_row(blocks, after=()):
        moved = [blocks[0]] + [swap(blocks[i], "blk", i) for i in range(1, rows)]
        return place_rows(place, moved, after)

    vectors = jnp.concatenate(
        [bias_qv, bias_out, norm1_gain, norm1_bias, bias_down, norm2_gain, norm2_bias, bias_up]
    ).reshape(-1, width)
    row = jnp.concatenate([pick(lengths, position), position[None]])
    blocks = gather_row(tokens)
    blocks, cotangent = lax.optimization_barrier((blocks, cotangent))
    blocks = in_order(blocks)
    cotangents = in_order(gather_row(cotangent))
    normed, inverse, q, k, v, prob, context, row_tokens = attend(
        row, blocks, w_qkv, w_out, vectors
    )
    active, slope, o0, o1, o2, o3, lowered, first, vector_two, sum_two, normed_far = feed(
        normed, w_up, w_down, vectors, cotangents
    )
    keep_down, send_down = grad_down(place, active, lowered, shares)
    got_down = swap(send_down, "blk", 1)
    raised, keep_up, send_up, grad_bias_up = grad_up(place, lowered, slope, w_down, first)
    got_up = swap(send_up, "blk", 1)
    outputs = scatter_row([o0, o1, o2, o3], [raised])
    attended, vector_one, sum_one = first_back(
        raised, w_up, sum_two, normed_far, inverse, vectors, [outputs]
    )

    def chunks(array):
        return array.reshape((2,) * (1 + dp_bits) + (-1, array.shape[-1]))

    def thirds(kept, arrived):
        return [(kept, arrived, s) for s in range(3)]

    feed_group = Group(
        [
            thirds(chunks(keep_down), chunks(got_down)),
            thirds(chunks(keep_up), chunks(got_up)),
        ],
        (), bits, names,
    )
    sent = feed_group.step([attended])
    keeps, sends, small_keep, small_send, grads = attend_back(
        place, attended, [vector_one, vector_two, grad_bias_up],
        [row_tokens, context, prob, q, k, v, w_out], shares, [sent[0]],
    )
    gots = [swap(send, "blk", 1) for send in sends]
    small_got = swap(small_send, "blk", 1)
    sent = feed_group.step([grads])
    tokens_parts = grad_tokens(sum_one, grads, w_qkv, slots, [sent[0]])
    own_group = Group(
        [[(chunks(keep), chunks(got), 0) for keep, got in zip(keeps, gots)]],
        (chunks(small_keep), chunks(small_got)), bits, names,
    )
    sent = own_group.step([tokens_parts[0]])
    for stage in range(2, dp_bits + 1):
        sent = feed_group.step([sent[0]])
        if stage > 2:
            sent = own_group.step([sent[0]])
    sent = own_group.step([sent[0]])
    feed_pieces = feed_group.finish([sent[0]])
    sent = own_group.step([feed_pieces[0]])
    own_pieces = own_group.finish([sent[0]])

    share = width // shares
    down, up = place_feed(place, feed_pieces, share, shares)
    (
        grad_w_qkv, grad_w_out, sum_qv, sum_out, sum_gain_one, sum_shift_one, sum_up, sum_down,
        sum_gain_two, sum_shift_two,
    ) = place_own(place, own_pieces, share, shares)
    return (
        outputs,
        scatter_row(tokens_parts),
        grad_w_qkv,
        sum_qv[0],
        grad_w_out,
        sum_out[0],
        sum_gain_one[0],
        sum_shift_one[0],
        up,
        sum_up[0],
        down,
        sum_down[0],
        sum_gain_two[0],
        sum_shift_two[0],
    )


def solution(mesh):
    row_spec = P("dp", "blk", None)
    in_specs = (row_spec, P("dp", None)) + (P(),) * 12 + (row_spec,)
    wide, flat = P("dp", None), P("dp")
    out_specs = (
        row_spec, row_spec, wide, flat, wide, flat, flat, flat, wide, flat, wide, flat, flat, flat,
    )
    return jax.shard_map(shards, mesh=mesh, in_specs=in_specs, out_specs=out_specs, check_vma=False)
```

time: 772 us -> 193 us (0.25)
  waiting for transfers between devices: 493 us -> 55.6 us
  matrix products: 104 us -> 0 us
  Pallas kernels: 0 us -> 83 us
  local copies, waits for them, and re-layouts: 62.5 us -> 16.3 us
  blocking collectives: 43.7 us -> 0 us
  other arithmetic: 42.6 us -> 0.83 us
  starting transfers between devices: 1.45 us -> 35.3 us
  between operations: 17 us -> 1.07 us
    reduce_scatter x3 -> x0, waiting for transfers between devices: 263 us -> none  [the longest x1 164 us: shards(): lax.psum_scatter(grad_w_down, 'dp', scatter_dimension=0, tiled=True)]
    unnamed x6 -> x0, waiting for transfers between devices: 130 us -> none
    dot_general x36 -> x0, matrix products: 104 us -> none  [the longest x4 24.7 us: contract_rows(): lax.dot_general(left, right, (((0,), (0,)), ((), ())), preferred_element_...]
    pallas_call x0 -> x23, Pallas kernels: none -> 83 us  [call(): pl.pallas_call(body, in_specs=[SMEM] * len(scalars) + [VMEM] * len(arrays...]
    ppermute x7 -> x44, waiting for transfers between devices: 100 us -> 55.6 us  [swap(): lax.ppermute(block, axis, [(i, i ^ bit) for i in range(lax.axis_size(axis...]
    unnamed x1 -> x0, blocking collectives: 36.8 us -> none
    ppermute x7 -> x44, starting transfers between devices: 1.25 us -> 35.3 us  [swap(): lax.ppermute(block, axis, [(i, i ^ bit) for i in range(lax.axis_size(axis...]
    convert_element_type x18 -> x0, other arithmetic: 25.5 us -> none  [the longest x1 3.26 us: shards(): queries = (projected[:, :model_width] + bias_qv[:model_width]).astype(jnp...]
  transfers between devices with their start and end apart: 12 -> 44, of which waited for: 10 -> 14; matrix products, arithmetic and copies ran while one was open for 16% -> 3% of each run, Pallas kernels for 0% -> 32%
where the time goes in v2:
time: 193 us; the launch traced here: 192 us
  Pallas kernels  83 us (43%)
  waiting for transfers between devices  55.6 us (29%)
  starting transfers between devices  35.3 us (18%)
  local copies, waits for them, and re-layouts  16.3 us (8%)
    pallas_call x23, Pallas kernels, call(): pl.pallas_call(body, in_specs=[SMEM] * len(scalars) + [VMEM] * len(arrays...  83 us
    ppermute x44, waiting for transfers between devices, swap(): lax.ppermute(block, axis, [(i, i ^ bit) for i in range(lax.axis_size(axis...  55.6 us
    ppermute x44, starting transfers between devices, swap(): lax.ppermute(block, axis, [(i, i ^ bit) for i in range(lax.axis_size(axis...  35.3 us
    unnamed x39, local copies, waits for them, and re-layouts  14.2 us
  transfers between devices with their start and end apart: 44, of which 14 were waited for; matrix products, arithmetic and copies ran while one was open for 3% of the time, Pallas kernels for 32%

profile of v2, /device:TPU:0, one launch (start us, length us, event | category | flops | bytes accessed | tf_op | source)
XLA Modules:
  0.0 192.1 jit_solution(9793189454113148106)
XLA Ops:
  0.7 1.3 dynamic-slice_bitcast_fusion.4
  2.6 2.6 %collective-permute-start = (bf16[128,768]{1,0:T(8,128)(2,1)S(1)}, bf16[128,768]{1,0:T(8,128)(2,1)S(1)}, u32[]{:S(2)}, u32[]{:S(2)}) collective-permute-start(bf16[128,768]{1,0:T(8,128)(2,1)S(1)} %get-tuple-element.215), channel_id=1, source_target_pairs={{0,2},{1,3},{2,0},{3,1},{4,6},{5,7},{6,4},{7,5},{8,10},{9,11},{10,... | collective-permute-start | bytes 589832 | tf_op jit(solution)/shard_map/ppermute | solution.py:577
  10.9 3.6 %collective-permute-done.1.refs_4_ = bf16[128,768]{1,0:T(8,128)(2,1)S(1)} collective-permute-done((bf16[128,768]{1,0:T(8,128)(2,1)S(1)}, bf16[128,768]{1,0:T(8,128)(2,1)S(1)}, u32[]{:S(2)}, u32[]{:S(2)}) %collective-permute-start.1) | collective-permute-done | bytes 196640 | tf_op jit(solution)/shard_map/ppermute | solution.py:577
  14.6 1.5 collective-permute-start.5
  16.7 13.0 %attend.1 = (f32[512,768]{1,0:T(8,128)S(1)}, f32[512,1]{1,0:T(8,128)S(1)}, bf16[512,768]{1,0:T(8,128)(2,1)}, bf16[512,768]{1,0:T(8,128)(2,1)}, bf16[512,768]{1,0...) custom-call(s32[9]{0:T(128)S(1)} %pad_add_fusion.1.refs_0_, ...), custom_call_target="tpu_custom_call" | custom-call | flops 20000000000 | tf_op jit(solution)/shard_map/attend/pallas_call | solution.py:46
  29.8 11.1 %feed.1 = (bf16[512,3072]{1,0:T(8,128)(2,1)S(1)}, bf16[512,3072]{1,0:T(8,128)(2,1)S(1)}, bf16[128,768]{1,0:T(8,128)(2,1)S(1)}, bf16[128,768]{1,0:T(8,128)(2,1)},...) custom-call(f32[512,768]{1,0:T(8,128)S(1)} %get-tuple-element.116.re, ...), custom_call_target="tpu_custom_call" | custom-call | flops 20000000000 | tf_op jit(solution)/shard_map/feed/pallas_call | solution.py:46
  40.9 5.4 %grad_down.1 = (bf16[2,8,96,768]{3,2,1,0:T(8,128)(2,1)S(1)}, bf16[2,8,96,768]{3,2,1,0:T(8,128)(2,1)}) custom-call(s32[2]{0:T(128)S(1)} %pad_add_fusion.refs_0_, bf16[512,3072]{1,0:T(8,128)(2,1)S(1)} %get-tuple-element.139.refs_1_, bf16[512,768]{1,0:T(8,128)(2,1)S(1)} %get-tuple-element.122.refs_1_.refs_2_), custom_call_target="tpu_custom_call" | custom-call | flops 20000000000 | tf_op jit(solution)/shard_map/grad_down/pallas_call | solution.py:46
  46.7 6.4 %grad_up.1 = (bf16[512,3072]{1,0:T(8,128)(2,1)S(1)}, bf16[2,768,768]{2,1,0:T(8,128)(2,1)S(1)}, bf16[2,768,768]{2,1,0:T(8,128)(2,1)}, f32[4,768]{1,0:T(4,128)S(1)}) custom-call(s32[2]{0:T(128)S(1)} %pad_add_fusion.refs_0_, bf16[512,768]{1,0:T(8,128)(2,1)S(1)} %get-tuple-element.122.refs_1_.refs_2_, bf16[512,3072]{1,0:T(8,128)(2,1)S(1)} %get-tuple-element.123.refs_2_, ...), custom_call_target="tpu_custom_call" | custom-call | flops 10000000 | tf_op jit(solution)/shard_map/grad_up/pallas_call | solution.py:46
  53.2 1.4 copy-done.2
  54.6 1.7 copy-done.4
  56.9 1.8 collective-permute-start.7
  58.7 2.3 %collective-permute-done.6.refs_2_ = bf16[128,768]{1,0:T(8,128)(2,1)S(1)} collective-permute-done((bf16[128,768]{1,0:T(8,128)(2,1)}, bf16[128,768]{1,0:T(8,128)(2,1)S(1)}, u32[]{:S(2)}, u32[]{:S(2)}) %collective-permute-start.6) | collective-permute-done | bytes 196640 | tf_op jit(solution)/shard_map/ppermute | solution.py:577
  61.1 3.8 %collective-permute-done.7.refs_3_ = bf16[128,768]{1,0:T(8,128)(2,1)S(1)} collective-permute-done((bf16[128,768]{1,0:T(8,128)(2,1)}, bf16[128,768]{1,0:T(8,128)(2,1)S(1)}, u32[]{:S(2)}, u32[]{:S(2)}) %collective-permute-start.7) | collective-permute-done | bytes 196640 | tf_op jit(solution)/shard_map/ppermute | solution.py:577
  64.8 2.6 %collective-permute-done.8.refs_4_ = bf16[128,768]{1,0:T(8,128)(2,1)S(1)} collective-permute-done((bf16[128,768]{1,0:T(8,128)(2,1)S(1)}, bf16[128,768]{1,0:T(8,128)(2,1)S(1)}, u32[]{:S(2)}, u32[]{:S(2)}) %collective-permute-start.8) | collective-permute-done | bytes 196640 | tf_op jit(solution)/shard_map/ppermute | solution.py:577
  67.4 1.9 copy-done.5
  69.3 1.5 place_rows.2.refs_6_
  71.5 1.1 copy-done.7
  72.6 2.3 %copy-done.8 = bf16[768,3072]{1,0:T(8,128)(2,1)S(1)} copy-done((bf16[768,3072]{1,0:T(8,128)(2,1)S(1)}, bf16[768,3072]{1,0:T(8,128)(2,1)}, u32[]{:S(2)}) %copy-start.8) | copy-done | bytes 4718616
  75.0 6.5 %first_back.1 = (bf16[512,768]{1,0:T(8,128)(2,1)S(1)}, f32[8,768]{1,0:T(8,128)S(1)}, f32[512,768]{1,0:T(8,128)}) custom-call(bf16[512,3072]{1,0:T(8,128)(2,1)S(1)} %copy-done.6, f32[512,1]{1,0:T(8,128)S(1)} %copy-done.10, f32[12,768]{1,0:T(8,128)S(1)} %reshape.67.refs_5_.refs_1_.refs_2_, bf16[768,3072]{1,0:T(8,128)(2,1)S(1)} %copy-done.8, ...), custom_call_target="tpu_custom_call" | custom-call | flops 20000000000 | tf_op jit(solution)/shard_map/first_back/pallas_call | solution.py:46
  81.5 2.6 %cut_units.4 = (bf16[8,192,256]{2,1,0:T(8,128)(2,1)S(1)}, bf16[8,192,256]{2,1,0:T(8,128)(2,1)S(1)}, bf16[8,192,256]{2,1,0:T(8,128)(2,1)S(1)}) custom-call(s32[4]{0:T(128)S(1)} %pad_add_fusion.2.refs_0_, bf16[2,2,2,2,96,768]{5,4,3,2,1,0:T(8,128)(2,1)S(1)} %bitcast.43, bf16[2,2,2,2,96,768]{5,4,3,2,1,0:T(8,128)(2,1)} %bitcast.16.refs_2_, ...), custom_call_target="tpu_custom_call" | custom-call | tf_op jit(solution)/shard_map/cut_units/pallas_call | solution.py:46
  84.1 1.6 collective-permute-start.12
  85.7 1.6 collective-permute-start.13
  87.3 1.5 collective-permute-start.11
  88.8 17.6 %attend_back.1 = (bf16[2,768,256]{2,1,0:T(8,128)(2,1)S(1)}, bf16[2,768,256]{2,1,0:T(8,128)(2,1)S(1)}, bf16[2,768,256]{2,1,0:T(8,128)(2,1)S(1)}, bf16[2,768,256]{...) custom-call(s32[2]{0:T(128)S(1)} %pad_add_fusion.refs_0_, ...), custom_call_target="tpu_custom_call" | custom-call | flops 40000000000 | tf_op jit(solution)/shard_map/attend_back/pallas_call | solution.py:46
  106.9 2.6 %cut_units.5 = (bf16[8,192,256]{2,1,0:T(8,128)(2,1)S(1)}, bf16[8,192,256]{2,1,0:T(8,128)(2,1)S(1)}, bf16[8,192,256]{2,1,0:T(8,128)(2,1)S(1)}) custom-call(s32[4]{0:T(128)S(1)} %pad_add_fusion.2.refs_0_, bf16[2,2,2,2,96,768]{5,4,3,2,1,0:T(8,128)(2,1)S(1)} %bitcast.44, bf16[2,2,2,2,96,768]{5,4,3,2,1,0:T(8,128)(2,1)} %bitcast.16.refs_2_, ...), custom_call_target="tpu_custom_call" | custom-call | tf_op jit(solution)/shard_map/cut_units/pallas_call | solution.py:46
  110.2 0.8 halve.8
  112.5 4.6 %grad_tokens.1 = (bf16[128,768]{1,0:T(8,128)(2,1)S(1)}, bf16[128,768]{1,0:T(8,128)(2,1)S(1)}, bf16[128,768]{1,0:T(8,128)(2,1)S(1)}, bf16[128,768]{1,0:T(8,128)(2,1)S(1)}) custom-call(bf16[512,2304]{1,0:T(8,128)(2,1)S(1)} %get-tuple-element.145.refs_7_.refs_0_, f32[512,768]{1,0:T(8,128)} %get-tuple-element.146.refs_1_, bf16[768,2304]{1,0:T(8,128)(2,1)} %refs_2_.1, ...), custom_call_target="tpu_custom_call" | custom-call | flops 10000000000 | tf_op jit(solution)/shard_map/grad_tokens/pallas_call | solution.py:46
  117.8 1.6 collective-permute-start.21
  119.4 2.7 %collective-permute-done.25.refs_4_ = bf16[4,192,256]{2,1,0:T(8,128)(2,1)S(1)} collective-permute-done((bf16[4,192,256]{2,1,0:T(8,128)(2,1)S(1)}, bf16[4,192,256]{2,1,0:T(8,128)(2,1)S(1)}, u32[]{:S(2)}, u32[]{:S(2)}) %collective-permute-start.25) | collective-permute-done | bytes 393248 | tf_op jit(solution)/shard_map/ppermute | solution.py:577
  122.1 1.4 collective-permute-done.26.refs_6_
  125.3 1.6 collective-permute-start.23
  126.9 1.5 collective-permute-start.29
  128.4 8.0 %collective-permute-done.28.refs_4_ = bf16[2,192,256]{2,1,0:T(8,128)(2,1)S(1)} collective-permute-done((bf16[2,192,256]{2,1,0:T(8,128)(2,1)S(1)}, bf16[2,192,256]{2,1,0:T(8,128)(2,1)S(1)}, u32[]{:S(2)}, u32[]{:S(2)}) %collective-permute-start.28) | collective-permute-done | bytes 196640 | tf_op jit(solution)/shard_map/ppermute | solution.py:577
  136.3 1.6 collective-permute-start.27
  138.3 3.7 %collective-permute-done.27.refs_2_ = bf16[2,192,256]{2,1,0:T(8,128)(2,1)S(1)} collective-permute-done((bf16[2,192,256]{2,1,0:T(8,128)(2,1)S(1)}, bf16[2,192,256]{2,1,0:T(8,128)(2,1)S(1)}, u32[]{:S(2)}, u32[]{:S(2)}) %collective-permute-start.27) | collective-permute-done | bytes 196640 | tf_op jit(solution)/shard_map/ppermute | solution.py:577
  142.7 2.7 %collective-permute-start.36 = (bf16[1,576,256]{2,1,0:T(8,128)(2,1)S(1)}, bf16[1,576,256]{2,1,0:T(8,128)(2,1)S(1)}, u32[]{:S(2)}, u32[]{:S(2)}) collective-permute-start(bf16[1,576,256]{2,1,0:T(8,128)(2,1)S(1)} %get-tuple-element.182.refs_7_), channel_id=1, source_target_pairs={{0,16},{4,20},{8,24},{12,28},{16,0},{20,4},{24,8},{28,12},{1,17},{... | collective-permute-start | bytes 884744 | tf_op jit(solution)/shard_map/ppermute | solution.py:577
  147.3 1.6 collective-permute-start.31
  149.5 7.4 %collective-permute-done.31.refs_4_ = bf16[4,96,256]{2,1,0:T(8,128)(2,1)S(1)} collective-permute-done((bf16[4,96,256]{2,1,0:T(8,128)(2,1)S(1)}, bf16[4,96,256]{2,1,0:T(8,128)(2,1)S(1)}, u32[]{:S(2)}, u32[]{:S(2)}) %collective-permute-start.31) | collective-permute-done | bytes 196640 | tf_op jit(solution)/shard_map/ppermute | solution.py:577
  158.7 1.5 collective-permute-start.34
  160.2 1.2 collective-permute-start.35
  161.3 5.9 %collective-permute-done.34.refs_4_ = bf16[2,96,256]{2,1,0:T(8,128)(2,1)S(1)} collective-permute-done((bf16[2,96,256]{2,1,0:T(8,128)(2,1)S(1)}, bf16[2,96,256]{2,1,0:T(8,128)(2,1)S(1)}, u32[]{:S(2)}, u32[]{:S(2)}) %collective-permute-start.34) | collective-permute-done | bytes 98336 | tf_op jit(solution)/shard_map/ppermute | solution.py:577
  169.1 8.1 %collective-permute-done.37.refs_2_ = bf16[1,304,256]{2,1,0:T(8,128)(2,1)S(1)} collective-permute-done((bf16[1,304,256]{2,1,0:T(8,128)(2,1)S(1)}, bf16[1,304,256]{2,1,0:T(8,128)(2,1)S(1)}, u32[]{:S(2)}, u32[]{:S(2)}) %collective-permute-start.37) | collective-permute-done | bytes 155680 | tf_op jit(solution)/shard_map/ppermute | solution.py:577
  179.1 1.1 collective-permute-start.16
  180.6 3.7 %collective-permute-done.39.refs_3_ = bf16[1,304,256]{2,1,0:T(8,128)(2,1)S(1)} collective-permute-done((bf16[1,304,256]{2,1,0:T(8,128)(2,1)S(1)}, bf16[1,304,256]{2,1,0:T(8,128)(2,1)S(1)}, u32[]{:S(2)}, u32[]{:S(2)}) %collective-permute-start.39) | collective-permute-done | bytes 155680 | tf_op jit(solution)/shard_map/ppermute | solution.py:577
  184.3 1.9 %collective-permute-done.16.refs_4_ = bf16[128,768]{1,0:T(8,128)(2,1)S(1)} collective-permute-done((bf16[128,768]{1,0:T(8,128)(2,1)S(1)}, bf16[128,768]{1,0:T(8,128)(2,1)S(1)}, u32[]{:S(2)}, u32[]{:S(2)}) %collective-permute-start.16) | collective-permute-done | bytes 196640 | tf_op jit(solution)/shard_map/ppermute | solution.py:577
  186.2 1.5 place_rows.3
  187.7 1.6 place_own.1
  189.9 2.2 %place_feed.1 = (f32[384,768]{1,0:T(8,128)}, f32[96,3072]{1,0:T(8,128)}) custom-call(s32[2]{0:T(128)S(1)} %pad_add_fusion.refs_0_, bf16[1,576,256]{2,1,0:T(8,128)(2,1)S(1)} %halve.13.refs_7_.refs_1_, bf16[1,576,256]{2,1,0:T(8,128)(2,1)S(1)} %collective-permute-done.41.refs_2_, bf16[1,576,256]{2,1,0:T(8,128)(2,1)S(1)} %collective-permute-done.42.refs_3_, ...), custom_call_target="tpu_custom_call" | custom-call | tf_op jit(solution)/shard_map/place_feed/pallas_call | solution.py:46
  (114 shorter events, 24.0 us)
Async XLA Ops:
  0.7 13.9 %copy-start.11 = (bf16[4,128,768]{2,1,0:T(8,128)(2,1)S(1)}, bf16[4,128,768]{2,1,0:T(8,128)(2,1)}, u32[]{:S(2)}) copy-start(bf16[4,128,768]{2,1,0:T(8,128)(2,1)} %param.29) | copy-start | bytes 2359300
  2.0 8.9 %collective-permute-start.2 = (bf16[128,768]{1,0:T(8,128)(2,1)S(1)}, bf16[128,768]{1,0:T(8,128)(2,1)S(1)}, u32[]{:S(2)}, u32[]{:S(2)}) collective-permute-start(bf16[128,768]{1,0:T(8,128)(2,1)S(1)} %get-tuple-element.214), channel_id=1, source_target_pairs={{0,1},{1,0},{2,3},{3,2},{4,5},{5,4},{6,7},{7,6},{8,9},{9,8},{10,11... | collective-permute-start | bytes 589832 | tf_op jit(solution)/shard_map/ppermute | solution.py:577
  2.6 8.4 %collective-permute-start = (bf16[128,768]{1,0:T(8,128)(2,1)S(1)}, bf16[128,768]{1,0:T(8,128)(2,1)S(1)}, u32[]{:S(2)}, u32[]{:S(2)}) collective-permute-start(bf16[128,768]{1,0:T(8,128)(2,1)S(1)} %get-tuple-element.215), channel_id=1, source_target_pairs={{0,2},{1,3},{2,0},{3,1},{4,6},{5,7},{6,4},{7,5},{8,10},{9,11},{10,... | collective-permute-start | bytes 589832 | tf_op jit(solution)/shard_map/ppermute | solution.py:577
  5.1 9.4 %collective-permute-start.1 = (bf16[128,768]{1,0:T(8,128)(2,1)S(1)}, bf16[128,768]{1,0:T(8,128)(2,1)S(1)}, u32[]{:S(2)}, u32[]{:S(2)}) collective-permute-start(bf16[128,768]{1,0:T(8,128)(2,1)S(1)} %get-tuple-element.217), channel_id=1, source_target_pairs={{0,3},{1,2},{2,1},{3,0},{4,7},{5,6},{6,5},{7,4},{8,11},{9,10},{10,... | collective-permute-start | bytes 589832 | tf_op jit(solution)/shard_map/ppermute | solution.py:577
  14.6 15.1 %collective-permute-start.5 = (bf16[128,768]{1,0:T(8,128)(2,1)S(1)}, bf16[128,768]{1,0:T(8,128)(2,1)S(1)}, u32[]{:S(2)}, u32[]{:S(2)}) collective-permute-start(bf16[128,768]{1,0:T(8,128)(2,1)S(1)} %get-tuple-element.210), channel_id=1, source_target_pairs={{0,3},{1,2},{2,1},{3,0},{4,7},{5,6},{6,5},{7,4},{8,11},{9,10},{10,... | collective-permute-start | bytes 589832 | tf_op jit(solution)/shard_map/ppermute | solution.py:577
  16.1 13.6 %collective-permute-start.4 = (bf16[128,768]{1,0:T(8,128)(2,1)S(1)}, bf16[128,768]{1,0:T(8,128)(2,1)S(1)}, u32[]{:S(2)}, u32[]{:S(2)}) collective-permute-start(bf16[128,768]{1,0:T(8,128)(2,1)S(1)} %get-tuple-element.211), channel_id=1, source_target_pairs={{0,2},{1,3},{2,0},{3,1},{4,6},{5,7},{6,4},{7,5},{8,10},{9,11},{10,... | collective-permute-start | bytes 589832 | tf_op jit(solution)/shard_map/ppermute | solution.py:577
  16.4 13.3 %slice-start.1 = ((s8[4718592]{0:T(1024)(128)(4,1)}), s8[524288]{0:T(1024)(128)(4,1)S(1)}, s32[]{:S(2)}) async-start(s8[4718592]{0:T(1024)(128)(4,1)} %bitcast.47), calls=%async_computation.1 | async-start | bytes 1048576
  16.4 13.3 %slice-start.3 = ((s8[4718592]{0:T(1024)(128)(4,1)}), s8[524288]{0:T(1024)(128)(4,1)S(1)}, s32[]{:S(2)}) async-start(s8[4718592]{0:T(1024)(128)(4,1)} %bitcast.65), calls=%async_computation.3 | async-start | bytes 1048576
  16.4 13.3 %collective-permute-start.3 = (bf16[128,768]{1,0:T(8,128)(2,1)S(1)}, bf16[128,768]{1,0:T(8,128)(2,1)S(1)}, u32[]{:S(2)}, u32[]{:S(2)}) collective-permute-start(bf16[128,768]{1,0:T(8,128)(2,1)S(1)} %get-tuple-element.212), channel_id=1, source_target_pairs={{0,1},{1,0},{2,3},{3,2},{4,5},{5,4},{6,7},{7,6},{8,9},{9,8},{10,11... | collective-permute-start | bytes 589832 | tf_op jit(solution)/shard_map/ppermute | solution.py:577
  46.3 35.2 %collective-permute-start.9 = (bf16[2,8,96,768]{3,2,1,0:T(8,128)(2,1)}, bf16[2,8,96,768]{3,2,1,0:T(8,128)(2,1)}, u32[]{:S(2)}, u32[]{:S(2)}) collective-permute-start(bf16[2,8,96,768]{3,2,1,0:T(8,128)(2,1)} %get-tuple-element.141), channel_id=1, source_target_pairs={{0,1},{1,0},{2,3},{3,2},{4,5},{5,4},{6,7},{7,6},{8,9},{9,8},{10,11... | collective-permute-start | bytes 7077896 | tf_op jit(solution)/shard_map/ppermute | solution.py:577
  56.4 25.1 %collective-permute-start.10 = (bf16[2,768,768]{2,1,0:T(8,128)(2,1)}, bf16[2,768,768]{2,1,0:T(8,128)(2,1)}, u32[]{:S(2)}, u32[]{:S(2)}) collective-permute-start(bf16[2,768,768]{2,1,0:T(8,128)(2,1)} %get-tuple-element.143), channel_id=1, source_target_pairs={{0,1},{1,0},{2,3},{3,2},{4,5},{5,4},{6,7},{7,6},{8,9},{9,8},{10,11... | collective-permute-start | bytes 7077896 | tf_op jit(solution)/shard_map/ppermute | solution.py:577
  56.4 4.7 %collective-permute-start.6 = (bf16[128,768]{1,0:T(8,128)(2,1)}, bf16[128,768]{1,0:T(8,128)(2,1)S(1)}, u32[]{:S(2)}, u32[]{:S(2)}) collective-permute-start(bf16[128,768]{1,0:T(8,128)(2,1)} %get-tuple-element.119), channel_id=1, source_target_pairs={{0,1},{1,0},{2,3},{3,2},{4,5},{5,4},{6,7},{7,6},{8,9},{9,8},{10,11... | collective-permute-start | bytes 589832 | tf_op jit(solution)/shard_map/ppermute | solution.py:577
  56.9 8.0 %collective-permute-start.7 = (bf16[128,768]{1,0:T(8,128)(2,1)}, bf16[128,768]{1,0:T(8,128)(2,1)S(1)}, u32[]{:S(2)}, u32[]{:S(2)}) collective-permute-start(bf16[128,768]{1,0:T(8,128)(2,1)} %get-tuple-element.120), channel_id=1, source_target_pairs={{0,2},{1,3},{2,0},{3,1},{4,6},{5,7},{6,4},{7,5},{8,10},{9,11},{10,... | collective-permute-start | bytes 589832 | tf_op jit(solution)/shard_map/ppermute | solution.py:577
  58.7 8.8 %collective-permute-start.8 = (bf16[128,768]{1,0:T(8,128)(2,1)S(1)}, bf16[128,768]{1,0:T(8,128)(2,1)S(1)}, u32[]{:S(2)}, u32[]{:S(2)}) collective-permute-start(bf16[128,768]{1,0:T(8,128)(2,1)S(1)} %get-tuple-element.121), channel_id=1, source_target_pairs={{0,3},{1,2},{2,1},{3,0},{4,7},{5,6},{6,5},{7,4},{8,11},{9,10},{10,... | collective-permute-start | bytes 589832 | tf_op jit(solution)/shard_map/ppermute | solution.py:577
  84.1 25.5 %collective-permute-start.12 = (bf16[8,192,256]{2,1,0:T(8,128)(2,1)S(1)}, bf16[8,192,256]{2,1,0:T(8,128)(2,1)S(1)}, u32[]{:S(2)}, u32[]{:S(2)}) collective-permute-start(bf16[8,192,256]{2,1,0:T(8,128)(2,1)S(1)} %get-tuple-element.149), channel_id=1, source_target_pairs={{0,4},{4,0},{8,12},{12,8},{16,20},{20,16},{24,28},{28,24},{1,5},{5... | collective-permute-start | bytes 2359304 | tf_op jit(solution)/shard_map/ppermute | solution.py:577
  85.7 24.0 %collective-permute-start.13 = (bf16[8,192,256]{2,1,0:T(8,128)(2,1)S(1)}, bf16[8,192,256]{2,1,0:T(8,128)(2,1)S(1)}, u32[]{:S(2)}, u32[]{:S(2)}) collective-permute-start(bf16[8,192,256]{2,1,0:T(8,128)(2,1)S(1)} %get-tuple-element.151), channel_id=1, source_target_pairs={{0,8},{4,12},{8,0},{12,4},{16,24},{20,28},{24,16},{28,20},{1,9},{5... | collective-permute-start | bytes 2359304 | tf_op jit(solution)/shard_map/ppermute | solution.py:577
  87.3 22.9 %collective-permute-start.11 = (bf16[8,192,256]{2,1,0:T(8,128)(2,1)S(1)}, bf16[8,192,256]{2,1,0:T(8,128)(2,1)S(1)}, u32[]{:S(2)}, u32[]{:S(2)}) collective-permute-start(bf16[8,192,256]{2,1,0:T(8,128)(2,1)S(1)} %get-tuple-element.144.refs_12_.refs_5_), channel_id=1, source_target_pairs={{0,2},{1,3},{2,0},{3,1},{4,6},{5,7},{6,4},{7,5},{8,10},{9,11},{10,... | collective-permute-start | bytes 2359304 | tf_op jit(solution)/shard_map/ppermute | solution.py:577
  106.4 5.7 %collective-permute-start.17 = (bf16[2,768,256]{2,1,0:T(8,128)(2,1)S(1)}, bf16[2,768,256]{2,1,0:T(8,128)(2,1)S(1)}, u32[]{:S(2)}, u32[]{:S(2)}) collective-permute-start(bf16[2,768,256]{2,1,0:T(8,128)(2,1)S(1)} %get-tuple-element.158), channel_id=1, source_target_pairs={{0,1},{1,0},{2,3},{3,2},{4,5},{5,4},{6,7},{7,6},{8,9},{9,8},{10,11... | collective-permute-start | bytes 2359304 | tf_op jit(solution)/shard_map/ppermute | solution.py:577
  106.4 5.0 %collective-permute-start.20 = (bf16[2,8,16,256]{3,2,1,0:T(8,128)(2,1)S(1)}, bf16[2,8,16,256]{3,2,1,0:T(8,128)(2,1)S(1)}, u32[]{:S(2)}, u32[]{:S(2)}) collective-permute-start(bf16[2,8,16,256]{3,2,1,0:T(8,128)(2,1)S(1)} %get-tuple-element.164), channel_id=1, source_target_pairs={{0,1},{1,0},{2,3},{3,2},{4,5},{5,4},{6,7},{7,6},{8,9},{9,8},{10,11... | collective-permute-start | bytes 393224 | tf_op jit(solution)/shard_map/ppermute | solution.py:577
  109.6 7.5 %collective-permute-start.18 = (bf16[2,768,256]{2,1,0:T(8,128)(2,1)S(1)}, bf16[2,768,256]{2,1,0:T(8,128)(2,1)S(1)}, u32[]{:S(2)}, u32[]{:S(2)}) collective-permute-start(bf16[2,768,256]{2,1,0:T(8,128)(2,1)S(1)} %get-tuple-element.160), channel_id=1, source_target_pairs={{0,1},{1,0},{2,3},{3,2},{4,5},{5,4},{6,7},{7,6},{8,9},{9,8},{10,11... | collective-permute-start | bytes 2359304 | tf_op jit(solution)/shard_map/ppermute | solution.py:577
  109.7 7.4 %collective-permute-start.19 = (bf16[2,768,256]{2,1,0:T(8,128)(2,1)S(1)}, bf16[2,768,256]{2,1,0:T(8,128)(2,1)S(1)}, u32[]{:S(2)}, u32[]{:S(2)}) collective-permute-start(bf16[2,768,256]{2,1,0:T(8,128)(2,1)S(1)} %get-tuple-element.162), channel_id=1, source_target_pairs={{0,1},{1,0},{2,3},{3,2},{4,5},{5,4},{6,7},{7,6},{8,9},{9,8},{10,11... | collective-permute-start | bytes 2359304 | tf_op jit(solution)/shard_map/ppermute | solution.py:577
  111.0 11.2 %collective-permute-start.25 = (bf16[4,192,256]{2,1,0:T(8,128)(2,1)S(1)}, bf16[4,192,256]{2,1,0:T(8,128)(2,1)S(1)}, u32[]{:S(2)}, u32[]{:S(2)}) collective-permute-start(bf16[4,192,256]{2,1,0:T(8,128)(2,1)S(1)} %get-tuple-element.173), channel_id=1, source_target_pairs={{0,8},{4,12},{8,0},{12,4},{16,24},{20,28},{24,16},{28,20},{1,9},{5... | collective-permute-start | bytes 1179656 | tf_op jit(solution)/shard_map/ppermute | solution.py:577
  111.5 12.0 %collective-permute-start.26 = (bf16[4,192,256]{2,1,0:T(8,128)(2,1)S(1)}, bf16[4,192,256]{2,1,0:T(8,128)(2,1)S(1)}, u32[]{:S(2)}, u32[]{:S(2)}) collective-permute-start(bf16[4,192,256]{2,1,0:T(8,128)(2,1)S(1)} %get-tuple-element.175), channel_id=1, source_target_pairs={{0,2},{1,3},{2,0},{3,1},{4,6},{5,7},{6,4},{7,5},{8,10},{9,11},{10,... | collective-permute-start | bytes 1179656 | tf_op jit(solution)/shard_map/ppermute | solution.py:577
  112.0 11.5 %collective-permute-start.24 = (bf16[4,192,256]{2,1,0:T(8,128)(2,1)S(1)}, bf16[4,192,256]{2,1,0:T(8,128)(2,1)S(1)}, u32[]{:S(2)}, u32[]{:S(2)}) collective-permute-start(bf16[4,192,256]{2,1,0:T(8,128)(2,1)S(1)} %get-tuple-element.152.refs_3_), channel_id=1, source_target_pairs={{0,4},{4,0},{8,12},{12,8},{16,20},{20,16},{24,28},{28,24},{1,5},{5... | collective-permute-start | bytes 1179656 | tf_op jit(solution)/shard_map/ppermute | solution.py:577
  117.8 28.3 %collective-permute-start.21 = (bf16[8,112,256]{2,1,0:T(8,128)(2,1)S(1)}, bf16[8,112,256]{2,1,0:T(8,128)(2,1)S(1)}, u32[]{:S(2)}, u32[]{:S(2)}) collective-permute-start(bf16[8,112,256]{2,1,0:T(8,128)(2,1)S(1)} %get-tuple-element.165.refs_9_.refs_7_), channel_id=1, source_target_pairs={{0,2},{1,3},{2,0},{3,1},{4,6},{5,7},{6,4},{7,5},{8,10},{9,11},{10,... | collective-permute-start | bytes 1376264 | tf_op jit(solution)/shard_map/ppermute | solution.py:577
  124.2 12.2 %collective-permute-start.28 = (bf16[2,192,256]{2,1,0:T(8,128)(2,1)S(1)}, bf16[2,192,256]{2,1,0:T(8,128)(2,1)S(1)}, u32[]{:S(2)}, u32[]{:S(2)}) collective-permute-start(bf16[2,192,256]{2,1,0:T(8,128)(2,1)S(1)} %get-tuple-element.179), channel_id=1, source_target_pairs={{0,2},{1,3},{2,0},{3,1},{4,6},{5,7},{6,4},{7,5},{8,10},{9,11},{10,... | collective-permute-start | bytes 589832 | tf_op jit(solution)/shard_map/ppermute | solution.py:577
  124.8 21.3 %collective-permute-start.22 = (bf16[8,96,256]{2,1,0:T(8,128)(2,1)S(1)}, bf16[8,96,256]{2,1,0:T(8,128)(2,1)S(1)}, u32[]{:S(2)}, u32[]{:S(2)}) collective-permute-start(bf16[8,96,256]{2,1,0:T(8,128)(2,1)S(1)} %get-tuple-element.168), channel_id=1, source_target_pairs={{0,4},{4,0},{8,12},{12,8},{16,20},{20,16},{24,28},{28,24},{1,5},{5... | collective-permute-start | bytes 1179656 | tf_op jit(solution)/shard_map/ppermute | solution.py:577
  125.3 20.8 %collective-permute-start.23 = (bf16[8,96,256]{2,1,0:T(8,128)(2,1)S(1)}, bf16[8,96,256]{2,1,0:T(8,128)(2,1)S(1)}, u32[]{:S(2)}, u32[]{:S(2)}) collective-permute-start(bf16[8,96,256]{2,1,0:T(8,128)(2,1)S(1)} %get-tuple-element.170), channel_id=1, source_target_pairs={{0,8},{4,12},{8,0},{12,4},{16,24},{20,28},{24,16},{28,20},{1,9},{5... | collective-permute-start | bytes 1179656 | tf_op jit(solution)/shard_map/ppermute | solution.py:577
  126.9 11.5 %collective-permute-start.29 = (bf16[2,192,256]{2,1,0:T(8,128)(2,1)S(1)}, bf16[2,192,256]{2,1,0:T(8,128)(2,1)S(1)}, u32[]{:S(2)}, u32[]{:S(2)}) collective-permute-start(bf16[2,192,256]{2,1,0:T(8,128)(2,1)S(1)} %get-tuple-element.181), channel_id=1, source_target_pairs={{0,4},{4,0},{8,12},{12,8},{16,20},{20,16},{24,28},{28,24},{1,5},{5... | collective-permute-start | bytes 589832 | tf_op jit(solution)/shard_map/ppermute | solution.py:577
  136.3 5.7 %collective-permute-start.27 = (bf16[2,192,256]{2,1,0:T(8,128)(2,1)S(1)}, bf16[2,192,256]{2,1,0:T(8,128)(2,1)S(1)}, u32[]{:S(2)}, u32[]{:S(2)}) collective-permute-start(bf16[2,192,256]{2,1,0:T(8,128)(2,1)S(1)} %get-tuple-element.177.refs_7_), channel_id=1, source_target_pairs={{0,8},{4,12},{8,0},{12,4},{16,24},{20,28},{24,16},{28,20},{1,9},{5... | collective-permute-start | bytes 589832 | tf_op jit(solution)/shard_map/ppermute | solution.py:577
  142.7 14.8 %collective-permute-start.36 = (bf16[1,576,256]{2,1,0:T(8,128)(2,1)S(1)}, bf16[1,576,256]{2,1,0:T(8,128)(2,1)S(1)}, u32[]{:S(2)}, u32[]{:S(2)}) collective-permute-start(bf16[1,576,256]{2,1,0:T(8,128)(2,1)S(1)} %get-tuple-element.182.refs_7_), channel_id=1, source_target_pairs={{0,16},{4,20},{8,24},{12,28},{16,0},{20,4},{24,8},{28,12},{1,17},{... | collective-permute-start | bytes 884744 | tf_op jit(solution)/shard_map/ppermute | solution.py:577
  146.8 10.1 %collective-permute-start.30 = (bf16[4,112,256]{2,1,0:T(8,128)(2,1)S(1)}, bf16[4,112,256]{2,1,0:T(8,128)(2,1)S(1)}, u32[]{:S(2)}, u32[]{:S(2)}) collective-permute-start(bf16[4,112,256]{2,1,0:T(8,128)(2,1)S(1)} %get-tuple-element.184.refs_7_), channel_id=1, source_target_pairs={{0,4},{4,0},{8,12},{12,8},{16,20},{20,16},{24,28},{28,24},{1,5},{5... | collective-permute-start | bytes 688136 | tf_op jit(solution)/shard_map/ppermute | solution.py:577
  147.3 9.5 %collective-permute-start.31 = (bf16[4,96,256]{2,1,0:T(8,128)(2,1)S(1)}, bf16[4,96,256]{2,1,0:T(8,128)(2,1)S(1)}, u32[]{:S(2)}, u32[]{:S(2)}) collective-permute-start(bf16[4,96,256]{2,1,0:T(8,128)(2,1)S(1)} %get-tuple-element.186), channel_id=1, source_target_pairs={{0,8},{4,12},{8,0},{12,4},{16,24},{20,28},{24,16},{28,20},{1,9},{5... | collective-permute-start | bytes 589832 | tf_op jit(solution)/shard_map/ppermute | solution.py:577
  148.9 7.9 %collective-permute-start.32 = (bf16[4,96,256]{2,1,0:T(8,128)(2,1)S(1)}, bf16[4,96,256]{2,1,0:T(8,128)(2,1)S(1)}, u32[]{:S(2)}, u32[]{:S(2)}) collective-permute-start(bf16[4,96,256]{2,1,0:T(8,128)(2,1)S(1)} %get-tuple-element.188), channel_id=1, source_target_pairs={{0,2},{1,3},{2,0},{3,1},{4,6},{5,7},{6,4},{7,5},{8,10},{9,11},{10,... | collective-permute-start | bytes 589832 | tf_op jit(solution)/shard_map/ppermute | solution.py:577
  158.1 20.5 %collective-permute-start.42 = (bf16[1,576,256]{2,1,0:T(8,128)(2,1)S(1)}, bf16[1,576,256]{2,1,0:T(8,128)(2,1)S(1)}, u32[]{:S(2)}, u32[]{:S(2)}) collective-permute-start(bf16[1,576,256]{2,1,0:T(8,128)(2,1)S(1)} %halve.13.refs_7_.refs_1_), channel_id=1, source_target_pairs={{0,2},{1,3},{2,0},{3,1},{4,6},{5,7},{6,4},{7,5},{8,10},{9,11},{10,... | collective-permute-start | bytes 884744 | tf_op jit(solution)/shard_map/ppermute | solution.py:577
  158.7 8.6 %collective-permute-start.33 = (bf16[2,112,256]{2,1,0:T(8,128)(2,1)S(1)}, bf16[2,112,256]{2,1,0:T(8,128)(2,1)S(1)}, u32[]{:S(2)}, u32[]{:S(2)}) collective-permute-start(bf16[2,112,256]{2,1,0:T(8,128)(2,1)S(1)} %get-tuple-element.190.refs_3_), channel_id=1, source_target_pairs={{0,8},{4,12},{8,0},{12,4},{16,24},{20,28},{24,16},{28,20},{1,9},{5... | collective-permute-start | bytes 344072 | tf_op jit(solution)/shard_map/ppermute | solution.py:577
  158.7 8.6 %collective-permute-start.34 = (bf16[2,96,256]{2,1,0:T(8,128)(2,1)S(1)}, bf16[2,96,256]{2,1,0:T(8,128)(2,1)S(1)}, u32[]{:S(2)}, u32[]{:S(2)}) collective-permute-start(bf16[2,96,256]{2,1,0:T(8,128)(2,1)S(1)} %get-tuple-element.192), channel_id=1, source_target_pairs={{0,2},{1,3},{2,0},{3,1},{4,6},{5,7},{6,4},{7,5},{8,10},{9,11},{10,... | collective-permute-start | bytes 294920 | tf_op jit(solution)/shard_map/ppermute | solution.py:577
  160.2 7.1 %collective-permute-start.35 = (bf16[2,96,256]{2,1,0:T(8,128)(2,1)S(1)}, bf16[2,96,256]{2,1,0:T(8,128)(2,1)S(1)}, u32[]{:S(2)}, u32[]{:S(2)}) collective-permute-start(bf16[2,96,256]{2,1,0:T(8,128)(2,1)S(1)} %get-tuple-element.194), channel_id=1, source_target_pairs={{0,4},{4,0},{8,12},{12,8},{16,20},{20,16},{24,28},{28,24},{1,5},{5... | collective-permute-start | bytes 294920 | tf_op jit(solution)/shard_map/ppermute | solution.py:577
  167.3 24.9 %copy-start.1 = (s32[4,8]{1,0:T(4,128)S(1)}, s32[4,8]{1,0:T(4,128)}, u32[]{:S(2)}) copy-start(s32[4,8]{1,0:T(4,128)} %param.16) | copy-start | bytes 388
  167.8 9.4 %collective-permute-start.37 = (bf16[1,304,256]{2,1,0:T(8,128)(2,1)S(1)}, bf16[1,304,256]{2,1,0:T(8,128)(2,1)S(1)}, u32[]{:S(2)}, u32[]{:S(2)}) collective-permute-start(bf16[1,304,256]{2,1,0:T(8,128)(2,1)S(1)} %get-tuple-element.197.refs_3_), channel_id=1, source_target_pairs={{0,16},{4,20},{8,24},{12,28},{16,0},{20,4},{24,8},{28,12},{1,17},{... | collective-permute-start | bytes 466952 | tf_op jit(solution)/shard_map/ppermute | solution.py:577
  168.6 10.5 %collective-permute-start.14 = (bf16[128,768]{1,0:T(8,128)(2,1)S(1)}, bf16[128,768]{1,0:T(8,128)(2,1)S(1)}, u32[]{:S(2)}, u32[]{:S(2)}) collective-permute-start(bf16[128,768]{1,0:T(8,128)(2,1)S(1)} %get-tuple-element.154), channel_id=1, source_target_pairs={{0,1},{1,0},{2,3},{3,2},{4,5},{5,4},{6,7},{7,6},{8,9},{9,8},{10,11... | collective-permute-start | bytes 589832 | tf_op jit(solution)/shard_map/ppermute | solution.py:577
  168.6 11.5 %collective-permute-start.15 = (bf16[128,768]{1,0:T(8,128)(2,1)S(1)}, bf16[128,768]{1,0:T(8,128)(2,1)S(1)}, u32[]{:S(2)}, u32[]{:S(2)}) collective-permute-start(bf16[128,768]{1,0:T(8,128)(2,1)S(1)} %get-tuple-element.155), channel_id=1, source_target_pairs={{0,2},{1,3},{2,0},{3,1},{4,6},{5,7},{6,4},{7,5},{8,10},{9,11},{10,... | collective-permute-start | bytes 589832 | tf_op jit(solution)/shard_map/ppermute | solution.py:577
  177.8 6.4 %collective-permute-start.39 = (bf16[1,304,256]{2,1,0:T(8,128)(2,1)S(1)}, bf16[1,304,256]{2,1,0:T(8,128)(2,1)S(1)}, u32[]{:S(2)}, u32[]{:S(2)}) collective-permute-start(bf16[1,304,256]{2,1,0:T(8,128)(2,1)S(1)} %halve.15.refs_1_), channel_id=1, source_target_pairs={{0,2},{1,3},{2,0},{3,1},{4,6},{5,7},{6,4},{7,5},{8,10},{9,11},{10,... | collective-permute-start | bytes 466952 | tf_op jit(solution)/shard_map/ppermute | solution.py:577
  178.5 11.4 %collective-permute-start.41 = (bf16[1,576,256]{2,1,0:T(8,128)(2,1)S(1)}, bf16[1,576,256]{2,1,0:T(8,128)(2,1)S(1)}, u32[]{:S(2)}, u32[]{:S(2)}) collective-permute-start(bf16[1,576,256]{2,1,0:T(8,128)(2,1)S(1)} %halve.13.refs_7_.refs_1_), channel_id=1, source_target_pairs={{0,1},{1,0},{2,3},{3,2},{4,5},{5,4},{6,7},{7,6},{8,9},{9,8},{10,11... | collective-permute-start | bytes 884744 | tf_op jit(solution)/shard_map/ppermute | solution.py:577
  178.5 11.4 %collective-permute-start.43 = (bf16[1,576,256]{2,1,0:T(8,128)(2,1)S(1)}, bf16[1,576,256]{2,1,0:T(8,128)(2,1)S(1)}, u32[]{:S(2)}, u32[]{:S(2)}) collective-permute-start(bf16[1,576,256]{2,1,0:T(8,128)(2,1)S(1)} %collective-permute-done.42.refs_3_), channel_id=1, source_target_pairs={{0,1},{1,0},{2,3},{3,2},{4,5},{5,4},{6,7},{7,6},{8,9},{9,8},{10,11... | collective-permute-start | bytes 884744 | tf_op jit(solution)/shard_map/ppermute | solution.py:577
  179.1 7.1 %collective-permute-start.16 = (bf16[128,768]{1,0:T(8,128)(2,1)S(1)}, bf16[128,768]{1,0:T(8,128)(2,1)S(1)}, u32[]{:S(2)}, u32[]{:S(2)}) collective-permute-start(bf16[128,768]{1,0:T(8,128)(2,1)S(1)} %get-tuple-element.156), channel_id=1, source_target_pairs={{0,3},{1,2},{2,1},{3,0},{4,7},{5,6},{6,5},{7,4},{8,11},{9,10},{10,... | collective-permute-start | bytes 589832 | tf_op jit(solution)/shard_map/ppermute | solution.py:577
  180.1 7.6 %collective-permute-start.38 = (bf16[1,304,256]{2,1,0:T(8,128)(2,1)S(1)}, bf16[1,304,256]{2,1,0:T(8,128)(2,1)S(1)}, u32[]{:S(2)}, u32[]{:S(2)}) collective-permute-start(bf16[1,304,256]{2,1,0:T(8,128)(2,1)S(1)} %halve.15.refs_1_), channel_id=1, source_target_pairs={{0,1},{1,0},{2,3},{3,2},{4,5},{5,4},{6,7},{7,6},{8,9},{9,8},{10,11... | collective-permute-start | bytes 466952 | tf_op jit(solution)/shard_map/ppermute | solution.py:577
  184.3 3.4 %collective-permute-start.40 = (bf16[1,304,256]{2,1,0:T(8,128)(2,1)S(1)}, bf16[1,304,256]{2,1,0:T(8,128)(2,1)S(1)}, u32[]{:S(2)}, u32[]{:S(2)}) collective-permute-start(bf16[1,304,256]{2,1,0:T(8,128)(2,1)S(1)} %collective-permute-done.39.refs_3_), channel_id=1, source_target_pairs={{0,1},{1,0},{2,3},{3,2},{4,5},{5,4},{6,7},{7,6},{8,9},{9,8},{10,11... | collective-permute-start | bytes 466952 | tf_op jit(solution)/shard_map/ppermute | solution.py:577
  (12 other events, 61.8 us)

commit v3 on v2

v3 whole, which is shorter than its diff:
```python
import functools
import math

import jax
import jax.numpy as jnp
from jax import lax
from jax.experimental import pallas as pl
from jax.experimental.pallas import tpu as pltpu
from jax.sharding import PartitionSpec as P

HEADS = 12
EPSILON = 1e-12
MASKED = -1e30
f32 = jnp.float32
bf16 = jnp.bfloat16
NN = (((1,), (0,)), ((), ()))
NT = (((1,), (1,)), ((), ()))
TN = (((0,), (0,)), ((), ()))
VMEM = pl.BlockSpec(memory_space=pltpu.VMEM)
SMEM = pl.BlockSpec(memory_space=pltpu.SMEM)
HBM = pl.BlockSpec(memory_space=pltpu.HBM)
ANY = pl.BlockSpec(memory_space=pl.ANY)


WEIGHTS = {
    "prepare": 10**12, "attend": 10**12, "feed": 10**12, "grad_up": 10**12,
    "grad_down": 10**12, "attend_back": 10**12, "grad_tokens": 10**12,
}


def dot(left, right, dims=NN):
    return lax.dot_general(left, right, dims, preferred_element_type=f32)


def call(
    kernel, name, scalars, arrays, outs, scratch=(), far=(), far_outs=(), copies=0, room=10, after=()
):
    scratch = list(scratch)
    if copies:
        scratch.append(pltpu.SemaphoreType.DMA((copies,)))
    first, last = len(scalars) + len(arrays) + len(far), len(after)
    results = len(outs) + len(far_outs)
    mark = jax.ShapeDtypeStruct((8, 128), f32)

    def body(*refs):
        mine = refs[first + last :]
        mine[results][...] = jnp.zeros(mark.shape, mark.dtype)
        kernel(*refs[:first], *mine[:results], *mine[results + 1 :])

    return pl.pallas_call(
        body,
        in_specs=[SMEM] * len(scalars) + [VMEM] * len(arrays) + [HBM] * len(far) + [VMEM] * last,
        out_specs=[VMEM] * len(outs) + [HBM] * len(far_outs) + [VMEM],
        out_shape=[*outs, *[pltpu.HBM(a.shape, a.dtype) for a in far_outs], mark],
        scratch_shapes=scratch,
        compiler_params=pltpu.CompilerParams(vmem_limit_bytes=room * 2**20),
        cost_estimate=pl.CostEstimate(
            flops=WEIGHTS.get(name, 0), bytes_accessed=0, transcendentals=0
        ),
        name=name,
    )(
        *scalars, *arrays, *[pltpu.with_memory_space_constraint(a, pltpu.HBM) for a in far], *after
    )


def shape(*dims, dtype=bf16):
    return jax.ShapeDtypeStruct(dims, dtype)


def cut(i, size):
    return pl.ds(pl.multiple_of(i * size, size), size)


def copy(source, target, semaphore):
    return pltpu.make_async_copy(source, target, semaphore)


def column_sum(values):
    return jnp.sum(values, axis=0, keepdims=True)


def row_mean(values):
    return jnp.mean(values, axis=-1, keepdims=True)


def normalize(inputs):
    centre = inputs - row_mean(inputs)
    inverse = lax.rsqrt(row_mean(centre * centre) + EPSILON)
    return centre * inverse, inverse


def normalize_back(scaled, normed, inverse):
    return inverse * (scaled - row_mean(scaled) - normed * row_mean(scaled * normed))


BIAS_Q, BIAS_V, BIAS_OUT, GAIN_ONE, SHIFT_ONE, BIAS_DOWN, GAIN_TWO, SHIFT_TWO, BIAS_UP = range(9)


def vector(ref, row):
    return ref[row : row + 1, :]


def only(rows, h, height):
    parts = [jnp.zeros((height, rows.shape[1]), rows.dtype)] * (rows.shape[0] // height)
    parts[h] = rows[h * height : (h + 1) * height, :]
    return jnp.concatenate(parts)


def prepare_kernel(row_ref, w_qkv, w_out, qkv_near, out_near, mask, sems, *, pages, slots):
    load_qkv = copy(w_qkv, qkv_near, sems.at[0])
    load_qkv.start()
    load_out = copy(w_out, out_near, sems.at[1])
    load_out.start()
    count = mask.shape[0]
    position = row_ref[pages]

    def page_of(shape, dim):
        at = lax.broadcasted_iota(jnp.int32, shape, dim)
        slot = ((at // slots) ^ position) * slots + at % slots
        page = jnp.zeros(shape, jnp.int32)
        end = 0
        for c in range(pages):
            end = end + row_ref[c]
            page = page + (slot >= end).astype(jnp.int32)
        return page

    mask[...] = jnp.where(
        page_of((count, count), 0) == page_of((1, count), 1), 0.0, MASKED
    )
    load_qkv.wait()
    load_out.wait()


def prepare(row, w_qkv, w_out, slots, count):
    return call(
        functools.partial(prepare_kernel, pages=row.shape[0] - 1, slots=slots),
        "prepare", [row], [],
        [shape(*w_qkv.shape), shape(*w_out.shape), shape(count, count, dtype=f32)],
        far=[w_qkv, w_out], copies=2,
    )[:3]


def attend_kernel(
    x0, x1, x2, x3, vectors, w_qkv, w_out, mask,
    normed_out, inverse_out, q_out, k_out, v_out, prob_out, context_out, tokens_out,
    tokens, q_kept, k_kept, v_kept, context_kept, probs_kept, sems, *, head_width,
):
    slots = x0.shape[0]
    count, width = tokens.shape
    wide = 4 * head_width
    groups = width // wide
    kept = ((0, q_kept, q_out), (1, k_kept, k_out), (2, v_kept, v_out), (3, context_kept, context_out))

    def keep(i, number, source, target):
        here = cut(i, wide)
        return copy(source.at[:, here], target.at[:, here], sems.at[number * groups + i])

    def keep_probs(i, h):
        return copy(
            probs_kept.at[4 * i + h], prob_out.at[4 * i + h], sems.at[4 * groups + 1 + 4 * i + h]
        )

    for i, block in enumerate((x0, x1, x2, x3)):
        tokens[i * slots : (i + 1) * slots, :] = block[...]
    keep_tokens = copy(tokens, tokens_out, sems.at[4 * groups])
    keep_tokens.start()

    @pl.loop(0, groups)
    def _(i):
        here = cut(i, wide)
        x = tokens[...]
        q = (dot(x, w_qkv[:, here]) + vectors[BIAS_Q : BIAS_Q + 1, here]).astype(bf16)
        k = dot(x, w_qkv[:, cut(i + groups, wide)]).astype(bf16)
        v = dot(x, w_qkv[:, cut(i + 2 * groups, wide)]) + vectors[BIAS_V : BIAS_V + 1, here]
        v = v.astype(bf16)
        q_kept[:, here] = q
        k_kept[:, here] = k
        v_kept[:, here] = v
        q_turned = (q * jnp.asarray(1.0 / math.sqrt(head_width), bf16)).T
        v_turned = v.T
        context = []
        for h in range(4):
            scores = dot(k, only(q_turned, h, head_width)) + mask[...]
            powers = jnp.exp(scores - jnp.max(scores, axis=0, keepdims=True))
            probs = (powers * (1.0 / jnp.sum(powers, axis=0, keepdims=True))).astype(bf16)
            probs_kept[4 * i + h] = probs
            keep_probs(i, h).start()
            context.append(dot(v_turned[h * head_width : (h + 1) * head_width, :], probs))
        context_kept[:, here] = jnp.concatenate(context).astype(bf16).T
        for number, source, target in kept:
            keep(i, number, source, target).start()

    attended = dot(context_kept[...], w_out[...]) + vector(vectors, BIAS_OUT)
    normed, inverse = normalize(tokens[...].astype(f32) + attended)
    normed_out[...] = normed
    inverse_out[...] = inverse
    for i in range(groups):
        for number, source, target in kept:
            keep(i, number, source, target).wait()
        for h in range(4):
            keep_probs(i, h).wait()
    keep_tokens.wait()


def attend(blocks, vectors, w_qkv, w_out, mask):
    slots, width = blocks[0].shape
    count = slots * len(blocks)
    groups = HEADS // 4
    narrow = shape(count, width)
    rows = pltpu.VMEM((count, width), bf16)
    return call(
        functools.partial(attend_kernel, head_width=width // HEADS),
        "attend", [], [*blocks, vectors, w_qkv, w_out, mask],
        [shape(count, width, dtype=f32), shape(count, 1, dtype=f32)],
        [rows, rows, rows, rows, rows, pltpu.VMEM((HEADS, count, count), bf16)],
        far_outs=[narrow, narrow, narrow, shape(HEADS, count, count), narrow, narrow],
        copies=4 * groups + 1 + HEADS, room=24,
    )[:8]


def feed_kernel(
    place, normed_one, vectors, c0, c1, c2, c3, w_up, w_down,
    keep_active, send_active, slope_out, lowered_out, first_out, r0, r1, r2, r3, vector_out,
    sum_out, normed_far, total, sems, *, shares,
):
    width = w_up.shape[0]
    hidden = w_up.shape[1]
    keep_normed = copy(normed_one, normed_far, sems.at[0])
    keep_normed.start()
    first_norm = normed_one[...] * vector(vectors, GAIN_ONE) + vector(vectors, SHIFT_ONE)
    first_out[...] = first_norm.astype(bf16)
    total[...] = first_norm + vector(vectors, BIAS_DOWN)
    odd = place[0] == 1
    rows = hidden // shares // 4
    apart = send_active is not None

    @pl.loop(0, hidden // width)
    def _(i):
        here = cut(i, width)
        raised = dot(first_out[...], w_up[:, here]) + vectors[pl.ds(BIAS_UP + i, 1), :]
        cumulative = 0.5 * (1.0 + lax.erf(raised * (1.0 / math.sqrt(2.0))))
        activated = (raised * cumulative).astype(bf16)
        bell = jnp.exp(-0.5 * raised * raised) * (1.0 / math.sqrt(2.0 * math.pi))
        slope_out[:, here] = (cumulative + raised * bell).astype(bf16)
        total[...] += dot(activated, w_down[here, :])
        turned = activated.T
        if apart:
            count = width // rows // 4
            for d in range(count):
                for x in range(2):
                    at = (d * 4 + x * 2) * rows
                    even_part = turned[at : at + rows, :]
                    odd_part = turned[at + rows : at + 2 * rows, :]
                    keep_active[x, i * count + d] = jnp.where(odd, odd_part, even_part)
                    send_active[x, i * count + d] = jnp.where(odd, even_part, odd_part)
        else:
            keep_active[here, :] = turned

    normed, inverse = normalize(total[...])
    gain = vector(vectors, GAIN_TWO)
    result = (normed * gain + vector(vectors, SHIFT_TWO)).astype(bf16)
    slots = c0.shape[0]
    for i, block in enumerate((r0, r1, r2, r3)):
        block[...] = result[i * slots : (i + 1) * slots, :]
    upstream = jnp.concatenate([c0[...], c1[...], c2[...], c3[...]]).astype(f32)
    grad_sum = normalize_back(upstream * gain, normed, inverse)
    total[...] = grad_sum
    keep_sum = copy(total, sum_out, sems.at[1])
    keep_sum.start()
    lowered = grad_sum.astype(bf16)
    lowered_out[...] = lowered
    vector_out[0:1, :] = column_sum(upstream * normed)
    vector_out[1:2, :] = column_sum(upstream)
    vector_out[2:3, :] = column_sum(lowered.astype(f32))
    keep_sum.wait()
    keep_normed.wait()


def feed(place, normed, vectors, cotangents, w_up, w_down, shares):
    count, width = normed.shape
    hidden = w_up.shape[1]
    rows = hidden // shares // 4
    narrow, full = shape(count, width), shape(count, width, dtype=f32)
    apart = rows % 16 == 0 and width % (4 * rows) == 0
    kernel = functools.partial(feed_kernel, shares=shares)
    if apart:
        active = [shape(2, shares, rows, count)] * 2
    else:
        active = [shape(hidden, count)]
        whole = kernel

        def kernel(*refs):
            whole(*refs[:10], None, *refs[10:])

    made = call(
        kernel, "feed", [place], [normed, vectors, *cotangents, w_up, w_down],
        active + [shape(count, hidden), narrow, narrow]
        + [shape(*cotangents[0].shape)] * 4 + [shape(8, width, dtype=f32)],
        [pltpu.VMEM((count, width), f32)], far_outs=[full, full], copies=2, room=14,
    )[:-1]
    if apart:
        return made
    parts = jnp.moveaxis(made[0].reshape(shares, 2, 2, rows, count), 0, 2)
    odd = place[0] == 1
    keep = jnp.where(odd, parts[:, 1], parts[:, 0])
    send = jnp.where(odd, parts[:, 0], parts[:, 1])
    return [keep, send, *made[1:]]


def grad_up_kernel(
    place, lowered, slope, first, w_down, inverse_one, vectors, w_up, sum_two, normed_one,
    keep, send, bias_out, attended_out, vector_out, sum_out,
    turned, raised_kept, weights, normed, total, sems,
):
    width = lowered.shape[1]
    loads = (copy(w_up, weights, sems.at[0]), copy(sum_two, total, sems.at[1]), copy(normed_one, normed, sems.at[2]))
    for one in loads:
        one.start()
    turned[...] = first[...].T

    def work(b):
        here = cut(b, width)
        raised = dot(lowered[...], w_down[here, :], NT) * slope[:, here].astype(f32)
        raised = raised.astype(bf16)
        raised_kept[:, here] = raised
        bias_out[pl.ds(b, 1), :] = column_sum(raised.astype(f32))
        return dot(turned[...], raised).astype(bf16)

    @pl.loop(0, 2)
    def _(x):
        send[x] = work(2 * x + 1 - place[0])
        keep[x] = work(2 * x + place[0])

    for one in loads:
        one.wait()
    upstream = total[...] + dot(raised_kept[...], weights[...], NT)
    grad_sum = normalize_back(
        upstream * vector(vectors, GAIN_ONE), normed[...], inverse_one[...]
    )
    total[...] = grad_sum
    keep_sum = copy(total, sum_out, sems.at[3])
    keep_sum.start()
    attended = grad_sum.astype(bf16)
    attended_out[...] = attended
    vector_out[0:1, :] = column_sum(upstream * normed[...])
    vector_out[1:2, :] = column_sum(upstream)
    vector_out[2:3, :] = column_sum(attended.astype(f32))
    keep_sum.wait()


def grad_up(place, lowered, slope, first, w_down, inverse, vectors, w_up, sum_two, normed):
    count, width = lowered.shape
    hidden = w_down.shape[0]
    full = pltpu.VMEM((count, width), f32)
    return call(
        grad_up_kernel, "grad_up", [place], [lowered, slope, first, w_down, inverse, vectors],
        [shape(2, width, width)] * 2
        + [shape(hidden // width, width, dtype=f32), shape(count, width)]
        + [shape(8, width, dtype=f32)],
        [
            pltpu.VMEM((width, count), bf16), pltpu.VMEM((count, hidden), bf16),
            pltpu.VMEM((width, hidden), bf16), full, full,
        ],
        far=[w_up, sum_two, normed], far_outs=[shape(count, width, dtype=f32)], copies=4, room=28,
    )


def grad_down_kernel(active, other_active, lowered, other_lowered, down):
    _, shares, rows, count = active.shape
    width = lowered.shape[1]

    for x in range(2):

        @pl.loop(0, shares, step=2)
        def _(d):
            mine = active[x, pl.ds(d, 2)].reshape(2 * rows, count)
            other = other_active[x, pl.ds(d, 2)].reshape(2 * rows, count)
            value = dot(mine, lowered[...]) + dot(other, other_lowered[...])
            down[x, pl.ds(d, 2)] = value.astype(bf16).reshape(2, rows, width)


def grad_down(active, other_active, lowered, other_lowered, after):
    _, shares, rows, _ = active.shape
    return call(
        grad_down_kernel, "grad_down", [], [active, other_active, lowered, other_lowered],
        [shape(2, shares, rows, lowered.shape[1])], after=after,
    )


def small_pieces(shares, width):
    q, v, gain_one, shift_one, out, gain_two, shift_two, down, up = range(9)
    share = width // shares

    def flat(row, first):
        return row + first // width, first % width

    def pieces(d):
        at = d * share
        return (
            (flat(q, 2 * at), flat(q, 2 * at + share), (out, at)),
            ((gain_one, at), (shift_one, at), (down, at)),
            ((gain_two, at), (shift_two, at), flat(up, 4 * at)),
            tuple(flat(up, 4 * at + j * share) for j in (1, 2, 3)),
        )

    return [pieces(d) for d in range(shares)]


def attend_back_kernel(
    place, attended, vector_one, vector_two, bias_up, tokens, context, prob, q_ref, k_ref, v_ref, w_out,
    grads_out, keep_0, keep_1, keep_2, send_0, send_1, send_2, small_keep, small_send,
    rows_kept, turned, turned_context, probs_kept, q_kept, k_kept, v_kept, weights, sums, small, sems,
    *, head_width,
):
    count, width = attended.shape
    wide = 4 * head_width
    groups = width // wide
    shares = small_keep.shape[1]

    def load(i):
        here = cut(i, wide)
        pairs = [
            (w_out.at[here, :], weights.at[here, :]),
            (v_ref.at[:, here], v_kept.at[:, here]),
            (q_ref.at[:, here], q_kept.at[:, here]),
            (k_ref.at[:, here], k_kept.at[:, here]),
        ]
        pairs = pairs + [(prob.at[4 * i + h], probs_kept.at[4 * i + h]) for h in range(4)]
        return [copy(s, t, sems.at[8 * i + n]) for n, (s, t) in enumerate(pairs)]

    load_tokens = copy(tokens, rows_kept.at[0], sems.at[8 * groups])
    load_context = copy(context, rows_kept.at[1], sems.at[8 * groups + 1])
    for one in load(0):
        one.start()
    load_tokens.start()
    load_context.start()
    head = lax.broadcasted_iota(jnp.int32, (count, wide), 1) // head_width
    none = jnp.zeros((count, wide), bf16)
    odd = place[0] == 1

    @pl.loop(0, groups)
    def _(i):
        here = cut(i, wide)

        @pl.when(i + 1 < groups)
        def _():
            for one in load(i + 1):
                one.start()

        waits = load(i)
        waits[0].wait()
        grad_context = dot(attended[...], weights[here, :], NT).astype(bf16)
        context_turned = grad_context.T
        scaling = jnp.asarray(1.0 / math.sqrt(head_width), bf16)
        for one in waits[1:4]:
            one.wait()
        scaled_q = q_kept[:, here] * scaling
        k_turned = (k_kept[:, here] * scaling).T
        v = v_kept[:, here]

        @pl.when(i == 0)
        def _():
            load_tokens.wait()
            turned[...] = rows_kept[0].T
            load_context.wait()
            turned_context[...] = rows_kept[1].T

        for one in waits[4:]:
            one.wait()
        grad_k = jnp.zeros((count, wide), f32)
        grad_v = grad_k
        grad_q = []
        for h in range(4):
            mine = head == h
            probs = probs_kept[4 * i + h]
            wider = probs.astype(f32)
            weighted = wider * dot(v, only(context_turned, h, head_width))
            balance = jnp.sum(weighted, axis=0, keepdims=True)
            grad_scores = (weighted - wider * balance).astype(bf16)
            grad_v = grad_v + dot(probs, jnp.where(mine, grad_context, none))
            grad_k = grad_k + dot(grad_scores, jnp.where(mine, scaled_q, none))
            grad_q.append(dot(k_turned[h * head_width : (h + 1) * head_width, :], grad_scores))
        grad_q = jnp.concatenate(grad_q).astype(bf16).T
        grad_k = grad_k.astype(bf16)
        grad_v = grad_v.astype(bf16)
        grads_out[:, here] = grad_q
        grads_out[:, cut(i + groups, wide)] = grad_k
        grads_out[:, cut(i + 2 * groups, wide)] = grad_v
        sums[0:1, here] = column_sum(grad_q.astype(f32))
        sums[1:2, here] = column_sum(grad_v.astype(f32))
        pieces = (
            dot(turned[...], grad_q).astype(bf16),
            dot(turned[...], grad_k).astype(bf16),
            dot(turned[...], grad_v).astype(bf16),
            dot(turned_context[...], attended[:, here]).astype(bf16),
        )
        for s, (keep, send) in enumerate(((keep_0, send_0), (keep_1, send_1), (keep_2, send_2))):

            @pl.when(i == s)
            def _(keep=keep, send=send):
                for x in range(2):
                    keep[x] = jnp.where(odd, pieces[2 * x + 1], pieces[2 * x])
                    send[x] = jnp.where(odd, pieces[2 * x], pieces[2 * x + 1])

    sums[2:5, :] = vector_one[0:3, :]
    sums[5:8, :] = vector_two[0:3, :]
    sums[8:12, :] = bias_up[...]
    share = width // shares
    small[...] = jnp.zeros_like(small)
    for d, by_blk in enumerate(small_pieces(shares, width)):
        for b, three in enumerate(by_blk):
            for j, (row, column) in enumerate(three):
                small[b, d, j : j + 1, 0:share] = sums[row : row + 1, column : column + share]
    for x in range(2):
        even_part = small[2 * x].astype(bf16)
        odd_part = small[2 * x + 1].astype(bf16)
        small_keep[x] = jnp.where(odd, odd_part, even_part)
        small_send[x] = jnp.where(odd, even_part, odd_part)


def attend_back(place, attended, small, far, shares, after):
    count, width = attended.shape
    wide = 4 * (width // HEADS)
    groups = width // wide
    rows, turned = pltpu.VMEM((count, width), bf16), pltpu.VMEM((width, count), bf16)
    grads, keep_0, keep_1, keep_2, send_0, send_1, send_2, small_keep, small_send, mark = call(
        functools.partial(attend_back_kernel, head_width=width // HEADS),
        "attend_back", [place], [attended, *small],
        [shape(count, 3 * width)] + [shape(2, width, wide)] * 6 + [shape(2, shares, 16, wide)] * 2,
        [
            pltpu.VMEM((2, count, width), bf16), turned, turned,
            pltpu.VMEM((HEADS, count, count), bf16), rows, rows, rows,
            pltpu.VMEM((width, width), bf16),
            pltpu.VMEM((16, width), f32), pltpu.VMEM((4, shares, 16, wide), f32),
        ],
        far=far, copies=8 * groups + 2, room=26, after=after,
    )
    return [keep_0, keep_1, keep_2], [send_0, send_1, send_2], small_keep, small_send, grads, mark


def grad_tokens_kernel(grads, w_qkv, sum_one, r0, r1, r2, r3, total, sems):
    load = copy(sum_one, total, sems.at[0])
    load.start()
    product = dot(grads[...], w_qkv[...], NT)
    load.wait()
    result = (total[...] + product).astype(bf16)
    slots = r0.shape[0]
    for i, block in enumerate((r0, r1, r2, r3)):
        block[...] = result[i * slots : (i + 1) * slots, :]


def grad_tokens(sum_one, grads, w_qkv, slots, after):
    count, width = sum_one.shape
    *blocks, mark = call(
        grad_tokens_kernel, "grad_tokens", [], [grads, w_qkv], [shape(slots, width)] * 4,
        [pltpu.VMEM((count, width), f32)], far=[sum_one], copies=1, room=12, after=after,
    )
    return blocks, mark


def swap(block, axis, bit):
    return lax.ppermute(block, axis, [(i, i ^ bit) for i in range(lax.axis_size(axis))])


def pick(block, index, dim=0):
    return lax.dynamic_index_in_dim(block, index, dim, keepdims=False)


def every(count, work):
    if count <= 8:
        for number in range(count):
            work(number)
    else:
        pl.loop(0, count)(work)


def cut_units(bits, units, extra, orders, flip, after):
    parts, dims = len(orders), len(orders[0])
    arrays, numbers = [], {}
    for array in [a for unit in units for terms, _ in unit for a in terms] + list(extra):
        if id(array) not in numbers:
            numbers[id(array)] = len(arrays)
            arrays.append(array)
    rows = arrays[0].shape[-2]
    size = sum({id(terms[0]): terms[0].shape[-1] for terms, _ in units[0]}.values()) // parts
    more = [extra[0].shape[-2] if extra and s == 0 else 0 for s in range(parts)]
    outs = [shape(2 ** (dims - 1), len(units) * rows + m, size) for m in more]

    def kernel(bits_ref, *refs):
        ins, results = refs[: len(arrays)], refs[len(arrays) :]

        def added(terms, at):
            total = ins[numbers[id(terms[0])]][at]
            for term in terms[1:]:
                total = total + ins[numbers[id(term)]][at]
            return total

        def work(number):
            for s, order in enumerate(orders):
                index = [None] * dims
                index[order[0]] = bits_ref[order[0]] ^ flip
                for i, n in enumerate(order[1:]):
                    index[n] = (number >> (dims - 2 - i)) & 1
                for u, unit in enumerate(units):
                    terms, column = unit[s]
                    at = (*index, slice(None), slice(column * size, (column + 1) * size))
                    results[s][number, u * rows : (u + 1) * rows] = added(terms, at)
                if more[s]:
                    results[s][number, len(units) * rows :] = added(extra, tuple(index))

        every(2 ** (dims - 1), work)

    *made, mark = call(kernel, "cut_units", [bits], arrays, outs, after=after)
    return made, mark


def halve(bits, pairs, axes, join, after=()):
    taken = pairs[0][0].shape[0] // (2 if axes else 1)
    sizes = [a.shape[1] for a, _ in pairs]
    width = pairs[0][0].shape[2]
    flips = (1, 0) if axes else (0,)
    outs = [shape(taken, sum(sizes), width)] if join else [shape(taken, n, width) for n in sizes]
    arrays = [a for pair in pairs for a in pair]

    def kernel(bits_ref, *refs):
        ins, results = refs[: len(arrays)], refs[len(arrays) :]

        def work(number):
            for f, flip in enumerate(flips):
                for s in range(len(pairs)):
                    at = number + ((bits_ref[axes[s]] ^ flip) * taken if axes else 0)
                    total = ins[2 * s][at] + ins[2 * s + 1][at]
                    if join:
                        first = sum(sizes[:s])
                        results[f][number, first : first + sizes[s]] = total
                    else:
                        results[f * len(pairs) + s][number] = total

        every(taken, work)

    *made, mark = call(kernel, "halve", [bits], arrays, outs * len(flips), room=6, after=after)
    return made[: len(outs)], made[len(outs) :], mark


class Group:
    def __init__(self, units, extra, bits, names):
        self.units, self.extra, self.bits, self.names = units, extra, bits, names
        size = len(names)
        turn = [0, size - 1, size - 2]
        rest = list(range(size - 3, 0, -1))
        self.orders = [turn[s:] + turn[:s] + rest for s in range(3)]
        self.stage = 0
        self.pairs = None

    def send(self, blocks):
        return [
            swap(block, *self.names[order[self.stage]]) for block, order in zip(blocks, self.orders)
        ]

    def begin(self, after):
        sent, mark = cut_units(self.bits, self.units, self.extra, self.orders, 1, after)
        self.arrived = self.send(sent)
        return mark

    def rest(self, after):
        keep, mark = cut_units(self.bits, self.units, self.extra, self.orders, 0, after)
        self.pairs = list(zip(keep, self.arrived))
        self.stage = 1
        return mark

    def step(self, after):
        axes = [order[self.stage] for order in self.orders]
        sent, keep, mark = halve(self.bits, self.pairs, axes, self.stage == 3, after)
        self.pairs = list(zip(keep, self.send(sent)))
        self.stage += 1
        return mark

    def finish(self, after):
        (own,), _, mark = halve(self.bits, self.pairs, None, False, after)
        across = swap(own, "blk", 2)
        return (own, swap(own, "blk", 1), across, swap(across, "blk", 1)), mark


def chosen(place, b, refs):
    relative = place[1] ^ b
    values = [ref[...] for ref in refs]
    return jnp.where(
        relative < 2,
        jnp.where(relative == 0, values[0], values[1]),
        jnp.where(relative == 2, values[2], values[3]),
    ).astype(f32)


def place_feed(place, pieces, rows, shares):
    size = pieces[0].shape[2]
    width = 3 * size

    def kernel(place_ref, p0, p1, p2, p3, down, up):
        for b in range(4):
            for s in range(3):
                at = 2 * s * rows
                columns = slice(s * size, (s + 1) * size)
                value = chosen(place_ref, b, [p.at[0, at : at + rows] for p in (p0, p1, p2, p3)])
                down[b * rows : (b + 1) * rows, columns] = value
                at = at + rows
                columns = slice(b * width + s * size, b * width + (s + 1) * size)
                value = chosen(place_ref, b, [p.at[0, at : at + rows] for p in (p0, p1, p2, p3)])
                up[:, columns] = value

    return call(
        kernel, "place_feed", [place], pieces,
        [shape(4 * rows, width, dtype=f32), shape(rows, 4 * width, dtype=f32)],
    )[:2]


def place_own(place, pieces, rows, shares):
    size = pieces[0].shape[2]
    width = 3 * size
    share = width // shares
    extra = pieces[0].shape[1] - 3 * rows

    def kernel(place_ref, p0, p1, p2, p3, qkv, out, *small):
        refs = (p0, p1, p2, p3)
        bias_qv, bias_out, gain_one, shift_one, bias_up, bias_down, gain_two, shift_two = small
        for b in range(4):
            for s in range(3):
                at = s * rows + (extra if s else 0)
                value = chosen(place_ref, b, [p.at[0, at : at + rows] for p in refs])
                columns = slice(s * size, (s + 1) * size)
                if b == 3:
                    out[:, columns] = value
                else:
                    qkv[:, b * width + s * size : b * width + (s + 1) * size] = value
            value = chosen(place_ref, b, [p.at[0, rows : rows + extra] for p in refs])
            targets = (
                ((bias_qv, 0), (bias_qv, 1), (bias_out, 0)),
                ((gain_one, 0), (shift_one, 0), (bias_down, 0)),
                ((gain_two, 0), (shift_two, 0), (bias_up, 0)),
                ((bias_up, 1), (bias_up, 2), (bias_up, 3)),
            )[b]
            for j, (ref, part) in enumerate(targets):
                ref[:, part * share : (part + 1) * share] = value[j : j + 1, 0:share]

    vectors = [shape(1, n * share, dtype=f32) for n in (2, 1, 1, 1, 4, 1, 1, 1)]
    return call(
        kernel, "place_own", [place], pieces,
        [shape(rows, 3 * width, dtype=f32), shape(rows, width, dtype=f32), *vectors],
    )[:10]


def place_rows(place, blocks, after):
    slots, width = blocks[0].shape

    def kernel(place_ref, *refs):
        for i in range(4):
            refs[4][place_ref[1] ^ i] = refs[i][...]

    return call(kernel, "place_rows", [place], blocks, [shape(4, slots, width)], after=after)


def shards(
    tokens, lengths, w_qkv, bias_qv, w_out, bias_out, norm1_gain, norm1_bias, w_up, bias_up,
    w_down, bias_down, norm2_gain, norm2_bias, cotangent,
):
    rows, slots, width = tokens.shape
    shares = lax.axis_size("dp")
    dp_bits = shares.bit_length() - 1
    position = lax.axis_index("blk").astype(jnp.int32)
    group = lax.axis_index("dp").astype(jnp.int32)
    place = jnp.stack([position % 2, position])
    names = [("blk", 2)] + [("dp", 1 << i) for i in reversed(range(dp_bits))]
    bits = jnp.stack([position // 2] + [(group >> i) % 2 for i in reversed(range(dp_bits))])

    def gather_row(array):
        return [pick(array, position)] + [
            swap(pick(array, position ^ i), "blk", i) for i in (2, 3, 1)
        ]

    def in_order(blocks):
        return [blocks[0], blocks[3], blocks[1], blocks[2]]

    def scatter_row(blocks, after=()):
        moved = [blocks[0]] + [swap(blocks[i], "blk", i) for i in range(1, rows)]
        return place_rows(place, moved, after)

    vectors = jnp.concatenate(
        [bias_qv, bias_out, norm1_gain, norm1_bias, bias_down, norm2_gain, norm2_bias, bias_up]
    ).reshape(-1, width)
    row = jnp.concatenate([pick(lengths, position), position[None]])
    blocks = gather_row(tokens)
    blocks, cotangent = lax.optimization_barrier((blocks, cotangent))
    blocks = in_order(blocks)
    cotangents = in_order(gather_row(cotangent))
    qkv_near, out_near, mask = prepare(row, w_qkv, w_out, slots, rows * slots)
    normed, inverse, q, k, v, prob, context, row_tokens = attend(
        blocks, vectors, qkv_near, out_near, mask
    )
    keep_active, send_active, slope, lowered, first, o0, o1, o2, o3, vector_two, sum_two, normed = feed(
        place, normed, vectors, cotangents, w_up, w_down, shares
    )
    got_active, got_lowered = swap(send_active, "blk", 1), swap(lowered, "blk", 1)
    keep_up, send_up, grad_bias_up, attended, vector_one, sum_one, mark = grad_up(
        place, lowered, slope, first, w_down, inverse, vectors, w_up, sum_two, normed
    )
    got_up = swap(send_up, "blk", 1)
    outputs, mark = scatter_row([o0, o1, o2, o3], [mark])
    down, mark = grad_down(keep_active, got_active, lowered, got_lowered, [mark])

    def chunks(array):
        return array.reshape((2,) * (1 + dp_bits) + (-1, array.shape[-1]))

    down, keep_up, got_up = chunks(down), chunks(keep_up), chunks(got_up)
    feed_group = Group(
        [[([down], s) for s in range(3)], [([keep_up, got_up], s) for s in range(3)]],
        (), bits, names,
    )
    mark = feed_group.begin([mark])
    keeps, sends, small_keep, small_send, grads, mark = attend_back(
        place, attended, [vector_one, vector_two, grad_bias_up],
        [row_tokens, context, prob, q, k, v, w_out], shares, [mark],
    )
    gots = [swap(send, "blk", 1) for send in sends]
    small_got = swap(small_send, "blk", 1)
    mark = feed_group.rest([mark])
    mark = feed_group.step([mark])
    own_group = Group(
        [[([chunks(keep), chunks(got)], 0) for keep, got in zip(keeps, gots)]],
        (chunks(small_keep), chunks(small_got)), bits, names,
    )
    mark = own_group.begin([mark])
    tokens_parts, mark = grad_tokens(sum_one, grads, w_qkv, slots, [mark])
    mark = own_group.rest([mark])
    for _ in range(dp_bits - 1):
        mark = feed_group.step([mark])
        mark = own_group.step([mark])
    mark = own_group.step([mark])
    feed_pieces, mark = feed_group.finish([mark])
    token_grads, mark = scatter_row(tokens_parts, [mark])
    own_pieces, mark = own_group.finish([mark])

    share = width // shares
    down, up = place_feed(place, feed_pieces, share, shares)
    (
        grad_w_qkv, grad_w_out, sum_qv, sum_out, sum_gain_one, sum_shift_one, sum_up, sum_down,
        sum_gain_two, sum_shift_two,
    ) = place_own(place, own_pieces, share, shares)
    return (
        outputs,
        token_grads,
        grad_w_qkv,
        sum_qv[0],
        grad_w_out,
        sum_out[0],
        sum_gain_one[0],
        sum_shift_one[0],
        up,
        sum_up[0],
        down,
        sum_down[0],
        sum_gain_two[0],
        sum_shift_two[0],
    )


def solution(mesh):
    row_spec = P("dp", "blk", None)
    in_specs = (row_spec, P("dp", None)) + (P(),) * 12 + (row_spec,)
    wide, flat = P("dp", None), P("dp")
    out_specs = (
        row_spec, row_spec, wide, flat, wide, flat, flat, flat, wide, flat, wide, flat, flat, flat,
    )
    return jax.shard_map(shards, mesh=mesh, in_specs=in_specs, out_specs=out_specs, check_vma=False)
```

time: 193 us -> 176 us (0.912)
  waiting for transfers between devices: 55.6 us -> 29.7 us
  Pallas kernels: 83 us -> 94.1 us
  local copies, waits for them, and re-layouts: 16.3 us -> 10.2 us
  starting transfers between devices: 35.3 us -> 39 us
    ppermute x44 -> x45, waiting for transfers between devices: 55.6 us -> 29.7 us  [swap(): lax.ppermute(block, axis, [(i, i ^ bit) for i in range(lax.axis_size(axis...]
    pallas_call x23, Pallas kernels: 83 us -> 94.1 us  [call(): pl.pallas_call(body, in_specs=[SMEM] * len(scalars) + [VMEM] * len(arrays...]
    unnamed x39, local copies, waits for them, and re-layouts: 14.2 us -> 6.52 us
    ppermute x44 -> x45, starting transfers between devices: 35.3 us -> 39 us  [swap(): lax.ppermute(block, axis, [(i, i ^ bit) for i in range(lax.axis_size(axis...]
  transfers between devices with their start and end apart: 44 -> 45, of which waited for: 14 -> 10; matrix products, arithmetic and copies ran while one was open for 3% -> 4% of each run, Pallas kernels for 32% -> 42%
where the time goes in v3:
time: 176 us; the launch traced here: 175 us
  Pallas kernels  94.1 us (53%)
  starting transfers between devices  39 us (22%)
  waiting for transfers between devices  29.7 us (17%)
  local copies, waits for them, and re-layouts  10.2 us (6%)
    pallas_call x23, Pallas kernels, call(): pl.pallas_call(body, in_specs=[SMEM] * len(scalars) + [VMEM] * len(arrays...  94.1 us
    ppermute x45, starting transfers between devices, swap(): lax.ppermute(block, axis, [(i, i ^ bit) for i in range(lax.axis_size(axis...  39 us
    ppermute x45, waiting for transfers between devices, swap(): lax.ppermute(block, axis, [(i, i ^ bit) for i in range(lax.axis_size(axis...  29.7 us
    unnamed x39, local copies, waits for them, and re-layouts  6.52 us
  transfers between devices with their start and end apart: 45, of which 10 were waited for; matrix products, arithmetic and copies ran while one was open for 4% of the time, Pallas kernels for 42%

profile of v3, /device:TPU:0, one launch (start us, length us, event | category | flops | bytes accessed | tf_op | source)
XLA Modules:
  0.0 174.9 jit_solution(8290576477323012066)
XLA Ops:
  0.7 2.0 %dynamic-slice_bitcast_fusion.4 = (bf16[128,768]{1,0:T(8,128)(2,1)}, bf16[128,768]{1,0:T(8,128)(2,1)}, bf16[128,768]{1,0:T(8,128)(2,1)S(1)}, bf16[128,768]{1,0:T(8,128)(2,1)}) fusion(bf16[4,128,768]{2,1,0:T(8,128)(2,1)} %param.15, s32[]{:T(128)S(6)} %select_n.46, s32[]{:T(128)S(6)} %select_n.44, s32[]{:T(128)S(6)} %select_n.43, s32[]{:T(128)S(6)} %select_n.45), kind=kLoop, calls=%fused_computation.4 | loop fusion | bytes 1572880 | tf_op jit(solution)/shard_map/jit(dynamic_index_in_dim)/squeeze | solution.py:566
  2.7 2.9 %collective-permute-start = (bf16[128,768]{1,0:T(8,128)(2,1)}, bf16[128,768]{1,0:T(8,128)(2,1)}, u32[]{:S(2)}, u32[]{:S(2)}) collective-permute-start(bf16[128,768]{1,0:T(8,128)(2,1)} %get-tuple-element.261), channel_id=1, source_target_pairs={{0,2},{1,3},{2,0},{3,1},{4,6},{5,7},{6,4},{7,5},{8,10},{9,11},{10,... | collective-permute-start | bytes 589832 | tf_op jit(solution)/shard_map/ppermute | solution.py:562
  11.5 3.5 %prepare.1 = (bf16[768,2304]{1,0:T(8,128)(2,1)S(1)}, bf16[768,768]{1,0:T(8,128)(2,1)S(1)}, f32[512,512]{1,0:T(8,128)S(1)}, f32[8,128]{1,0:T(8,128)}) custom-call(s32[9]{0:T(128)S(1)} %pad_add_fusion.1.refs_0_, bf16[768,2304]{1,0:T(8,128)(2,1)} %refs_1_.3, bf16[768,768]{1,0:T(8,128)(2,1)} %refs_11_.1), custom_call_target="tpu_custom_call" | custom-call | flops 999999995904 | tf_op jit(solution)/shard_map/prepare/pallas_call | solution.py:50
  15.2 0.9 dynamic-slice_bitcast_fusion
  16.5 1.6 collective-permute-start.4
  18.3 12.4 %attend.1 = (f32[512,768]{1,0:T(8,128)S(1)}, f32[512,1]{1,0:T(8,128)S(1)}, bf16[512,768]{1,0:T(8,128)(2,1)}, bf16[512,768]{1,0:T(8,128)(2,1)}, bf16[512,768]{1,0...) custom-call(bf16[128,768]{1,0:T(8,128)(2,1)S(1)} %get-tuple-element., ...), custom_call_target="tpu_custom_call" | custom-call | flops 999999995904 | tf_op jit(solution)/shard_map/attend/pallas_call | solution.py:50
  30.7 13.4 %feed.1 = (bf16[2,8,96,512]{3,2,1,0:T(8,128)(2,1)S(1)}, bf16[2,8,96,512]{3,2,1,0:T(8,128)(2,1)}, bf16[512,3072]{1,0:T(8,128)(2,1)S(1)}, bf16[512,768]{1,0:T(8,12...) custom-call(s32[2]{0:T(128)S(1)} %pad_add_fusion.refs_0_, ...), custom_call_target="tpu_custom_call" | custom-call | flops 999999995904 | tf_op jit(solution)/shard_map/feed/pallas_call | solution.py:50
  44.6 1.6 collective-permute-start.7
  46.8 12.9 %grad_up.1 = (bf16[2,768,768]{2,1,0:T(8,128)(2,1)S(1)}, bf16[2,768,768]{2,1,0:T(8,128)(2,1)}, f32[4,768]{1,0:T(4,128)S(1)}, bf16[512,768]{1,0:T(8,128)(2,1)S(1)}...) custom-call(s32[2]{0:T(128)S(1)} %pad_add_fusion.refs_0_, ...), custom_call_target="tpu_custom_call" | custom-call | flops 999999995904 | tf_op jit(solution)/shard_map/grad_up/pallas_call | solution.py:50
  60.2 2.1 %place_rows.2 = (bf16[4,128,768]{2,1,0:T(8,128)(2,1)}, f32[8,128]{1,0:T(8,128)S(1)}) custom-call(s32[2]{0:T(128)S(1)} %pad_add_fusion.refs_0_, bf16[128,768]{1,0:T(8,128)(2,1)S(1)} %get-tuple-element.144.refs_1_, bf16[128,768]{1,0:T(8,128)(2,1)} %collective-permute-done.6.refs_2_, bf16[128,768]{1,0:T(8,128)(2,1)} %collective-permute-done.7.refs_3_, ...), custom_call_target="tpu_custom_call" | custom-call | tf_op jit(solution)/shard_map/place_rows/pallas_call | solution.py:50
  62.3 5.7 %grad_down.1 = (bf16[2,8,96,768]{3,2,1,0:T(8,128)(2,1)S(1)}, f32[8,128]{1,0:T(8,128)S(1)}) custom-call(bf16[2,8,96,512]{3,2,1,0:T(8,128)(2,1)S(1)} %get-tuple-element.166.refs_0_, bf16[2,8,96,512]{3,2,1,0:T(8,128)(2,1)} %collective-permute-done.9.refs_1_, bf16[512,768]{1,0:T(8,128)(2,1)} %get-tuple-element.148.refs_1_.refs_2_, ...), custom_call_target="tpu_custom_call" | custom-call | flops 999999995904 | tf_op jit(solution)/shard_map/grad_down/pallas_call | solution.py:50
  68.0 4.2 %cut_units.4 = (bf16[8,192,256]{2,1,0:T(8,128)(2,1)}, bf16[8,192,256]{2,1,0:T(8,128)(2,1)}, bf16[8,192,256]{2,1,0:T(8,128)(2,1)}, f32[8,128]{1,0:T(8,128)S(1)}) custom-call(s32[4]{0:T(128)S(1)} %pad_add_fusion.2.refs_0_, bf16[2,2,2,2,96,768]{5,4,3,2,1,0:T(8,128)(2,1)S(1)} %bitcast.44, bf16[2,2,2,2,96,768]{5,4,3,2,1,0:T(8,128)(2,1)S(1)} %bitcast.42, ...), custom_call_target="tpu_custom_call" | custom-call | tf_op jit(solution)/shard_map/cut_units/pallas_call | solution.py:50
  72.2 1.6 collective-permute-start.16
  73.8 1.5 collective-permute-start.17
  75.4 1.6 collective-permute-start.18
  76.9 17.8 %attend_back.1 = (bf16[512,2304]{1,0:T(8,128)(2,1)S(1)}, bf16[2,768,256]{2,1,0:T(8,128)(2,1)S(1)}, bf16[2,768,256]{2,1,0:T(8,128)(2,1)S(1)}, bf16[2,768,256]{2,1...) custom-call(s32[2]{0:T(128)S(1)} %pad_add_fusion.refs_0_, ...), custom_call_target="tpu_custom_call" | custom-call | flops 999999995904 | tf_op jit(solution)/shard_map/attend_back/pallas_call | solution.py:50
  95.4 2.0 %cut_units.5 = (bf16[8,192,256]{2,1,0:T(8,128)(2,1)S(1)}, bf16[8,192,256]{2,1,0:T(8,128)(2,1)S(1)}, bf16[8,192,256]{2,1,0:T(8,128)(2,1)S(1)}, f32[8,128]{1,0:T(8,128)S(1)}) custom-call(s32[4]{0:T(128)S(1)} %pad_add_fusion.2.refs_0_, bf16[2,2,2,2,96,768]{5,4,3,2,1,0:T(8,128)(2,1)S(1)} %bitcast.45, bf16[2,2,2,2,96,768]{5,4,3,2,1,0:T(8,128)(2,1)S(1)} %bitcast.43, ...), custom_call_target="tpu_custom_call" | custom-call | tf_op jit(solution)/shard_map/cut_units/pallas_call | solution.py:50
  97.4 2.8 %halve.8 = (bf16[4,192,256]{2,1,0:T(8,128)(2,1)S(1)}, bf16[4,192,256]{2,1,0:T(8,128)(2,1)}, bf16[4,192,256]{2,1,0:T(8,128)(2,1)}, bf16[4,192,256]{2,1,0:T(8,128)...) custom-call(s32[4]{0:T(128)S(1)} %pad_add_fusion.2.refs_0_, ...), custom_call_target="tpu_custom_call" | custom-call | tf_op jit(solution)/shard_map/halve/pallas_call | solution.py:50
  100.9 1.2 collective-permute-done.15
  103.0 1.7 cut_units.6
  104.7 1.6 collective-permute-start.28
  106.3 1.5 collective-permute-start.29
  107.9 4.3 %collective-permute-done.22.refs_2_ = bf16[4,192,256]{2,1,0:T(8,128)(2,1)S(1)} collective-permute-done((bf16[4,192,256]{2,1,0:T(8,128)(2,1)S(1)}, bf16[4,192,256]{2,1,0:T(8,128)(2,1)S(1)}, u32[]{:S(2)}, u32[]{:S(2)}) %collective-permute-start.22) | collective-permute-done | bytes 393248 | tf_op jit(solution)/shard_map/ppermute | solution.py:562
  113.4 3.5 %grad_tokens.1 = (bf16[128,768]{1,0:T(8,128)(2,1)S(1)}, bf16[128,768]{1,0:T(8,128)(2,1)S(1)}, bf16[128,768]{1,0:T(8,128)(2,1)S(1)}, bf16[128,768]{1,0:T(8,128)(2,1)S(1)}, f32[8,128]{1,0:T(8,128)S(1)}) custom-call(bf16[512,2304]{1,0:T(8,128)(2,1)S(1)} %get-tuple-element.174.refs_0_, bf16[768,2304]{1,0:T(8,128)(2,1)S(1)} %copy-done.14, ...), custom_call_target="tpu_custom_call" | custom-call | flops 999999995904 | tf_op jit(solution)/shard_map/grad_tokens/pallas_call | solution.py:50
  117.9 1.2 halve.9
  119.1 1.6 collective-permute-start.25
  121.8 3.5 %collective-permute-done.30.refs_6_ = bf16[8,96,256]{2,1,0:T(8,128)(2,1)} collective-permute-done((bf16[8,96,256]{2,1,0:T(8,128)(2,1)}, bf16[8,96,256]{2,1,0:T(8,128)(2,1)}, u32[]{:S(2)}, u32[]{:S(2)}) %collective-permute-start.30) | collective-permute-done | bytes 393248 | tf_op jit(solution)/shard_map/ppermute | solution.py:562
  125.3 1.4 halve.10
  126.7 1.0 collective-permute-start.32
  127.7 1.6 collective-permute-start.33
  130.5 2.6 %collective-permute-start.31 = (bf16[1,576,256]{2,1,0:T(8,128)(2,1)S(1)}, bf16[1,576,256]{2,1,0:T(8,128)(2,1)S(1)}, u32[]{:S(2)}, u32[]{:S(2)}) collective-permute-start(bf16[1,576,256]{2,1,0:T(8,128)(2,1)S(1)} %get-tuple-element.221), channel_id=1, source_target_pairs={{0,16},{4,20},{8,24},{12,28},{16,0},{20,4},{24,8},{28,12},{1,17},{... | collective-permute-start | bytes 884744 | tf_op jit(solution)/shard_map/ppermute | solution.py:562
  133.1 2.2 %collective-permute-done.33.refs_4_ = bf16[4,96,256]{2,1,0:T(8,128)(2,1)S(1)} collective-permute-done((bf16[4,96,256]{2,1,0:T(8,128)(2,1)S(1)}, bf16[4,96,256]{2,1,0:T(8,128)(2,1)S(1)}, u32[]{:S(2)}, u32[]{:S(2)}) %collective-permute-start.33) | collective-permute-done | bytes 196640 | tf_op jit(solution)/shard_map/ppermute | solution.py:562
  136.0 1.8 %collective-permute-start.35 = (bf16[2,112,256]{2,1,0:T(8,128)(2,1)S(1)}, bf16[2,112,256]{2,1,0:T(8,128)(2,1)S(1)}, u32[]{:S(2)}, u32[]{:S(2)}) collective-permute-start(bf16[2,112,256]{2,1,0:T(8,128)(2,1)S(1)} %get-tuple-element.230), channel_id=1, source_target_pairs={{0,8},{4,12},{8,0},{12,4},{16,24},{20,28},{24,16},{28,20},{1,9},{5... | collective-permute-start | bytes 344072 | tf_op jit(solution)/shard_map/ppermute | solution.py:562
  137.8 0.8 collective-permute-start.37
  138.6 3.8 %collective-permute-done.36.refs_4_ = bf16[2,96,256]{2,1,0:T(8,128)(2,1)S(1)} collective-permute-done((bf16[2,96,256]{2,1,0:T(8,128)(2,1)S(1)}, bf16[2,96,256]{2,1,0:T(8,128)(2,1)S(1)}, u32[]{:S(2)}, u32[]{:S(2)}) %collective-permute-start.36) | collective-permute-done | bytes 98336 | tf_op jit(solution)/shard_map/ppermute | solution.py:562
  143.0 0.8 collective-permute-done.31.refs_2_
  144.3 1.5 collective-permute-start.43
  146.4 1.3 collective-permute-start.21
  147.7 3.1 %collective-permute-start.38 = (bf16[1,304,256]{2,1,0:T(8,128)(2,1)S(1)}, bf16[1,304,256]{2,1,0:T(8,128)(2,1)S(1)}, u32[]{:S(2)}, u32[]{:S(2)}) collective-permute-start(bf16[1,304,256]{2,1,0:T(8,128)(2,1)S(1)} %get-tuple-element.240), channel_id=1, source_target_pairs={{0,16},{4,20},{8,24},{12,28},{16,0},{20,4},{24,8},{28,12},{1,17},{... | collective-permute-start | bytes 466952 | tf_op jit(solution)/shard_map/ppermute | solution.py:562
  150.8 7.2 %collective-permute-done.20.refs_3_ = bf16[128,768]{1,0:T(8,128)(2,1)S(1)} collective-permute-done((bf16[128,768]{1,0:T(8,128)(2,1)S(1)}, bf16[128,768]{1,0:T(8,128)(2,1)S(1)}, u32[]{:S(2)}, u32[]{:S(2)}) %collective-permute-start.20) | collective-permute-done | bytes 196640 | tf_op jit(solution)/shard_map/ppermute | solution.py:562
  158.1 1.4 collective-permute-done.21.refs_4_
  159.4 1.5 place_rows.3
  160.9 1.1 halve.15
  162.4 1.6 collective-permute-start.42
  164.6 4.0 %collective-permute-done.40.refs_3_ = bf16[1,304,256]{2,1,0:T(8,128)(2,1)S(1)} collective-permute-done((bf16[1,304,256]{2,1,0:T(8,128)(2,1)S(1)}, bf16[1,304,256]{2,1,0:T(8,128)(2,1)S(1)}, u32[]{:S(2)}, u32[]{:S(2)}) %collective-permute-start.40) | collective-permute-done | bytes 155680 | tf_op jit(solution)/shard_map/ppermute | solution.py:562
  168.5 1.4 collective-permute-done.41.refs_4_
  169.9 1.7 place_own.1
  172.7 2.1 %place_feed.1 = (f32[384,768]{1,0:T(8,128)}, f32[96,3072]{1,0:T(8,128)}, f32[8,128]{1,0:T(8,128)}) custom-call(s32[2]{0:T(128)S(1)} %copy-done.11, bf16[1,576,256]{2,1,0:T(8,128)(2,1)S(1)} %get-tuple-element.249.refs_1_, bf16[1,576,256]{2,1,0:T(8,128)(2,1)S(1)} %collective-permute-done.42.refs_2_, bf16[1,576,256]{2,1,0:T(8,128)(2,1)S(1)} %collective-permute-done.43.refs_3_, ...), custom_call_target="tpu_custom_call" | custom-call | tf_op jit(solution)/shard_map/place_feed/pallas_call | solution.py:50
  (114 shorter events, 19.1 us)
Async XLA Ops:
  2.7 12.4 %collective-permute-start = (bf16[128,768]{1,0:T(8,128)(2,1)}, bf16[128,768]{1,0:T(8,128)(2,1)}, u32[]{:S(2)}, u32[]{:S(2)}) collective-permute-start(bf16[128,768]{1,0:T(8,128)(2,1)} %get-tuple-element.261), channel_id=1, source_target_pairs={{0,2},{1,3},{2,0},{3,1},{4,6},{5,7},{6,4},{7,5},{8,10},{9,11},{10,... | collective-permute-start | bytes 589832 | tf_op jit(solution)/shard_map/ppermute | solution.py:562
  5.7 9.5 %collective-permute-start.1 = (bf16[128,768]{1,0:T(8,128)(2,1)}, bf16[128,768]{1,0:T(8,128)(2,1)}, u32[]{:S(2)}, u32[]{:S(2)}) collective-permute-start(bf16[128,768]{1,0:T(8,128)(2,1)} %get-tuple-element.263), channel_id=1, source_target_pairs={{0,3},{1,2},{2,1},{3,0},{4,7},{5,6},{6,5},{7,4},{8,11},{9,10},{10,... | collective-permute-start | bytes 589832 | tf_op jit(solution)/shard_map/ppermute | solution.py:562
  5.7 9.5 %collective-permute-start.2 = (bf16[128,768]{1,0:T(8,128)(2,1)}, bf16[128,768]{1,0:T(8,128)(2,1)}, u32[]{:S(2)}, u32[]{:S(2)}) collective-permute-start(bf16[128,768]{1,0:T(8,128)(2,1)} %get-tuple-element.260), channel_id=1, source_target_pairs={{0,1},{1,0},{2,3},{3,2},{4,5},{5,4},{6,7},{7,6},{8,9},{9,8},{10,11... | collective-permute-start | bytes 589832 | tf_op jit(solution)/shard_map/ppermute | solution.py:562
  15.1 154.8 %copy-start.10 = (s32[2]{0:T(128)}, s32[2]{0:T(128)S(1)}, u32[]{:S(2)}) copy-start(s32[2]{0:T(128)S(1)} %pad_add_fusion.refs_0_) | copy-start | bytes 28
  16.1 14.6 %collective-permute-start.3 = (bf16[128,768]{1,0:T(8,128)(2,1)}, bf16[128,768]{1,0:T(8,128)(2,1)}, u32[]{:S(2)}, u32[]{:S(2)}) collective-permute-start(bf16[128,768]{1,0:T(8,128)(2,1)} %get-tuple-element.258), channel_id=1, source_target_pairs={{0,1},{1,0},{2,3},{3,2},{4,5},{5,4},{6,7},{7,6},{8,9},{9,8},{10,11... | collective-permute-start | bytes 589832 | tf_op jit(solution)/shard_map/ppermute | solution.py:562
  16.5 14.2 %collective-permute-start.4 = (bf16[128,768]{1,0:T(8,128)(2,1)}, bf16[128,768]{1,0:T(8,128)(2,1)}, u32[]{:S(2)}, u32[]{:S(2)}) collective-permute-start(bf16[128,768]{1,0:T(8,128)(2,1)} %get-tuple-element.257), channel_id=1, source_target_pairs={{0,2},{1,3},{2,0},{3,1},{4,6},{5,7},{6,4},{7,5},{8,10},{9,11},{10,... | collective-permute-start | bytes 589832 | tf_op jit(solution)/shard_map/ppermute | solution.py:562
  18.1 12.6 %collective-permute-start.5 = (bf16[128,768]{1,0:T(8,128)(2,1)}, bf16[128,768]{1,0:T(8,128)(2,1)}, u32[]{:S(2)}, u32[]{:S(2)}) collective-permute-start(bf16[128,768]{1,0:T(8,128)(2,1)} %get-tuple-element.256), channel_id=1, source_target_pairs={{0,3},{1,2},{2,1},{3,0},{4,7},{5,6},{6,5},{7,4},{8,11},{9,10},{10,... | collective-permute-start | bytes 589832 | tf_op jit(solution)/shard_map/ppermute | solution.py:562
  44.2 15.5 %collective-permute-start.6 = (bf16[128,768]{1,0:T(8,128)(2,1)}, bf16[128,768]{1,0:T(8,128)(2,1)}, u32[]{:S(2)}, u32[]{:S(2)}) collective-permute-start(bf16[128,768]{1,0:T(8,128)(2,1)} %get-tuple-element.145), channel_id=1, source_target_pairs={{0,1},{1,0},{2,3},{3,2},{4,5},{5,4},{6,7},{7,6},{8,9},{9,8},{10,11... | collective-permute-start | bytes 589832 | tf_op jit(solution)/shard_map/ppermute | solution.py:562
  44.6 15.6 %collective-permute-start.7 = (bf16[128,768]{1,0:T(8,128)(2,1)}, bf16[128,768]{1,0:T(8,128)(2,1)}, u32[]{:S(2)}, u32[]{:S(2)}) collective-permute-start(bf16[128,768]{1,0:T(8,128)(2,1)} %get-tuple-element.146), channel_id=1, source_target_pairs={{0,2},{1,3},{2,0},{3,1},{4,6},{5,7},{6,4},{7,5},{8,10},{9,11},{10,... | collective-permute-start | bytes 589832 | tf_op jit(solution)/shard_map/ppermute | solution.py:562
  46.2 14.0 %collective-permute-start.8 = (bf16[128,768]{1,0:T(8,128)(2,1)}, bf16[128,768]{1,0:T(8,128)(2,1)}, u32[]{:S(2)}, u32[]{:S(2)}) collective-permute-start(bf16[128,768]{1,0:T(8,128)(2,1)} %get-tuple-element.147), channel_id=1, source_target_pairs={{0,3},{1,2},{2,1},{3,0},{4,7},{5,6},{6,5},{7,4},{8,11},{9,10},{10,... | collective-permute-start | bytes 589832 | tf_op jit(solution)/shard_map/ppermute | solution.py:562
  46.2 16.0 %collective-permute-start.9 = (bf16[2,8,96,512]{3,2,1,0:T(8,128)(2,1)}, bf16[2,8,96,512]{3,2,1,0:T(8,128)(2,1)}, u32[]{:S(2)}, u32[]{:S(2)}) collective-permute-start(bf16[2,8,96,512]{3,2,1,0:T(8,128)(2,1)} %get-tuple-element.167), channel_id=1, source_target_pairs={{0,1},{1,0},{2,3},{3,2},{4,5},{5,4},{6,7},{7,6},{8,9},{9,8},{10,11... | collective-permute-start | bytes 4718600 | tf_op jit(solution)/shard_map/ppermute | solution.py:562
  46.7 15.5 %collective-permute-start.10 = (bf16[512,768]{1,0:T(8,128)(2,1)}, bf16[512,768]{1,0:T(8,128)(2,1)}, u32[]{:S(2)}, u32[]{:S(2)}) collective-permute-start(bf16[512,768]{1,0:T(8,128)(2,1)} %get-tuple-element.148.refs_1_.refs_2_), channel_id=1, source_target_pairs={{0,1},{1,0},{2,3},{3,2},{4,5},{5,4},{6,7},{7,6},{8,9},{9,8},{10,11... | collective-permute-start | bytes 2359304 | tf_op jit(solution)/shard_map/ppermute | solution.py:562
  59.6 8.3 %collective-permute-start.11 = (bf16[2,768,768]{2,1,0:T(8,128)(2,1)}, bf16[2,768,768]{2,1,0:T(8,128)(2,1)}, u32[]{:S(2)}, u32[]{:S(2)}) collective-permute-start(bf16[2,768,768]{2,1,0:T(8,128)(2,1)} %get-tuple-element.171), channel_id=1, source_target_pairs={{0,1},{1,0},{2,3},{3,2},{4,5},{5,4},{6,7},{7,6},{8,9},{9,8},{10,11... | collective-permute-start | bytes 7077896 | tf_op jit(solution)/shard_map/ppermute | solution.py:562
  72.2 23.1 %collective-permute-start.16 = (bf16[8,192,256]{2,1,0:T(8,128)(2,1)}, bf16[8,192,256]{2,1,0:T(8,128)(2,1)}, u32[]{:S(2)}, u32[]{:S(2)}) collective-permute-start(bf16[8,192,256]{2,1,0:T(8,128)(2,1)} %get-tuple-element.186), channel_id=1, source_target_pairs={{0,2},{1,3},{2,0},{3,1},{4,6},{5,7},{6,4},{7,5},{8,10},{9,11},{10,... | collective-permute-start | bytes 2359304 | tf_op jit(solution)/shard_map/ppermute | solution.py:562
  73.8 23.6 %collective-permute-start.17 = (bf16[8,192,256]{2,1,0:T(8,128)(2,1)}, bf16[8,192,256]{2,1,0:T(8,128)(2,1)}, u32[]{:S(2)}, u32[]{:S(2)}) collective-permute-start(bf16[8,192,256]{2,1,0:T(8,128)(2,1)} %get-tuple-element.188), channel_id=1, source_target_pairs={{0,4},{4,0},{8,12},{12,8},{16,20},{20,16},{24,28},{28,24},{1,5},{5... | collective-permute-start | bytes 2359304 | tf_op jit(solution)/shard_map/ppermute | solution.py:562
  75.4 22.0 %collective-permute-start.18 = (bf16[8,192,256]{2,1,0:T(8,128)(2,1)}, bf16[8,192,256]{2,1,0:T(8,128)(2,1)}, u32[]{:S(2)}, u32[]{:S(2)}) collective-permute-start(bf16[8,192,256]{2,1,0:T(8,128)(2,1)} %get-tuple-element.190), channel_id=1, source_target_pairs={{0,8},{4,12},{8,0},{12,4},{16,24},{20,28},{24,16},{28,20},{1,9},{5... | collective-permute-start | bytes 2359304 | tf_op jit(solution)/shard_map/ppermute | solution.py:562
  76.9 18.5 %copy-start.3 = (bf16[2,8,96,768]{3,2,1,0:T(8,128)(2,1)S(1)}, bf16[2,8,96,768]{3,2,1,0:T(8,128)(2,1)}, u32[]{:S(2)}) copy-start(bf16[2,8,96,768]{3,2,1,0:T(8,128)(2,1)} %copy-done.2) | copy-start | bytes 7077892
  94.8 7.8 %collective-permute-start.12 = (bf16[2,768,256]{2,1,0:T(8,128)(2,1)S(1)}, bf16[2,768,256]{2,1,0:T(8,128)(2,1)S(1)}, u32[]{:S(2)}, u32[]{:S(2)}) collective-permute-start(bf16[2,768,256]{2,1,0:T(8,128)(2,1)S(1)} %get-tuple-element.177), channel_id=1, source_target_pairs={{0,1},{1,0},{2,3},{3,2},{4,5},{5,4},{6,7},{7,6},{8,9},{9,8},{10,11... | collective-permute-start | bytes 2359304 | tf_op jit(solution)/shard_map/ppermute | solution.py:562
  94.8 8.1 %collective-permute-start.13 = (bf16[2,768,256]{2,1,0:T(8,128)(2,1)S(1)}, bf16[2,768,256]{2,1,0:T(8,128)(2,1)S(1)}, u32[]{:S(2)}, u32[]{:S(2)}) collective-permute-start(bf16[2,768,256]{2,1,0:T(8,128)(2,1)S(1)} %get-tuple-element.179), channel_id=1, source_target_pairs={{0,1},{1,0},{2,3},{3,2},{4,5},{5,4},{6,7},{7,6},{8,9},{9,8},{10,11... | collective-permute-start | bytes 2359304 | tf_op jit(solution)/shard_map/ppermute | solution.py:562
  95.3 7.6 %collective-permute-start.14 = (bf16[2,768,256]{2,1,0:T(8,128)(2,1)S(1)}, bf16[2,768,256]{2,1,0:T(8,128)(2,1)S(1)}, u32[]{:S(2)}, u32[]{:S(2)}) collective-permute-start(bf16[2,768,256]{2,1,0:T(8,128)(2,1)S(1)} %get-tuple-element.181), channel_id=1, source_target_pairs={{0,1},{1,0},{2,3},{3,2},{4,5},{5,4},{6,7},{7,6},{8,9},{9,8},{10,11... | collective-permute-start | bytes 2359304 | tf_op jit(solution)/shard_map/ppermute | solution.py:562
  100.2 11.9 %collective-permute-start.22 = (bf16[4,192,256]{2,1,0:T(8,128)(2,1)S(1)}, bf16[4,192,256]{2,1,0:T(8,128)(2,1)S(1)}, u32[]{:S(2)}, u32[]{:S(2)}) collective-permute-start(bf16[4,192,256]{2,1,0:T(8,128)(2,1)S(1)} %get-tuple-element.199), channel_id=1, source_target_pairs={{0,4},{4,0},{8,12},{12,8},{16,20},{20,16},{24,28},{28,24},{1,5},{5... | collective-permute-start | bytes 1179656 | tf_op jit(solution)/shard_map/ppermute | solution.py:562
  100.7 1.3 collective-permute-start.15
  102.1 15.5 %collective-permute-start.23 = (bf16[4,192,256]{2,1,0:T(8,128)(2,1)}, bf16[4,192,256]{2,1,0:T(8,128)(2,1)}, u32[]{:S(2)}, u32[]{:S(2)}) collective-permute-start(bf16[4,192,256]{2,1,0:T(8,128)(2,1)} %get-tuple-element.201), channel_id=1, source_target_pairs={{0,8},{4,12},{8,0},{12,4},{16,24},{20,28},{24,16},{28,20},{1,9},{5... | collective-permute-start | bytes 1179656 | tf_op jit(solution)/shard_map/ppermute | solution.py:562
  102.6 15.0 %collective-permute-start.24 = (bf16[4,192,256]{2,1,0:T(8,128)(2,1)}, bf16[4,192,256]{2,1,0:T(8,128)(2,1)}, u32[]{:S(2)}, u32[]{:S(2)}) collective-permute-start(bf16[4,192,256]{2,1,0:T(8,128)(2,1)} %get-tuple-element.203), channel_id=1, source_target_pairs={{0,2},{1,3},{2,0},{3,1},{4,6},{5,7},{6,4},{7,5},{8,10},{9,11},{10,... | collective-permute-start | bytes 1179656 | tf_op jit(solution)/shard_map/ppermute | solution.py:562
  104.7 20.6 %collective-permute-start.28 = (bf16[8,112,256]{2,1,0:T(8,128)(2,1)}, bf16[8,112,256]{2,1,0:T(8,128)(2,1)}, u32[]{:S(2)}, u32[]{:S(2)}) collective-permute-start(bf16[8,112,256]{2,1,0:T(8,128)(2,1)} %get-tuple-element.213), channel_id=1, source_target_pairs={{0,2},{1,3},{2,0},{3,1},{4,6},{5,7},{6,4},{7,5},{8,10},{9,11},{10,... | collective-permute-start | bytes 1376264 | tf_op jit(solution)/shard_map/ppermute | solution.py:562
  106.3 14.9 %collective-permute-start.29 = (bf16[8,96,256]{2,1,0:T(8,128)(2,1)}, bf16[8,96,256]{2,1,0:T(8,128)(2,1)}, u32[]{:S(2)}, u32[]{:S(2)}) collective-permute-start(bf16[8,96,256]{2,1,0:T(8,128)(2,1)} %get-tuple-element.215), channel_id=1, source_target_pairs={{0,4},{4,0},{8,12},{12,8},{16,20},{20,16},{24,28},{28,24},{1,5},{5... | collective-permute-start | bytes 1179656 | tf_op jit(solution)/shard_map/ppermute | solution.py:562
  112.9 12.4 %collective-permute-start.30 = (bf16[8,96,256]{2,1,0:T(8,128)(2,1)}, bf16[8,96,256]{2,1,0:T(8,128)(2,1)}, u32[]{:S(2)}, u32[]{:S(2)}) collective-permute-start(bf16[8,96,256]{2,1,0:T(8,128)(2,1)} %get-tuple-element.217), channel_id=1, source_target_pairs={{0,8},{4,12},{8,0},{12,4},{16,24},{20,28},{24,16},{28,20},{1,9},{5... | collective-permute-start | bytes 1179656 | tf_op jit(solution)/shard_map/ppermute | solution.py:562
  119.1 10.2 %collective-permute-start.25 = (bf16[2,192,256]{2,1,0:T(8,128)(2,1)S(1)}, bf16[2,192,256]{2,1,0:T(8,128)(2,1)S(1)}, u32[]{:S(2)}, u32[]{:S(2)}) collective-permute-start(bf16[2,192,256]{2,1,0:T(8,128)(2,1)S(1)} %get-tuple-element.207), channel_id=1, source_target_pairs={{0,8},{4,12},{8,0},{12,4},{16,24},{20,28},{24,16},{28,20},{1,9},{5... | collective-permute-start | bytes 589832 | tf_op jit(solution)/shard_map/ppermute | solution.py:562
  120.7 9.1 %collective-permute-start.26 = (bf16[2,192,256]{2,1,0:T(8,128)(2,1)S(1)}, bf16[2,192,256]{2,1,0:T(8,128)(2,1)S(1)}, u32[]{:S(2)}, u32[]{:S(2)}) collective-permute-start(bf16[2,192,256]{2,1,0:T(8,128)(2,1)S(1)} %get-tuple-element.209), channel_id=1, source_target_pairs={{0,2},{1,3},{2,0},{3,1},{4,6},{5,7},{6,4},{7,5},{8,10},{9,11},{10,... | collective-permute-start | bytes 589832 | tf_op jit(solution)/shard_map/ppermute | solution.py:562
  121.3 8.6 %collective-permute-start.27 = (bf16[2,192,256]{2,1,0:T(8,128)(2,1)S(1)}, bf16[2,192,256]{2,1,0:T(8,128)(2,1)S(1)}, u32[]{:S(2)}, u32[]{:S(2)}) collective-permute-start(bf16[2,192,256]{2,1,0:T(8,128)(2,1)S(1)} %get-tuple-element.211), channel_id=1, source_target_pairs={{0,4},{4,0},{8,12},{12,8},{16,20},{20,16},{24,28},{28,24},{1,5},{5... | collective-permute-start | bytes 589832 | tf_op jit(solution)/shard_map/ppermute | solution.py:562
  126.7 8.6 %collective-permute-start.32 = (bf16[4,112,256]{2,1,0:T(8,128)(2,1)S(1)}, bf16[4,112,256]{2,1,0:T(8,128)(2,1)S(1)}, u32[]{:S(2)}, u32[]{:S(2)}) collective-permute-start(bf16[4,112,256]{2,1,0:T(8,128)(2,1)S(1)} %get-tuple-element.223), channel_id=1, source_target_pairs={{0,4},{4,0},{8,12},{12,8},{16,20},{20,16},{24,28},{28,24},{1,5},{5... | collective-permute-start | bytes 688136 | tf_op jit(solution)/shard_map/ppermute | solution.py:562
  127.7 7.6 %collective-permute-start.33 = (bf16[4,96,256]{2,1,0:T(8,128)(2,1)S(1)}, bf16[4,96,256]{2,1,0:T(8,128)(2,1)S(1)}, u32[]{:S(2)}, u32[]{:S(2)}) collective-permute-start(bf16[4,96,256]{2,1,0:T(8,128)(2,1)S(1)} %get-tuple-element.225), channel_id=1, source_target_pairs={{0,8},{4,12},{8,0},{12,4},{16,24},{20,28},{24,16},{28,20},{1,9},{5... | collective-permute-start | bytes 589832 | tf_op jit(solution)/shard_map/ppermute | solution.py:562
  129.3 6.0 %collective-permute-start.34 = (bf16[4,96,256]{2,1,0:T(8,128)(2,1)S(1)}, bf16[4,96,256]{2,1,0:T(8,128)(2,1)S(1)}, u32[]{:S(2)}, u32[]{:S(2)}) collective-permute-start(bf16[4,96,256]{2,1,0:T(8,128)(2,1)S(1)} %get-tuple-element.227), channel_id=1, source_target_pairs={{0,2},{1,3},{2,0},{3,1},{4,6},{5,7},{6,4},{7,5},{8,10},{9,11},{10,... | collective-permute-start | bytes 589832 | tf_op jit(solution)/shard_map/ppermute | solution.py:562
  130.5 13.3 %collective-permute-start.31 = (bf16[1,576,256]{2,1,0:T(8,128)(2,1)S(1)}, bf16[1,576,256]{2,1,0:T(8,128)(2,1)S(1)}, u32[]{:S(2)}, u32[]{:S(2)}) collective-permute-start(bf16[1,576,256]{2,1,0:T(8,128)(2,1)S(1)} %get-tuple-element.221), channel_id=1, source_target_pairs={{0,16},{4,20},{8,24},{12,28},{16,0},{20,4},{24,8},{28,12},{1,17},{... | collective-permute-start | bytes 884744 | tf_op jit(solution)/shard_map/ppermute | solution.py:562
  135.3 39.6 %copy-start.1 = (s32[4,8]{1,0:T(4,128)S(1)}, s32[4,8]{1,0:T(4,128)}, u32[]{:S(2)}) copy-start(s32[4,8]{1,0:T(4,128)} %param.16) | copy-start | bytes 388
  136.0 6.4 %collective-permute-start.35 = (bf16[2,112,256]{2,1,0:T(8,128)(2,1)S(1)}, bf16[2,112,256]{2,1,0:T(8,128)(2,1)S(1)}, u32[]{:S(2)}, u32[]{:S(2)}) collective-permute-start(bf16[2,112,256]{2,1,0:T(8,128)(2,1)S(1)} %get-tuple-element.230), channel_id=1, source_target_pairs={{0,8},{4,12},{8,0},{12,4},{16,24},{20,28},{24,16},{28,20},{1,9},{5... | collective-permute-start | bytes 344072 | tf_op jit(solution)/shard_map/ppermute | solution.py:562
  137.8 4.6 %collective-permute-start.36 = (bf16[2,96,256]{2,1,0:T(8,128)(2,1)S(1)}, bf16[2,96,256]{2,1,0:T(8,128)(2,1)S(1)}, u32[]{:S(2)}, u32[]{:S(2)}) collective-permute-start(bf16[2,96,256]{2,1,0:T(8,128)(2,1)S(1)} %get-tuple-element.232), channel_id=1, source_target_pairs={{0,2},{1,3},{2,0},{3,1},{4,6},{5,7},{6,4},{7,5},{8,10},{9,11},{10,... | collective-permute-start | bytes 294920 | tf_op jit(solution)/shard_map/ppermute | solution.py:562
  137.8 4.6 %collective-permute-start.37 = (bf16[2,96,256]{2,1,0:T(8,128)(2,1)S(1)}, bf16[2,96,256]{2,1,0:T(8,128)(2,1)S(1)}, u32[]{:S(2)}, u32[]{:S(2)}) collective-permute-start(bf16[2,96,256]{2,1,0:T(8,128)(2,1)S(1)} %get-tuple-element.234), channel_id=1, source_target_pairs={{0,4},{4,0},{8,12},{12,8},{16,20},{20,16},{24,28},{28,24},{1,5},{5... | collective-permute-start | bytes 294920 | tf_op jit(solution)/shard_map/ppermute | solution.py:562
  144.3 19.7 %collective-permute-start.43 = (bf16[1,576,256]{2,1,0:T(8,128)(2,1)S(1)}, bf16[1,576,256]{2,1,0:T(8,128)(2,1)S(1)}, u32[]{:S(2)}, u32[]{:S(2)}) collective-permute-start(bf16[1,576,256]{2,1,0:T(8,128)(2,1)S(1)} %get-tuple-element.249.refs_1_), channel_id=1, source_target_pairs={{0,2},{1,3},{2,0},{3,1},{4,6},{5,7},{6,4},{7,5},{8,10},{9,11},{10,... | collective-permute-start | bytes 884744 | tf_op jit(solution)/shard_map/ppermute | solution.py:562
  145.9 5.0 %collective-permute-start.19 = (bf16[128,768]{1,0:T(8,128)(2,1)S(1)}, bf16[128,768]{1,0:T(8,128)(2,1)S(1)}, u32[]{:S(2)}, u32[]{:S(2)}) collective-permute-start(bf16[128,768]{1,0:T(8,128)(2,1)S(1)} %get-tuple-element.195), channel_id=1, source_target_pairs={{0,1},{1,0},{2,3},{3,2},{4,5},{5,4},{6,7},{7,6},{8,9},{9,8},{10,11... | collective-permute-start | bytes 589832 | tf_op jit(solution)/shard_map/ppermute | solution.py:562
  145.9 12.2 %collective-permute-start.20 = (bf16[128,768]{1,0:T(8,128)(2,1)S(1)}, bf16[128,768]{1,0:T(8,128)(2,1)S(1)}, u32[]{:S(2)}, u32[]{:S(2)}) collective-permute-start(bf16[128,768]{1,0:T(8,128)(2,1)S(1)} %get-tuple-element.196), channel_id=1, source_target_pairs={{0,2},{1,3},{2,0},{3,1},{4,6},{5,7},{6,4},{7,5},{8,10},{9,11},{10,... | collective-permute-start | bytes 589832 | tf_op jit(solution)/shard_map/ppermute | solution.py:562
  146.4 13.0 %collective-permute-start.21 = (bf16[128,768]{1,0:T(8,128)(2,1)S(1)}, bf16[128,768]{1,0:T(8,128)(2,1)S(1)}, u32[]{:S(2)}, u32[]{:S(2)}) collective-permute-start(bf16[128,768]{1,0:T(8,128)(2,1)S(1)} %get-tuple-element.197), channel_id=1, source_target_pairs={{0,3},{1,2},{2,1},{3,0},{4,7},{5,6},{6,5},{7,4},{8,11},{9,10},{10,... | collective-permute-start | bytes 589832 | tf_op jit(solution)/shard_map/ppermute | solution.py:562
  147.7 13.2 %collective-permute-start.38 = (bf16[1,304,256]{2,1,0:T(8,128)(2,1)S(1)}, bf16[1,304,256]{2,1,0:T(8,128)(2,1)S(1)}, u32[]{:S(2)}, u32[]{:S(2)}) collective-permute-start(bf16[1,304,256]{2,1,0:T(8,128)(2,1)S(1)} %get-tuple-element.240), channel_id=1, source_target_pairs={{0,16},{4,20},{8,24},{12,28},{16,0},{20,4},{24,8},{28,12},{1,17},{... | collective-permute-start | bytes 466952 | tf_op jit(solution)/shard_map/ppermute | solution.py:562
  162.0 6.5 %collective-permute-start.40 = (bf16[1,304,256]{2,1,0:T(8,128)(2,1)S(1)}, bf16[1,304,256]{2,1,0:T(8,128)(2,1)S(1)}, u32[]{:S(2)}, u32[]{:S(2)}) collective-permute-start(bf16[1,304,256]{2,1,0:T(8,128)(2,1)S(1)} %get-tuple-element.242.refs_1_), channel_id=1, source_target_pairs={{0,2},{1,3},{2,0},{3,1},{4,6},{5,7},{6,4},{7,5},{8,10},{9,11},{10,... | collective-permute-start | bytes 466952 | tf_op jit(solution)/shard_map/ppermute | solution.py:562
  162.4 9.8 %collective-permute-start.42 = (bf16[1,576,256]{2,1,0:T(8,128)(2,1)S(1)}, bf16[1,576,256]{2,1,0:T(8,128)(2,1)S(1)}, u32[]{:S(2)}, u32[]{:S(2)}) collective-permute-start(bf16[1,576,256]{2,1,0:T(8,128)(2,1)S(1)} %get-tuple-element.249.refs_1_), channel_id=1, source_target_pairs={{0,1},{1,0},{2,3},{3,2},{4,5},{5,4},{6,7},{7,6},{8,9},{9,8},{10,11... | collective-permute-start | bytes 884744 | tf_op jit(solution)/shard_map/ppermute | solution.py:562
  164.1 8.1 %collective-permute-start.44 = (bf16[1,576,256]{2,1,0:T(8,128)(2,1)S(1)}, bf16[1,576,256]{2,1,0:T(8,128)(2,1)S(1)}, u32[]{:S(2)}, u32[]{:S(2)}) collective-permute-start(bf16[1,576,256]{2,1,0:T(8,128)(2,1)S(1)} %collective-permute-done.43.refs_3_), channel_id=1, source_target_pairs={{0,1},{1,0},{2,3},{3,2},{4,5},{5,4},{6,7},{7,6},{8,9},{9,8},{10,11... | collective-permute-start | bytes 884744 | tf_op jit(solution)/shard_map/ppermute | solution.py:562
  164.1 4.5 %collective-permute-start.39 = (bf16[1,304,256]{2,1,0:T(8,128)(2,1)S(1)}, bf16[1,304,256]{2,1,0:T(8,128)(2,1)S(1)}, u32[]{:S(2)}, u32[]{:S(2)}) collective-permute-start(bf16[1,304,256]{2,1,0:T(8,128)(2,1)S(1)} %get-tuple-element.242.refs_1_), channel_id=1, source_target_pairs={{0,1},{1,0},{2,3},{3,2},{4,5},{5,4},{6,7},{7,6},{8,9},{9,8},{10,11... | collective-permute-start | bytes 466952 | tf_op jit(solution)/shard_map/ppermute | solution.py:562
  168.5 1.4 collective-permute-start.41
  (13 other events, 67.7 us)

commit v4 on v3

--- a/solution.py
+++ b/solution.py
@@ -23,8 +23,9 @@
 
 
 WEIGHTS = {
-    "prepare": 10**12, "attend": 10**12, "feed": 10**12, "grad_up": 10**12,
-    "grad_down": 10**12, "attend_back": 10**12, "grad_tokens": 10**12,
+    "prepare": 60 * 10**9, "attend": 60 * 10**9, "feed": 60 * 10**9, "grad_up": 60 * 10**9,
+    "grad_down": 60 * 10**9, "attend_back": 60 * 10**9, "grad_tokens": 60 * 10**9,
+    "halve": 5 * 10**9, "cut_units": 5 * 10**9, "place_feed": 5 * 10**9,
 }
 
 
@@ -106,11 +107,20 @@
     return jnp.concatenate(parts)
 
 
-def prepare_kernel(row_ref, w_qkv, w_out, qkv_near, out_near, mask, sems, *, pages, slots):
+def prepare_kernel(
+    row_ref, b0, b1, b2, b3, b4, b5, b6, b7, w_qkv, w_out, qkv_near, out_near, mask, vectors, sems,
+    *, pages, slots,
+):
     load_qkv = copy(w_qkv, qkv_near, sems.at[0])
     load_qkv.start()
     load_out = copy(w_out, out_near, sems.at[1])
     load_out.start()
+    width = vectors.shape[1]
+    row = 0
+    for part in (b0, b1, b2, b3, b4, b5, b6, b7):
+        for i in range(part.shape[0] // width):
+            vectors[row : row + 1, :] = part[i * width : (i + 1) * width].reshape(1, width)
+            row += 1
     count = mask.shape[0]
     position = row_ref[pages]
 
@@ -131,13 +141,18 @@
     load_out.wait()
 
 
-def prepare(row, w_qkv, w_out, slots, count):
+def prepare(row, biases, w_qkv, w_out, slots, count):
+    width = w_out.shape[0]
+    rows = sum(b.shape[0] for b in biases) // width
     return call(
         functools.partial(prepare_kernel, pages=row.shape[0] - 1, slots=slots),
-        "prepare", [row], [],
-        [shape(*w_qkv.shape), shape(*w_out.shape), shape(count, count, dtype=f32)],
+        "prepare", [row], biases,
+        [
+            shape(*w_qkv.shape), shape(*w_out.shape), shape(count, count, dtype=f32),
+            shape(rows, width, dtype=f32),
+        ],
         far=[w_qkv, w_out], copies=2,
-    )[:3]
+    )[:4]
 
 
 def attend_kernel(
@@ -221,12 +236,10 @@
 def feed_kernel(
     place, normed_one, vectors, c0, c1, c2, c3, w_up, w_down,
     keep_active, send_active, slope_out, lowered_out, first_out, r0, r1, r2, r3, vector_out,
-    sum_out, normed_far, total, sems, *, shares,
+    sum_out, total, *, shares,
 ):
     width = w_up.shape[0]
     hidden = w_up.shape[1]
-    keep_normed = copy(normed_one, normed_far, sems.at[0])
-    keep_normed.start()
     first_norm = normed_one[...] * vector(vectors, GAIN_ONE) + vector(vectors, SHIFT_ONE)
     first_out[...] = first_norm.astype(bf16)
     total[...] = first_norm + vector(vectors, BIAS_DOWN)
@@ -264,16 +277,12 @@
         block[...] = result[i * slots : (i + 1) * slots, :]
     upstream = jnp.concatenate([c0[...], c1[...], c2[...], c3[...]]).astype(f32)
     grad_sum = normalize_back(upstream * gain, normed, inverse)
-    total[...] = grad_sum
-    keep_sum = copy(total, sum_out, sems.at[1])
-    keep_sum.start()
+    sum_out[...] = grad_sum
     lowered = grad_sum.astype(bf16)
     lowered_out[...] = lowered
     vector_out[0:1, :] = column_sum(upstream * normed)
     vector_out[1:2, :] = column_sum(upstream)
     vector_out[2:3, :] = column_sum(lowered.astype(f32))
-    keep_sum.wait()
-    keep_normed.wait()
 
 
 def feed(place, normed, vectors, cotangents, w_up, w_down, shares):
@@ -295,8 +304,8 @@
     made = call(
         kernel, "feed", [place], [normed, vectors, *cotangents, w_up, w_down],
         active + [shape(count, hidden), narrow, narrow]
-        + [shape(*cotangents[0].shape)] * 4 + [shape(8, width, dtype=f32)],
-        [pltpu.VMEM((count, width), f32)], far_outs=[full, full], copies=2, room=14,
+        + [shape(*cotangents[0].shape)] * 4 + [shape(8, width, dtype=f32), full],
+        [pltpu.VMEM((count, width), f32)], room=14,
     )[:-1]
     if apart:
         return made
@@ -308,14 +317,12 @@
 
 
 def grad_up_kernel(
-    place, lowered, slope, first, w_down, inverse_one, vectors, w_up, sum_two, normed_one,
-    keep, send, bias_out, attended_out, vector_out, sum_out,
-    turned, raised_kept, weights, normed, total, sems,
+    place, lowered, slope, first, w_down, inverse_one, vectors, sum_two, normed, w_up,
+    keep, send, bias_out, attended_out, vector_out, sum_out, turned, raised_kept, weights, sems,
 ):
     width = lowered.shape[1]
-    loads = (copy(w_up, weights, sems.at[0]), copy(sum_two, total, sems.at[1]), copy(normed_one, normed, sems.at[2]))
-    for one in loads:
-        one.start()
+    load = copy(w_up, weights, sems.at[0])
+    load.start()
     turned[...] = first[...].T
 
     def work(b):
@@ -331,41 +338,47 @@
         send[x] = work(2 * x + 1 - place[0])
         keep[x] = work(2 * x + place[0])
 
-    for one in loads:
-        one.wait()
-    upstream = total[...] + dot(raised_kept[...], weights[...], NT)
+    load.wait()
+    upstream = sum_two[...] + dot(raised_kept[...], weights[...], NT)
     grad_sum = normalize_back(
         upstream * vector(vectors, GAIN_ONE), normed[...], inverse_one[...]
     )
-    total[...] = grad_sum
-    keep_sum = copy(total, sum_out, sems.at[3])
-    keep_sum.start()
+    sum_out[...] = grad_sum
     attended = grad_sum.astype(bf16)
     attended_out[...] = attended
     vector_out[0:1, :] = column_sum(upstream * normed[...])
     vector_out[1:2, :] = column_sum(upstream)
     vector_out[2:3, :] = column_sum(attended.astype(f32))
-    keep_sum.wait()
 
 
 def grad_up(place, lowered, slope, first, w_down, inverse, vectors, w_up, sum_two, normed):
     count, width = lowered.shape
     hidden = w_down.shape[0]
-    full = pltpu.VMEM((count, width), f32)
     return call(
-        grad_up_kernel, "grad_up", [place], [lowered, slope, first, w_down, inverse, vectors],
+        grad_up_kernel, "grad_up", [place],
+        [lowered, slope, first, w_down, inverse, vectors, sum_two, normed],
         [shape(2, width, width)] * 2
         + [shape(hidden // width, width, dtype=f32), shape(count, width)]
-        + [shape(8, width, dtype=f32)],
+        + [shape(8, width, dtype=f32), shape(count, width, dtype=f32)],
         [
             pltpu.VMEM((width, count), bf16), pltpu.VMEM((count, hidden), bf16),
-            pltpu.VMEM((width, hidden), bf16), full, full,
+            pltpu.VMEM((width, hidden), bf16),
         ],
-        far=[w_up, sum_two, normed], far_outs=[shape(count, width, dtype=f32)], copies=4, room=28,
-    )
-
-
-def grad_down_kernel(active, other_active, lowered, other_lowered, down):
+        far=[w_up], copies=1, room=28,
+    )
+
+
+def place_rows(place, blocks, rows, sems):
+    copies = [copy(block, rows.at[place[1] ^ i], sems.at[i]) for i, block in enumerate(blocks)]
+    for one in copies:
+        one.start()
+    return copies
+
+
+def grad_down_kernel(
+    place, active, other_active, lowered, other_lowered, r0, r1, r2, r3, down, rows_out, sems
+):
+    copies = place_rows(place, (r0, r1, r2, r3), rows_out, sems)
     _, shares, rows, count = active.shape
     width = lowered.shape[1]
 
@@ -378,12 +391,17 @@
             value = dot(mine, lowered[...]) + dot(other, other_lowered[...])
             down[x, pl.ds(d, 2)] = value.astype(bf16).reshape(2, rows, width)
 
-
-def grad_down(active, other_active, lowered, other_lowered, after):
+    for one in copies:
+        one.wait()
+
+
+def grad_down(place, active, other_active, lowered, other_lowered, blocks, after):
     _, shares, rows, _ = active.shape
+    slots, width = blocks[0].shape
     return call(
-        grad_down_kernel, "grad_down", [], [active, other_active, lowered, other_lowered],
-        [shape(2, shares, rows, lowered.shape[1])], after=after,
+        grad_down_kernel, "grad_down", [place],
+        [active, other_active, lowered, other_lowered, *blocks],
+        [shape(2, shares, rows, width)], far_outs=[shape(4, slots, width)], copies=4, after=after,
     )
 
 
@@ -538,12 +556,8 @@
     return [keep_0, keep_1, keep_2], [send_0, send_1, send_2], small_keep, small_send, grads, mark
 
 
-def grad_tokens_kernel(grads, w_qkv, sum_one, r0, r1, r2, r3, total, sems):
-    load = copy(sum_one, total, sems.at[0])
-    load.start()
-    product = dot(grads[...], w_qkv[...], NT)
-    load.wait()
-    result = (total[...] + product).astype(bf16)
+def grad_tokens_kernel(grads, w_qkv, sum_one, r0, r1, r2, r3):
+    result = (sum_one[...] + dot(grads[...], w_qkv[...], NT)).astype(bf16)
     slots = r0.shape[0]
     for i, block in enumerate((r0, r1, r2, r3)):
         block[...] = result[i * slots : (i + 1) * slots, :]
@@ -552,8 +566,8 @@
 def grad_tokens(sum_one, grads, w_qkv, slots, after):
     count, width = sum_one.shape
     *blocks, mark = call(
-        grad_tokens_kernel, "grad_tokens", [], [grads, w_qkv], [shape(slots, width)] * 4,
-        [pltpu.VMEM((count, width), f32)], far=[sum_one], copies=1, room=12, after=after,
+        grad_tokens_kernel, "grad_tokens", [], [grads, w_qkv, sum_one], [shape(slots, width)] * 4,
+        room=12, after=after,
     )
     return blocks, mark
 
@@ -691,11 +705,12 @@
     ).astype(f32)
 
 
-def place_feed(place, pieces, rows, shares):
+def place_feed(place, pieces, rows, blocks, after):
     size = pieces[0].shape[2]
     width = 3 * size
 
-    def kernel(place_ref, p0, p1, p2, p3, down, up):
+    def kernel(place_ref, p0, p1, p2, p3, r0, r1, r2, r3, down, up, rows_out, sems):
+        copies = place_rows(place_ref, (r0, r1, r2, r3), rows_out, sems)
         for b in range(4):
             for s in range(3):
                 at = 2 * s * rows
@@ -706,14 +721,17 @@
                 columns = slice(b * width + s * size, b * width + (s + 1) * size)
                 value = chosen(place_ref, b, [p.at[0, at : at + rows] for p in (p0, p1, p2, p3)])
                 up[:, columns] = value
+        for one in copies:
+            one.wait()
 
     return call(
-        kernel, "place_feed", [place], pieces,
+        kernel, "place_feed", [place], [*pieces, *blocks],
         [shape(4 * rows, width, dtype=f32), shape(rows, 4 * width, dtype=f32)],
-    )[:2]
-
-
-def place_own(place, pieces, rows, shares):
+        far_outs=[shape(4, *blocks[0].shape)], copies=4, after=after,
+    )
+
+
+def place_own(place, pieces, rows, shares, after):
     size = pieces[0].shape[2]
     width = 3 * size
     share = width // shares
@@ -745,17 +763,8 @@
     return call(
         kernel, "place_own", [place], pieces,
         [shape(rows, 3 * width, dtype=f32), shape(rows, width, dtype=f32), *vectors],
+        after=after,
     )[:10]
-
-
-def place_rows(place, blocks, after):
-    slots, width = blocks[0].shape
-
-    def kernel(place_ref, *refs):
-        for i in range(4):
-            refs[4][place_ref[1] ^ i] = refs[i][...]
-
-    return call(kernel, "place_rows", [place], blocks, [shape(4, slots, width)], after=after)
 
 
 def shards(
@@ -779,23 +788,24 @@
     def in_order(blocks):
         return [blocks[0], blocks[3], blocks[1], blocks[2]]
 
-    def scatter_row(blocks, after=()):
-        moved = [blocks[0]] + [swap(blocks[i], "blk", i) for i in range(1, rows)]
-        return place_rows(place, moved, after)
-
-    vectors = jnp.concatenate(
-        [bias_qv, bias_out, norm1_gain, norm1_bias, bias_down, norm2_gain, norm2_bias, bias_up]
-    ).reshape(-1, width)
+    def scatter_row(blocks):
+        return [blocks[0]] + [swap(blocks[i], "blk", i) for i in range(1, rows)]
+
+    biases = [
+        bias_qv, bias_out, norm1_gain, norm1_bias, bias_down, norm2_gain, norm2_bias, bias_up
+    ]
     row = jnp.concatenate([pick(lengths, position), position[None]])
     blocks = gather_row(tokens)
     blocks, cotangent = lax.optimization_barrier((blocks, cotangent))
     blocks = in_order(blocks)
     cotangents = in_order(gather_row(cotangent))
-    qkv_near, out_near, mask = prepare(row, w_qkv, w_out, slots, rows * slots)
+    qkv_near, out_near, mask, vectors = prepare(
+        row, biases, w_qkv, w_out, slots, rows * slots
+    )
     normed, inverse, q, k, v, prob, context, row_tokens = attend(
         blocks, vectors, qkv_near, out_near, mask
     )
-    keep_active, send_active, slope, lowered, first, o0, o1, o2, o3, vector_two, sum_two, normed = feed(
+    keep_active, send_active, slope, lowered, first, o0, o1, o2, o3, vector_two, sum_two = feed(
         place, normed, vectors, cotangents, w_up, w_down, shares
     )
     got_active, got_lowered = swap(send_active, "blk", 1), swap(lowered, "blk", 1)
@@ -803,8 +813,9 @@
         place, lowered, slope, first, w_down, inverse, vectors, w_up, sum_two, normed
     )
     got_up = swap(send_up, "blk", 1)
-    outputs, mark = scatter_row([o0, o1, o2, o3], [mark])
-    down, mark = grad_down(keep_active, got_active, lowered, got_lowered, [mark])
+    down, outputs, mark = grad_down(
+        place, keep_active, got_active, lowered, got_lowered, scatter_row([o0, o1, o2, o3]), [mark]
+    )
 
     def chunks(array):
         return array.reshape((2,) * (1 + dp_bits) + (-1, array.shape[-1]))
@@ -833,17 +844,17 @@
     for _ in range(dp_bits - 1):
         mark = feed_group.step([mark])
         mark = own_group.step([mark])
+    share = width // shares
+    feed_pieces, mark = feed_group.finish([mark])
     mark = own_group.step([mark])
-    feed_pieces, mark = feed_group.finish([mark])
-    token_grads, mark = scatter_row(tokens_parts, [mark])
     own_pieces, mark = own_group.finish([mark])
-
-    share = width // shares
-    down, up = place_feed(place, feed_pieces, share, shares)
+    down, up, token_grads, mark = place_feed(
+        place, feed_pieces, share, scatter_row(tokens_parts), [mark]
+    )
     (
         grad_w_qkv, grad_w_out, sum_qv, sum_out, sum_gain_one, sum_shift_one, sum_up, sum_down,
         sum_gain_two, sum_shift_two,
-    ) = place_own(place, own_pieces, share, shares)
+    ) = place_own(place, own_pieces, share, shares, [mark])
     return (
         outputs,
         token_grads,

time: 176 us -> 151 us (0.86)
  Pallas kernels: 94.1 us -> 71.8 us
  waiting for transfers between devices: 29.7 us -> 35.2 us
  starting transfers between devices: 39 us -> 34.2 us
  local copies, waits for them, and re-layouts: 10.2 us -> 6.92 us
    pallas_call x23 -> x21, Pallas kernels: 94.1 us -> 71.8 us  [call(): pl.pallas_call(body, in_specs=[SMEM] * len(scalars) + [VMEM] * len(arrays...]
    ppermute x45, waiting for transfers between devices: 29.7 us -> 35.2 us  [swap(): lax.ppermute(block, axis, [(i, i ^ bit) for i in range(lax.axis_size(axis...]
    ppermute x45, starting transfers between devices: 39 us -> 34.2 us  [swap(): lax.ppermute(block, axis, [(i, i ^ bit) for i in range(lax.axis_size(axis...]
    unnamed x39 -> x32, local copies, waits for them, and re-layouts: 6.52 us -> 5.57 us
  transfers between devices with their start and end apart: 45 -> 45, of which waited for: 10 -> 13; matrix products, arithmetic and copies ran while one was open for 4% -> 0% of each run, Pallas kernels for 42% -> 39%
where the time goes in v4:
time: 151 us; the launch traced here: 150 us
  Pallas kernels  71.8 us (48%)
  waiting for transfers between devices  35.2 us (23%)
  starting transfers between devices  34.2 us (23%)
  local copies, waits for them, and re-layouts  6.92 us (5%)
    pallas_call x21, Pallas kernels, call(): pl.pallas_call(body, in_specs=[SMEM] * len(scalars) + [VMEM] * len(arrays...  71.8 us
    ppermute x45, waiting for transfers between devices, swap(): lax.ppermute(block, axis, [(i, i ^ bit) for i in range(lax.axis_size(axis...  35.2 us
    ppermute x45, starting transfers between devices, swap(): lax.ppermute(block, axis, [(i, i ^ bit) for i in range(lax.axis_size(axis...  34.2 us
    unnamed x32, local copies, waits for them, and re-layouts  5.57 us
  transfers between devices with their start and end apart: 45, of which 13 were waited for; matrix products, arithmetic and copies ran while one was open for 0% of the time, Pallas kernels for 39%

profile of v4, /device:TPU:0, one launch (start us, length us, event | category | flops | bytes accessed | tf_op | source)
XLA Modules:
  0.0 150.0 jit_solution(11443991566738355698)
XLA Ops:
  0.7 1.3 dynamic-slice_bitcast_fusion.4
  2.0 3.0 %collective-permute-start = (bf16[128,768]{1,0:T(8,128)(2,1)S(1)}, bf16[128,768]{1,0:T(8,128)(2,1)S(1)}, u32[]{:S(2)}, u32[]{:S(2)}) collective-permute-start(bf16[128,768]{1,0:T(8,128)(2,1)S(1)} %get-tuple-element.261), channel_id=1, source_target_pairs={{0,2},{1,3},{2,0},{3,1},{4,6},{5,7},{6,4},{7,5},{8,10},{9,11},{10,... | collective-permute-start | bytes 589832 | tf_op jit(solution)/shard_map/ppermute | solution.py:576
  5.3 0.7 copy-done.3
  6.0 0.7 copy-done.4
  6.7 0.7 copy-done.5
  7.3 0.7 copy-done.6
  8.0 0.7 copy-done.7
  8.7 0.7 copy-done.8
  9.4 0.7 copy-done.9
  10.1 0.7 copy-done.10
  10.8 3.7 %prepare.1 = (bf16[768,2304]{1,0:T(8,128)(2,1)S(1)}, bf16[768,768]{1,0:T(8,128)(2,1)S(1)}, f32[512,512]{1,0:T(8,128)S(1)}, f32[12,768]{1,0:T(8,128)S(1)}, f32[8,128]{1,0:T(8,128)}) custom-call(s32[9]{0:T(128)S(1)} %pad_add_fusion.1.refs_0_, f32[1536]{0:T(1024)S(1)} %copy-done.4, f32[768]{0:T(1024)S(1)} %copy-done.5, f32[768]{0:T(1024)S(1)} %copy-done.6, ...), custom_call_target="tpu_custom_call" | custom-call | flops 60000002048 | tf_op jit(solution)/shard_map/prepare/pallas_call | solution.py:51
  15.2 1.7 %collective-permute-start.4 = (bf16[128,768]{1,0:T(8,128)(2,1)S(1)}, bf16[128,768]{1,0:T(8,128)(2,1)S(1)}, u32[]{:S(2)}, u32[]{:S(2)}) collective-permute-start(bf16[128,768]{1,0:T(8,128)(2,1)S(1)} %get-tuple-element.257), channel_id=1, source_target_pairs={{0,2},{1,3},{2,0},{3,1},{4,6},{5,7},{6,4},{7,5},{8,10},{9,11},{10,... | collective-permute-start | bytes 589832 | tf_op jit(solution)/shard_map/ppermute | solution.py:576
  17.0 11.2 %attend.1 = (f32[512,768]{1,0:T(8,128)S(1)}, f32[512,1]{1,0:T(8,128)S(1)}, bf16[512,768]{1,0:T(8,128)(2,1)}, bf16[512,768]{1,0:T(8,128)(2,1)}, bf16[512,768]{1,0...) custom-call(bf16[128,768]{1,0:T(8,128)(2,1)S(1)} %get-tuple-element., ...), custom_call_target="tpu_custom_call" | custom-call | flops 60000002048 | tf_op jit(solution)/shard_map/attend/pallas_call | solution.py:51
  28.2 10.4 %feed.1 = (bf16[2,8,96,512]{3,2,1,0:T(8,128)(2,1)S(1)}, bf16[2,8,96,512]{3,2,1,0:T(8,128)(2,1)S(1)}, bf16[512,3072]{1,0:T(8,128)(2,1)S(1)}, bf16[512,768]{1,0:T(...) custom-call(s32[2]{0:T(128)S(1)} %pad_add_fusion.refs_0_, ...), custom_call_target="tpu_custom_call" | custom-call | flops 60000002048 | tf_op jit(solution)/shard_map/feed/pallas_call | solution.py:51
  39.2 1.7 %collective-permute-start.10 = (bf16[128,768]{1,0:T(8,128)(2,1)S(1)}, bf16[128,768]{1,0:T(8,128)(2,1)S(1)}, u32[]{:S(2)}, u32[]{:S(2)}) collective-permute-start(bf16[128,768]{1,0:T(8,128)(2,1)S(1)} %get-tuple-element.151), channel_id=1, source_target_pairs={{0,3},{1,2},{2,1},{3,0},{4,7},{5,6},{6,5},{7,4},{8,11},{9,10},{10,... | collective-permute-start | bytes 589832 | tf_op jit(solution)/shard_map/ppermute | solution.py:576
  41.3 9.8 %grad_up.1 = (bf16[2,768,768]{2,1,0:T(8,128)(2,1)S(1)}, bf16[2,768,768]{2,1,0:T(8,128)(2,1)S(1)}, f32[4,768]{1,0:T(4,128)S(1)}, bf16[512,768]{1,0:T(8,128)(2,1)S...) custom-call(s32[2]{0:T(128)S(1)} %pad_add_fusion.refs_0_, ...), custom_call_target="tpu_custom_call" | custom-call | flops 60000002048 | tf_op jit(solution)/shard_map/grad_up/pallas_call | solution.py:51
  51.3 4.4 %grad_down.1 = (bf16[2,8,96,768]{3,2,1,0:T(8,128)(2,1)S(1)}, bf16[4,128,768]{2,1,0:T(8,128)(2,1)}, f32[8,128]{1,0:T(8,128)S(1)}) custom-call(s32[2]{0:T(128)S(1)} %pad_add_fusion.refs_0_, bf16[2,8,96,512]{3,2,1,0:T(8,128)(2,1)S(1)} %get-tuple-element.145.refs_1_, bf16[2,8,96,512]{3,2,1,0:T(8,128)(2,1)S(1)} %collective-permute-done.6.refs_2_, ...), custom_call_target="tpu_custom_call" | custom-call | flops 60000002048 | tf_op jit(solution)/shard_map/grad_down/pallas_call | solution.py:51
  55.7 0.7 cut_units.4
  56.5 1.8 %collective-permute-start.12 = (bf16[8,192,256]{2,1,0:T(8,128)(2,1)S(1)}, bf16[8,192,256]{2,1,0:T(8,128)(2,1)S(1)}, u32[]{:S(2)}, u32[]{:S(2)}) collective-permute-start(bf16[8,192,256]{2,1,0:T(8,128)(2,1)S(1)} %get-tuple-element.175), channel_id=1, source_target_pairs={{0,2},{1,3},{2,0},{3,1},{4,6},{5,7},{6,4},{7,5},{8,10},{9,11},{10,... | collective-permute-start | bytes 2359304 | tf_op jit(solution)/shard_map/ppermute | solution.py:576
  58.3 1.5 %collective-permute-start.13 = (bf16[8,192,256]{2,1,0:T(8,128)(2,1)S(1)}, bf16[8,192,256]{2,1,0:T(8,128)(2,1)S(1)}, u32[]{:S(2)}, u32[]{:S(2)}) collective-permute-start(bf16[8,192,256]{2,1,0:T(8,128)(2,1)S(1)} %get-tuple-element.177), channel_id=1, source_target_pairs={{0,4},{4,0},{8,12},{12,8},{16,20},{20,16},{24,28},{28,24},{1,5},{5... | collective-permute-start | bytes 2359304 | tf_op jit(solution)/shard_map/ppermute | solution.py:576
  59.8 1.6 %collective-permute-start.14 = (bf16[8,192,256]{2,1,0:T(8,128)(2,1)S(1)}, bf16[8,192,256]{2,1,0:T(8,128)(2,1)S(1)}, u32[]{:S(2)}, u32[]{:S(2)}) collective-permute-start(bf16[8,192,256]{2,1,0:T(8,128)(2,1)S(1)} %get-tuple-element.179), channel_id=1, source_target_pairs={{0,8},{4,12},{8,0},{12,4},{16,24},{20,28},{24,16},{28,20},{1,9},{5... | collective-permute-start | bytes 2359304 | tf_op jit(solution)/shard_map/ppermute | solution.py:576
  61.4 17.7 %attend_back.1 = (bf16[512,2304]{1,0:T(8,128)(2,1)S(1)}, bf16[2,768,256]{2,1,0:T(8,128)(2,1)S(1)}, bf16[2,768,256]{2,1,0:T(8,128)(2,1)S(1)}, bf16[2,768,256]{2,1...) custom-call(s32[2]{0:T(128)S(1)} %pad_add_fusion.refs_0_, ...), custom_call_target="tpu_custom_call" | custom-call | flops 60000002048 | tf_op jit(solution)/shard_map/attend_back/pallas_call | solution.py:51
  79.7 0.7 cut_units.5
  80.9 0.8 halve.8
  82.3 1.5 %collective-permute-done.21 = bf16[2,8,16,256]{3,2,1,0:T(8,128)(2,1)S(1)} collective-permute-done((bf16[2,8,16,256]{3,2,1,0:T(8,128)(2,1)S(1)}, bf16[2,8,16,256]{3,2,1,0:T(8,128)(2,1)S(1)}, u32[]{:S(2)}, u32[]{:S(2)}) %collective-permute-start.21) | collective-permute-done | bytes 131104 | tf_op jit(solution)/shard_map/ppermute | solution.py:576
  84.8 0.7 cut_units.6
  85.6 1.5 %collective-permute-start.25 = (bf16[8,112,256]{2,1,0:T(8,128)(2,1)S(1)}, bf16[8,112,256]{2,1,0:T(8,128)(2,1)S(1)}, u32[]{:S(2)}, u32[]{:S(2)}) collective-permute-start(bf16[8,112,256]{2,1,0:T(8,128)(2,1)S(1)} %get-tuple-element.208), channel_id=1, source_target_pairs={{0,2},{1,3},{2,0},{3,1},{4,6},{5,7},{6,4},{7,5},{8,10},{9,11},{10,... | collective-permute-start | bytes 1376264 | tf_op jit(solution)/shard_map/ppermute | solution.py:576
  87.6 2.0 %grad_tokens.1 = (bf16[128,768]{1,0:T(8,128)(2,1)S(1)}, bf16[128,768]{1,0:T(8,128)(2,1)S(1)}, bf16[128,768]{1,0:T(8,128)(2,1)S(1)}, bf16[128,768]{1,0:T(8,128)(2,1)S(1)}, f32[8,128]{1,0:T(8,128)S(1)}) custom-call(bf16[512,2304]{1,0:T(8,128)(2,1)S(1)} %get-tuple-element.195.refs_0_, bf16[768,2304]{1,0:T(8,128)(2,1)S(1)} %copy-done.2, ...), custom_call_target="tpu_custom_call" | custom-call | flops 60000002048 | tf_op jit(solution)/shard_map/grad_tokens/pallas_call | solution.py:51
  89.7 0.7 cut_units.7
  90.4 3.4 %collective-permute-done.15.refs_2_ = bf16[4,192,256]{2,1,0:T(8,128)(2,1)S(1)} collective-permute-done((bf16[4,192,256]{2,1,0:T(8,128)(2,1)S(1)}, bf16[4,192,256]{2,1,0:T(8,128)(2,1)S(1)}, u32[]{:S(2)}, u32[]{:S(2)}) %collective-permute-start.15) | collective-permute-done | bytes 393248 | tf_op jit(solution)/shard_map/ppermute | solution.py:576
  94.2 0.9 collective-permute-done.16.refs_4_
  95.2 1.1 collective-permute-done.17.refs_6_
  96.3 0.7 halve.9
  97.0 1.7 %collective-permute-start.22 = (bf16[2,192,256]{2,1,0:T(8,128)(2,1)S(1)}, bf16[2,192,256]{2,1,0:T(8,128)(2,1)S(1)}, u32[]{:S(2)}, u32[]{:S(2)}) collective-permute-start(bf16[2,192,256]{2,1,0:T(8,128)(2,1)S(1)} %get-tuple-element.202), channel_id=1, source_target_pairs={{0,8},{4,12},{8,0},{12,4},{16,24},{20,28},{24,16},{28,20},{1,9},{5... | collective-permute-start | bytes 589832 | tf_op jit(solution)/shard_map/ppermute | solution.py:576
  99.1 2.2 %collective-permute-done.26.refs_4_ = bf16[8,96,256]{2,1,0:T(8,128)(2,1)S(1)} collective-permute-done((bf16[8,96,256]{2,1,0:T(8,128)(2,1)S(1)}, bf16[8,96,256]{2,1,0:T(8,128)(2,1)S(1)}, u32[]{:S(2)}, u32[]{:S(2)}) %collective-permute-start.26) | collective-permute-done | bytes 393248 | tf_op jit(solution)/shard_map/ppermute | solution.py:576
  101.8 3.7 %collective-permute-done.27.refs_6_ = bf16[8,96,256]{2,1,0:T(8,128)(2,1)S(1)} collective-permute-done((bf16[8,96,256]{2,1,0:T(8,128)(2,1)S(1)}, bf16[8,96,256]{2,1,0:T(8,128)(2,1)S(1)}, u32[]{:S(2)}, u32[]{:S(2)}) %collective-permute-start.27) | collective-permute-done | bytes 393248 | tf_op jit(solution)/shard_map/ppermute | solution.py:576
  107.4 1.6 %collective-permute-start.30 = (bf16[4,96,256]{2,1,0:T(8,128)(2,1)S(1)}, bf16[4,96,256]{2,1,0:T(8,128)(2,1)S(1)}, u32[]{:S(2)}, u32[]{:S(2)}) collective-permute-start(bf16[4,96,256]{2,1,0:T(8,128)(2,1)S(1)} %get-tuple-element.220), channel_id=1, source_target_pairs={{0,8},{4,12},{8,0},{12,4},{16,24},{20,28},{24,16},{28,20},{1,9},{5... | collective-permute-start | bytes 589832 | tf_op jit(solution)/shard_map/ppermute | solution.py:576
  110.1 2.7 %collective-permute-start.28 = (bf16[1,576,256]{2,1,0:T(8,128)(2,1)S(1)}, bf16[1,576,256]{2,1,0:T(8,128)(2,1)S(1)}, u32[]{:S(2)}, u32[]{:S(2)}) collective-permute-start(bf16[1,576,256]{2,1,0:T(8,128)(2,1)S(1)} %get-tuple-element.216), channel_id=1, source_target_pairs={{0,16},{4,20},{8,24},{12,28},{16,0},{20,4},{24,8},{28,12},{1,17},{... | collective-permute-start | bytes 884744 | tf_op jit(solution)/shard_map/ppermute | solution.py:576
  112.8 1.8 %collective-permute-done.30.refs_4_ = bf16[4,96,256]{2,1,0:T(8,128)(2,1)S(1)} collective-permute-done((bf16[4,96,256]{2,1,0:T(8,128)(2,1)S(1)}, bf16[4,96,256]{2,1,0:T(8,128)(2,1)S(1)}, u32[]{:S(2)}, u32[]{:S(2)}) %collective-permute-start.30) | collective-permute-done | bytes 196640 | tf_op jit(solution)/shard_map/ppermute | solution.py:576
  116.4 2.2 %collective-permute-start.40 = (bf16[2,96,256]{2,1,0:T(8,128)(2,1)S(1)}, bf16[2,96,256]{2,1,0:T(8,128)(2,1)S(1)}, u32[]{:S(2)}, u32[]{:S(2)}) collective-permute-start(bf16[2,96,256]{2,1,0:T(8,128)(2,1)S(1)} %get-tuple-element.235), channel_id=1, source_target_pairs={{0,4},{4,0},{8,12},{12,8},{16,20},{20,16},{24,28},{28,24},{1,5},{5... | collective-permute-start | bytes 294920 | tf_op jit(solution)/shard_map/ppermute | solution.py:576
  118.6 6.4 %collective-permute-done.28.refs_2_ = bf16[1,576,256]{2,1,0:T(8,128)(2,1)S(1)} collective-permute-done((bf16[1,576,256]{2,1,0:T(8,128)(2,1)S(1)}, bf16[1,576,256]{2,1,0:T(8,128)(2,1)S(1)}, u32[]{:S(2)}, u32[]{:S(2)}) %collective-permute-start.28) | collective-permute-done | bytes 294944 | tf_op jit(solution)/shard_map/ppermute | solution.py:576
  127.0 1.6 %collective-permute-start.36 = (bf16[128,768]{1,0:T(8,128)(2,1)S(1)}, bf16[128,768]{1,0:T(8,128)(2,1)S(1)}, u32[]{:S(2)}, u32[]{:S(2)}) collective-permute-start(bf16[128,768]{1,0:T(8,128)(2,1)S(1)} %get-tuple-element.228), channel_id=1, source_target_pairs={{0,2},{1,3},{2,0},{3,1},{4,6},{5,7},{6,4},{7,5},{8,10},{9,11},{10,... | collective-permute-start | bytes 589832 | tf_op jit(solution)/shard_map/ppermute | solution.py:576
  128.9 6.7 %collective-permute-done.41.refs_2_ = bf16[1,304,256]{2,1,0:T(8,128)(2,1)S(1)} collective-permute-done((bf16[1,304,256]{2,1,0:T(8,128)(2,1)S(1)}, bf16[1,304,256]{2,1,0:T(8,128)(2,1)S(1)}, u32[]{:S(2)}, u32[]{:S(2)}) %collective-permute-start.41) | collective-permute-done | bytes 155680 | tf_op jit(solution)/shard_map/ppermute | solution.py:576
  136.6 1.6 %collective-permute-start.43 = (bf16[1,304,256]{2,1,0:T(8,128)(2,1)S(1)}, bf16[1,304,256]{2,1,0:T(8,128)(2,1)S(1)}, u32[]{:S(2)}, u32[]{:S(2)}) collective-permute-start(bf16[1,304,256]{2,1,0:T(8,128)(2,1)S(1)} %get-tuple-element.242.refs_1_), channel_id=1, source_target_pairs={{0,2},{1,3},{2,0},{3,1},{4,6},{5,7},{6,4},{7,5},{8,10},{9,11},{10,... | collective-permute-start | bytes 466952 | tf_op jit(solution)/shard_map/ppermute | solution.py:576
  138.1 1.3 collective-permute-done.36.refs_7_
  139.4 5.4 %collective-permute-done.43.refs_3_ = bf16[1,304,256]{2,1,0:T(8,128)(2,1)S(1)} collective-permute-done((bf16[1,304,256]{2,1,0:T(8,128)(2,1)S(1)}, bf16[1,304,256]{2,1,0:T(8,128)(2,1)S(1)}, u32[]{:S(2)}, u32[]{:S(2)}) %collective-permute-start.43) | collective-permute-done | bytes 155680 | tf_op jit(solution)/shard_map/ppermute | solution.py:576
  144.9 2.9 %place_feed.1 = (f32[384,768]{1,0:T(8,128)}, f32[96,3072]{1,0:T(8,128)}, bf16[4,128,768]{2,1,0:T(8,128)(2,1)}, f32[8,128]{1,0:T(8,128)S(1)}) custom-call(s32[2]{0:T(128)S(1)} %pad_add_fusion.refs_0_, bf16[1,576,256]{2,1,0:T(8,128)(2,1)S(1)} %get-tuple-element.225.refs_1_, bf16[1,576,256]{2,1,0:T(8,128)(2,1)S(1)} %collective-permute-done.32.refs_2_, ...), custom_call_target="tpu_custom_call" | custom-call | flops 5000000000 | tf_op jit(solution)/shard_map/place_feed/pallas_call | solution.py:51
  147.8 1.7 %place_own.1 = (f32[96,2304]{1,0:T(8,128)}, f32[96,768]{1,0:T(8,128)}, f32[1,192]{1,0:T(1,128)}, f32[1,96]{1,0:T(1,128)}, f32[1,96]{1,0:T(1,128)}, /*index=5*/f3...) custom-call(s32[2]{0:T(128)S(1)} %pad_add_fusion.refs_0_, ...), custom_call_target="tpu_custom_call" | custom-call | tf_op jit(solution)/shard_map/place_own/pallas_call | solution.py:51
  (104 shorter events, 15.6 us)
Async XLA Ops:
  2.0 12.7 %collective-permute-start = (bf16[128,768]{1,0:T(8,128)(2,1)S(1)}, bf16[128,768]{1,0:T(8,128)(2,1)S(1)}, u32[]{:S(2)}, u32[]{:S(2)}) collective-permute-start(bf16[128,768]{1,0:T(8,128)(2,1)S(1)} %get-tuple-element.261), channel_id=1, source_target_pairs={{0,2},{1,3},{2,0},{3,1},{4,6},{5,7},{6,4},{7,5},{8,10},{9,11},{10,... | collective-permute-start | bytes 589832 | tf_op jit(solution)/shard_map/ppermute | solution.py:576
  5.0 9.7 %collective-permute-start.1 = (bf16[128,768]{1,0:T(8,128)(2,1)S(1)}, bf16[128,768]{1,0:T(8,128)(2,1)S(1)}, u32[]{:S(2)}, u32[]{:S(2)}) collective-permute-start(bf16[128,768]{1,0:T(8,128)(2,1)S(1)} %get-tuple-element.263), channel_id=1, source_target_pairs={{0,3},{1,2},{2,1},{3,0},{4,7},{5,6},{6,5},{7,4},{8,11},{9,10},{10,... | collective-permute-start | bytes 589832 | tf_op jit(solution)/shard_map/ppermute | solution.py:576
  5.0 9.7 %collective-permute-start.2 = (bf16[128,768]{1,0:T(8,128)(2,1)S(1)}, bf16[128,768]{1,0:T(8,128)(2,1)S(1)}, u32[]{:S(2)}, u32[]{:S(2)}) collective-permute-start(bf16[128,768]{1,0:T(8,128)(2,1)S(1)} %get-tuple-element.260), channel_id=1, source_target_pairs={{0,1},{1,0},{2,3},{3,2},{4,5},{5,4},{6,7},{7,6},{8,9},{9,8},{10,11... | collective-permute-start | bytes 589832 | tf_op jit(solution)/shard_map/ppermute | solution.py:576
  10.8 17.4 %slice-start = ((s8[4718592]{0:T(1024)(128)(4,1)}), s8[4194304]{0:T(1024)(128)(4,1)S(1)}, s32[]{:S(2)}) async-start(s8[4718592]{0:T(1024)(128)(4,1)} %bitcast.42), calls=%async_computation | async-start | bytes 8388608
  10.8 17.4 %slice-start.2 = ((s8[4718592]{0:T(1024)(128)(4,1)}), s8[4194304]{0:T(1024)(128)(4,1)S(1)}, s32[]{:S(2)}) async-start(s8[4718592]{0:T(1024)(128)(4,1)} %bitcast.44), calls=%async_computation.2 | async-start | bytes 8388608
  14.7 13.5 %slice-start.1 = ((s8[4718592]{0:T(1024)(128)(4,1)}), s8[524288]{0:T(1024)(128)(4,1)S(1)}, s32[]{:S(2)}) async-start(s8[4718592]{0:T(1024)(128)(4,1)} %bitcast.42), calls=%async_computation.1 | async-start | bytes 1048576
  14.8 13.3 %collective-permute-start.3 = (bf16[128,768]{1,0:T(8,128)(2,1)S(1)}, bf16[128,768]{1,0:T(8,128)(2,1)S(1)}, u32[]{:S(2)}, u32[]{:S(2)}) collective-permute-start(bf16[128,768]{1,0:T(8,128)(2,1)S(1)} %get-tuple-element.258), channel_id=1, source_target_pairs={{0,1},{1,0},{2,3},{3,2},{4,5},{5,4},{6,7},{7,6},{8,9},{9,8},{10,11... | collective-permute-start | bytes 589832 | tf_op jit(solution)/shard_map/ppermute | solution.py:576
  15.2 12.9 %collective-permute-start.4 = (bf16[128,768]{1,0:T(8,128)(2,1)S(1)}, bf16[128,768]{1,0:T(8,128)(2,1)S(1)}, u32[]{:S(2)}, u32[]{:S(2)}) collective-permute-start(bf16[128,768]{1,0:T(8,128)(2,1)S(1)} %get-tuple-element.257), channel_id=1, source_target_pairs={{0,2},{1,3},{2,0},{3,1},{4,6},{5,7},{6,4},{7,5},{8,10},{9,11},{10,... | collective-permute-start | bytes 589832 | tf_op jit(solution)/shard_map/ppermute | solution.py:576
  16.9 11.3 %collective-permute-start.5 = (bf16[128,768]{1,0:T(8,128)(2,1)S(1)}, bf16[128,768]{1,0:T(8,128)(2,1)S(1)}, u32[]{:S(2)}, u32[]{:S(2)}) collective-permute-start(bf16[128,768]{1,0:T(8,128)(2,1)S(1)} %get-tuple-element.256), channel_id=1, source_target_pairs={{0,3},{1,2},{2,1},{3,0},{4,7},{5,6},{6,5},{7,4},{8,11},{9,10},{10,... | collective-permute-start | bytes 589832 | tf_op jit(solution)/shard_map/ppermute | solution.py:576
  38.6 12.6 %collective-permute-start.6 = (bf16[2,8,96,512]{3,2,1,0:T(8,128)(2,1)S(1)}, bf16[2,8,96,512]{3,2,1,0:T(8,128)(2,1)S(1)}, u32[]{:S(2)}, u32[]{:S(2)}) collective-permute-start(bf16[2,8,96,512]{3,2,1,0:T(8,128)(2,1)S(1)} %get-tuple-element.146), channel_id=1, source_target_pairs={{0,1},{1,0},{2,3},{3,2},{4,5},{5,4},{6,7},{7,6},{8,9},{9,8},{10,11... | collective-permute-start | bytes 4718600 | tf_op jit(solution)/shard_map/ppermute | solution.py:576
  39.0 12.3 %collective-permute-start.7 = (bf16[512,768]{1,0:T(8,128)(2,1)S(1)}, bf16[512,768]{1,0:T(8,128)(2,1)S(1)}, u32[]{:S(2)}, u32[]{:S(2)}) collective-permute-start(bf16[512,768]{1,0:T(8,128)(2,1)S(1)} %get-tuple-element.147.refs_1_.refs_3_), channel_id=1, source_target_pairs={{0,1},{1,0},{2,3},{3,2},{4,5},{5,4},{6,7},{7,6},{8,9},{9,8},{10,11... | collective-permute-start | bytes 2359304 | tf_op jit(solution)/shard_map/ppermute | solution.py:576
  39.2 12.0 %collective-permute-start.10 = (bf16[128,768]{1,0:T(8,128)(2,1)S(1)}, bf16[128,768]{1,0:T(8,128)(2,1)S(1)}, u32[]{:S(2)}, u32[]{:S(2)}) collective-permute-start(bf16[128,768]{1,0:T(8,128)(2,1)S(1)} %get-tuple-element.151), channel_id=1, source_target_pairs={{0,3},{1,2},{2,1},{3,0},{4,7},{5,6},{6,5},{7,4},{8,11},{9,10},{10,... | collective-permute-start | bytes 589832 | tf_op jit(solution)/shard_map/ppermute | solution.py:576
  40.8 10.4 %collective-permute-start.8 = (bf16[128,768]{1,0:T(8,128)(2,1)S(1)}, bf16[128,768]{1,0:T(8,128)(2,1)S(1)}, u32[]{:S(2)}, u32[]{:S(2)}) collective-permute-start(bf16[128,768]{1,0:T(8,128)(2,1)S(1)} %get-tuple-element.149), channel_id=1, source_target_pairs={{0,1},{1,0},{2,3},{3,2},{4,5},{5,4},{6,7},{7,6},{8,9},{9,8},{10,11... | collective-permute-start | bytes 589832 | tf_op jit(solution)/shard_map/ppermute | solution.py:576
  41.0 10.3 %collective-permute-start.9 = (bf16[128,768]{1,0:T(8,128)(2,1)S(1)}, bf16[128,768]{1,0:T(8,128)(2,1)S(1)}, u32[]{:S(2)}, u32[]{:S(2)}) collective-permute-start(bf16[128,768]{1,0:T(8,128)(2,1)S(1)} %get-tuple-element.150), channel_id=1, source_target_pairs={{0,2},{1,3},{2,0},{3,1},{4,6},{5,7},{6,4},{7,5},{8,10},{9,11},{10,... | collective-permute-start | bytes 589832 | tf_op jit(solution)/shard_map/ppermute | solution.py:576
  51.1 4.6 %collective-permute-start.11 = (bf16[2,768,768]{2,1,0:T(8,128)(2,1)S(1)}, bf16[2,768,768]{2,1,0:T(8,128)(2,1)S(1)}, u32[]{:S(2)}, u32[]{:S(2)}) collective-permute-start(bf16[2,768,768]{2,1,0:T(8,128)(2,1)S(1)} %get-tuple-element.160), channel_id=1, source_target_pairs={{0,1},{1,0},{2,3},{3,2},{4,5},{5,4},{6,7},{7,6},{8,9},{9,8},{10,11... | collective-permute-start | bytes 7077896 | tf_op jit(solution)/shard_map/ppermute | solution.py:576
  56.5 23.1 %collective-permute-start.12 = (bf16[8,192,256]{2,1,0:T(8,128)(2,1)S(1)}, bf16[8,192,256]{2,1,0:T(8,128)(2,1)S(1)}, u32[]{:S(2)}, u32[]{:S(2)}) collective-permute-start(bf16[8,192,256]{2,1,0:T(8,128)(2,1)S(1)} %get-tuple-element.175), channel_id=1, source_target_pairs={{0,2},{1,3},{2,0},{3,1},{4,6},{5,7},{6,4},{7,5},{8,10},{9,11},{10,... | collective-permute-start | bytes 2359304 | tf_op jit(solution)/shard_map/ppermute | solution.py:576
  58.3 22.2 %collective-permute-start.13 = (bf16[8,192,256]{2,1,0:T(8,128)(2,1)S(1)}, bf16[8,192,256]{2,1,0:T(8,128)(2,1)S(1)}, u32[]{:S(2)}, u32[]{:S(2)}) collective-permute-start(bf16[8,192,256]{2,1,0:T(8,128)(2,1)S(1)} %get-tuple-element.177), channel_id=1, source_target_pairs={{0,4},{4,0},{8,12},{12,8},{16,20},{20,16},{24,28},{28,24},{1,5},{5... | collective-permute-start | bytes 2359304 | tf_op jit(solution)/shard_map/ppermute | solution.py:576
  59.8 21.2 %collective-permute-start.14 = (bf16[8,192,256]{2,1,0:T(8,128)(2,1)S(1)}, bf16[8,192,256]{2,1,0:T(8,128)(2,1)S(1)}, u32[]{:S(2)}, u32[]{:S(2)}) collective-permute-start(bf16[8,192,256]{2,1,0:T(8,128)(2,1)S(1)} %get-tuple-element.179), channel_id=1, source_target_pairs={{0,8},{4,12},{8,0},{12,4},{16,24},{20,28},{24,16},{28,20},{1,9},{5... | collective-permute-start | bytes 2359304 | tf_op jit(solution)/shard_map/ppermute | solution.py:576
  79.0 5.2 %collective-permute-start.18 = (bf16[2,768,256]{2,1,0:T(8,128)(2,1)S(1)}, bf16[2,768,256]{2,1,0:T(8,128)(2,1)S(1)}, u32[]{:S(2)}, u32[]{:S(2)}) collective-permute-start(bf16[2,768,256]{2,1,0:T(8,128)(2,1)S(1)} %get-tuple-element.188), channel_id=1, source_target_pairs={{0,1},{1,0},{2,3},{3,2},{4,5},{5,4},{6,7},{7,6},{8,9},{9,8},{10,11... | collective-permute-start | bytes 2359304 | tf_op jit(solution)/shard_map/ppermute | solution.py:576
  79.1 5.7 %collective-permute-start.19 = (bf16[2,768,256]{2,1,0:T(8,128)(2,1)S(1)}, bf16[2,768,256]{2,1,0:T(8,128)(2,1)S(1)}, u32[]{:S(2)}, u32[]{:S(2)}) collective-permute-start(bf16[2,768,256]{2,1,0:T(8,128)(2,1)S(1)} %get-tuple-element.190), channel_id=1, source_target_pairs={{0,1},{1,0},{2,3},{3,2},{4,5},{5,4},{6,7},{7,6},{8,9},{9,8},{10,11... | collective-permute-start | bytes 2359304 | tf_op jit(solution)/shard_map/ppermute | solution.py:576
  79.6 5.2 %collective-permute-start.20 = (bf16[2,768,256]{2,1,0:T(8,128)(2,1)S(1)}, bf16[2,768,256]{2,1,0:T(8,128)(2,1)S(1)}, u32[]{:S(2)}, u32[]{:S(2)}) collective-permute-start(bf16[2,768,256]{2,1,0:T(8,128)(2,1)S(1)} %get-tuple-element.192), channel_id=1, source_target_pairs={{0,1},{1,0},{2,3},{3,2},{4,5},{5,4},{6,7},{7,6},{8,9},{9,8},{10,11... | collective-permute-start | bytes 2359304 | tf_op jit(solution)/shard_map/ppermute | solution.py:576
  80.4 3.4 %collective-permute-start.21 = (bf16[2,8,16,256]{3,2,1,0:T(8,128)(2,1)S(1)}, bf16[2,8,16,256]{3,2,1,0:T(8,128)(2,1)S(1)}, u32[]{:S(2)}, u32[]{:S(2)}) collective-permute-start(bf16[2,8,16,256]{3,2,1,0:T(8,128)(2,1)S(1)} %get-tuple-element.194), channel_id=1, source_target_pairs={{0,1},{1,0},{2,3},{3,2},{4,5},{5,4},{6,7},{7,6},{8,9},{9,8},{10,11... | collective-permute-start | bytes 393224 | tf_op jit(solution)/shard_map/ppermute | solution.py:576
  81.7 12.0 %collective-permute-start.15 = (bf16[4,192,256]{2,1,0:T(8,128)(2,1)S(1)}, bf16[4,192,256]{2,1,0:T(8,128)(2,1)S(1)}, u32[]{:S(2)}, u32[]{:S(2)}) collective-permute-start(bf16[4,192,256]{2,1,0:T(8,128)(2,1)S(1)} %get-tuple-element.182), channel_id=1, source_target_pairs={{0,4},{4,0},{8,12},{12,8},{16,20},{20,16},{24,28},{28,24},{1,5},{5... | collective-permute-start | bytes 1179656 | tf_op jit(solution)/shard_map/ppermute | solution.py:576
  83.8 11.3 %collective-permute-start.16 = (bf16[4,192,256]{2,1,0:T(8,128)(2,1)S(1)}, bf16[4,192,256]{2,1,0:T(8,128)(2,1)S(1)}, u32[]{:S(2)}, u32[]{:S(2)}) collective-permute-start(bf16[4,192,256]{2,1,0:T(8,128)(2,1)S(1)} %get-tuple-element.184), channel_id=1, source_target_pairs={{0,8},{4,12},{8,0},{12,4},{16,24},{20,28},{24,16},{28,20},{1,9},{5... | collective-permute-start | bytes 1179656 | tf_op jit(solution)/shard_map/ppermute | solution.py:576
  84.3 12.0 %collective-permute-start.17 = (bf16[4,192,256]{2,1,0:T(8,128)(2,1)S(1)}, bf16[4,192,256]{2,1,0:T(8,128)(2,1)S(1)}, u32[]{:S(2)}, u32[]{:S(2)}) collective-permute-start(bf16[4,192,256]{2,1,0:T(8,128)(2,1)S(1)} %get-tuple-element.186), channel_id=1, source_target_pairs={{0,2},{1,3},{2,0},{3,1},{4,6},{5,7},{6,4},{7,5},{8,10},{9,11},{10,... | collective-permute-start | bytes 1179656 | tf_op jit(solution)/shard_map/ppermute | solution.py:576
  85.6 20.5 %collective-permute-start.25 = (bf16[8,112,256]{2,1,0:T(8,128)(2,1)S(1)}, bf16[8,112,256]{2,1,0:T(8,128)(2,1)S(1)}, u32[]{:S(2)}, u32[]{:S(2)}) collective-permute-start(bf16[8,112,256]{2,1,0:T(8,128)(2,1)S(1)} %get-tuple-element.208), channel_id=1, source_target_pairs={{0,2},{1,3},{2,0},{3,1},{4,6},{5,7},{6,4},{7,5},{8,10},{9,11},{10,... | collective-permute-start | bytes 1376264 | tf_op jit(solution)/shard_map/ppermute | solution.py:576
  87.1 14.2 %collective-permute-start.26 = (bf16[8,96,256]{2,1,0:T(8,128)(2,1)S(1)}, bf16[8,96,256]{2,1,0:T(8,128)(2,1)S(1)}, u32[]{:S(2)}, u32[]{:S(2)}) collective-permute-start(bf16[8,96,256]{2,1,0:T(8,128)(2,1)S(1)} %get-tuple-element.210), channel_id=1, source_target_pairs={{0,4},{4,0},{8,12},{12,8},{16,20},{20,16},{24,28},{28,24},{1,5},{5... | collective-permute-start | bytes 1179656 | tf_op jit(solution)/shard_map/ppermute | solution.py:576
  93.8 11.7 %collective-permute-start.27 = (bf16[8,96,256]{2,1,0:T(8,128)(2,1)S(1)}, bf16[8,96,256]{2,1,0:T(8,128)(2,1)S(1)}, u32[]{:S(2)}, u32[]{:S(2)}) collective-permute-start(bf16[8,96,256]{2,1,0:T(8,128)(2,1)S(1)} %get-tuple-element.212), channel_id=1, source_target_pairs={{0,8},{4,12},{8,0},{12,4},{16,24},{20,28},{24,16},{28,20},{1,9},{5... | collective-permute-start | bytes 1179656 | tf_op jit(solution)/shard_map/ppermute | solution.py:576
  97.0 12.0 %collective-permute-start.22 = (bf16[2,192,256]{2,1,0:T(8,128)(2,1)S(1)}, bf16[2,192,256]{2,1,0:T(8,128)(2,1)S(1)}, u32[]{:S(2)}, u32[]{:S(2)}) collective-permute-start(bf16[2,192,256]{2,1,0:T(8,128)(2,1)S(1)} %get-tuple-element.202), channel_id=1, source_target_pairs={{0,8},{4,12},{8,0},{12,4},{16,24},{20,28},{24,16},{28,20},{1,9},{5... | collective-permute-start | bytes 589832 | tf_op jit(solution)/shard_map/ppermute | solution.py:576
  98.6 10.9 %collective-permute-start.23 = (bf16[2,192,256]{2,1,0:T(8,128)(2,1)S(1)}, bf16[2,192,256]{2,1,0:T(8,128)(2,1)S(1)}, u32[]{:S(2)}, u32[]{:S(2)}) collective-permute-start(bf16[2,192,256]{2,1,0:T(8,128)(2,1)S(1)} %get-tuple-element.204), channel_id=1, source_target_pairs={{0,2},{1,3},{2,0},{3,1},{4,6},{5,7},{6,4},{7,5},{8,10},{9,11},{10,... | collective-permute-start | bytes 589832 | tf_op jit(solution)/shard_map/ppermute | solution.py:576
  101.3 8.2 %collective-permute-start.24 = (bf16[2,192,256]{2,1,0:T(8,128)(2,1)S(1)}, bf16[2,192,256]{2,1,0:T(8,128)(2,1)S(1)}, u32[]{:S(2)}, u32[]{:S(2)}) collective-permute-start(bf16[2,192,256]{2,1,0:T(8,128)(2,1)S(1)} %get-tuple-element.206), channel_id=1, source_target_pairs={{0,4},{4,0},{8,12},{12,8},{16,20},{20,16},{24,28},{28,24},{1,5},{5... | collective-permute-start | bytes 589832 | tf_op jit(solution)/shard_map/ppermute | solution.py:576
  106.8 7.8 %collective-permute-start.29 = (bf16[4,112,256]{2,1,0:T(8,128)(2,1)S(1)}, bf16[4,112,256]{2,1,0:T(8,128)(2,1)S(1)}, u32[]{:S(2)}, u32[]{:S(2)}) collective-permute-start(bf16[4,112,256]{2,1,0:T(8,128)(2,1)S(1)} %get-tuple-element.218), channel_id=1, source_target_pairs={{0,4},{4,0},{8,12},{12,8},{16,20},{20,16},{24,28},{28,24},{1,5},{5... | collective-permute-start | bytes 688136 | tf_op jit(solution)/shard_map/ppermute | solution.py:576
  107.4 7.2 %collective-permute-start.30 = (bf16[4,96,256]{2,1,0:T(8,128)(2,1)S(1)}, bf16[4,96,256]{2,1,0:T(8,128)(2,1)S(1)}, u32[]{:S(2)}, u32[]{:S(2)}) collective-permute-start(bf16[4,96,256]{2,1,0:T(8,128)(2,1)S(1)} %get-tuple-element.220), channel_id=1, source_target_pairs={{0,8},{4,12},{8,0},{12,4},{16,24},{20,28},{24,16},{28,20},{1,9},{5... | collective-permute-start | bytes 589832 | tf_op jit(solution)/shard_map/ppermute | solution.py:576
  108.9 5.7 %collective-permute-start.31 = (bf16[4,96,256]{2,1,0:T(8,128)(2,1)S(1)}, bf16[4,96,256]{2,1,0:T(8,128)(2,1)S(1)}, u32[]{:S(2)}, u32[]{:S(2)}) collective-permute-start(bf16[4,96,256]{2,1,0:T(8,128)(2,1)S(1)} %get-tuple-element.222), channel_id=1, source_target_pairs={{0,2},{1,3},{2,0},{3,1},{4,6},{5,7},{6,4},{7,5},{8,10},{9,11},{10,... | collective-permute-start | bytes 589832 | tf_op jit(solution)/shard_map/ppermute | solution.py:576
  110.1 14.9 %collective-permute-start.28 = (bf16[1,576,256]{2,1,0:T(8,128)(2,1)S(1)}, bf16[1,576,256]{2,1,0:T(8,128)(2,1)S(1)}, u32[]{:S(2)}, u32[]{:S(2)}) collective-permute-start(bf16[1,576,256]{2,1,0:T(8,128)(2,1)S(1)} %get-tuple-element.216), channel_id=1, source_target_pairs={{0,16},{4,20},{8,24},{12,28},{16,0},{20,4},{24,8},{28,12},{1,17},{... | collective-permute-start | bytes 884744 | tf_op jit(solution)/shard_map/ppermute | solution.py:576
  115.2 11.0 %collective-permute-start.38 = (bf16[2,112,256]{2,1,0:T(8,128)(2,1)S(1)}, bf16[2,112,256]{2,1,0:T(8,128)(2,1)S(1)}, u32[]{:S(2)}, u32[]{:S(2)}) collective-permute-start(bf16[2,112,256]{2,1,0:T(8,128)(2,1)S(1)} %get-tuple-element.231), channel_id=1, source_target_pairs={{0,8},{4,12},{8,0},{12,4},{16,24},{20,28},{24,16},{28,20},{1,9},{5... | collective-permute-start | bytes 344072 | tf_op jit(solution)/shard_map/ppermute | solution.py:576
  115.9 10.4 %collective-permute-start.39 = (bf16[2,96,256]{2,1,0:T(8,128)(2,1)S(1)}, bf16[2,96,256]{2,1,0:T(8,128)(2,1)S(1)}, u32[]{:S(2)}, u32[]{:S(2)}) collective-permute-start(bf16[2,96,256]{2,1,0:T(8,128)(2,1)S(1)} %get-tuple-element.233), channel_id=1, source_target_pairs={{0,2},{1,3},{2,0},{3,1},{4,6},{5,7},{6,4},{7,5},{8,10},{9,11},{10,... | collective-permute-start | bytes 294920 | tf_op jit(solution)/shard_map/ppermute | solution.py:576
  116.4 9.8 %collective-permute-start.40 = (bf16[2,96,256]{2,1,0:T(8,128)(2,1)S(1)}, bf16[2,96,256]{2,1,0:T(8,128)(2,1)S(1)}, u32[]{:S(2)}, u32[]{:S(2)}) collective-permute-start(bf16[2,96,256]{2,1,0:T(8,128)(2,1)S(1)} %get-tuple-element.235), channel_id=1, source_target_pairs={{0,4},{4,0},{8,12},{12,8},{16,20},{20,16},{24,28},{28,24},{1,5},{5... | collective-permute-start | bytes 294920 | tf_op jit(solution)/shard_map/ppermute | solution.py:576
  125.6 10.0 %collective-permute-start.33 = (bf16[1,576,256]{2,1,0:T(8,128)(2,1)S(1)}, bf16[1,576,256]{2,1,0:T(8,128)(2,1)S(1)}, u32[]{:S(2)}, u32[]{:S(2)}) collective-permute-start(bf16[1,576,256]{2,1,0:T(8,128)(2,1)S(1)} %get-tuple-element.225.refs_1_), channel_id=1, source_target_pairs={{0,2},{1,3},{2,0},{3,1},{4,6},{5,7},{6,4},{7,5},{8,10},{9,11},{10,... | collective-permute-start | bytes 884744 | tf_op jit(solution)/shard_map/ppermute | solution.py:576
  126.8 8.7 %collective-permute-start.41 = (bf16[1,304,256]{2,1,0:T(8,128)(2,1)S(1)}, bf16[1,304,256]{2,1,0:T(8,128)(2,1)S(1)}, u32[]{:S(2)}, u32[]{:S(2)}) collective-permute-start(bf16[1,304,256]{2,1,0:T(8,128)(2,1)S(1)} %get-tuple-element.238), channel_id=1, source_target_pairs={{0,16},{4,20},{8,24},{12,28},{16,0},{20,4},{24,8},{28,12},{1,17},{... | collective-permute-start | bytes 466952 | tf_op jit(solution)/shard_map/ppermute | solution.py:576
  126.9 9.7 %collective-permute-start.35 = (bf16[128,768]{1,0:T(8,128)(2,1)S(1)}, bf16[128,768]{1,0:T(8,128)(2,1)S(1)}, u32[]{:S(2)}, u32[]{:S(2)}) collective-permute-start(bf16[128,768]{1,0:T(8,128)(2,1)S(1)} %get-tuple-element.227), channel_id=1, source_target_pairs={{0,1},{1,0},{2,3},{3,2},{4,5},{5,4},{6,7},{7,6},{8,9},{9,8},{10,11... | collective-permute-start | bytes 589832 | tf_op jit(solution)/shard_map/ppermute | solution.py:576
  127.0 12.4 %collective-permute-start.36 = (bf16[128,768]{1,0:T(8,128)(2,1)S(1)}, bf16[128,768]{1,0:T(8,128)(2,1)S(1)}, u32[]{:S(2)}, u32[]{:S(2)}) collective-permute-start(bf16[128,768]{1,0:T(8,128)(2,1)S(1)} %get-tuple-element.228), channel_id=1, source_target_pairs={{0,2},{1,3},{2,0},{3,1},{4,6},{5,7},{6,4},{7,5},{8,10},{9,11},{10,... | collective-permute-start | bytes 589832 | tf_op jit(solution)/shard_map/ppermute | solution.py:576
  128.5 16.3 %collective-permute-start.37 = (bf16[128,768]{1,0:T(8,128)(2,1)S(1)}, bf16[128,768]{1,0:T(8,128)(2,1)S(1)}, u32[]{:S(2)}, u32[]{:S(2)}) collective-permute-start(bf16[128,768]{1,0:T(8,128)(2,1)S(1)} %get-tuple-element.229), channel_id=1, source_target_pairs={{0,3},{1,2},{2,1},{3,0},{4,7},{5,6},{6,5},{7,4},{8,11},{9,10},{10,... | collective-permute-start | bytes 589832 | tf_op jit(solution)/shard_map/ppermute | solution.py:576
  135.5 9.4 %collective-permute-start.32 = (bf16[1,576,256]{2,1,0:T(8,128)(2,1)S(1)}, bf16[1,576,256]{2,1,0:T(8,128)(2,1)S(1)}, u32[]{:S(2)}, u32[]{:S(2)}) collective-permute-start(bf16[1,576,256]{2,1,0:T(8,128)(2,1)S(1)} %get-tuple-element.225.refs_1_), channel_id=1, source_target_pairs={{0,1},{1,0},{2,3},{3,2},{4,5},{5,4},{6,7},{7,6},{8,9},{9,8},{10,11... | collective-permute-start | bytes 884744 | tf_op jit(solution)/shard_map/ppermute | solution.py:576
  135.6 9.2 %collective-permute-start.34 = (bf16[1,576,256]{2,1,0:T(8,128)(2,1)S(1)}, bf16[1,576,256]{2,1,0:T(8,128)(2,1)S(1)}, u32[]{:S(2)}, u32[]{:S(2)}) collective-permute-start(bf16[1,576,256]{2,1,0:T(8,128)(2,1)S(1)} %collective-permute-done.33.refs_3_), channel_id=1, source_target_pairs={{0,1},{1,0},{2,3},{3,2},{4,5},{5,4},{6,7},{7,6},{8,9},{9,8},{10,11... | collective-permute-start | bytes 884744 | tf_op jit(solution)/shard_map/ppermute | solution.py:576
  136.6 8.3 %collective-permute-start.43 = (bf16[1,304,256]{2,1,0:T(8,128)(2,1)S(1)}, bf16[1,304,256]{2,1,0:T(8,128)(2,1)S(1)}, u32[]{:S(2)}, u32[]{:S(2)}) collective-permute-start(bf16[1,304,256]{2,1,0:T(8,128)(2,1)S(1)} %get-tuple-element.242.refs_1_), channel_id=1, source_target_pairs={{0,2},{1,3},{2,0},{3,1},{4,6},{5,7},{6,4},{7,5},{8,10},{9,11},{10,... | collective-permute-start | bytes 466952 | tf_op jit(solution)/shard_map/ppermute | solution.py:576
  139.4 8.3 %collective-permute-start.42 = (bf16[1,304,256]{2,1,0:T(8,128)(2,1)S(1)}, bf16[1,304,256]{2,1,0:T(8,128)(2,1)S(1)}, u32[]{:S(2)}, u32[]{:S(2)}) collective-permute-start(bf16[1,304,256]{2,1,0:T(8,128)(2,1)S(1)} %get-tuple-element.242.refs_1_), channel_id=1, source_target_pairs={{0,1},{1,0},{2,3},{3,2},{4,5},{5,4},{6,7},{7,6},{8,9},{9,8},{10,11... | collective-permute-start | bytes 466952 | tf_op jit(solution)/shard_map/ppermute | solution.py:576
  144.9 2.9 %collective-permute-start.44 = (bf16[1,304,256]{2,1,0:T(8,128)(2,1)S(1)}, bf16[1,304,256]{2,1,0:T(8,128)(2,1)S(1)}, u32[]{:S(2)}, u32[]{:S(2)}) collective-permute-start(bf16[1,304,256]{2,1,0:T(8,128)(2,1)S(1)} %collective-permute-done.43.refs_3_), channel_id=1, source_target_pairs={{0,1},{1,0},{2,3},{3,2},{4,5},{5,4},{6,7},{7,6},{8,9},{9,8},{10,11... | collective-permute-start | bytes 466952 | tf_op jit(solution)/shard_map/ppermute | solution.py:576
  (13 other events, 35.4 us)

commit v5 on v4

--- a/solution.py
+++ b/solution.py
@@ -24,8 +24,8 @@
 
 WEIGHTS = {
     "prepare": 60 * 10**9, "attend": 60 * 10**9, "feed": 60 * 10**9, "grad_up": 60 * 10**9,
-    "grad_down": 60 * 10**9, "attend_back": 60 * 10**9, "grad_tokens": 60 * 10**9,
-    "halve": 5 * 10**9, "cut_units": 5 * 10**9, "place_feed": 5 * 10**9,
+    "grad_down": 60 * 10**9, "attend_back": 60 * 10**9, "grad_tokens": 60 * 10**8,
+    "halve": 200 * 10**7, "cut_units": 200 * 10**7, "place_feed": 200 * 10**7,
 }
 
 
@@ -247,7 +247,7 @@
     rows = hidden // shares // 4
     apart = send_active is not None
 
-    @pl.loop(0, hidden // width)
+    @pl.loop(0, hidden // width, unroll=True)
     def _(i):
         here = cut(i, width)
         raised = dot(first_out[...], w_up[:, here]) + vectors[pl.ds(BIAS_UP + i, 1), :]
@@ -384,7 +384,7 @@
 
     for x in range(2):
 
-        @pl.loop(0, shares, step=2)
+        @pl.loop(0, shares, step=2, unroll=shares <= 8)
         def _(d):
             mine = active[x, pl.ds(d, 2)].reshape(2 * rows, count)
             other = other_active[x, pl.ds(d, 2)].reshape(2 * rows, count)
@@ -433,7 +433,9 @@
     count, width = attended.shape
     wide = 4 * head_width
     groups = width // wide
-    shares = small_keep.shape[1]
+    shares = small.shape[1]
+    rows = width // shares
+    joined = small_keep is None
 
     def load(i):
         here = cut(i, wide)
@@ -456,7 +458,7 @@
     none = jnp.zeros((count, wide), bf16)
     odd = place[0] == 1
 
-    @pl.loop(0, groups)
+    @pl.loop(0, groups, unroll=True)
     def _(i):
         here = cut(i, wide)
 
@@ -492,9 +494,13 @@
             mine = head == h
             probs = probs_kept[4 * i + h]
             wider = probs.astype(f32)
-            weighted = wider * dot(v, only(context_turned, h, head_width))
-            balance = jnp.sum(weighted, axis=0, keepdims=True)
-            grad_scores = (weighted - wider * balance).astype(bf16)
+            lines = slice(h * head_width, (h + 1) * head_width)
+            balance = column_sum(
+                context_turned[lines, :].astype(f32)
+                * turned_context[pl.ds(i * wide + h * head_width, head_width), :].astype(f32)
+            )
+            weighted = dot(v, only(context_turned, h, head_width)) - balance
+            grad_scores = (wider * weighted).astype(bf16)
             grad_v = grad_v + dot(probs, jnp.where(mine, grad_context, none))
             grad_k = grad_k + dot(grad_scores, jnp.where(mine, scaled_q, none))
             grad_q.append(dot(k_turned[h * head_width : (h + 1) * head_width, :], grad_scores))
@@ -515,10 +521,17 @@
         for s, (keep, send) in enumerate(((keep_0, send_0), (keep_1, send_1), (keep_2, send_2))):
 
             @pl.when(i == s)
-            def _(keep=keep, send=send):
+            def _(s=s, keep=keep, send=send):
                 for x in range(2):
-                    keep[x] = jnp.where(odd, pieces[2 * x + 1], pieces[2 * x])
-                    send[x] = jnp.where(odd, pieces[2 * x], pieces[2 * x + 1])
+                    kept = jnp.where(odd, pieces[2 * x + 1], pieces[2 * x])
+                    sent = jnp.where(odd, pieces[2 * x], pieces[2 * x + 1])
+                    if s or not joined:
+                        keep[x] = kept
+                        send[x] = sent
+                    else:
+                        for d in range(shares):
+                            keep[x, d, 0:rows, :] = kept[d * rows : (d + 1) * rows, :]
+                            send[x, d, 0:rows, :] = sent[d * rows : (d + 1) * rows, :]
 
     sums[2:5, :] = vector_one[0:3, :]
     sums[5:8, :] = vector_two[0:3, :]
@@ -532,8 +545,14 @@
     for x in range(2):
         even_part = small[2 * x].astype(bf16)
         odd_part = small[2 * x + 1].astype(bf16)
-        small_keep[x] = jnp.where(odd, odd_part, even_part)
-        small_send[x] = jnp.where(odd, even_part, odd_part)
+        kept = jnp.where(odd, odd_part, even_part)
+        sent = jnp.where(odd, even_part, odd_part)
+        if joined:
+            keep_0[x, :, rows:, :] = kept
+            send_0[x, :, rows:, :] = sent
+        else:
+            small_keep[x] = kept
+            small_send[x] = sent
 
 
 def attend_back(place, attended, small, far, shares, after):
@@ -541,10 +560,20 @@
     wide = 4 * (width // HEADS)
     groups = width // wide
     rows, turned = pltpu.VMEM((count, width), bf16), pltpu.VMEM((width, count), bf16)
-    grads, keep_0, keep_1, keep_2, send_0, send_1, send_2, small_keep, small_send, mark = call(
-        functools.partial(attend_back_kernel, head_width=width // HEADS),
-        "attend_back", [place], [attended, *small],
-        [shape(count, 3 * width)] + [shape(2, width, wide)] * 6 + [shape(2, shares, 16, wide)] * 2,
+    share = width // shares
+    joined = share % 16 == 0
+    plain, extra = shape(2, width, wide), [shape(2, shares, 16, wide)] * 2
+    first = shape(2, shares, share + 16, wide) if joined else plain
+    inner = functools.partial(attend_back_kernel, head_width=width // HEADS)
+
+    def kernel(*refs):
+        if joined:
+            refs = (*refs[:19], None, None, *refs[19:])
+        inner(*refs)
+
+    grads, keep_0, keep_1, keep_2, send_0, send_1, send_2, *small, mark = call(
+        kernel, "attend_back", [place], [attended, *small],
+        [shape(count, 3 * width)] + [first, plain, plain] * 2 + ([] if joined else extra),
         [
             pltpu.VMEM((2, count, width), bf16), turned, turned,
             pltpu.VMEM((HEADS, count, count), bf16), rows, rows, rows,
@@ -553,7 +582,7 @@
         ],
         far=far, copies=8 * groups + 2, room=26, after=after,
     )
-    return [keep_0, keep_1, keep_2], [send_0, send_1, send_2], small_keep, small_send, grads, mark
+    return [keep_0, keep_1, keep_2], [send_0, send_1, send_2], small, grads, mark
 
 
 def grad_tokens_kernel(grads, w_qkv, sum_one, r0, r1, r2, r3):
@@ -595,10 +624,10 @@
         if id(array) not in numbers:
             numbers[id(array)] = len(arrays)
             arrays.append(array)
-    rows = arrays[0].shape[-2]
+    rows = [units[0][s][0][0].shape[-2] for s in range(parts)]
     size = sum({id(terms[0]): terms[0].shape[-1] for terms, _ in units[0]}.values()) // parts
     more = [extra[0].shape[-2] if extra and s == 0 else 0 for s in range(parts)]
-    outs = [shape(2 ** (dims - 1), len(units) * rows + m, size) for m in more]
+    outs = [shape(2 ** (dims - 1), len(units) * r + m, size) for r, m in zip(rows, more)]
 
     def kernel(bits_ref, *refs):
         ins, results = refs[: len(arrays)], refs[len(arrays) :]
@@ -618,9 +647,9 @@
                 for u, unit in enumerate(units):
                     terms, column = unit[s]
                     at = (*index, slice(None), slice(column * size, (column + 1) * size))
-                    results[s][number, u * rows : (u + 1) * rows] = added(terms, at)
+                    results[s][number, u * rows[s] : (u + 1) * rows[s]] = added(terms, at)
                 if more[s]:
-                    results[s][number, len(units) * rows :] = added(extra, tuple(index))
+                    results[s][number, len(units) * rows[s] :] = added(extra, tuple(index))
 
         every(2 ** (dims - 1), work)
 
@@ -628,16 +657,21 @@
     return made, mark
 
 
-def halve(bits, pairs, axes, join, after=()):
+def halve(bits, pairs, axes, join, after=(), place=None, blocks=()):
     taken = pairs[0][0].shape[0] // (2 if axes else 1)
     sizes = [a.shape[1] for a, _ in pairs]
     width = pairs[0][0].shape[2]
     flips = (1, 0) if axes else (0,)
     outs = [shape(taken, sum(sizes), width)] if join else [shape(taken, n, width) for n in sizes]
+    outs = outs * len(flips)
     arrays = [a for pair in pairs for a in pair]
 
-    def kernel(bits_ref, *refs):
-        ins, results = refs[: len(arrays)], refs[len(arrays) :]
+    def kernel(*refs):
+        copies = []
+        if blocks:
+            place_ref, *refs, sems = refs
+            copies = place_rows(place_ref, refs[1 + len(arrays) : 5 + len(arrays)], refs[-1], sems)
+        bits_ref, ins, results = refs[0], refs[1 : 1 + len(arrays)], refs[1 + len(arrays) + len(blocks) :]
 
         def work(number):
             for f, flip in enumerate(flips):
@@ -651,9 +685,17 @@
                         results[f * len(pairs) + s][number] = total
 
         every(taken, work)
-
-    *made, mark = call(kernel, "halve", [bits], arrays, outs * len(flips), room=6, after=after)
-    return made[: len(outs)], made[len(outs) :], mark
+        for one in copies:
+            one.wait()
+
+    far_outs = [shape(4, *blocks[0].shape)] if blocks else []
+    *made, mark = call(
+        kernel, "halve", [place, bits] if blocks else [bits], arrays + list(blocks), outs,
+        far_outs=far_outs, copies=len(blocks), room=6, after=after,
+    )
+    made, rows = made[: len(outs)], made[len(outs) :]
+    half = len(outs) // len(flips)
+    return made[:half], made[half:], mark, *rows
 
 
 class Group:
@@ -682,12 +724,14 @@
         self.stage = 1
         return mark
 
-    def step(self, after):
+    def step(self, after, place=None, blocks=()):
         axes = [order[self.stage] for order in self.orders]
-        sent, keep, mark = halve(self.bits, self.pairs, axes, self.stage == 3, after)
+        sent, keep, mark, *rows = halve(
+            self.bits, self.pairs, axes, self.stage == 3, after, place, blocks
+        )
         self.pairs = list(zip(keep, self.send(sent)))
         self.stage += 1
-        return mark
+        return (mark, *rows) if rows else mark
 
     def finish(self, after):
         (own,), _, mark = halve(self.bits, self.pairs, None, False, after)
@@ -705,12 +749,11 @@
     ).astype(f32)
 
 
-def place_feed(place, pieces, rows, blocks, after):
+def place_feed(place, pieces, rows, after):
     size = pieces[0].shape[2]
     width = 3 * size
 
-    def kernel(place_ref, p0, p1, p2, p3, r0, r1, r2, r3, down, up, rows_out, sems):
-        copies = place_rows(place_ref, (r0, r1, r2, r3), rows_out, sems)
+    def kernel(place_ref, p0, p1, p2, p3, down, up):
         for b in range(4):
             for s in range(3):
                 at = 2 * s * rows
@@ -721,13 +764,10 @@
                 columns = slice(b * width + s * size, b * width + (s + 1) * size)
                 value = chosen(place_ref, b, [p.at[0, at : at + rows] for p in (p0, p1, p2, p3)])
                 up[:, columns] = value
-        for one in copies:
-            one.wait()
 
     return call(
-        kernel, "place_feed", [place], [*pieces, *blocks],
-        [shape(4 * rows, width, dtype=f32), shape(rows, 4 * width, dtype=f32)],
-        far_outs=[shape(4, *blocks[0].shape)], copies=4, after=after,
+        kernel, "place_feed", [place], pieces,
+        [shape(4 * rows, width, dtype=f32), shape(rows, 4 * width, dtype=f32)], after=after,
     )
 
 
@@ -826,31 +866,32 @@
         (), bits, names,
     )
     mark = feed_group.begin([mark])
-    keeps, sends, small_keep, small_send, grads, mark = attend_back(
+    keeps, sends, small, grads, mark = attend_back(
         place, attended, [vector_one, vector_two, grad_bias_up],
         [row_tokens, context, prob, q, k, v, w_out], shares, [mark],
     )
     gots = [swap(send, "blk", 1) for send in sends]
-    small_got = swap(small_send, "blk", 1)
+    small = [chunks(small[0]), chunks(swap(small[1], "blk", 1))] if small else ()
+    own_group = Group(
+        [[([chunks(keep), chunks(got)], 0) for keep, got in zip(keeps, gots)]], small, bits, names
+    )
+    share = width // shares
     mark = feed_group.rest([mark])
     mark = feed_group.step([mark])
-    own_group = Group(
-        [[([chunks(keep), chunks(got)], 0) for keep, got in zip(keeps, gots)]],
-        (chunks(small_keep), chunks(small_got)), bits, names,
-    )
     mark = own_group.begin([mark])
     tokens_parts, mark = grad_tokens(sum_one, grads, w_qkv, slots, [mark])
     mark = own_group.rest([mark])
-    for _ in range(dp_bits - 1):
+    for _ in range(dp_bits - 3):
         mark = feed_group.step([mark])
         mark = own_group.step([mark])
-    share = width // shares
+    mark = feed_group.step([mark])
+    mark = own_group.step([mark])
+    mark = feed_group.step([mark])
+    mark = own_group.step([mark])
     feed_pieces, mark = feed_group.finish([mark])
-    mark = own_group.step([mark])
+    mark, token_grads = own_group.step([mark], place, scatter_row(tokens_parts))
     own_pieces, mark = own_group.finish([mark])
-    down, up, token_grads, mark = place_feed(
-        place, feed_pieces, share, scatter_row(tokens_parts), [mark]
-    )
+    down, up, mark = place_feed(place, feed_pieces, share, [mark])
     (
         grad_w_qkv, grad_w_out, sum_qv, sum_out, sum_gain_one, sum_shift_one, sum_up, sum_down,
         sum_gain_two, sum_shift_two,
@@ -859,17 +900,17 @@
         outputs,
         token_grads,
         grad_w_qkv,
-        sum_qv[0],
+        sum_qv.reshape(-1),
         grad_w_out,
-        sum_out[0],
-        sum_gain_one[0],
-        sum_shift_one[0],
+        sum_out.reshape(-1),
+        sum_gain_one.reshape(-1),
+        sum_shift_one.reshape(-1),
         up,
-        sum_up[0],
+        sum_up.reshape(-1),
         down,
-        sum_down[0],
-        sum_gain_two[0],
-        sum_shift_two[0],
+        sum_down.reshape(-1),
+        sum_gain_two.reshape(-1),
+        sum_shift_two.reshape(-1),
     )
 
 

time: 151 us -> 146 us (0.967)
  waiting for transfers between devices: 35.2 us -> 29.9 us
  starting transfers between devices: 34.2 us -> 39.2 us
  Pallas kernels: 71.8 us -> 67.1 us
    ppermute x45 -> x44, waiting for transfers between devices: 35.2 us -> 29.9 us  [swap(): lax.ppermute(block, axis, [(i, i ^ bit) for i in range(lax.axis_size(axis...]
    ppermute x45 -> x44, starting transfers between devices: 34.2 us -> 39.2 us  [swap(): lax.ppermute(block, axis, [(i, i ^ bit) for i in range(lax.axis_size(axis...]
    pallas_call x21, Pallas kernels: 71.8 us -> 67.1 us  [call(): pl.pallas_call(body, in_specs=[SMEM] * len(scalars) + [VMEM] * len(arrays...]
  transfers between devices with their start and end apart: 45 -> 44, of which waited for: 13 -> 13; matrix products, arithmetic and copies ran while one was open for 0% -> 0% of each run, Pallas kernels for 39% -> 38%
where the time goes in v5:
time: 146 us; the launch traced here: 145 us
  Pallas kernels  67.1 us (46%)
  starting transfers between devices  39.2 us (27%)
  waiting for transfers between devices  29.9 us (20%)
  local copies, waits for them, and re-layouts  6.92 us (5%)
    pallas_call x21, Pallas kernels, call(): pl.pallas_call(body, in_specs=[SMEM] * len(scalars) + [VMEM] * len(arrays...  67.1 us
    ppermute x44, starting transfers between devices, swap(): lax.ppermute(block, axis, [(i, i ^ bit) for i in range(lax.axis_size(axis...  39.2 us
    ppermute x44, waiting for transfers between devices, swap(): lax.ppermute(block, axis, [(i, i ^ bit) for i in range(lax.axis_size(axis...  29.9 us
    unnamed x32, local copies, waits for them, and re-layouts  5.57 us
  transfers between devices with their start and end apart: 44, of which 13 were waited for; matrix products, arithmetic and copies ran while one was open for 0% of the time, Pallas kernels for 38%

profile of v5, /device:TPU:0, one launch (start us, length us, event | category | flops | bytes accessed | tf_op | source)
XLA Modules:
  0.0 145.0 jit_solution(4171389629426773869)
XLA Ops:
  0.7 1.3 dynamic-slice_bitcast_fusion.4
  2.0 3.0 %collective-permute-start = (bf16[128,768]{1,0:T(8,128)(2,1)S(1)}, bf16[128,768]{1,0:T(8,128)(2,1)S(1)}, u32[]{:S(2)}, u32[]{:S(2)}) collective-permute-start(bf16[128,768]{1,0:T(8,128)(2,1)S(1)} %get-tuple-element.257), channel_id=1, source_target_pairs={{0,2},{1,3},{2,0},{3,1},{4,6},{5,7},{6,4},{7,5},{8,10},{9,11},{10,... | collective-permute-start | bytes 589832 | tf_op jit(solution)/shard_map/ppermute | solution.py:605
  5.3 0.7 copy-done.3
  10.8 3.7 %prepare.1 = (bf16[768,2304]{1,0:T(8,128)(2,1)S(1)}, bf16[768,768]{1,0:T(8,128)(2,1)S(1)}, f32[512,512]{1,0:T(8,128)S(1)}, f32[12,768]{1,0:T(8,128)S(1)}, f32[8,128]{1,0:T(8,128)}) custom-call(s32[9]{0:T(128)S(1)} %pad_add_fusion.1.refs_0_, f32[1536]{0:T(1024)S(1)} %copy-done.4, f32[768]{0:T(1024)S(1)} %copy-done.5, f32[768]{0:T(1024)S(1)} %copy-done.6, ...), custom_call_target="tpu_custom_call" | custom-call | flops 60000002048 | tf_op jit(solution)/shard_map/prepare/pallas_call | solution.py:51
  15.2 1.7 %collective-permute-start.4 = (bf16[128,768]{1,0:T(8,128)(2,1)S(1)}, bf16[128,768]{1,0:T(8,128)(2,1)S(1)}, u32[]{:S(2)}, u32[]{:S(2)}) collective-permute-start(bf16[128,768]{1,0:T(8,128)(2,1)S(1)} %get-tuple-element.253), channel_id=1, source_target_pairs={{0,2},{1,3},{2,0},{3,1},{4,6},{5,7},{6,4},{7,5},{8,10},{9,11},{10,... | collective-permute-start | bytes 589832 | tf_op jit(solution)/shard_map/ppermute | solution.py:605
  17.0 11.2 %attend.1 = (f32[512,768]{1,0:T(8,128)S(1)}, f32[512,1]{1,0:T(8,128)S(1)}, bf16[512,768]{1,0:T(8,128)(2,1)}, bf16[512,768]{1,0:T(8,128)(2,1)}, bf16[512,768]{1,0...) custom-call(bf16[128,768]{1,0:T(8,128)(2,1)S(1)} %get-tuple-element., ...), custom_call_target="tpu_custom_call" | custom-call | flops 60000002048 | tf_op jit(solution)/shard_map/attend/pallas_call | solution.py:51
  28.2 8.9 %feed.1 = (bf16[2,8,96,512]{3,2,1,0:T(8,128)(2,1)S(1)}, bf16[2,8,96,512]{3,2,1,0:T(8,128)(2,1)S(1)}, bf16[512,3072]{1,0:T(8,128)(2,1)S(1)}, bf16[512,768]{1,0:T(...) custom-call(s32[2]{0:T(128)S(1)} %pad_add_fusion.refs_0_, ...), custom_call_target="tpu_custom_call" | custom-call | flops 60000002048 | tf_op jit(solution)/shard_map/feed/pallas_call | solution.py:51
  37.7 1.7 %collective-permute-start.10 = (bf16[128,768]{1,0:T(8,128)(2,1)S(1)}, bf16[128,768]{1,0:T(8,128)(2,1)S(1)}, u32[]{:S(2)}, u32[]{:S(2)}) collective-permute-start(bf16[128,768]{1,0:T(8,128)(2,1)S(1)} %get-tuple-element.149), channel_id=1, source_target_pairs={{0,3},{1,2},{2,1},{3,0},{4,7},{5,6},{6,5},{7,4},{8,11},{9,10},{10,... | collective-permute-start | bytes 589832 | tf_op jit(solution)/shard_map/ppermute | solution.py:605
  39.8 9.8 %grad_up.1 = (bf16[2,768,768]{2,1,0:T(8,128)(2,1)S(1)}, bf16[2,768,768]{2,1,0:T(8,128)(2,1)S(1)}, f32[4,768]{1,0:T(4,128)S(1)}, bf16[512,768]{1,0:T(8,128)(2,1)S...) custom-call(s32[2]{0:T(128)S(1)} %pad_add_fusion.refs_0_, ...), custom_call_target="tpu_custom_call" | custom-call | flops 60000002048 | tf_op jit(solution)/shard_map/grad_up/pallas_call | solution.py:51
  49.8 3.9 %grad_down.1 = (bf16[2,8,96,768]{3,2,1,0:T(8,128)(2,1)S(1)}, bf16[4,128,768]{2,1,0:T(8,128)(2,1)}, f32[8,128]{1,0:T(8,128)S(1)}) custom-call(s32[2]{0:T(128)S(1)} %pad_add_fusion.refs_0_, bf16[2,8,96,512]{3,2,1,0:T(8,128)(2,1)S(1)} %get-tuple-element.143.refs_1_, bf16[2,8,96,512]{3,2,1,0:T(8,128)(2,1)S(1)} %collective-permute-done.6.refs_2_, ...), custom_call_target="tpu_custom_call" | custom-call | flops 60000002048 | tf_op jit(solution)/shard_map/grad_down/pallas_call | solution.py:51
  54.3 0.7 cut_units.4
  55.0 1.8 %collective-permute-start.15 = (bf16[8,192,256]{2,1,0:T(8,128)(2,1)S(1)}, bf16[8,192,256]{2,1,0:T(8,128)(2,1)S(1)}, u32[]{:S(2)}, u32[]{:S(2)}) collective-permute-start(bf16[8,192,256]{2,1,0:T(8,128)(2,1)S(1)} %get-tuple-element.181), channel_id=1, source_target_pairs={{0,2},{1,3},{2,0},{3,1},{4,6},{5,7},{6,4},{7,5},{8,10},{9,11},{10,... | collective-permute-start | bytes 2359304 | tf_op jit(solution)/shard_map/ppermute | solution.py:605
  56.8 1.5 %collective-permute-start.16 = (bf16[8,192,256]{2,1,0:T(8,128)(2,1)S(1)}, bf16[8,192,256]{2,1,0:T(8,128)(2,1)S(1)}, u32[]{:S(2)}, u32[]{:S(2)}) collective-permute-start(bf16[8,192,256]{2,1,0:T(8,128)(2,1)S(1)} %get-tuple-element.183), channel_id=1, source_target_pairs={{0,4},{4,0},{8,12},{12,8},{16,20},{20,16},{24,28},{28,24},{1,5},{5... | collective-permute-start | bytes 2359304 | tf_op jit(solution)/shard_map/ppermute | solution.py:605
  58.3 1.6 %collective-permute-start.17 = (bf16[8,192,256]{2,1,0:T(8,128)(2,1)S(1)}, bf16[8,192,256]{2,1,0:T(8,128)(2,1)S(1)}, u32[]{:S(2)}, u32[]{:S(2)}) collective-permute-start(bf16[8,192,256]{2,1,0:T(8,128)(2,1)S(1)} %get-tuple-element.185), channel_id=1, source_target_pairs={{0,8},{4,12},{8,0},{12,4},{16,24},{20,28},{24,16},{28,20},{1,9},{5... | collective-permute-start | bytes 2359304 | tf_op jit(solution)/shard_map/ppermute | solution.py:605
  59.9 14.8 %attend_back.1 = (bf16[512,2304]{1,0:T(8,128)(2,1)S(1)}, bf16[2,8,112,256]{3,2,1,0:T(8,128)(2,1)S(1)}, bf16[2,768,256]{2,1,0:T(8,128)(2,1)S(1)}, bf16[2,768,256]...) custom-call(s32[2]{0:T(128)S(1)} %pad_add_fusion.refs_0_, ...), custom_call_target="tpu_custom_call" | custom-call | flops 60000002048 | tf_op jit(solution)/shard_map/attend_back/pallas_call | solution.py:51
  75.4 0.7 cut_units.5
  76.1 1.2 collective-permute-done.17.refs_6_
  77.3 0.8 halve.8
  78.7 1.6 %collective-permute-start.22 = (bf16[4,192,256]{2,1,0:T(8,128)(2,1)S(1)}, bf16[4,192,256]{2,1,0:T(8,128)(2,1)S(1)}, u32[]{:S(2)}, u32[]{:S(2)}) collective-permute-start(bf16[4,192,256]{2,1,0:T(8,128)(2,1)S(1)} %get-tuple-element.199), channel_id=1, source_target_pairs={{0,8},{4,12},{8,0},{12,4},{16,24},{20,28},{24,16},{28,20},{1,9},{5... | collective-permute-start | bytes 1179656 | tf_op jit(solution)/shard_map/ppermute | solution.py:605
  80.3 0.8 collective-permute-start.23
  81.8 1.3 collective-permute-start.18
  83.1 1.5 %collective-permute-start.19 = (bf16[8,96,256]{2,1,0:T(8,128)(2,1)S(1)}, bf16[8,96,256]{2,1,0:T(8,128)(2,1)S(1)}, u32[]{:S(2)}, u32[]{:S(2)}) collective-permute-start(bf16[8,96,256]{2,1,0:T(8,128)(2,1)S(1)} %get-tuple-element.193), channel_id=1, source_target_pairs={{0,4},{4,0},{8,12},{12,8},{16,20},{20,16},{24,28},{28,24},{1,5},{5... | collective-permute-start | bytes 1179656 | tf_op jit(solution)/shard_map/ppermute | solution.py:605
  84.6 5.6 %collective-permute-done.21.refs_2_ = bf16[4,192,256]{2,1,0:T(8,128)(2,1)S(1)} collective-permute-done((bf16[4,192,256]{2,1,0:T(8,128)(2,1)S(1)}, bf16[4,192,256]{2,1,0:T(8,128)(2,1)S(1)}, u32[]{:S(2)}, u32[]{:S(2)}) %collective-permute-start.21) | collective-permute-done | bytes 393248 | tf_op jit(solution)/shard_map/ppermute | solution.py:605
  90.2 1.6 %collective-permute-start.20 = (bf16[8,96,256]{2,1,0:T(8,128)(2,1)S(1)}, bf16[8,96,256]{2,1,0:T(8,128)(2,1)S(1)}, u32[]{:S(2)}, u32[]{:S(2)}) collective-permute-start(bf16[8,96,256]{2,1,0:T(8,128)(2,1)S(1)} %get-tuple-element.195), channel_id=1, source_target_pairs={{0,8},{4,12},{8,0},{12,4},{16,24},{20,28},{24,16},{28,20},{1,9},{5... | collective-permute-start | bytes 1179656 | tf_op jit(solution)/shard_map/ppermute | solution.py:605
  91.8 2.0 %grad_tokens.1 = (bf16[128,768]{1,0:T(8,128)(2,1)S(1)}, bf16[128,768]{1,0:T(8,128)(2,1)S(1)}, bf16[128,768]{1,0:T(8,128)(2,1)S(1)}, bf16[128,768]{1,0:T(8,128)(2,1)S(1)}, f32[8,128]{1,0:T(8,128)S(1)}) custom-call(bf16[512,2304]{1,0:T(8,128)(2,1)S(1)} %get-tuple-element.177.refs_0_, bf16[768,2304]{1,0:T(8,128)(2,1)S(1)} %copy-done.2, ...), custom_call_target="tpu_custom_call" | custom-call | flops 6000000000 | tf_op jit(solution)/shard_map/grad_tokens/pallas_call | solution.py:51
  96.9 1.1 collective-permute-start.29
  98.0 1.9 %collective-permute-done.20.refs_6_ = bf16[8,96,256]{2,1,0:T(8,128)(2,1)S(1)} collective-permute-done((bf16[8,96,256]{2,1,0:T(8,128)(2,1)S(1)}, bf16[8,96,256]{2,1,0:T(8,128)(2,1)S(1)}, u32[]{:S(2)}, u32[]{:S(2)}) %collective-permute-start.20) | collective-permute-done | bytes 393248 | tf_op jit(solution)/shard_map/ppermute | solution.py:605
  99.9 2.2 %collective-permute-done.18.refs_2_ = bf16[8,112,256]{2,1,0:T(8,128)(2,1)S(1)} collective-permute-done((bf16[8,112,256]{2,1,0:T(8,128)(2,1)S(1)}, bf16[8,112,256]{2,1,0:T(8,128)(2,1)S(1)}, u32[]{:S(2)}, u32[]{:S(2)}) %collective-permute-start.18) | collective-permute-done | bytes 458784 | tf_op jit(solution)/shard_map/ppermute | solution.py:605
  102.8 0.9 collective-permute-start.24
  103.8 0.9 collective-permute-start.25
  104.6 1.2 collective-permute-start.26
  107.0 2.7 %collective-permute-start.36 = (bf16[1,576,256]{2,1,0:T(8,128)(2,1)S(1)}, bf16[1,576,256]{2,1,0:T(8,128)(2,1)S(1)}, u32[]{:S(2)}, u32[]{:S(2)}) collective-permute-start(bf16[1,576,256]{2,1,0:T(8,128)(2,1)S(1)} %get-tuple-element.229), channel_id=1, source_target_pairs={{0,16},{4,20},{8,24},{12,28},{16,0},{20,4},{24,8},{28,12},{1,17},{... | collective-permute-start | bytes 884744 | tf_op jit(solution)/shard_map/ppermute | solution.py:605
  109.7 1.1 collective-permute-start.34
  110.7 0.8 collective-permute-start.35
  112.8 1.7 %collective-permute-start.31 = (bf16[2,96,256]{2,1,0:T(8,128)(2,1)S(1)}, bf16[2,96,256]{2,1,0:T(8,128)(2,1)S(1)}, u32[]{:S(2)}, u32[]{:S(2)}) collective-permute-start(bf16[2,96,256]{2,1,0:T(8,128)(2,1)S(1)} %get-tuple-element.221), channel_id=1, source_target_pairs={{0,2},{1,3},{2,0},{3,1},{4,6},{5,7},{6,4},{7,5},{8,10},{9,11},{10,... | collective-permute-start | bytes 294920 | tf_op jit(solution)/shard_map/ppermute | solution.py:605
  114.5 5.3 %collective-permute-done.36.refs_2_ = bf16[1,576,256]{2,1,0:T(8,128)(2,1)S(1)} collective-permute-done((bf16[1,576,256]{2,1,0:T(8,128)(2,1)S(1)}, bf16[1,576,256]{2,1,0:T(8,128)(2,1)S(1)}, u32[]{:S(2)}, u32[]{:S(2)}) %collective-permute-start.36) | collective-permute-done | bytes 294944 | tf_op jit(solution)/shard_map/ppermute | solution.py:605
  119.8 1.3 collective-permute-start.32
  121.7 1.0 collective-permute-start.42
  122.7 1.0 collective-permute-done.31.refs_5_
  123.7 0.7 collective-permute-done.32.refs_7_
  124.4 1.5 %halve.14 = (bf16[1,304,256]{2,1,0:T(8,128)(2,1)S(1)}, bf16[1,304,256]{2,1,0:T(8,128)(2,1)S(1)}, bf16[4,128,768]{2,1,0:T(8,128)(2,1)}, f32[8,128]{1,0:T(8,128)S(1)}) custom-call(s32[2]{0:T(128)S(1)} %pad_add_fusion.refs_0_, s32[4]{0:T(128)S(1)} %pad_add_fusion.2.refs_0_.refs_1_, bf16[2,112,256]{2,1,0:T(8,128)(2,1)S(1)} %get-tuple-element.218.refs_2_, ...), custom_call_target="tpu_custom_call" | custom-call | flops 2000000000 | tf_op jit(solution)/shard_map/halve/pallas_call | solution.py:51
  125.9 2.3 %collective-permute-start.37 = (bf16[1,304,256]{2,1,0:T(8,128)(2,1)S(1)}, bf16[1,304,256]{2,1,0:T(8,128)(2,1)S(1)}, u32[]{:S(2)}, u32[]{:S(2)}) collective-permute-start(bf16[1,304,256]{2,1,0:T(8,128)(2,1)S(1)} %get-tuple-element.234), channel_id=1, source_target_pairs={{0,16},{4,20},{8,24},{12,28},{16,0},{20,4},{24,8},{28,12},{1,17},{... | collective-permute-start | bytes 466952 | tf_op jit(solution)/shard_map/ppermute | solution.py:605
  128.2 1.4 collective-permute-done.42.refs_3_
  129.6 5.0 %collective-permute-done.37.refs_2_ = bf16[1,304,256]{2,1,0:T(8,128)(2,1)S(1)} collective-permute-done((bf16[1,304,256]{2,1,0:T(8,128)(2,1)S(1)}, bf16[1,304,256]{2,1,0:T(8,128)(2,1)S(1)}, u32[]{:S(2)}, u32[]{:S(2)}) %collective-permute-start.37) | collective-permute-done | bytes 155680 | tf_op jit(solution)/shard_map/ppermute | solution.py:605
  135.2 1.6 %collective-permute-start.39 = (bf16[1,304,256]{2,1,0:T(8,128)(2,1)S(1)}, bf16[1,304,256]{2,1,0:T(8,128)(2,1)S(1)}, u32[]{:S(2)}, u32[]{:S(2)}) collective-permute-start(bf16[1,304,256]{2,1,0:T(8,128)(2,1)S(1)} %get-tuple-element.236.refs_1_), channel_id=1, source_target_pairs={{0,2},{1,3},{2,0},{3,1},{4,6},{5,7},{6,4},{7,5},{8,10},{9,11},{10,... | collective-permute-start | bytes 466952 | tf_op jit(solution)/shard_map/ppermute | solution.py:605
  136.8 3.7 %collective-permute-done.39.refs_3_ = bf16[1,304,256]{2,1,0:T(8,128)(2,1)S(1)} collective-permute-done((bf16[1,304,256]{2,1,0:T(8,128)(2,1)S(1)}, bf16[1,304,256]{2,1,0:T(8,128)(2,1)S(1)}, u32[]{:S(2)}, u32[]{:S(2)}) %collective-permute-start.39) | collective-permute-done | bytes 155680 | tf_op jit(solution)/shard_map/ppermute | solution.py:605
  140.5 2.2 %place_feed.1 = (f32[384,768]{1,0:T(8,128)}, f32[96,3072]{1,0:T(8,128)}, f32[8,128]{1,0:T(8,128)S(1)}) custom-call(s32[2]{0:T(128)S(1)} %pad_add_fusion.refs_0_, bf16[1,576,256]{2,1,0:T(8,128)(2,1)S(1)} %get-tuple-element.237.refs_1_, bf16[1,576,256]{2,1,0:T(8,128)(2,1)S(1)} %collective-permute-done.41.refs_2_, ...), custom_call_target="tpu_custom_call" | custom-call | flops 2000000000 | tf_op jit(solution)/shard_map/place_feed/pallas_call | solution.py:51
  142.8 1.6 %place_own.1 = (f32[96,2304]{1,0:T(8,128)}, f32[96,768]{1,0:T(8,128)}, f32[1,192]{1,0:T(1,128)}, f32[1,96]{1,0:T(1,128)}, f32[1,96]{1,0:T(1,128)}, /*index=5*/f3...) custom-call(s32[2]{0:T(128)S(1)} %pad_add_fusion.refs_0_, ...), custom_call_target="tpu_custom_call" | custom-call | tf_op jit(solution)/shard_map/place_own/pallas_call | solution.py:51
  (102 shorter events, 17.4 us)
Async XLA Ops:
  2.0 12.7 %collective-permute-start = (bf16[128,768]{1,0:T(8,128)(2,1)S(1)}, bf16[128,768]{1,0:T(8,128)(2,1)S(1)}, u32[]{:S(2)}, u32[]{:S(2)}) collective-permute-start(bf16[128,768]{1,0:T(8,128)(2,1)S(1)} %get-tuple-element.257), channel_id=1, source_target_pairs={{0,2},{1,3},{2,0},{3,1},{4,6},{5,7},{6,4},{7,5},{8,10},{9,11},{10,... | collective-permute-start | bytes 589832 | tf_op jit(solution)/shard_map/ppermute | solution.py:605
  5.0 9.7 %collective-permute-start.1 = (bf16[128,768]{1,0:T(8,128)(2,1)S(1)}, bf16[128,768]{1,0:T(8,128)(2,1)S(1)}, u32[]{:S(2)}, u32[]{:S(2)}) collective-permute-start(bf16[128,768]{1,0:T(8,128)(2,1)S(1)} %get-tuple-element.259), channel_id=1, source_target_pairs={{0,3},{1,2},{2,1},{3,0},{4,7},{5,6},{6,5},{7,4},{8,11},{9,10},{10,... | collective-permute-start | bytes 589832 | tf_op jit(solution)/shard_map/ppermute | solution.py:605
  5.0 9.7 %collective-permute-start.2 = (bf16[128,768]{1,0:T(8,128)(2,1)S(1)}, bf16[128,768]{1,0:T(8,128)(2,1)S(1)}, u32[]{:S(2)}, u32[]{:S(2)}) collective-permute-start(bf16[128,768]{1,0:T(8,128)(2,1)S(1)} %get-tuple-element.256), channel_id=1, source_target_pairs={{0,1},{1,0},{2,3},{3,2},{4,5},{5,4},{6,7},{7,6},{8,9},{9,8},{10,11... | collective-permute-start | bytes 589832 | tf_op jit(solution)/shard_map/ppermute | solution.py:605
  10.8 17.4 %slice-start = ((s8[4718592]{0:T(1024)(128)(4,1)}), s8[4194304]{0:T(1024)(128)(4,1)S(1)}, s32[]{:S(2)}) async-start(s8[4718592]{0:T(1024)(128)(4,1)} %bitcast.40), calls=%async_computation | async-start | bytes 8388608
  10.8 17.4 %slice-start.2 = ((s8[4718592]{0:T(1024)(128)(4,1)}), s8[4194304]{0:T(1024)(128)(4,1)S(1)}, s32[]{:S(2)}) async-start(s8[4718592]{0:T(1024)(128)(4,1)} %bitcast.42), calls=%async_computation.2 | async-start | bytes 8388608
  14.7 13.5 %slice-start.1 = ((s8[4718592]{0:T(1024)(128)(4,1)}), s8[524288]{0:T(1024)(128)(4,1)S(1)}, s32[]{:S(2)}) async-start(s8[4718592]{0:T(1024)(128)(4,1)} %bitcast.40), calls=%async_computation.1 | async-start | bytes 1048576
  14.7 13.5 %slice-start.3 = ((s8[4718592]{0:T(1024)(128)(4,1)}), s8[524288]{0:T(1024)(128)(4,1)S(1)}, s32[]{:S(2)}) async-start(s8[4718592]{0:T(1024)(128)(4,1)} %bitcast.42), calls=%async_computation.3 | async-start | bytes 1048576
  14.8 13.3 %collective-permute-start.3 = (bf16[128,768]{1,0:T(8,128)(2,1)S(1)}, bf16[128,768]{1,0:T(8,128)(2,1)S(1)}, u32[]{:S(2)}, u32[]{:S(2)}) collective-permute-start(bf16[128,768]{1,0:T(8,128)(2,1)S(1)} %get-tuple-element.254), channel_id=1, source_target_pairs={{0,1},{1,0},{2,3},{3,2},{4,5},{5,4},{6,7},{7,6},{8,9},{9,8},{10,11... | collective-permute-start | bytes 589832 | tf_op jit(solution)/shard_map/ppermute | solution.py:605
  15.2 12.9 %collective-permute-start.4 = (bf16[128,768]{1,0:T(8,128)(2,1)S(1)}, bf16[128,768]{1,0:T(8,128)(2,1)S(1)}, u32[]{:S(2)}, u32[]{:S(2)}) collective-permute-start(bf16[128,768]{1,0:T(8,128)(2,1)S(1)} %get-tuple-element.253), channel_id=1, source_target_pairs={{0,2},{1,3},{2,0},{3,1},{4,6},{5,7},{6,4},{7,5},{8,10},{9,11},{10,... | collective-permute-start | bytes 589832 | tf_op jit(solution)/shard_map/ppermute | solution.py:605
  16.9 11.3 %collective-permute-start.5 = (bf16[128,768]{1,0:T(8,128)(2,1)S(1)}, bf16[128,768]{1,0:T(8,128)(2,1)S(1)}, u32[]{:S(2)}, u32[]{:S(2)}) collective-permute-start(bf16[128,768]{1,0:T(8,128)(2,1)S(1)} %get-tuple-element.252), channel_id=1, source_target_pairs={{0,3},{1,2},{2,1},{3,0},{4,7},{5,6},{6,5},{7,4},{8,11},{9,10},{10,... | collective-permute-start | bytes 589832 | tf_op jit(solution)/shard_map/ppermute | solution.py:605
  37.2 12.6 %collective-permute-start.6 = (bf16[2,8,96,512]{3,2,1,0:T(8,128)(2,1)S(1)}, bf16[2,8,96,512]{3,2,1,0:T(8,128)(2,1)S(1)}, u32[]{:S(2)}, u32[]{:S(2)}) collective-permute-start(bf16[2,8,96,512]{3,2,1,0:T(8,128)(2,1)S(1)} %get-tuple-element.144), channel_id=1, source_target_pairs={{0,1},{1,0},{2,3},{3,2},{4,5},{5,4},{6,7},{7,6},{8,9},{9,8},{10,11... | collective-permute-start | bytes 4718600 | tf_op jit(solution)/shard_map/ppermute | solution.py:605
  37.5 12.3 %collective-permute-start.7 = (bf16[512,768]{1,0:T(8,128)(2,1)S(1)}, bf16[512,768]{1,0:T(8,128)(2,1)S(1)}, u32[]{:S(2)}, u32[]{:S(2)}) collective-permute-start(bf16[512,768]{1,0:T(8,128)(2,1)S(1)} %get-tuple-element.145.refs_1_.refs_3_), channel_id=1, source_target_pairs={{0,1},{1,0},{2,3},{3,2},{4,5},{5,4},{6,7},{7,6},{8,9},{9,8},{10,11... | collective-permute-start | bytes 2359304 | tf_op jit(solution)/shard_map/ppermute | solution.py:605
  37.7 12.0 %collective-permute-start.10 = (bf16[128,768]{1,0:T(8,128)(2,1)S(1)}, bf16[128,768]{1,0:T(8,128)(2,1)S(1)}, u32[]{:S(2)}, u32[]{:S(2)}) collective-permute-start(bf16[128,768]{1,0:T(8,128)(2,1)S(1)} %get-tuple-element.149), channel_id=1, source_target_pairs={{0,3},{1,2},{2,1},{3,0},{4,7},{5,6},{6,5},{7,4},{8,11},{9,10},{10,... | collective-permute-start | bytes 589832 | tf_op jit(solution)/shard_map/ppermute | solution.py:605
  39.3 10.4 %collective-permute-start.8 = (bf16[128,768]{1,0:T(8,128)(2,1)S(1)}, bf16[128,768]{1,0:T(8,128)(2,1)S(1)}, u32[]{:S(2)}, u32[]{:S(2)}) collective-permute-start(bf16[128,768]{1,0:T(8,128)(2,1)S(1)} %get-tuple-element.147), channel_id=1, source_target_pairs={{0,1},{1,0},{2,3},{3,2},{4,5},{5,4},{6,7},{7,6},{8,9},{9,8},{10,11... | collective-permute-start | bytes 589832 | tf_op jit(solution)/shard_map/ppermute | solution.py:605
  39.5 10.3 %collective-permute-start.9 = (bf16[128,768]{1,0:T(8,128)(2,1)S(1)}, bf16[128,768]{1,0:T(8,128)(2,1)S(1)}, u32[]{:S(2)}, u32[]{:S(2)}) collective-permute-start(bf16[128,768]{1,0:T(8,128)(2,1)S(1)} %get-tuple-element.148), channel_id=1, source_target_pairs={{0,2},{1,3},{2,0},{3,1},{4,6},{5,7},{6,4},{7,5},{8,10},{9,11},{10,... | collective-permute-start | bytes 589832 | tf_op jit(solution)/shard_map/ppermute | solution.py:605
  49.7 4.6 %collective-permute-start.11 = (bf16[2,768,768]{2,1,0:T(8,128)(2,1)S(1)}, bf16[2,768,768]{2,1,0:T(8,128)(2,1)S(1)}, u32[]{:S(2)}, u32[]{:S(2)}) collective-permute-start(bf16[2,768,768]{2,1,0:T(8,128)(2,1)S(1)} %get-tuple-element.168), channel_id=1, source_target_pairs={{0,1},{1,0},{2,3},{3,2},{4,5},{5,4},{6,7},{7,6},{8,9},{9,8},{10,11... | collective-permute-start | bytes 7077896 | tf_op jit(solution)/shard_map/ppermute | solution.py:605
  55.0 20.3 %collective-permute-start.15 = (bf16[8,192,256]{2,1,0:T(8,128)(2,1)S(1)}, bf16[8,192,256]{2,1,0:T(8,128)(2,1)S(1)}, u32[]{:S(2)}, u32[]{:S(2)}) collective-permute-start(bf16[8,192,256]{2,1,0:T(8,128)(2,1)S(1)} %get-tuple-element.181), channel_id=1, source_target_pairs={{0,2},{1,3},{2,0},{3,1},{4,6},{5,7},{6,4},{7,5},{8,10},{9,11},{10,... | collective-permute-start | bytes 2359304 | tf_op jit(solution)/shard_map/ppermute | solution.py:605
  56.8 19.3 %collective-permute-start.16 = (bf16[8,192,256]{2,1,0:T(8,128)(2,1)S(1)}, bf16[8,192,256]{2,1,0:T(8,128)(2,1)S(1)}, u32[]{:S(2)}, u32[]{:S(2)}) collective-permute-start(bf16[8,192,256]{2,1,0:T(8,128)(2,1)S(1)} %get-tuple-element.183), channel_id=1, source_target_pairs={{0,4},{4,0},{8,12},{12,8},{16,20},{20,16},{24,28},{28,24},{1,5},{5... | collective-permute-start | bytes 2359304 | tf_op jit(solution)/shard_map/ppermute | solution.py:605
  58.3 19.0 %collective-permute-start.17 = (bf16[8,192,256]{2,1,0:T(8,128)(2,1)S(1)}, bf16[8,192,256]{2,1,0:T(8,128)(2,1)S(1)}, u32[]{:S(2)}, u32[]{:S(2)}) collective-permute-start(bf16[8,192,256]{2,1,0:T(8,128)(2,1)S(1)} %get-tuple-element.185), channel_id=1, source_target_pairs={{0,8},{4,12},{8,0},{12,4},{16,24},{20,28},{24,16},{28,20},{1,9},{5... | collective-permute-start | bytes 2359304 | tf_op jit(solution)/shard_map/ppermute | solution.py:605
  74.7 6.4 %collective-permute-start.12 = (bf16[2,8,112,256]{3,2,1,0:T(8,128)(2,1)S(1)}, bf16[2,8,112,256]{3,2,1,0:T(8,128)(2,1)S(1)}, u32[]{:S(2)}, u32[]{:S(2)}) collective-permute-start(bf16[2,8,112,256]{3,2,1,0:T(8,128)(2,1)S(1)} %get-tuple-element.172), channel_id=1, source_target_pairs={{0,1},{1,0},{2,3},{3,2},{4,5},{5,4},{6,7},{7,6},{8,9},{9,8},{10,11... | collective-permute-start | bytes 2752520 | tf_op jit(solution)/shard_map/ppermute | solution.py:605
  74.8 5.5 %collective-permute-start.13 = (bf16[2,768,256]{2,1,0:T(8,128)(2,1)S(1)}, bf16[2,768,256]{2,1,0:T(8,128)(2,1)S(1)}, u32[]{:S(2)}, u32[]{:S(2)}) collective-permute-start(bf16[2,768,256]{2,1,0:T(8,128)(2,1)S(1)} %get-tuple-element.174), channel_id=1, source_target_pairs={{0,1},{1,0},{2,3},{3,2},{4,5},{5,4},{6,7},{7,6},{8,9},{9,8},{10,11... | collective-permute-start | bytes 2359304 | tf_op jit(solution)/shard_map/ppermute | solution.py:605
  75.3 5.8 %collective-permute-start.14 = (bf16[2,768,256]{2,1,0:T(8,128)(2,1)S(1)}, bf16[2,768,256]{2,1,0:T(8,128)(2,1)S(1)}, u32[]{:S(2)}, u32[]{:S(2)}) collective-permute-start(bf16[2,768,256]{2,1,0:T(8,128)(2,1)S(1)} %get-tuple-element.176), channel_id=1, source_target_pairs={{0,1},{1,0},{2,3},{3,2},{4,5},{5,4},{6,7},{7,6},{8,9},{9,8},{10,11... | collective-permute-start | bytes 2359304 | tf_op jit(solution)/shard_map/ppermute | solution.py:605
  78.1 12.1 %collective-permute-start.21 = (bf16[4,192,256]{2,1,0:T(8,128)(2,1)S(1)}, bf16[4,192,256]{2,1,0:T(8,128)(2,1)S(1)}, u32[]{:S(2)}, u32[]{:S(2)}) collective-permute-start(bf16[4,192,256]{2,1,0:T(8,128)(2,1)S(1)} %get-tuple-element.197), channel_id=1, source_target_pairs={{0,4},{4,0},{8,12},{12,8},{16,20},{20,16},{24,28},{28,24},{1,5},{5... | collective-permute-start | bytes 1179656 | tf_op jit(solution)/shard_map/ppermute | solution.py:605
  78.7 15.9 %collective-permute-start.22 = (bf16[4,192,256]{2,1,0:T(8,128)(2,1)S(1)}, bf16[4,192,256]{2,1,0:T(8,128)(2,1)S(1)}, u32[]{:S(2)}, u32[]{:S(2)}) collective-permute-start(bf16[4,192,256]{2,1,0:T(8,128)(2,1)S(1)} %get-tuple-element.199), channel_id=1, source_target_pairs={{0,8},{4,12},{8,0},{12,4},{16,24},{20,28},{24,16},{28,20},{1,9},{5... | collective-permute-start | bytes 1179656 | tf_op jit(solution)/shard_map/ppermute | solution.py:605
  80.3 14.3 %collective-permute-start.23 = (bf16[4,192,256]{2,1,0:T(8,128)(2,1)S(1)}, bf16[4,192,256]{2,1,0:T(8,128)(2,1)S(1)}, u32[]{:S(2)}, u32[]{:S(2)}) collective-permute-start(bf16[4,192,256]{2,1,0:T(8,128)(2,1)S(1)} %get-tuple-element.201), channel_id=1, source_target_pairs={{0,2},{1,3},{2,0},{3,1},{4,6},{5,7},{6,4},{7,5},{8,10},{9,11},{10,... | collective-permute-start | bytes 1179656 | tf_op jit(solution)/shard_map/ppermute | solution.py:605
  81.8 20.3 %collective-permute-start.18 = (bf16[8,112,256]{2,1,0:T(8,128)(2,1)S(1)}, bf16[8,112,256]{2,1,0:T(8,128)(2,1)S(1)}, u32[]{:S(2)}, u32[]{:S(2)}) collective-permute-start(bf16[8,112,256]{2,1,0:T(8,128)(2,1)S(1)} %get-tuple-element.191), channel_id=1, source_target_pairs={{0,2},{1,3},{2,0},{3,1},{4,6},{5,7},{6,4},{7,5},{8,10},{9,11},{10,... | collective-permute-start | bytes 1376264 | tf_op jit(solution)/shard_map/ppermute | solution.py:605
  83.1 13.8 %collective-permute-start.19 = (bf16[8,96,256]{2,1,0:T(8,128)(2,1)S(1)}, bf16[8,96,256]{2,1,0:T(8,128)(2,1)S(1)}, u32[]{:S(2)}, u32[]{:S(2)}) collective-permute-start(bf16[8,96,256]{2,1,0:T(8,128)(2,1)S(1)} %get-tuple-element.193), channel_id=1, source_target_pairs={{0,4},{4,0},{8,12},{12,8},{16,20},{20,16},{24,28},{28,24},{1,5},{5... | collective-permute-start | bytes 1179656 | tf_op jit(solution)/shard_map/ppermute | solution.py:605
  90.2 9.7 %collective-permute-start.20 = (bf16[8,96,256]{2,1,0:T(8,128)(2,1)S(1)}, bf16[8,96,256]{2,1,0:T(8,128)(2,1)S(1)}, u32[]{:S(2)}, u32[]{:S(2)}) collective-permute-start(bf16[8,96,256]{2,1,0:T(8,128)(2,1)S(1)} %get-tuple-element.195), channel_id=1, source_target_pairs={{0,8},{4,12},{8,0},{12,4},{16,24},{20,28},{24,16},{28,20},{1,9},{5... | collective-permute-start | bytes 1179656 | tf_op jit(solution)/shard_map/ppermute | solution.py:605
  95.3 9.4 %collective-permute-start.27 = (bf16[2,192,256]{2,1,0:T(8,128)(2,1)S(1)}, bf16[2,192,256]{2,1,0:T(8,128)(2,1)S(1)}, u32[]{:S(2)}, u32[]{:S(2)}) collective-permute-start(bf16[2,192,256]{2,1,0:T(8,128)(2,1)S(1)} %get-tuple-element.211), channel_id=1, source_target_pairs={{0,8},{4,12},{8,0},{12,4},{16,24},{20,28},{24,16},{28,20},{1,9},{5... | collective-permute-start | bytes 589832 | tf_op jit(solution)/shard_map/ppermute | solution.py:605
  95.8 10.6 %collective-permute-start.28 = (bf16[2,192,256]{2,1,0:T(8,128)(2,1)S(1)}, bf16[2,192,256]{2,1,0:T(8,128)(2,1)S(1)}, u32[]{:S(2)}, u32[]{:S(2)}) collective-permute-start(bf16[2,192,256]{2,1,0:T(8,128)(2,1)S(1)} %get-tuple-element.213), channel_id=1, source_target_pairs={{0,2},{1,3},{2,0},{3,1},{4,6},{5,7},{6,4},{7,5},{8,10},{9,11},{10,... | collective-permute-start | bytes 589832 | tf_op jit(solution)/shard_map/ppermute | solution.py:605
  96.9 9.5 %collective-permute-start.29 = (bf16[2,192,256]{2,1,0:T(8,128)(2,1)S(1)}, bf16[2,192,256]{2,1,0:T(8,128)(2,1)S(1)}, u32[]{:S(2)}, u32[]{:S(2)}) collective-permute-start(bf16[2,192,256]{2,1,0:T(8,128)(2,1)S(1)} %get-tuple-element.215), channel_id=1, source_target_pairs={{0,4},{4,0},{8,12},{12,8},{16,20},{20,16},{24,28},{28,24},{1,5},{5... | collective-permute-start | bytes 589832 | tf_op jit(solution)/shard_map/ppermute | solution.py:605
  102.8 8.7 %collective-permute-start.24 = (bf16[4,112,256]{2,1,0:T(8,128)(2,1)S(1)}, bf16[4,112,256]{2,1,0:T(8,128)(2,1)S(1)}, u32[]{:S(2)}, u32[]{:S(2)}) collective-permute-start(bf16[4,112,256]{2,1,0:T(8,128)(2,1)S(1)} %get-tuple-element.205), channel_id=1, source_target_pairs={{0,4},{4,0},{8,12},{12,8},{16,20},{20,16},{24,28},{28,24},{1,5},{5... | collective-permute-start | bytes 688136 | tf_op jit(solution)/shard_map/ppermute | solution.py:605
  103.8 5.9 %collective-permute-start.25 = (bf16[4,96,256]{2,1,0:T(8,128)(2,1)S(1)}, bf16[4,96,256]{2,1,0:T(8,128)(2,1)S(1)}, u32[]{:S(2)}, u32[]{:S(2)}) collective-permute-start(bf16[4,96,256]{2,1,0:T(8,128)(2,1)S(1)} %get-tuple-element.207), channel_id=1, source_target_pairs={{0,8},{4,12},{8,0},{12,4},{16,24},{20,28},{24,16},{28,20},{1,9},{5... | collective-permute-start | bytes 589832 | tf_op jit(solution)/shard_map/ppermute | solution.py:605
  104.6 6.1 %collective-permute-start.26 = (bf16[4,96,256]{2,1,0:T(8,128)(2,1)S(1)}, bf16[4,96,256]{2,1,0:T(8,128)(2,1)S(1)}, u32[]{:S(2)}, u32[]{:S(2)}) collective-permute-start(bf16[4,96,256]{2,1,0:T(8,128)(2,1)S(1)} %get-tuple-element.209), channel_id=1, source_target_pairs={{0,2},{1,3},{2,0},{3,1},{4,6},{5,7},{6,4},{7,5},{8,10},{9,11},{10,... | collective-permute-start | bytes 589832 | tf_op jit(solution)/shard_map/ppermute | solution.py:605
  107.0 12.8 %collective-permute-start.36 = (bf16[1,576,256]{2,1,0:T(8,128)(2,1)S(1)}, bf16[1,576,256]{2,1,0:T(8,128)(2,1)S(1)}, u32[]{:S(2)}, u32[]{:S(2)}) collective-permute-start(bf16[1,576,256]{2,1,0:T(8,128)(2,1)S(1)} %get-tuple-element.229), channel_id=1, source_target_pairs={{0,16},{4,20},{8,24},{12,28},{16,0},{20,4},{24,8},{28,12},{1,17},{... | collective-permute-start | bytes 884744 | tf_op jit(solution)/shard_map/ppermute | solution.py:605
  109.6 3.2 %collective-permute-start.33 = (bf16[128,768]{1,0:T(8,128)(2,1)S(1)}, bf16[128,768]{1,0:T(8,128)(2,1)S(1)}, u32[]{:S(2)}, u32[]{:S(2)}) collective-permute-start(bf16[128,768]{1,0:T(8,128)(2,1)S(1)} %get-tuple-element.225), channel_id=1, source_target_pairs={{0,1},{1,0},{2,3},{3,2},{4,5},{5,4},{6,7},{7,6},{8,9},{9,8},{10,11... | collective-permute-start | bytes 589832 | tf_op jit(solution)/shard_map/ppermute | solution.py:605
  109.7 12.0 %collective-permute-start.34 = (bf16[128,768]{1,0:T(8,128)(2,1)S(1)}, bf16[128,768]{1,0:T(8,128)(2,1)S(1)}, u32[]{:S(2)}, u32[]{:S(2)}) collective-permute-start(bf16[128,768]{1,0:T(8,128)(2,1)S(1)} %get-tuple-element.226), channel_id=1, source_target_pairs={{0,2},{1,3},{2,0},{3,1},{4,6},{5,7},{6,4},{7,5},{8,10},{9,11},{10,... | collective-permute-start | bytes 589832 | tf_op jit(solution)/shard_map/ppermute | solution.py:605
  110.7 11.9 %collective-permute-start.35 = (bf16[128,768]{1,0:T(8,128)(2,1)S(1)}, bf16[128,768]{1,0:T(8,128)(2,1)S(1)}, u32[]{:S(2)}, u32[]{:S(2)}) collective-permute-start(bf16[128,768]{1,0:T(8,128)(2,1)S(1)} %get-tuple-element.227), channel_id=1, source_target_pairs={{0,3},{1,2},{2,1},{3,0},{4,7},{5,6},{6,5},{7,4},{8,11},{9,10},{10,... | collective-permute-start | bytes 589832 | tf_op jit(solution)/shard_map/ppermute | solution.py:605
  112.2 12.3 %collective-permute-start.30 = (bf16[2,112,256]{2,1,0:T(8,128)(2,1)S(1)}, bf16[2,112,256]{2,1,0:T(8,128)(2,1)S(1)}, u32[]{:S(2)}, u32[]{:S(2)}) collective-permute-start(bf16[2,112,256]{2,1,0:T(8,128)(2,1)S(1)} %get-tuple-element.219), channel_id=1, source_target_pairs={{0,8},{4,12},{8,0},{12,4},{16,24},{20,28},{24,16},{28,20},{1,9},{5... | collective-permute-start | bytes 344072 | tf_op jit(solution)/shard_map/ppermute | solution.py:605
  112.8 10.8 %collective-permute-start.31 = (bf16[2,96,256]{2,1,0:T(8,128)(2,1)S(1)}, bf16[2,96,256]{2,1,0:T(8,128)(2,1)S(1)}, u32[]{:S(2)}, u32[]{:S(2)}) collective-permute-start(bf16[2,96,256]{2,1,0:T(8,128)(2,1)S(1)} %get-tuple-element.221), channel_id=1, source_target_pairs={{0,2},{1,3},{2,0},{3,1},{4,6},{5,7},{6,4},{7,5},{8,10},{9,11},{10,... | collective-permute-start | bytes 294920 | tf_op jit(solution)/shard_map/ppermute | solution.py:605
  119.8 4.6 %collective-permute-start.32 = (bf16[2,96,256]{2,1,0:T(8,128)(2,1)S(1)}, bf16[2,96,256]{2,1,0:T(8,128)(2,1)S(1)}, u32[]{:S(2)}, u32[]{:S(2)}) collective-permute-start(bf16[2,96,256]{2,1,0:T(8,128)(2,1)S(1)} %get-tuple-element.223), channel_id=1, source_target_pairs={{0,4},{4,0},{8,12},{12,8},{16,20},{20,16},{24,28},{28,24},{1,5},{5... | collective-permute-start | bytes 294920 | tf_op jit(solution)/shard_map/ppermute | solution.py:605
  121.7 7.9 %collective-permute-start.42 = (bf16[1,576,256]{2,1,0:T(8,128)(2,1)S(1)}, bf16[1,576,256]{2,1,0:T(8,128)(2,1)S(1)}, u32[]{:S(2)}, u32[]{:S(2)}) collective-permute-start(bf16[1,576,256]{2,1,0:T(8,128)(2,1)S(1)} %get-tuple-element.237.refs_1_), channel_id=1, source_target_pairs={{0,2},{1,3},{2,0},{3,1},{4,6},{5,7},{6,4},{7,5},{8,10},{9,11},{10,... | collective-permute-start | bytes 884744 | tf_op jit(solution)/shard_map/ppermute | solution.py:605
  125.9 8.8 %collective-permute-start.37 = (bf16[1,304,256]{2,1,0:T(8,128)(2,1)S(1)}, bf16[1,304,256]{2,1,0:T(8,128)(2,1)S(1)}, u32[]{:S(2)}, u32[]{:S(2)}) collective-permute-start(bf16[1,304,256]{2,1,0:T(8,128)(2,1)S(1)} %get-tuple-element.234), channel_id=1, source_target_pairs={{0,16},{4,20},{8,24},{12,28},{16,0},{20,4},{24,8},{28,12},{1,17},{... | collective-permute-start | bytes 466952 | tf_op jit(solution)/shard_map/ppermute | solution.py:605
  128.2 12.3 %collective-permute-start.41 = (bf16[1,576,256]{2,1,0:T(8,128)(2,1)S(1)}, bf16[1,576,256]{2,1,0:T(8,128)(2,1)S(1)}, u32[]{:S(2)}, u32[]{:S(2)}) collective-permute-start(bf16[1,576,256]{2,1,0:T(8,128)(2,1)S(1)} %get-tuple-element.237.refs_1_), channel_id=1, source_target_pairs={{0,1},{1,0},{2,3},{3,2},{4,5},{5,4},{6,7},{7,6},{8,9},{9,8},{10,11... | collective-permute-start | bytes 884744 | tf_op jit(solution)/shard_map/ppermute | solution.py:605
  129.6 10.9 %collective-permute-start.43 = (bf16[1,576,256]{2,1,0:T(8,128)(2,1)S(1)}, bf16[1,576,256]{2,1,0:T(8,128)(2,1)S(1)}, u32[]{:S(2)}, u32[]{:S(2)}) collective-permute-start(bf16[1,576,256]{2,1,0:T(8,128)(2,1)S(1)} %collective-permute-done.42.refs_3_), channel_id=1, source_target_pairs={{0,1},{1,0},{2,3},{3,2},{4,5},{5,4},{6,7},{7,6},{8,9},{9,8},{10,11... | collective-permute-start | bytes 884744 | tf_op jit(solution)/shard_map/ppermute | solution.py:605
  135.2 5.3 %collective-permute-start.39 = (bf16[1,304,256]{2,1,0:T(8,128)(2,1)S(1)}, bf16[1,304,256]{2,1,0:T(8,128)(2,1)S(1)}, u32[]{:S(2)}, u32[]{:S(2)}) collective-permute-start(bf16[1,304,256]{2,1,0:T(8,128)(2,1)S(1)} %get-tuple-element.236.refs_1_), channel_id=1, source_target_pairs={{0,2},{1,3},{2,0},{3,1},{4,6},{5,7},{6,4},{7,5},{8,10},{9,11},{10,... | collective-permute-start | bytes 466952 | tf_op jit(solution)/shard_map/ppermute | solution.py:605
  136.8 6.0 %collective-permute-start.38 = (bf16[1,304,256]{2,1,0:T(8,128)(2,1)S(1)}, bf16[1,304,256]{2,1,0:T(8,128)(2,1)S(1)}, u32[]{:S(2)}, u32[]{:S(2)}) collective-permute-start(bf16[1,304,256]{2,1,0:T(8,128)(2,1)S(1)} %get-tuple-element.236.refs_1_), channel_id=1, source_target_pairs={{0,1},{1,0},{2,3},{3,2},{4,5},{5,4},{6,7},{7,6},{8,9},{9,8},{10,11... | collective-permute-start | bytes 466952 | tf_op jit(solution)/shard_map/ppermute | solution.py:605
  140.5 2.3 %collective-permute-start.40 = (bf16[1,304,256]{2,1,0:T(8,128)(2,1)S(1)}, bf16[1,304,256]{2,1,0:T(8,128)(2,1)S(1)}, u32[]{:S(2)}, u32[]{:S(2)}) collective-permute-start(bf16[1,304,256]{2,1,0:T(8,128)(2,1)S(1)} %collective-permute-done.39.refs_3_), channel_id=1, source_target_pairs={{0,1},{1,0},{2,3},{3,2},{4,5},{5,4},{6,7},{7,6},{8,9},{9,8},{10,11... | collective-permute-start | bytes 466952 | tf_op jit(solution)/shard_map/ppermute | solution.py:605
  (12 other events, 29.2 us)

commit v6 on v5

--- a/solution.py
+++ b/solution.py
@@ -25,7 +25,7 @@
 WEIGHTS = {
     "prepare": 60 * 10**9, "attend": 60 * 10**9, "feed": 60 * 10**9, "grad_up": 60 * 10**9,
     "grad_down": 60 * 10**9, "attend_back": 60 * 10**9, "grad_tokens": 60 * 10**8,
-    "halve": 200 * 10**7, "cut_units": 200 * 10**7, "place_feed": 200 * 10**7,
+    "halve": 200 * 10**7, "cut_units": 200 * 10**7, "place_all": 200 * 10**7,
 }
 
 
@@ -108,19 +108,17 @@
 
 
 def prepare_kernel(
-    row_ref, b0, b1, b2, b3, b4, b5, b6, b7, w_qkv, w_out, qkv_near, out_near, mask, vectors, sems,
-    *, pages, slots,
+    row_ref, w_qkv, w_out, b0, b1, b2, b3, b4, b5, b6, b7,
+    qkv_near, out_near, mask, vectors, s0, s1, s2, s3, s4, s5, s6, s7, sems, *, pages, slots,
 ):
+    pairs = zip((b0, b1, b2, b3, b4, b5, b6, b7), (s0, s1, s2, s3, s4, s5, s6, s7))
+    loads = [copy(a, b, sems.at[2 + i]) for i, (a, b) in enumerate(pairs)]
+    for one in loads:
+        one.start()
     load_qkv = copy(w_qkv, qkv_near, sems.at[0])
     load_qkv.start()
     load_out = copy(w_out, out_near, sems.at[1])
     load_out.start()
-    width = vectors.shape[1]
-    row = 0
-    for part in (b0, b1, b2, b3, b4, b5, b6, b7):
-        for i in range(part.shape[0] // width):
-            vectors[row : row + 1, :] = part[i * width : (i + 1) * width].reshape(1, width)
-            row += 1
     count = mask.shape[0]
     position = row_ref[pages]
 
@@ -137,6 +135,14 @@
     mask[...] = jnp.where(
         page_of((count, count), 0) == page_of((1, count), 1), 0.0, MASKED
     )
+    for one in loads:
+        one.wait()
+    width = vectors.shape[1]
+    row = 0
+    for part in (s0, s1, s2, s3, s4, s5, s6, s7):
+        for i in range(part.shape[0] // width):
+            vectors[row : row + 1, :] = part[i * width : (i + 1) * width].reshape(1, width)
+            row += 1
     load_qkv.wait()
     load_out.wait()
 
@@ -146,13 +152,14 @@
     rows = sum(b.shape[0] for b in biases) // width
     return call(
         functools.partial(prepare_kernel, pages=row.shape[0] - 1, slots=slots),
-        "prepare", [row], biases,
+        "prepare", [row], [],
         [
             shape(*w_qkv.shape), shape(*w_out.shape), shape(count, count, dtype=f32),
             shape(rows, width, dtype=f32),
         ],
-        far=[w_qkv, w_out], copies=2,
-    )[:4]
+        [pltpu.VMEM(b.shape, f32) for b in biases],
+        far=[w_qkv, w_out, *biases], copies=2 + len(biases),
+    )
 
 
 def attend_kernel(
@@ -369,6 +376,8 @@
 
 
 def place_rows(place, blocks, rows, sems):
+    if len(blocks[2].shape) == 3:
+        blocks = (*blocks[:2], blocks[2].at[0], blocks[3].at[1])
     copies = [copy(block, rows.at[place[1] ^ i], sems.at[i]) for i, block in enumerate(blocks)]
     for one in copies:
         one.start()
@@ -585,17 +594,18 @@
     return [keep_0, keep_1, keep_2], [send_0, send_1, send_2], small, grads, mark
 
 
-def grad_tokens_kernel(grads, w_qkv, sum_one, r0, r1, r2, r3):
+def grad_tokens_kernel(grads, w_qkv, sum_one, own, beside, across):
     result = (sum_one[...] + dot(grads[...], w_qkv[...], NT)).astype(bf16)
-    slots = r0.shape[0]
-    for i, block in enumerate((r0, r1, r2, r3)):
+    slots = own.shape[0]
+    for i, block in enumerate((own, beside, across.at[0], across.at[1])):
         block[...] = result[i * slots : (i + 1) * slots, :]
 
 
 def grad_tokens(sum_one, grads, w_qkv, slots, after):
     count, width = sum_one.shape
     *blocks, mark = call(
-        grad_tokens_kernel, "grad_tokens", [], [grads, w_qkv, sum_one], [shape(slots, width)] * 4,
+        grad_tokens_kernel, "grad_tokens", [], [grads, w_qkv, sum_one],
+        [shape(slots, width)] * 2 + [shape(2, slots, width)],
         room=12, after=after,
     )
     return blocks, mark
@@ -733,10 +743,10 @@
         self.stage += 1
         return (mark, *rows) if rows else mark
 
-    def finish(self, after):
-        (own,), _, mark = halve(self.bits, self.pairs, None, False, after)
+    def finish(self, after, place=None, blocks=()):
+        (own,), _, mark, *rows = halve(self.bits, self.pairs, None, False, after, place, blocks)
         across = swap(own, "blk", 2)
-        return (own, swap(own, "blk", 1), across, swap(across, "blk", 1)), mark
+        return (own, swap(own, "blk", 1), across, swap(across, "blk", 1)), mark, *rows
 
 
 def chosen(place, b, refs):
@@ -749,47 +759,35 @@
     ).astype(f32)
 
 
-def place_feed(place, pieces, rows, after):
-    size = pieces[0].shape[2]
+def place_all(place, feed_pieces, own_pieces, rows, shares, blocks, after):
+    size = own_pieces[0].shape[2]
     width = 3 * size
-
-    def kernel(place_ref, p0, p1, p2, p3, down, up):
+    share = width // shares
+    extra = own_pieces[0].shape[1] - 3 * rows
+    count = 8 + len(blocks)
+
+    def kernel(place_ref, *refs):
+        feed_refs, own_refs = refs[:4], refs[4:8]
+        down, up, qkv, out, bias_qv, bias_out, gain_one, shift_one, bias_up, bias_down, gain_two, shift_two = (
+            refs[count : count + 12]
+        )
+        copies = place_rows(place_ref, refs[8:12], refs[count + 12], refs[-1]) if blocks else []
         for b in range(4):
             for s in range(3):
+                columns = slice(s * size, (s + 1) * size)
+                wider = slice(b * width + s * size, b * width + (s + 1) * size)
                 at = 2 * s * rows
-                columns = slice(s * size, (s + 1) * size)
-                value = chosen(place_ref, b, [p.at[0, at : at + rows] for p in (p0, p1, p2, p3)])
+                value = chosen(place_ref, b, [p.at[0, at : at + rows] for p in feed_refs])
                 down[b * rows : (b + 1) * rows, columns] = value
                 at = at + rows
-                columns = slice(b * width + s * size, b * width + (s + 1) * size)
-                value = chosen(place_ref, b, [p.at[0, at : at + rows] for p in (p0, p1, p2, p3)])
-                up[:, columns] = value
-
-    return call(
-        kernel, "place_feed", [place], pieces,
-        [shape(4 * rows, width, dtype=f32), shape(rows, 4 * width, dtype=f32)], after=after,
-    )
-
-
-def place_own(place, pieces, rows, shares, after):
-    size = pieces[0].shape[2]
-    width = 3 * size
-    share = width // shares
-    extra = pieces[0].shape[1] - 3 * rows
-
-    def kernel(place_ref, p0, p1, p2, p3, qkv, out, *small):
-        refs = (p0, p1, p2, p3)
-        bias_qv, bias_out, gain_one, shift_one, bias_up, bias_down, gain_two, shift_two = small
-        for b in range(4):
-            for s in range(3):
+                up[:, wider] = chosen(place_ref, b, [p.at[0, at : at + rows] for p in feed_refs])
                 at = s * rows + (extra if s else 0)
-                value = chosen(place_ref, b, [p.at[0, at : at + rows] for p in refs])
-                columns = slice(s * size, (s + 1) * size)
+                value = chosen(place_ref, b, [p.at[0, at : at + rows] for p in own_refs])
                 if b == 3:
                     out[:, columns] = value
                 else:
-                    qkv[:, b * width + s * size : b * width + (s + 1) * size] = value
-            value = chosen(place_ref, b, [p.at[0, rows : rows + extra] for p in refs])
+                    qkv[:, wider] = value
+            value = chosen(place_ref, b, [p.at[0, rows : rows + extra] for p in own_refs])
             targets = (
                 ((bias_qv, 0), (bias_qv, 1), (bias_out, 0)),
                 ((gain_one, 0), (shift_one, 0), (bias_down, 0)),
@@ -797,14 +795,19 @@
                 ((bias_up, 1), (bias_up, 2), (bias_up, 3)),
             )[b]
             for j, (ref, part) in enumerate(targets):
-                ref[:, part * share : (part + 1) * share] = value[j : j + 1, 0:share]
-
-    vectors = [shape(1, n * share, dtype=f32) for n in (2, 1, 1, 1, 4, 1, 1, 1)]
+                ref[part * share : (part + 1) * share] = value[j, 0:share]
+        for one in copies:
+            one.wait()
+
+    vectors = [shape(n * share, dtype=f32) for n in (2, 1, 1, 1, 4, 1, 1, 1)]
     return call(
-        kernel, "place_own", [place], pieces,
-        [shape(rows, 3 * width, dtype=f32), shape(rows, width, dtype=f32), *vectors],
-        after=after,
-    )[:10]
+        kernel, "place_all", [place], [*feed_pieces, *own_pieces, *blocks],
+        [
+            shape(4 * rows, width, dtype=f32), shape(rows, 4 * width, dtype=f32),
+            shape(rows, 3 * width, dtype=f32), shape(rows, width, dtype=f32), *vectors,
+        ],
+        far_outs=[shape(4, *blocks[0].shape)] if blocks else [], copies=len(blocks), room=16, after=after,
+    )[:-1]
 
 
 def shards(
@@ -828,6 +831,11 @@
     def in_order(blocks):
         return [blocks[0], blocks[3], blocks[1], blocks[2]]
 
+    def scatter_pairs(blocks):
+        own, beside, pair = blocks
+        arrived = swap(pair, "blk", 2)
+        return [own, swap(beside, "blk", 1), arrived, swap(arrived, "blk", 1)]
+
     def scatter_row(blocks):
         return [blocks[0]] + [swap(blocks[i], "blk", i) for i in range(1, rows)]
 
@@ -835,13 +843,12 @@
         bias_qv, bias_out, norm1_gain, norm1_bias, bias_down, norm2_gain, norm2_bias, bias_up
     ]
     row = jnp.concatenate([pick(lengths, position), position[None]])
-    blocks = gather_row(tokens)
-    blocks, cotangent = lax.optimization_barrier((blocks, cotangent))
-    blocks = in_order(blocks)
+    blocks = in_order(gather_row(tokens))
+    qkv_near, out_near, mask, vectors, mark = prepare(
+        row, biases, w_qkv, w_out, slots, rows * slots
+    )
+    cotangent, _ = lax.optimization_barrier((cotangent, blocks[1]))
     cotangents = in_order(gather_row(cotangent))
-    qkv_near, out_near, mask, vectors = prepare(
-        row, biases, w_qkv, w_out, slots, rows * slots
-    )
     normed, inverse, q, k, v, prob, context, row_tokens = attend(
         blocks, vectors, qkv_near, out_near, mask
     )
@@ -889,28 +896,27 @@
     mark = feed_group.step([mark])
     mark = own_group.step([mark])
     feed_pieces, mark = feed_group.finish([mark])
-    mark, token_grads = own_group.step([mark], place, scatter_row(tokens_parts))
+    mark = own_group.step([mark])
     own_pieces, mark = own_group.finish([mark])
-    down, up, mark = place_feed(place, feed_pieces, share, [mark])
     (
-        grad_w_qkv, grad_w_out, sum_qv, sum_out, sum_gain_one, sum_shift_one, sum_up, sum_down,
-        sum_gain_two, sum_shift_two,
-    ) = place_own(place, own_pieces, share, shares, [mark])
+        down, up, grad_w_qkv, grad_w_out, sum_qv, sum_out, sum_gain_one, sum_shift_one, sum_up, sum_down,
+        sum_gain_two, sum_shift_two, token_grads,
+    ) = place_all(place, feed_pieces, own_pieces, share, shares, scatter_pairs(tokens_parts), [mark])
     return (
         outputs,
         token_grads,
         grad_w_qkv,
-        sum_qv.reshape(-1),
+        sum_qv,
         grad_w_out,
-        sum_out.reshape(-1),
-        sum_gain_one.reshape(-1),
-        sum_shift_one.reshape(-1),
+        sum_out,
+        sum_gain_one,
+        sum_shift_one,
         up,
-        sum_up.reshape(-1),
+        sum_up,
         down,
-        sum_down.reshape(-1),
-        sum_gain_two.reshape(-1),
-        sum_shift_two.reshape(-1),
+        sum_down,
+        sum_gain_two,
+        sum_shift_two,
     )
 
 

time: 146 us -> 139 us (0.952)
  local copies, waits for them, and re-layouts: 6.92 us -> 1.39 us
  starting transfers between devices: 39.2 us -> 41.2 us
    unnamed x32 -> x16, local copies, waits for them, and re-layouts: 5.57 us -> 0.04 us
    ppermute x44, starting transfers between devices: 39.2 us -> 41.2 us  [swap(): lax.ppermute(block, axis, [(i, i ^ bit) for i in range(lax.axis_size(axis...]
    pallas_call x21 -> x20, Pallas kernels: 67.1 us -> 65.9 us  [call(): pl.pallas_call(body, in_specs=[SMEM] * len(scalars) + [VMEM] * len(arrays...]
  transfers between devices with their start and end apart: 44 -> 44, of which waited for: 13 -> 14; matrix products, arithmetic and copies ran while one was open for 0% -> 0% of each run, Pallas kernels for 38% -> 38%
where the time goes in v6:
time: 139 us
  Pallas kernels  65.9 us (47%)
  starting transfers between devices  41.2 us (30%)
  waiting for transfers between devices  28.9 us (21%)
    pallas_call x20, Pallas kernels, call(): pl.pallas_call(body, in_specs=[SMEM] * len(scalars) + [VMEM] * len(arrays...  65.9 us
    ppermute x44, starting transfers between devices, swap(): lax.ppermute(block, axis, [(i, i ^ bit) for i in range(lax.axis_size(axis...  41.2 us
    ppermute x44, waiting for transfers between devices, swap(): lax.ppermute(block, axis, [(i, i ^ bit) for i in range(lax.axis_size(axis...  28.9 us
  transfers between devices with their start and end apart: 44, of which 14 were waited for; matrix products, arithmetic and copies ran while one was open for 0% of the time, Pallas kernels for 38%

profile of v6, /device:TPU:0, one launch (start us, length us, event | category | flops | bytes accessed | tf_op | source)
XLA Modules:
  0.0 138.7 jit_solution(11699573871769679861)
XLA Ops:
  0.7 1.3 dynamic-slice_bitcast_fusion.4
  2.5 2.6 %collective-permute-start.1 = (bf16[128,768]{1,0:T(8,128)(2,1)S(1)}, bf16[128,768]{1,0:T(8,128)(2,1)S(1)}, u32[]{:S(2)}, u32[]{:S(2)}) collective-permute-start(bf16[128,768]{1,0:T(8,128)(2,1)S(1)} %get-tuple-element.247), channel_id=1, source_target_pairs={{0,2},{1,3},{2,0},{3,1},{4,6},{5,7},{6,4},{7,5},{8,10},{9,11},{10,... | collective-permute-start | bytes 589832 | tf_op jit(solution)/shard_map/ppermute | solution.py:615
  5.2 3.9 %prepare.1 = (bf16[768,2304]{1,0:T(8,128)(2,1)S(1)}, bf16[768,768]{1,0:T(8,128)(2,1)S(1)}, f32[512,512]{1,0:T(8,128)S(1)}, f32[12,768]{1,0:T(8,128)S(1)}, f32[8,128]{1,0:T(8,128)}) custom-call(s32[9]{0:T(128)S(1)} %pad_add_fusion.1.refs_0_, bf16[768,2304]{1,0:T(8,128)(2,1)} %refs_1_.3, bf16[768,768]{1,0:T(8,128)(2,1)} %refs_11_.1, f32[1536]{0:T(1024)} %refs_3_.1, ...), custom_call_target="tpu_custom_call" | custom-call | flops 60000002048 | tf_op jit(solution)/shard_map/prepare/pallas_call | solution.py:51
  9.6 1.9 %collective-permute-start.4 = (bf16[128,768]{1,0:T(8,128)(2,1)S(1)}, bf16[128,768]{1,0:T(8,128)(2,1)S(1)}, u32[]{:S(2)}, u32[]{:S(2)}) collective-permute-start(bf16[128,768]{1,0:T(8,128)(2,1)S(1)} %get-tuple-element.241), channel_id=1, source_target_pairs={{0,2},{1,3},{2,0},{3,1},{4,6},{5,7},{6,4},{7,5},{8,10},{9,11},{10,... | collective-permute-start | bytes 589832 | tf_op jit(solution)/shard_map/ppermute | solution.py:615
  11.6 2.9 %collective-permute-done.2.refs_3_ = bf16[128,768]{1,0:T(8,128)(2,1)S(1)} collective-permute-done((bf16[128,768]{1,0:T(8,128)(2,1)S(1)}, bf16[128,768]{1,0:T(8,128)(2,1)S(1)}, u32[]{:S(2)}, u32[]{:S(2)}) %collective-permute-start.2) | collective-permute-done | bytes 196640 | tf_op jit(solution)/shard_map/ppermute | solution.py:615
  14.5 11.1 %attend.1 = (f32[512,768]{1,0:T(8,128)S(1)}, f32[512,1]{1,0:T(8,128)S(1)}, bf16[512,768]{1,0:T(8,128)(2,1)}, bf16[512,768]{1,0:T(8,128)(2,1)}, bf16[512,768]{1,0...) custom-call(bf16[128,768]{1,0:T(8,128)(2,1)S(1)} %get-tuple-element., ...), custom_call_target="tpu_custom_call" | custom-call | flops 60000002048 | tf_op jit(solution)/shard_map/attend/pallas_call | solution.py:51
  25.7 8.9 %feed.1 = (bf16[2,8,96,512]{3,2,1,0:T(8,128)(2,1)S(1)}, bf16[2,8,96,512]{3,2,1,0:T(8,128)(2,1)S(1)}, bf16[512,3072]{1,0:T(8,128)(2,1)S(1)}, bf16[512,768]{1,0:T(...) custom-call(s32[2]{0:T(128)S(1)} %pad_add_fusion.refs_0_, ...), custom_call_target="tpu_custom_call" | custom-call | flops 60000002048 | tf_op jit(solution)/shard_map/feed/pallas_call | solution.py:51
  35.1 1.9 %collective-permute-start.10 = (bf16[128,768]{1,0:T(8,128)(2,1)S(1)}, bf16[128,768]{1,0:T(8,128)(2,1)S(1)}, u32[]{:S(2)}, u32[]{:S(2)}) collective-permute-start(bf16[128,768]{1,0:T(8,128)(2,1)S(1)} %get-tuple-element.139), channel_id=1, source_target_pairs={{0,3},{1,2},{2,1},{3,0},{4,7},{5,6},{6,5},{7,4},{8,11},{9,10},{10,... | collective-permute-start | bytes 589832 | tf_op jit(solution)/shard_map/ppermute | solution.py:615
  37.4 9.8 %grad_up.1 = (bf16[2,768,768]{2,1,0:T(8,128)(2,1)S(1)}, bf16[2,768,768]{2,1,0:T(8,128)(2,1)S(1)}, f32[4,768]{1,0:T(4,128)S(1)}, bf16[512,768]{1,0:T(8,128)(2,1)S...) custom-call(s32[2]{0:T(128)S(1)} %pad_add_fusion.refs_0_, ...), custom_call_target="tpu_custom_call" | custom-call | flops 60000002048 | tf_op jit(solution)/shard_map/grad_up/pallas_call | solution.py:51
  47.5 3.9 %grad_down.1 = (bf16[2,8,96,768]{3,2,1,0:T(8,128)(2,1)S(1)}, bf16[4,128,768]{2,1,0:T(8,128)(2,1)}, f32[8,128]{1,0:T(8,128)S(1)}) custom-call(s32[2]{0:T(128)S(1)} %pad_add_fusion.refs_0_, bf16[2,8,96,512]{3,2,1,0:T(8,128)(2,1)S(1)} %get-tuple-element.133.refs_1_, bf16[2,8,96,512]{3,2,1,0:T(8,128)(2,1)S(1)} %collective-permute-done.6.refs_2_, ...), custom_call_target="tpu_custom_call" | custom-call | flops 60000002048 | tf_op jit(solution)/shard_map/grad_down/pallas_call | solution.py:51
  51.9 0.8 cut_units.4
  52.7 1.7 %collective-permute-start.12 = (bf16[8,192,256]{2,1,0:T(8,128)(2,1)S(1)}, bf16[8,192,256]{2,1,0:T(8,128)(2,1)S(1)}, u32[]{:S(2)}, u32[]{:S(2)}) collective-permute-start(bf16[8,192,256]{2,1,0:T(8,128)(2,1)S(1)} %get-tuple-element.163), channel_id=1, source_target_pairs={{0,2},{1,3},{2,0},{3,1},{4,6},{5,7},{6,4},{7,5},{8,10},{9,11},{10,... | collective-permute-start | bytes 2359304 | tf_op jit(solution)/shard_map/ppermute | solution.py:615
  54.4 1.5 %collective-permute-start.13 = (bf16[8,192,256]{2,1,0:T(8,128)(2,1)S(1)}, bf16[8,192,256]{2,1,0:T(8,128)(2,1)S(1)}, u32[]{:S(2)}, u32[]{:S(2)}) collective-permute-start(bf16[8,192,256]{2,1,0:T(8,128)(2,1)S(1)} %get-tuple-element.165), channel_id=1, source_target_pairs={{0,4},{4,0},{8,12},{12,8},{16,20},{20,16},{24,28},{28,24},{1,5},{5... | collective-permute-start | bytes 2359304 | tf_op jit(solution)/shard_map/ppermute | solution.py:615
  55.9 1.6 %collective-permute-start.14 = (bf16[8,192,256]{2,1,0:T(8,128)(2,1)S(1)}, bf16[8,192,256]{2,1,0:T(8,128)(2,1)S(1)}, u32[]{:S(2)}, u32[]{:S(2)}) collective-permute-start(bf16[8,192,256]{2,1,0:T(8,128)(2,1)S(1)} %get-tuple-element.167), channel_id=1, source_target_pairs={{0,8},{4,12},{8,0},{12,4},{16,24},{20,28},{24,16},{28,20},{1,9},{5... | collective-permute-start | bytes 2359304 | tf_op jit(solution)/shard_map/ppermute | solution.py:615
  57.5 14.8 %attend_back.1 = (bf16[512,2304]{1,0:T(8,128)(2,1)S(1)}, bf16[2,8,112,256]{3,2,1,0:T(8,128)(2,1)S(1)}, bf16[2,768,256]{2,1,0:T(8,128)(2,1)S(1)}, bf16[2,768,256]...) custom-call(s32[2]{0:T(128)S(1)} %pad_add_fusion.refs_0_, ...), custom_call_target="tpu_custom_call" | custom-call | flops 60000002048 | tf_op jit(solution)/shard_map/attend_back/pallas_call | solution.py:51
  72.9 0.8 cut_units.5
  73.8 1.2 collective-permute-done.14.refs_6_
  75.0 0.8 halve.8
  76.4 1.6 %collective-permute-start.16 = (bf16[4,192,256]{2,1,0:T(8,128)(2,1)S(1)}, bf16[4,192,256]{2,1,0:T(8,128)(2,1)S(1)}, u32[]{:S(2)}, u32[]{:S(2)}) collective-permute-start(bf16[4,192,256]{2,1,0:T(8,128)(2,1)S(1)} %get-tuple-element.172), channel_id=1, source_target_pairs={{0,8},{4,12},{8,0},{12,4},{16,24},{20,28},{24,16},{28,20},{1,9},{5... | collective-permute-start | bytes 1179656 | tf_op jit(solution)/shard_map/ppermute | solution.py:615
  77.9 0.9 collective-permute-start.17
  78.8 0.7 cut_units.6
  79.5 1.2 collective-permute-start.24
  80.7 1.5 %collective-permute-start.25 = (bf16[8,96,256]{2,1,0:T(8,128)(2,1)S(1)}, bf16[8,96,256]{2,1,0:T(8,128)(2,1)S(1)}, u32[]{:S(2)}, u32[]{:S(2)}) collective-permute-start(bf16[8,96,256]{2,1,0:T(8,128)(2,1)S(1)} %get-tuple-element.196), channel_id=1, source_target_pairs={{0,4},{4,0},{8,12},{12,8},{16,20},{20,16},{24,28},{28,24},{1,5},{5... | collective-permute-start | bytes 1179656 | tf_op jit(solution)/shard_map/ppermute | solution.py:615
  82.3 5.6 %collective-permute-done.15.refs_2_ = bf16[4,192,256]{2,1,0:T(8,128)(2,1)S(1)} collective-permute-done((bf16[4,192,256]{2,1,0:T(8,128)(2,1)S(1)}, bf16[4,192,256]{2,1,0:T(8,128)(2,1)S(1)}, u32[]{:S(2)}, u32[]{:S(2)}) %collective-permute-start.15) | collective-permute-done | bytes 393248 | tf_op jit(solution)/shard_map/ppermute | solution.py:615
  87.9 1.6 %collective-permute-start.26 = (bf16[8,96,256]{2,1,0:T(8,128)(2,1)S(1)}, bf16[8,96,256]{2,1,0:T(8,128)(2,1)S(1)}, u32[]{:S(2)}, u32[]{:S(2)}) collective-permute-start(bf16[8,96,256]{2,1,0:T(8,128)(2,1)S(1)} %get-tuple-element.198), channel_id=1, source_target_pairs={{0,8},{4,12},{8,0},{12,4},{16,24},{20,28},{24,16},{28,20},{1,9},{5... | collective-permute-start | bytes 1179656 | tf_op jit(solution)/shard_map/ppermute | solution.py:615
  89.5 2.0 %grad_tokens.1 = (bf16[128,768]{1,0:T(8,128)(2,1)S(1)}, bf16[128,768]{1,0:T(8,128)(2,1)S(1)}, bf16[2,128,768]{2,1,0:T(8,128)(2,1)S(1)}, f32[8,128]{1,0:T(8,128)S(1)}) custom-call(bf16[512,2304]{1,0:T(8,128)(2,1)S(1)} %get-tuple-element.181.refs_0_, bf16[768,2304]{1,0:T(8,128)(2,1)S(1)} %copy-done.2, f32[512,768]{1,0:T(8,128)S(1)} %get-tuple-element.182.refs_2_, ...), custom_call_target="tpu_custom_call" | custom-call | flops 6000000000 | tf_op jit(solution)/shard_map/grad_tokens/pallas_call | solution.py:51
  91.5 0.7 cut_units.7
  92.2 0.7 halve.9
  94.5 1.2 collective-permute-start.23
  95.7 1.9 %collective-permute-done.26.refs_6_ = bf16[8,96,256]{2,1,0:T(8,128)(2,1)S(1)} collective-permute-done((bf16[8,96,256]{2,1,0:T(8,128)(2,1)S(1)}, bf16[8,96,256]{2,1,0:T(8,128)(2,1)S(1)}, u32[]{:S(2)}, u32[]{:S(2)}) %collective-permute-start.26) | collective-permute-done | bytes 393248 | tf_op jit(solution)/shard_map/ppermute | solution.py:615
  97.6 2.3 %collective-permute-done.24.refs_2_ = bf16[8,112,256]{2,1,0:T(8,128)(2,1)S(1)} collective-permute-done((bf16[8,112,256]{2,1,0:T(8,128)(2,1)S(1)}, bf16[8,112,256]{2,1,0:T(8,128)(2,1)S(1)}, u32[]{:S(2)}, u32[]{:S(2)}) %collective-permute-start.24) | collective-permute-done | bytes 458784 | tf_op jit(solution)/shard_map/ppermute | solution.py:615
  99.8 0.7 halve.10
  100.5 1.0 collective-permute-start.28
  101.5 0.8 collective-permute-start.29
  102.2 1.3 collective-permute-start.30
  104.7 2.7 %collective-permute-start.27 = (bf16[1,576,256]{2,1,0:T(8,128)(2,1)S(1)}, bf16[1,576,256]{2,1,0:T(8,128)(2,1)S(1)}, u32[]{:S(2)}, u32[]{:S(2)}) collective-permute-start(bf16[1,576,256]{2,1,0:T(8,128)(2,1)S(1)} %get-tuple-element.202), channel_id=1, source_target_pairs={{0,16},{4,20},{8,24},{12,28},{16,0},{20,4},{24,8},{28,12},{1,17},{... | collective-permute-start | bytes 884744 | tf_op jit(solution)/shard_map/ppermute | solution.py:615
  107.3 0.8 collective-permute-start.42
  108.1 0.9 collective-permute-done.30.refs_6_
  109.7 2.1 %collective-permute-start.34 = (bf16[2,112,256]{2,1,0:T(8,128)(2,1)S(1)}, bf16[2,112,256]{2,1,0:T(8,128)(2,1)S(1)}, u32[]{:S(2)}, u32[]{:S(2)}) collective-permute-start(bf16[2,112,256]{2,1,0:T(8,128)(2,1)S(1)} %get-tuple-element.213), channel_id=1, source_target_pairs={{0,8},{4,12},{8,0},{12,4},{16,24},{20,28},{24,16},{28,20},{1,9},{5... | collective-permute-start | bytes 344072 | tf_op jit(solution)/shard_map/ppermute | solution.py:615
  112.4 2.4 %collective-permute-start.36 = (bf16[2,96,256]{2,1,0:T(8,128)(2,1)S(1)}, bf16[2,96,256]{2,1,0:T(8,128)(2,1)S(1)}, u32[]{:S(2)}, u32[]{:S(2)}) collective-permute-start(bf16[2,96,256]{2,1,0:T(8,128)(2,1)S(1)} %get-tuple-element.217), channel_id=1, source_target_pairs={{0,4},{4,0},{8,12},{12,8},{16,20},{20,16},{24,28},{28,24},{1,5},{5... | collective-permute-start | bytes 294920 | tf_op jit(solution)/shard_map/ppermute | solution.py:615
  114.8 2.7 %collective-permute-done.27.refs_2_ = bf16[1,576,256]{2,1,0:T(8,128)(2,1)S(1)} collective-permute-done((bf16[1,576,256]{2,1,0:T(8,128)(2,1)S(1)}, bf16[1,576,256]{2,1,0:T(8,128)(2,1)S(1)}, u32[]{:S(2)}, u32[]{:S(2)}) %collective-permute-start.27) | collective-permute-done | bytes 294944 | tf_op jit(solution)/shard_map/ppermute | solution.py:615
  119.0 2.0 %collective-permute-start.37 = (bf16[1,304,256]{2,1,0:T(8,128)(2,1)S(1)}, bf16[1,304,256]{2,1,0:T(8,128)(2,1)S(1)}, u32[]{:S(2)}, u32[]{:S(2)}) collective-permute-start(bf16[1,304,256]{2,1,0:T(8,128)(2,1)S(1)} %get-tuple-element.220), channel_id=1, source_target_pairs={{0,16},{4,20},{8,24},{12,28},{16,0},{20,4},{24,8},{28,12},{1,17},{... | collective-permute-start | bytes 466952 | tf_op jit(solution)/shard_map/ppermute | solution.py:615
  121.0 1.2 collective-permute-start.32
  122.8 4.9 %collective-permute-done.37.refs_2_ = bf16[1,304,256]{2,1,0:T(8,128)(2,1)S(1)} collective-permute-done((bf16[1,304,256]{2,1,0:T(8,128)(2,1)S(1)}, bf16[1,304,256]{2,1,0:T(8,128)(2,1)S(1)}, u32[]{:S(2)}, u32[]{:S(2)}) %collective-permute-start.37) | collective-permute-done | bytes 155680 | tf_op jit(solution)/shard_map/ppermute | solution.py:615
  128.3 2.1 %collective-permute-start.39 = (bf16[1,304,256]{2,1,0:T(8,128)(2,1)S(1)}, bf16[1,304,256]{2,1,0:T(8,128)(2,1)S(1)}, u32[]{:S(2)}, u32[]{:S(2)}) collective-permute-start(bf16[1,304,256]{2,1,0:T(8,128)(2,1)S(1)} %get-tuple-element.222.refs_5_), channel_id=1, source_target_pairs={{0,2},{1,3},{2,0},{3,1},{4,6},{5,7},{6,4},{7,5},{8,10},{9,11},{10,... | collective-permute-start | bytes 466952 | tf_op jit(solution)/shard_map/ppermute | solution.py:615
  130.9 3.0 %collective-permute-done.39.refs_7_ = bf16[1,304,256]{2,1,0:T(8,128)(2,1)S(1)} collective-permute-done((bf16[1,304,256]{2,1,0:T(8,128)(2,1)S(1)}, bf16[1,304,256]{2,1,0:T(8,128)(2,1)S(1)}, u32[]{:S(2)}, u32[]{:S(2)}) %collective-permute-start.39) | collective-permute-done | bytes 155680 | tf_op jit(solution)/shard_map/ppermute | solution.py:615
  133.9 1.4 collective-permute-done.40.refs_8_
  135.3 3.3 %place_all.1 = (f32[384,768]{1,0:T(8,128)}, f32[96,3072]{1,0:T(8,128)}, f32[96,2304]{1,0:T(8,128)}, f32[96,768]{1,0:T(8,128)}, f32[192]{0:T(256)}, /*index=5*/f3...) custom-call(s32[2]{0:T(128)S(1)} %pad_add_fusion.refs_0_, ...), custom_call_target="tpu_custom_call" | custom-call | flops 2000000000 | tf_op jit(solution)/shard_map/place_all/pallas_call | solution.py:51
  (84 shorter events, 11.1 us)
Async XLA Ops:
  2.0 7.4 %collective-permute-start = (bf16[128,768]{1,0:T(8,128)(2,1)S(1)}, bf16[128,768]{1,0:T(8,128)(2,1)S(1)}, u32[]{:S(2)}, u32[]{:S(2)}) collective-permute-start(bf16[128,768]{1,0:T(8,128)(2,1)S(1)} %get-tuple-element.245), channel_id=1, source_target_pairs={{0,1},{1,0},{2,3},{3,2},{4,5},{5,4},{6,7},{7,6},{8,9},{9,8},{10,11... | collective-permute-start | bytes 589832 | tf_op jit(solution)/shard_map/ppermute | solution.py:615
  2.5 9.1 %collective-permute-start.1 = (bf16[128,768]{1,0:T(8,128)(2,1)S(1)}, bf16[128,768]{1,0:T(8,128)(2,1)S(1)}, u32[]{:S(2)}, u32[]{:S(2)}) collective-permute-start(bf16[128,768]{1,0:T(8,128)(2,1)S(1)} %get-tuple-element.247), channel_id=1, source_target_pairs={{0,2},{1,3},{2,0},{3,1},{4,6},{5,7},{6,4},{7,5},{8,10},{9,11},{10,... | collective-permute-start | bytes 589832 | tf_op jit(solution)/shard_map/ppermute | solution.py:615
  5.0 9.4 %collective-permute-start.2 = (bf16[128,768]{1,0:T(8,128)(2,1)S(1)}, bf16[128,768]{1,0:T(8,128)(2,1)S(1)}, u32[]{:S(2)}, u32[]{:S(2)}) collective-permute-start(bf16[128,768]{1,0:T(8,128)(2,1)S(1)} %get-tuple-element.244), channel_id=1, source_target_pairs={{0,3},{1,2},{2,1},{3,0},{4,7},{5,6},{6,5},{7,4},{8,11},{9,10},{10,... | collective-permute-start | bytes 589832 | tf_op jit(solution)/shard_map/ppermute | solution.py:615
  5.2 20.5 %slice-start = ((s8[4718592]{0:T(1024)(128)(4,1)}), s8[4194304]{0:T(1024)(128)(4,1)S(1)}, s32[]{:S(2)}) async-start(s8[4718592]{0:T(1024)(128)(4,1)} %bitcast.33), calls=%async_computation | async-start | bytes 8388608
  5.2 20.5 %slice-start.2 = ((s8[4718592]{0:T(1024)(128)(4,1)}), s8[4194304]{0:T(1024)(128)(4,1)S(1)}, s32[]{:S(2)}) async-start(s8[4718592]{0:T(1024)(128)(4,1)} %bitcast.35), calls=%async_computation.2 | async-start | bytes 8388608
  9.3 16.4 %slice-start.1 = ((s8[4718592]{0:T(1024)(128)(4,1)}), s8[524288]{0:T(1024)(128)(4,1)S(1)}, s32[]{:S(2)}) async-start(s8[4718592]{0:T(1024)(128)(4,1)} %bitcast.33), calls=%async_computation.1 | async-start | bytes 1048576
  9.3 16.4 %slice-start.3 = ((s8[4718592]{0:T(1024)(128)(4,1)}), s8[524288]{0:T(1024)(128)(4,1)S(1)}, s32[]{:S(2)}) async-start(s8[4718592]{0:T(1024)(128)(4,1)} %bitcast.35), calls=%async_computation.3 | async-start | bytes 1048576
  9.4 16.2 %collective-permute-start.3 = (bf16[128,768]{1,0:T(8,128)(2,1)S(1)}, bf16[128,768]{1,0:T(8,128)(2,1)S(1)}, u32[]{:S(2)}, u32[]{:S(2)}) collective-permute-start(bf16[128,768]{1,0:T(8,128)(2,1)S(1)} %get-tuple-element.242), channel_id=1, source_target_pairs={{0,1},{1,0},{2,3},{3,2},{4,5},{5,4},{6,7},{7,6},{8,9},{9,8},{10,11... | collective-permute-start | bytes 589832 | tf_op jit(solution)/shard_map/ppermute | solution.py:615
  9.6 16.1 %collective-permute-start.4 = (bf16[128,768]{1,0:T(8,128)(2,1)S(1)}, bf16[128,768]{1,0:T(8,128)(2,1)S(1)}, u32[]{:S(2)}, u32[]{:S(2)}) collective-permute-start(bf16[128,768]{1,0:T(8,128)(2,1)S(1)} %get-tuple-element.241), channel_id=1, source_target_pairs={{0,2},{1,3},{2,0},{3,1},{4,6},{5,7},{6,4},{7,5},{8,10},{9,11},{10,... | collective-permute-start | bytes 589832 | tf_op jit(solution)/shard_map/ppermute | solution.py:615
  11.5 14.1 %collective-permute-start.5 = (bf16[128,768]{1,0:T(8,128)(2,1)S(1)}, bf16[128,768]{1,0:T(8,128)(2,1)S(1)}, u32[]{:S(2)}, u32[]{:S(2)}) collective-permute-start(bf16[128,768]{1,0:T(8,128)(2,1)S(1)} %get-tuple-element.240), channel_id=1, source_target_pairs={{0,3},{1,2},{2,1},{3,0},{4,7},{5,6},{6,5},{7,4},{8,11},{9,10},{10,... | collective-permute-start | bytes 589832 | tf_op jit(solution)/shard_map/ppermute | solution.py:615
  34.6 12.8 %collective-permute-start.6 = (bf16[2,8,96,512]{3,2,1,0:T(8,128)(2,1)S(1)}, bf16[2,8,96,512]{3,2,1,0:T(8,128)(2,1)S(1)}, u32[]{:S(2)}, u32[]{:S(2)}) collective-permute-start(bf16[2,8,96,512]{3,2,1,0:T(8,128)(2,1)S(1)} %get-tuple-element.134), channel_id=1, source_target_pairs={{0,1},{1,0},{2,3},{3,2},{4,5},{5,4},{6,7},{7,6},{8,9},{9,8},{10,11... | collective-permute-start | bytes 4718600 | tf_op jit(solution)/shard_map/ppermute | solution.py:615
  35.0 12.5 %collective-permute-start.7 = (bf16[512,768]{1,0:T(8,128)(2,1)S(1)}, bf16[512,768]{1,0:T(8,128)(2,1)S(1)}, u32[]{:S(2)}, u32[]{:S(2)}) collective-permute-start(bf16[512,768]{1,0:T(8,128)(2,1)S(1)} %get-tuple-element.135.refs_1_.refs_3_), channel_id=1, source_target_pairs={{0,1},{1,0},{2,3},{3,2},{4,5},{5,4},{6,7},{7,6},{8,9},{9,8},{10,11... | collective-permute-start | bytes 2359304 | tf_op jit(solution)/shard_map/ppermute | solution.py:615
  35.1 12.1 %collective-permute-start.10 = (bf16[128,768]{1,0:T(8,128)(2,1)S(1)}, bf16[128,768]{1,0:T(8,128)(2,1)S(1)}, u32[]{:S(2)}, u32[]{:S(2)}) collective-permute-start(bf16[128,768]{1,0:T(8,128)(2,1)S(1)} %get-tuple-element.139), channel_id=1, source_target_pairs={{0,3},{1,2},{2,1},{3,0},{4,7},{5,6},{6,5},{7,4},{8,11},{9,10},{10,... | collective-permute-start | bytes 589832 | tf_op jit(solution)/shard_map/ppermute | solution.py:615
  37.0 10.4 %collective-permute-start.8 = (bf16[128,768]{1,0:T(8,128)(2,1)S(1)}, bf16[128,768]{1,0:T(8,128)(2,1)S(1)}, u32[]{:S(2)}, u32[]{:S(2)}) collective-permute-start(bf16[128,768]{1,0:T(8,128)(2,1)S(1)} %get-tuple-element.137), channel_id=1, source_target_pairs={{0,1},{1,0},{2,3},{3,2},{4,5},{5,4},{6,7},{7,6},{8,9},{9,8},{10,11... | collective-permute-start | bytes 589832 | tf_op jit(solution)/shard_map/ppermute | solution.py:615
  37.1 10.4 %collective-permute-start.9 = (bf16[128,768]{1,0:T(8,128)(2,1)S(1)}, bf16[128,768]{1,0:T(8,128)(2,1)S(1)}, u32[]{:S(2)}, u32[]{:S(2)}) collective-permute-start(bf16[128,768]{1,0:T(8,128)(2,1)S(1)} %get-tuple-element.138), channel_id=1, source_target_pairs={{0,2},{1,3},{2,0},{3,1},{4,6},{5,7},{6,4},{7,5},{8,10},{9,11},{10,... | collective-permute-start | bytes 589832 | tf_op jit(solution)/shard_map/ppermute | solution.py:615
  47.3 4.6 %collective-permute-start.11 = (bf16[2,768,768]{2,1,0:T(8,128)(2,1)S(1)}, bf16[2,768,768]{2,1,0:T(8,128)(2,1)S(1)}, u32[]{:S(2)}, u32[]{:S(2)}) collective-permute-start(bf16[2,768,768]{2,1,0:T(8,128)(2,1)S(1)} %get-tuple-element.148), channel_id=1, source_target_pairs={{0,1},{1,0},{2,3},{3,2},{4,5},{5,4},{6,7},{7,6},{8,9},{9,8},{10,11... | collective-permute-start | bytes 7077896 | tf_op jit(solution)/shard_map/ppermute | solution.py:615
  52.7 20.2 %collective-permute-start.12 = (bf16[8,192,256]{2,1,0:T(8,128)(2,1)S(1)}, bf16[8,192,256]{2,1,0:T(8,128)(2,1)S(1)}, u32[]{:S(2)}, u32[]{:S(2)}) collective-permute-start(bf16[8,192,256]{2,1,0:T(8,128)(2,1)S(1)} %get-tuple-element.163), channel_id=1, source_target_pairs={{0,2},{1,3},{2,0},{3,1},{4,6},{5,7},{6,4},{7,5},{8,10},{9,11},{10,... | collective-permute-start | bytes 2359304 | tf_op jit(solution)/shard_map/ppermute | solution.py:615
  54.4 19.4 %collective-permute-start.13 = (bf16[8,192,256]{2,1,0:T(8,128)(2,1)S(1)}, bf16[8,192,256]{2,1,0:T(8,128)(2,1)S(1)}, u32[]{:S(2)}, u32[]{:S(2)}) collective-permute-start(bf16[8,192,256]{2,1,0:T(8,128)(2,1)S(1)} %get-tuple-element.165), channel_id=1, source_target_pairs={{0,4},{4,0},{8,12},{12,8},{16,20},{20,16},{24,28},{28,24},{1,5},{5... | collective-permute-start | bytes 2359304 | tf_op jit(solution)/shard_map/ppermute | solution.py:615
  55.9 19.1 %collective-permute-start.14 = (bf16[8,192,256]{2,1,0:T(8,128)(2,1)S(1)}, bf16[8,192,256]{2,1,0:T(8,128)(2,1)S(1)}, u32[]{:S(2)}, u32[]{:S(2)}) collective-permute-start(bf16[8,192,256]{2,1,0:T(8,128)(2,1)S(1)} %get-tuple-element.167), channel_id=1, source_target_pairs={{0,8},{4,12},{8,0},{12,4},{16,24},{20,28},{24,16},{28,20},{1,9},{5... | collective-permute-start | bytes 2359304 | tf_op jit(solution)/shard_map/ppermute | solution.py:615
  72.3 6.6 %collective-permute-start.18 = (bf16[2,8,112,256]{3,2,1,0:T(8,128)(2,1)S(1)}, bf16[2,8,112,256]{3,2,1,0:T(8,128)(2,1)S(1)}, u32[]{:S(2)}, u32[]{:S(2)}) collective-permute-start(bf16[2,8,112,256]{3,2,1,0:T(8,128)(2,1)S(1)} %get-tuple-element.176), channel_id=1, source_target_pairs={{0,1},{1,0},{2,3},{3,2},{4,5},{5,4},{6,7},{7,6},{8,9},{9,8},{10,11... | collective-permute-start | bytes 2752520 | tf_op jit(solution)/shard_map/ppermute | solution.py:615
  72.3 5.6 %collective-permute-start.19 = (bf16[2,768,256]{2,1,0:T(8,128)(2,1)S(1)}, bf16[2,768,256]{2,1,0:T(8,128)(2,1)S(1)}, u32[]{:S(2)}, u32[]{:S(2)}) collective-permute-start(bf16[2,768,256]{2,1,0:T(8,128)(2,1)S(1)} %get-tuple-element.178), channel_id=1, source_target_pairs={{0,1},{1,0},{2,3},{3,2},{4,5},{5,4},{6,7},{7,6},{8,9},{9,8},{10,11... | collective-permute-start | bytes 2359304 | tf_op jit(solution)/shard_map/ppermute | solution.py:615
  72.8 6.0 %collective-permute-start.20 = (bf16[2,768,256]{2,1,0:T(8,128)(2,1)S(1)}, bf16[2,768,256]{2,1,0:T(8,128)(2,1)S(1)}, u32[]{:S(2)}, u32[]{:S(2)}) collective-permute-start(bf16[2,768,256]{2,1,0:T(8,128)(2,1)S(1)} %get-tuple-element.180), channel_id=1, source_target_pairs={{0,1},{1,0},{2,3},{3,2},{4,5},{5,4},{6,7},{7,6},{8,9},{9,8},{10,11... | collective-permute-start | bytes 2359304 | tf_op jit(solution)/shard_map/ppermute | solution.py:615
  75.8 12.1 %collective-permute-start.15 = (bf16[4,192,256]{2,1,0:T(8,128)(2,1)S(1)}, bf16[4,192,256]{2,1,0:T(8,128)(2,1)S(1)}, u32[]{:S(2)}, u32[]{:S(2)}) collective-permute-start(bf16[4,192,256]{2,1,0:T(8,128)(2,1)S(1)} %get-tuple-element.170), channel_id=1, source_target_pairs={{0,4},{4,0},{8,12},{12,8},{16,20},{20,16},{24,28},{28,24},{1,5},{5... | collective-permute-start | bytes 1179656 | tf_op jit(solution)/shard_map/ppermute | solution.py:615
  76.4 15.9 %collective-permute-start.16 = (bf16[4,192,256]{2,1,0:T(8,128)(2,1)S(1)}, bf16[4,192,256]{2,1,0:T(8,128)(2,1)S(1)}, u32[]{:S(2)}, u32[]{:S(2)}) collective-permute-start(bf16[4,192,256]{2,1,0:T(8,128)(2,1)S(1)} %get-tuple-element.172), channel_id=1, source_target_pairs={{0,8},{4,12},{8,0},{12,4},{16,24},{20,28},{24,16},{28,20},{1,9},{5... | collective-permute-start | bytes 1179656 | tf_op jit(solution)/shard_map/ppermute | solution.py:615
  77.9 14.3 %collective-permute-start.17 = (bf16[4,192,256]{2,1,0:T(8,128)(2,1)S(1)}, bf16[4,192,256]{2,1,0:T(8,128)(2,1)S(1)}, u32[]{:S(2)}, u32[]{:S(2)}) collective-permute-start(bf16[4,192,256]{2,1,0:T(8,128)(2,1)S(1)} %get-tuple-element.174), channel_id=1, source_target_pairs={{0,2},{1,3},{2,0},{3,1},{4,6},{5,7},{6,4},{7,5},{8,10},{9,11},{10,... | collective-permute-start | bytes 1179656 | tf_op jit(solution)/shard_map/ppermute | solution.py:615
  79.5 20.3 %collective-permute-start.24 = (bf16[8,112,256]{2,1,0:T(8,128)(2,1)S(1)}, bf16[8,112,256]{2,1,0:T(8,128)(2,1)S(1)}, u32[]{:S(2)}, u32[]{:S(2)}) collective-permute-start(bf16[8,112,256]{2,1,0:T(8,128)(2,1)S(1)} %get-tuple-element.194), channel_id=1, source_target_pairs={{0,2},{1,3},{2,0},{3,1},{4,6},{5,7},{6,4},{7,5},{8,10},{9,11},{10,... | collective-permute-start | bytes 1376264 | tf_op jit(solution)/shard_map/ppermute | solution.py:615
  80.7 13.7 %collective-permute-start.25 = (bf16[8,96,256]{2,1,0:T(8,128)(2,1)S(1)}, bf16[8,96,256]{2,1,0:T(8,128)(2,1)S(1)}, u32[]{:S(2)}, u32[]{:S(2)}) collective-permute-start(bf16[8,96,256]{2,1,0:T(8,128)(2,1)S(1)} %get-tuple-element.196), channel_id=1, source_target_pairs={{0,4},{4,0},{8,12},{12,8},{16,20},{20,16},{24,28},{28,24},{1,5},{5... | collective-permute-start | bytes 1179656 | tf_op jit(solution)/shard_map/ppermute | solution.py:615
  87.9 9.7 %collective-permute-start.26 = (bf16[8,96,256]{2,1,0:T(8,128)(2,1)S(1)}, bf16[8,96,256]{2,1,0:T(8,128)(2,1)S(1)}, u32[]{:S(2)}, u32[]{:S(2)}) collective-permute-start(bf16[8,96,256]{2,1,0:T(8,128)(2,1)S(1)} %get-tuple-element.198), channel_id=1, source_target_pairs={{0,8},{4,12},{8,0},{12,4},{16,24},{20,28},{24,16},{28,20},{1,9},{5... | collective-permute-start | bytes 1179656 | tf_op jit(solution)/shard_map/ppermute | solution.py:615
  92.9 9.3 %collective-permute-start.21 = (bf16[2,192,256]{2,1,0:T(8,128)(2,1)S(1)}, bf16[2,192,256]{2,1,0:T(8,128)(2,1)S(1)}, u32[]{:S(2)}, u32[]{:S(2)}) collective-permute-start(bf16[2,192,256]{2,1,0:T(8,128)(2,1)S(1)} %get-tuple-element.188), channel_id=1, source_target_pairs={{0,8},{4,12},{8,0},{12,4},{16,24},{20,28},{24,16},{28,20},{1,9},{5... | collective-permute-start | bytes 589832 | tf_op jit(solution)/shard_map/ppermute | solution.py:615
  93.4 10.6 %collective-permute-start.22 = (bf16[2,192,256]{2,1,0:T(8,128)(2,1)S(1)}, bf16[2,192,256]{2,1,0:T(8,128)(2,1)S(1)}, u32[]{:S(2)}, u32[]{:S(2)}) collective-permute-start(bf16[2,192,256]{2,1,0:T(8,128)(2,1)S(1)} %get-tuple-element.190), channel_id=1, source_target_pairs={{0,2},{1,3},{2,0},{3,1},{4,6},{5,7},{6,4},{7,5},{8,10},{9,11},{10,... | collective-permute-start | bytes 589832 | tf_op jit(solution)/shard_map/ppermute | solution.py:615
  94.5 9.6 %collective-permute-start.23 = (bf16[2,192,256]{2,1,0:T(8,128)(2,1)S(1)}, bf16[2,192,256]{2,1,0:T(8,128)(2,1)S(1)}, u32[]{:S(2)}, u32[]{:S(2)}) collective-permute-start(bf16[2,192,256]{2,1,0:T(8,128)(2,1)S(1)} %get-tuple-element.192), channel_id=1, source_target_pairs={{0,4},{4,0},{8,12},{12,8},{16,20},{20,16},{24,28},{28,24},{1,5},{5... | collective-permute-start | bytes 589832 | tf_op jit(solution)/shard_map/ppermute | solution.py:615
  100.5 8.5 %collective-permute-start.28 = (bf16[4,112,256]{2,1,0:T(8,128)(2,1)S(1)}, bf16[4,112,256]{2,1,0:T(8,128)(2,1)S(1)}, u32[]{:S(2)}, u32[]{:S(2)}) collective-permute-start(bf16[4,112,256]{2,1,0:T(8,128)(2,1)S(1)} %get-tuple-element.204), channel_id=1, source_target_pairs={{0,4},{4,0},{8,12},{12,8},{16,20},{20,16},{24,28},{28,24},{1,5},{5... | collective-permute-start | bytes 688136 | tf_op jit(solution)/shard_map/ppermute | solution.py:615
  101.5 6.7 %collective-permute-start.29 = (bf16[4,96,256]{2,1,0:T(8,128)(2,1)S(1)}, bf16[4,96,256]{2,1,0:T(8,128)(2,1)S(1)}, u32[]{:S(2)}, u32[]{:S(2)}) collective-permute-start(bf16[4,96,256]{2,1,0:T(8,128)(2,1)S(1)} %get-tuple-element.206), channel_id=1, source_target_pairs={{0,8},{4,12},{8,0},{12,4},{16,24},{20,28},{24,16},{28,20},{1,9},{5... | collective-permute-start | bytes 589832 | tf_op jit(solution)/shard_map/ppermute | solution.py:615
  102.2 6.8 %collective-permute-start.30 = (bf16[4,96,256]{2,1,0:T(8,128)(2,1)S(1)}, bf16[4,96,256]{2,1,0:T(8,128)(2,1)S(1)}, u32[]{:S(2)}, u32[]{:S(2)}) collective-permute-start(bf16[4,96,256]{2,1,0:T(8,128)(2,1)S(1)} %get-tuple-element.208), channel_id=1, source_target_pairs={{0,2},{1,3},{2,0},{3,1},{4,6},{5,7},{6,4},{7,5},{8,10},{9,11},{10,... | collective-permute-start | bytes 589832 | tf_op jit(solution)/shard_map/ppermute | solution.py:615
  104.7 12.8 %collective-permute-start.27 = (bf16[1,576,256]{2,1,0:T(8,128)(2,1)S(1)}, bf16[1,576,256]{2,1,0:T(8,128)(2,1)S(1)}, u32[]{:S(2)}, u32[]{:S(2)}) collective-permute-start(bf16[1,576,256]{2,1,0:T(8,128)(2,1)S(1)} %get-tuple-element.202), channel_id=1, source_target_pairs={{0,16},{4,20},{8,24},{12,28},{16,0},{20,4},{24,8},{28,12},{1,17},{... | collective-permute-start | bytes 884744 | tf_op jit(solution)/shard_map/ppermute | solution.py:615
  107.3 14.9 %collective-permute-start.42 = (bf16[2,128,768]{2,1,0:T(8,128)(2,1)S(1)}, bf16[2,128,768]{2,1,0:T(8,128)(2,1)S(1)}, u32[]{:S(2)}, u32[]{:S(2)}) collective-permute-start(bf16[2,128,768]{2,1,0:T(8,128)(2,1)S(1)} %get-tuple-element.225), channel_id=1, source_target_pairs={{0,2},{1,3},{2,0},{3,1},{4,6},{5,7},{6,4},{7,5},{8,10},{9,11},{10,... | collective-permute-start | bytes 1179656 | tf_op jit(solution)/shard_map/ppermute | solution.py:615
  109.7 8.8 %collective-permute-start.34 = (bf16[2,112,256]{2,1,0:T(8,128)(2,1)S(1)}, bf16[2,112,256]{2,1,0:T(8,128)(2,1)S(1)}, u32[]{:S(2)}, u32[]{:S(2)}) collective-permute-start(bf16[2,112,256]{2,1,0:T(8,128)(2,1)S(1)} %get-tuple-element.213), channel_id=1, source_target_pairs={{0,8},{4,12},{8,0},{12,4},{16,24},{20,28},{24,16},{28,20},{1,9},{5... | collective-permute-start | bytes 344072 | tf_op jit(solution)/shard_map/ppermute | solution.py:615
  111.8 6.6 %collective-permute-start.35 = (bf16[2,96,256]{2,1,0:T(8,128)(2,1)S(1)}, bf16[2,96,256]{2,1,0:T(8,128)(2,1)S(1)}, u32[]{:S(2)}, u32[]{:S(2)}) collective-permute-start(bf16[2,96,256]{2,1,0:T(8,128)(2,1)S(1)} %get-tuple-element.215), channel_id=1, source_target_pairs={{0,2},{1,3},{2,0},{3,1},{4,6},{5,7},{6,4},{7,5},{8,10},{9,11},{10,... | collective-permute-start | bytes 294920 | tf_op jit(solution)/shard_map/ppermute | solution.py:615
  112.4 6.1 %collective-permute-start.36 = (bf16[2,96,256]{2,1,0:T(8,128)(2,1)S(1)}, bf16[2,96,256]{2,1,0:T(8,128)(2,1)S(1)}, u32[]{:S(2)}, u32[]{:S(2)}) collective-permute-start(bf16[2,96,256]{2,1,0:T(8,128)(2,1)S(1)} %get-tuple-element.217), channel_id=1, source_target_pairs={{0,4},{4,0},{8,12},{12,8},{16,20},{20,16},{24,28},{28,24},{1,5},{5... | collective-permute-start | bytes 294920 | tf_op jit(solution)/shard_map/ppermute | solution.py:615
  119.0 8.7 %collective-permute-start.37 = (bf16[1,304,256]{2,1,0:T(8,128)(2,1)S(1)}, bf16[1,304,256]{2,1,0:T(8,128)(2,1)S(1)}, u32[]{:S(2)}, u32[]{:S(2)}) collective-permute-start(bf16[1,304,256]{2,1,0:T(8,128)(2,1)S(1)} %get-tuple-element.220), channel_id=1, source_target_pairs={{0,16},{4,20},{8,24},{12,28},{16,0},{20,4},{24,8},{28,12},{1,17},{... | collective-permute-start | bytes 466952 | tf_op jit(solution)/shard_map/ppermute | solution.py:615
  121.0 9.3 %collective-permute-start.32 = (bf16[1,576,256]{2,1,0:T(8,128)(2,1)S(1)}, bf16[1,576,256]{2,1,0:T(8,128)(2,1)S(1)}, u32[]{:S(2)}, u32[]{:S(2)}) collective-permute-start(bf16[1,576,256]{2,1,0:T(8,128)(2,1)S(1)} %get-tuple-element.211.refs_1_), channel_id=1, source_target_pairs={{0,2},{1,3},{2,0},{3,1},{4,6},{5,7},{6,4},{7,5},{8,10},{9,11},{10,... | collective-permute-start | bytes 884744 | tf_op jit(solution)/shard_map/ppermute | solution.py:615
  122.2 8.6 %collective-permute-start.41 = (bf16[128,768]{1,0:T(8,128)(2,1)S(1)}, bf16[128,768]{1,0:T(8,128)(2,1)S(1)}, u32[]{:S(2)}, u32[]{:S(2)}) collective-permute-start(bf16[128,768]{1,0:T(8,128)(2,1)S(1)} %get-tuple-element.224), channel_id=1, source_target_pairs={{0,1},{1,0},{2,3},{3,2},{4,5},{5,4},{6,7},{7,6},{8,9},{9,8},{10,11... | collective-permute-start | bytes 589832 | tf_op jit(solution)/shard_map/ppermute | solution.py:615
  122.2 11.6 %collective-permute-start.43 = (bf16[2,128,768]{2,1,0:T(8,128)(2,1)S(1)}, bf16[2,128,768]{2,1,0:T(8,128)(2,1)S(1)}, u32[]{:S(2)}, u32[]{:S(2)}) collective-permute-start(bf16[2,128,768]{2,1,0:T(8,128)(2,1)S(1)} %collective-permute-done.42.refs_11_), channel_id=1, source_target_pairs={{0,1},{1,0},{2,3},{3,2},{4,5},{5,4},{6,7},{7,6},{8,9},{9,8},{10,11... | collective-permute-start | bytes 1179656 | tf_op jit(solution)/shard_map/ppermute | solution.py:615
  128.3 5.6 %collective-permute-start.39 = (bf16[1,304,256]{2,1,0:T(8,128)(2,1)S(1)}, bf16[1,304,256]{2,1,0:T(8,128)(2,1)S(1)}, u32[]{:S(2)}, u32[]{:S(2)}) collective-permute-start(bf16[1,304,256]{2,1,0:T(8,128)(2,1)S(1)} %get-tuple-element.222.refs_5_), channel_id=1, source_target_pairs={{0,2},{1,3},{2,0},{3,1},{4,6},{5,7},{6,4},{7,5},{8,10},{9,11},{10,... | collective-permute-start | bytes 466952 | tf_op jit(solution)/shard_map/ppermute | solution.py:615
  130.3 3.6 %collective-permute-start.31 = (bf16[1,576,256]{2,1,0:T(8,128)(2,1)S(1)}, bf16[1,576,256]{2,1,0:T(8,128)(2,1)S(1)}, u32[]{:S(2)}, u32[]{:S(2)}) collective-permute-start(bf16[1,576,256]{2,1,0:T(8,128)(2,1)S(1)} %get-tuple-element.211.refs_1_), channel_id=1, source_target_pairs={{0,1},{1,0},{2,3},{3,2},{4,5},{5,4},{6,7},{7,6},{8,9},{9,8},{10,11... | collective-permute-start | bytes 884744 | tf_op jit(solution)/shard_map/ppermute | solution.py:615
  130.3 4.9 %collective-permute-start.33 = (bf16[1,576,256]{2,1,0:T(8,128)(2,1)S(1)}, bf16[1,576,256]{2,1,0:T(8,128)(2,1)S(1)}, u32[]{:S(2)}, u32[]{:S(2)}) collective-permute-start(bf16[1,576,256]{2,1,0:T(8,128)(2,1)S(1)} %collective-permute-done.32.refs_3_), channel_id=1, source_target_pairs={{0,1},{1,0},{2,3},{3,2},{4,5},{5,4},{6,7},{7,6},{8,9},{9,8},{10,11... | collective-permute-start | bytes 884744 | tf_op jit(solution)/shard_map/ppermute | solution.py:615
  130.8 3.1 %collective-permute-start.38 = (bf16[1,304,256]{2,1,0:T(8,128)(2,1)S(1)}, bf16[1,304,256]{2,1,0:T(8,128)(2,1)S(1)}, u32[]{:S(2)}, u32[]{:S(2)}) collective-permute-start(bf16[1,304,256]{2,1,0:T(8,128)(2,1)S(1)} %get-tuple-element.222.refs_5_), channel_id=1, source_target_pairs={{0,1},{1,0},{2,3},{3,2},{4,5},{5,4},{6,7},{7,6},{8,9},{9,8},{10,11... | collective-permute-start | bytes 466952 | tf_op jit(solution)/shard_map/ppermute | solution.py:615
  133.9 1.4 collective-permute-start.40
  (4 other events, 22.5 us)

commit v7 on v6

--- a/solution.py
+++ b/solution.py
@@ -25,7 +25,7 @@
 WEIGHTS = {
     "prepare": 60 * 10**9, "attend": 60 * 10**9, "feed": 60 * 10**9, "grad_up": 60 * 10**9,
     "grad_down": 60 * 10**9, "attend_back": 60 * 10**9, "grad_tokens": 60 * 10**8,
-    "halve": 200 * 10**7, "cut_units": 200 * 10**7, "place_all": 200 * 10**7,
+    "halve": 150 * 10**7, "cut_units": 150 * 10**7, "place_all": 150 * 10**7,
 }
 
 
@@ -895,8 +895,8 @@
     mark = own_group.step([mark])
     mark = feed_group.step([mark])
     mark = own_group.step([mark])
+    mark = own_group.step([mark])
     feed_pieces, mark = feed_group.finish([mark])
-    mark = own_group.step([mark])
     own_pieces, mark = own_group.finish([mark])
     (
         down, up, grad_w_qkv, grad_w_out, sum_qv, sum_out, sum_gain_one, sum_shift_one, sum_up, sum_down,

time: 139 us -> 136 us (0.978)
  waiting for transfers between devices: 28.9 us -> 24.6 us
  starting transfers between devices: 41.2 us -> 42.8 us
    ppermute x44, waiting for transfers between devices: 28.9 us -> 24.6 us  [swap(): lax.ppermute(block, axis, [(i, i ^ bit) for i in range(lax.axis_size(axis...]
    ppermute x44, starting transfers between devices: 41.2 us -> 42.8 us  [swap(): lax.ppermute(block, axis, [(i, i ^ bit) for i in range(lax.axis_size(axis...]
  transfers between devices with their start and end apart: 44 -> 44, of which waited for: 14 -> 16; matrix products, arithmetic and copies ran while one was open for 0% -> 0% of each run, Pallas kernels for 38% -> 39%
where the time goes in v7:
time: 136 us
  Pallas kernels  65.8 us (48%)
  starting transfers between devices  42.8 us (31%)
  waiting for transfers between devices  24.6 us (18%)
  local copies, waits for them, and re-layouts  1.39 us (1%)
    pallas_call x20, Pallas kernels, call(): pl.pallas_call(body, in_specs=[SMEM] * len(scalars) + [VMEM] * len(arrays...  65.8 us
    ppermute x44, starting transfers between devices, swap(): lax.ppermute(block, axis, [(i, i ^ bit) for i in range(lax.axis_size(axis...  42.8 us
    ppermute x44, waiting for transfers between devices, swap(): lax.ppermute(block, axis, [(i, i ^ bit) for i in range(lax.axis_size(axis...  24.6 us
  transfers between devices with their start and end apart: 44, of which 16 were waited for; matrix products, arithmetic and copies ran while one was open for 0% of the time, Pallas kernels for 39%

profile of v7, /device:TPU:0, one launch (start us, length us, event | category | flops | bytes accessed | tf_op | source)
XLA Modules:
  0.0 135.9 jit_solution(17617841986919172003)
XLA Ops:
  0.7 1.3 dynamic-slice_bitcast_fusion.4
  2.5 2.6 %collective-permute-start.1 = (bf16[128,768]{1,0:T(8,128)(2,1)S(1)}, bf16[128,768]{1,0:T(8,128)(2,1)S(1)}, u32[]{:S(2)}, u32[]{:S(2)}) collective-permute-start(bf16[128,768]{1,0:T(8,128)(2,1)S(1)} %get-tuple-element.247), channel_id=1, source_target_pairs={{0,2},{1,3},{2,0},{3,1},{4,6},{5,7},{6,4},{7,5},{8,10},{9,11},{10,... | collective-permute-start | bytes 589832 | tf_op jit(solution)/shard_map/ppermute | solution.py:615
  5.2 3.9 %prepare.1 = (bf16[768,2304]{1,0:T(8,128)(2,1)S(1)}, bf16[768,768]{1,0:T(8,128)(2,1)S(1)}, f32[512,512]{1,0:T(8,128)S(1)}, f32[12,768]{1,0:T(8,128)S(1)}, f32[8,128]{1,0:T(8,128)}) custom-call(s32[9]{0:T(128)S(1)} %pad_add_fusion.1.refs_0_, bf16[768,2304]{1,0:T(8,128)(2,1)} %refs_1_.3, bf16[768,768]{1,0:T(8,128)(2,1)} %refs_11_.1, f32[1536]{0:T(1024)} %refs_3_.1, ...), custom_call_target="tpu_custom_call" | custom-call | flops 60000002048 | tf_op jit(solution)/shard_map/prepare/pallas_call | solution.py:51
  9.6 1.9 %collective-permute-start.4 = (bf16[128,768]{1,0:T(8,128)(2,1)S(1)}, bf16[128,768]{1,0:T(8,128)(2,1)S(1)}, u32[]{:S(2)}, u32[]{:S(2)}) collective-permute-start(bf16[128,768]{1,0:T(8,128)(2,1)S(1)} %get-tuple-element.241), channel_id=1, source_target_pairs={{0,2},{1,3},{2,0},{3,1},{4,6},{5,7},{6,4},{7,5},{8,10},{9,11},{10,... | collective-permute-start | bytes 589832 | tf_op jit(solution)/shard_map/ppermute | solution.py:615
  11.6 2.9 %collective-permute-done.2.refs_3_ = bf16[128,768]{1,0:T(8,128)(2,1)S(1)} collective-permute-done((bf16[128,768]{1,0:T(8,128)(2,1)S(1)}, bf16[128,768]{1,0:T(8,128)(2,1)S(1)}, u32[]{:S(2)}, u32[]{:S(2)}) %collective-permute-start.2) | collective-permute-done | bytes 196640 | tf_op jit(solution)/shard_map/ppermute | solution.py:615
  14.5 11.2 %attend.1 = (f32[512,768]{1,0:T(8,128)S(1)}, f32[512,1]{1,0:T(8,128)S(1)}, bf16[512,768]{1,0:T(8,128)(2,1)}, bf16[512,768]{1,0:T(8,128)(2,1)}, bf16[512,768]{1,0...) custom-call(bf16[128,768]{1,0:T(8,128)(2,1)S(1)} %get-tuple-element., ...), custom_call_target="tpu_custom_call" | custom-call | flops 60000002048 | tf_op jit(solution)/shard_map/attend/pallas_call | solution.py:51
  25.7 8.8 %feed.1 = (bf16[2,8,96,512]{3,2,1,0:T(8,128)(2,1)S(1)}, bf16[2,8,96,512]{3,2,1,0:T(8,128)(2,1)S(1)}, bf16[512,3072]{1,0:T(8,128)(2,1)S(1)}, bf16[512,768]{1,0:T(...) custom-call(s32[2]{0:T(128)S(1)} %pad_add_fusion.refs_0_, ...), custom_call_target="tpu_custom_call" | custom-call | flops 60000002048 | tf_op jit(solution)/shard_map/feed/pallas_call | solution.py:51
  35.1 1.9 %collective-permute-start.10 = (bf16[128,768]{1,0:T(8,128)(2,1)S(1)}, bf16[128,768]{1,0:T(8,128)(2,1)S(1)}, u32[]{:S(2)}, u32[]{:S(2)}) collective-permute-start(bf16[128,768]{1,0:T(8,128)(2,1)S(1)} %get-tuple-element.139), channel_id=1, source_target_pairs={{0,3},{1,2},{2,1},{3,0},{4,7},{5,6},{6,5},{7,4},{8,11},{9,10},{10,... | collective-permute-start | bytes 589832 | tf_op jit(solution)/shard_map/ppermute | solution.py:615
  37.4 9.8 %grad_up.1 = (bf16[2,768,768]{2,1,0:T(8,128)(2,1)S(1)}, bf16[2,768,768]{2,1,0:T(8,128)(2,1)S(1)}, f32[4,768]{1,0:T(4,128)S(1)}, bf16[512,768]{1,0:T(8,128)(2,1)S...) custom-call(s32[2]{0:T(128)S(1)} %pad_add_fusion.refs_0_, ...), custom_call_target="tpu_custom_call" | custom-call | flops 60000002048 | tf_op jit(solution)/shard_map/grad_up/pallas_call | solution.py:51
  47.4 3.9 %grad_down.1 = (bf16[2,8,96,768]{3,2,1,0:T(8,128)(2,1)S(1)}, bf16[4,128,768]{2,1,0:T(8,128)(2,1)}, f32[8,128]{1,0:T(8,128)S(1)}) custom-call(s32[2]{0:T(128)S(1)} %pad_add_fusion.refs_0_, bf16[2,8,96,512]{3,2,1,0:T(8,128)(2,1)S(1)} %get-tuple-element.133.refs_1_, bf16[2,8,96,512]{3,2,1,0:T(8,128)(2,1)S(1)} %collective-permute-done.6.refs_2_, ...), custom_call_target="tpu_custom_call" | custom-call | flops 60000002048 | tf_op jit(solution)/shard_map/grad_down/pallas_call | solution.py:51
  51.8 0.7 cut_units.4
  52.6 1.7 %collective-permute-start.12 = (bf16[8,192,256]{2,1,0:T(8,128)(2,1)S(1)}, bf16[8,192,256]{2,1,0:T(8,128)(2,1)S(1)}, u32[]{:S(2)}, u32[]{:S(2)}) collective-permute-start(bf16[8,192,256]{2,1,0:T(8,128)(2,1)S(1)} %get-tuple-element.163), channel_id=1, source_target_pairs={{0,2},{1,3},{2,0},{3,1},{4,6},{5,7},{6,4},{7,5},{8,10},{9,11},{10,... | collective-permute-start | bytes 2359304 | tf_op jit(solution)/shard_map/ppermute | solution.py:615
  54.2 1.5 %collective-permute-start.13 = (bf16[8,192,256]{2,1,0:T(8,128)(2,1)S(1)}, bf16[8,192,256]{2,1,0:T(8,128)(2,1)S(1)}, u32[]{:S(2)}, u32[]{:S(2)}) collective-permute-start(bf16[8,192,256]{2,1,0:T(8,128)(2,1)S(1)} %get-tuple-element.165), channel_id=1, source_target_pairs={{0,4},{4,0},{8,12},{12,8},{16,20},{20,16},{24,28},{28,24},{1,5},{5... | collective-permute-start | bytes 2359304 | tf_op jit(solution)/shard_map/ppermute | solution.py:615
  55.8 1.6 %collective-permute-start.14 = (bf16[8,192,256]{2,1,0:T(8,128)(2,1)S(1)}, bf16[8,192,256]{2,1,0:T(8,128)(2,1)S(1)}, u32[]{:S(2)}, u32[]{:S(2)}) collective-permute-start(bf16[8,192,256]{2,1,0:T(8,128)(2,1)S(1)} %get-tuple-element.167), channel_id=1, source_target_pairs={{0,8},{4,12},{8,0},{12,4},{16,24},{20,28},{24,16},{28,20},{1,9},{5... | collective-permute-start | bytes 2359304 | tf_op jit(solution)/shard_map/ppermute | solution.py:615
  57.3 14.8 %attend_back.1 = (bf16[512,2304]{1,0:T(8,128)(2,1)S(1)}, bf16[2,8,112,256]{3,2,1,0:T(8,128)(2,1)S(1)}, bf16[2,768,256]{2,1,0:T(8,128)(2,1)S(1)}, bf16[2,768,256]...) custom-call(s32[2]{0:T(128)S(1)} %pad_add_fusion.refs_0_, ...), custom_call_target="tpu_custom_call" | custom-call | flops 60000002048 | tf_op jit(solution)/shard_map/attend_back/pallas_call | solution.py:51
  72.8 0.7 cut_units.5
  73.6 1.2 collective-permute-done.14.refs_6_
  74.9 0.8 halve.8
  76.3 1.6 %collective-permute-start.16 = (bf16[4,192,256]{2,1,0:T(8,128)(2,1)S(1)}, bf16[4,192,256]{2,1,0:T(8,128)(2,1)S(1)}, u32[]{:S(2)}, u32[]{:S(2)}) collective-permute-start(bf16[4,192,256]{2,1,0:T(8,128)(2,1)S(1)} %get-tuple-element.172), channel_id=1, source_target_pairs={{0,8},{4,12},{8,0},{12,4},{16,24},{20,28},{24,16},{28,20},{1,9},{5... | collective-permute-start | bytes 1179656 | tf_op jit(solution)/shard_map/ppermute | solution.py:615
  77.9 0.8 collective-permute-start.17
  78.7 0.7 cut_units.6
  79.4 1.3 collective-permute-start.24
  80.7 1.5 %collective-permute-start.25 = (bf16[8,96,256]{2,1,0:T(8,128)(2,1)S(1)}, bf16[8,96,256]{2,1,0:T(8,128)(2,1)S(1)}, u32[]{:S(2)}, u32[]{:S(2)}) collective-permute-start(bf16[8,96,256]{2,1,0:T(8,128)(2,1)S(1)} %get-tuple-element.196), channel_id=1, source_target_pairs={{0,4},{4,0},{8,12},{12,8},{16,20},{20,16},{24,28},{28,24},{1,5},{5... | collective-permute-start | bytes 1179656 | tf_op jit(solution)/shard_map/ppermute | solution.py:615
  82.2 5.6 %collective-permute-done.15.refs_2_ = bf16[4,192,256]{2,1,0:T(8,128)(2,1)S(1)} collective-permute-done((bf16[4,192,256]{2,1,0:T(8,128)(2,1)S(1)}, bf16[4,192,256]{2,1,0:T(8,128)(2,1)S(1)}, u32[]{:S(2)}, u32[]{:S(2)}) %collective-permute-start.15) | collective-permute-done | bytes 393248 | tf_op jit(solution)/shard_map/ppermute | solution.py:615
  87.8 1.6 %collective-permute-start.26 = (bf16[8,96,256]{2,1,0:T(8,128)(2,1)S(1)}, bf16[8,96,256]{2,1,0:T(8,128)(2,1)S(1)}, u32[]{:S(2)}, u32[]{:S(2)}) collective-permute-start(bf16[8,96,256]{2,1,0:T(8,128)(2,1)S(1)} %get-tuple-element.198), channel_id=1, source_target_pairs={{0,8},{4,12},{8,0},{12,4},{16,24},{20,28},{24,16},{28,20},{1,9},{5... | collective-permute-start | bytes 1179656 | tf_op jit(solution)/shard_map/ppermute | solution.py:615
  89.4 2.0 %grad_tokens.1 = (bf16[128,768]{1,0:T(8,128)(2,1)S(1)}, bf16[128,768]{1,0:T(8,128)(2,1)S(1)}, bf16[2,128,768]{2,1,0:T(8,128)(2,1)S(1)}, f32[8,128]{1,0:T(8,128)S(1)}) custom-call(bf16[512,2304]{1,0:T(8,128)(2,1)S(1)} %get-tuple-element.181.refs_0_, bf16[768,2304]{1,0:T(8,128)(2,1)S(1)} %copy-done.2, f32[512,768]{1,0:T(8,128)S(1)} %get-tuple-element.182.refs_2_, ...), custom_call_target="tpu_custom_call" | custom-call | flops 6000000000 | tf_op jit(solution)/shard_map/grad_tokens/pallas_call | solution.py:51
  91.4 0.7 cut_units.7
  94.4 1.2 collective-permute-start.23
  95.6 1.8 %collective-permute-done.26.refs_6_ = bf16[8,96,256]{2,1,0:T(8,128)(2,1)S(1)} collective-permute-done((bf16[8,96,256]{2,1,0:T(8,128)(2,1)S(1)}, bf16[8,96,256]{2,1,0:T(8,128)(2,1)S(1)}, u32[]{:S(2)}, u32[]{:S(2)}) %collective-permute-start.26) | collective-permute-done | bytes 393248 | tf_op jit(solution)/shard_map/ppermute | solution.py:615
  97.4 2.3 %collective-permute-done.24.refs_2_ = bf16[8,112,256]{2,1,0:T(8,128)(2,1)S(1)} collective-permute-done((bf16[8,112,256]{2,1,0:T(8,128)(2,1)S(1)}, bf16[8,112,256]{2,1,0:T(8,128)(2,1)S(1)}, u32[]{:S(2)}, u32[]{:S(2)}) %collective-permute-start.24) | collective-permute-done | bytes 458784 | tf_op jit(solution)/shard_map/ppermute | solution.py:615
  99.7 0.7 halve.10
  100.4 0.9 collective-permute-start.28
  101.4 0.8 collective-permute-start.29
  102.1 1.3 collective-permute-start.30
  104.6 2.7 %collective-permute-start.27 = (bf16[1,576,256]{2,1,0:T(8,128)(2,1)S(1)}, bf16[1,576,256]{2,1,0:T(8,128)(2,1)S(1)}, u32[]{:S(2)}, u32[]{:S(2)}) collective-permute-start(bf16[1,576,256]{2,1,0:T(8,128)(2,1)S(1)} %get-tuple-element.202), channel_id=1, source_target_pairs={{0,16},{4,20},{8,24},{12,28},{16,0},{20,4},{24,8},{28,12},{1,17},{... | collective-permute-start | bytes 884744 | tf_op jit(solution)/shard_map/ppermute | solution.py:615
  108.4 1.5 %collective-permute-start.31 = (bf16[2,112,256]{2,1,0:T(8,128)(2,1)S(1)}, bf16[2,112,256]{2,1,0:T(8,128)(2,1)S(1)}, u32[]{:S(2)}, u32[]{:S(2)}) collective-permute-start(bf16[2,112,256]{2,1,0:T(8,128)(2,1)S(1)} %get-tuple-element.211), channel_id=1, source_target_pairs={{0,8},{4,12},{8,0},{12,4},{16,24},{20,28},{24,16},{28,20},{1,9},{5... | collective-permute-start | bytes 344072 | tf_op jit(solution)/shard_map/ppermute | solution.py:615
  109.9 1.1 collective-permute-start.32
  111.0 1.6 %collective-permute-start.33 = (bf16[2,96,256]{2,1,0:T(8,128)(2,1)S(1)}, bf16[2,96,256]{2,1,0:T(8,128)(2,1)S(1)}, u32[]{:S(2)}, u32[]{:S(2)}) collective-permute-start(bf16[2,96,256]{2,1,0:T(8,128)(2,1)S(1)} %get-tuple-element.215), channel_id=1, source_target_pairs={{0,4},{4,0},{8,12},{12,8},{16,20},{20,16},{24,28},{28,24},{1,5},{5... | collective-permute-start | bytes 294920 | tf_op jit(solution)/shard_map/ppermute | solution.py:615
  112.5 1.8 %collective-permute-start.42 = (bf16[2,128,768]{2,1,0:T(8,128)(2,1)S(1)}, bf16[2,128,768]{2,1,0:T(8,128)(2,1)S(1)}, u32[]{:S(2)}, u32[]{:S(2)}) collective-permute-start(bf16[2,128,768]{2,1,0:T(8,128)(2,1)S(1)} %get-tuple-element.225), channel_id=1, source_target_pairs={{0,2},{1,3},{2,0},{3,1},{4,6},{5,7},{6,4},{7,5},{8,10},{9,11},{10,... | collective-permute-start | bytes 1179656 | tf_op jit(solution)/shard_map/ppermute | solution.py:615
  114.4 1.3 collective-permute-done.32.refs_4_
  116.2 3.6 %collective-permute-start.37 = (bf16[1,304,256]{2,1,0:T(8,128)(2,1)S(1)}, bf16[1,304,256]{2,1,0:T(8,128)(2,1)S(1)}, u32[]{:S(2)}, u32[]{:S(2)}) collective-permute-start(bf16[1,304,256]{2,1,0:T(8,128)(2,1)S(1)} %get-tuple-element.220), channel_id=1, source_target_pairs={{0,16},{4,20},{8,24},{12,28},{16,0},{20,4},{24,8},{28,12},{1,17},{... | collective-permute-start | bytes 466952 | tf_op jit(solution)/shard_map/ppermute | solution.py:615
  121.0 1.8 %collective-permute-start.35 = (bf16[1,576,256]{2,1,0:T(8,128)(2,1)S(1)}, bf16[1,576,256]{2,1,0:T(8,128)(2,1)S(1)}, u32[]{:S(2)}, u32[]{:S(2)}) collective-permute-start(bf16[1,576,256]{2,1,0:T(8,128)(2,1)S(1)} %get-tuple-element.218.refs_1_), channel_id=1, source_target_pairs={{0,2},{1,3},{2,0},{3,1},{4,6},{5,7},{6,4},{7,5},{8,10},{9,11},{10,... | collective-permute-start | bytes 884744 | tf_op jit(solution)/shard_map/ppermute | solution.py:615
  123.2 1.5 %collective-permute-done.37.refs_2_ = bf16[1,304,256]{2,1,0:T(8,128)(2,1)S(1)} collective-permute-done((bf16[1,304,256]{2,1,0:T(8,128)(2,1)S(1)}, bf16[1,304,256]{2,1,0:T(8,128)(2,1)S(1)}, u32[]{:S(2)}, u32[]{:S(2)}) %collective-permute-start.37) | collective-permute-done | bytes 155680 | tf_op jit(solution)/shard_map/ppermute | solution.py:615
  125.3 1.6 %collective-permute-start.39 = (bf16[1,304,256]{2,1,0:T(8,128)(2,1)S(1)}, bf16[1,304,256]{2,1,0:T(8,128)(2,1)S(1)}, u32[]{:S(2)}, u32[]{:S(2)}) collective-permute-start(bf16[1,304,256]{2,1,0:T(8,128)(2,1)S(1)} %get-tuple-element.222.refs_5_), channel_id=1, source_target_pairs={{0,2},{1,3},{2,0},{3,1},{4,6},{5,7},{6,4},{7,5},{8,10},{9,11},{10,... | collective-permute-start | bytes 466952 | tf_op jit(solution)/shard_map/ppermute | solution.py:615
  126.8 2.1 %collective-permute-done.35.refs_3_ = bf16[1,576,256]{2,1,0:T(8,128)(2,1)S(1)} collective-permute-done((bf16[1,576,256]{2,1,0:T(8,128)(2,1)S(1)}, bf16[1,576,256]{2,1,0:T(8,128)(2,1)S(1)}, u32[]{:S(2)}, u32[]{:S(2)}) %collective-permute-start.35) | collective-permute-done | bytes 294944 | tf_op jit(solution)/shard_map/ppermute | solution.py:615
  129.5 1.6 %collective-permute-done.39.refs_7_ = bf16[1,304,256]{2,1,0:T(8,128)(2,1)S(1)} collective-permute-done((bf16[1,304,256]{2,1,0:T(8,128)(2,1)S(1)}, bf16[1,304,256]{2,1,0:T(8,128)(2,1)S(1)}, u32[]{:S(2)}, u32[]{:S(2)}) %collective-permute-start.39) | collective-permute-done | bytes 155680 | tf_op jit(solution)/shard_map/ppermute | solution.py:615
  131.1 1.4 %collective-permute-done.40.refs_8_ = bf16[1,304,256]{2,1,0:T(8,128)(2,1)S(1)} collective-permute-done((bf16[1,304,256]{2,1,0:T(8,128)(2,1)S(1)}, bf16[1,304,256]{2,1,0:T(8,128)(2,1)S(1)}, u32[]{:S(2)}, u32[]{:S(2)}) %collective-permute-start.40) | collective-permute-done | bytes 155680 | tf_op jit(solution)/shard_map/ppermute | solution.py:615
  132.5 3.3 %place_all.1 = (f32[384,768]{1,0:T(8,128)}, f32[96,3072]{1,0:T(8,128)}, f32[96,2304]{1,0:T(8,128)}, f32[96,768]{1,0:T(8,128)}, f32[192]{0:T(256)}, /*index=5*/f3...) custom-call(s32[2]{0:T(128)S(1)} %pad_add_fusion.refs_0_, ...), custom_call_target="tpu_custom_call" | custom-call | flops 1500000000 | tf_op jit(solution)/shard_map/place_all/pallas_call | solution.py:51
  (84 shorter events, 11.9 us)
Async XLA Ops:
  2.0 7.4 %collective-permute-start = (bf16[128,768]{1,0:T(8,128)(2,1)S(1)}, bf16[128,768]{1,0:T(8,128)(2,1)S(1)}, u32[]{:S(2)}, u32[]{:S(2)}) collective-permute-start(bf16[128,768]{1,0:T(8,128)(2,1)S(1)} %get-tuple-element.245), channel_id=1, source_target_pairs={{0,1},{1,0},{2,3},{3,2},{4,5},{5,4},{6,7},{7,6},{8,9},{9,8},{10,11... | collective-permute-start | bytes 589832 | tf_op jit(solution)/shard_map/ppermute | solution.py:615
  2.5 9.1 %collective-permute-start.1 = (bf16[128,768]{1,0:T(8,128)(2,1)S(1)}, bf16[128,768]{1,0:T(8,128)(2,1)S(1)}, u32[]{:S(2)}, u32[]{:S(2)}) collective-permute-start(bf16[128,768]{1,0:T(8,128)(2,1)S(1)} %get-tuple-element.247), channel_id=1, source_target_pairs={{0,2},{1,3},{2,0},{3,1},{4,6},{5,7},{6,4},{7,5},{8,10},{9,11},{10,... | collective-permute-start | bytes 589832 | tf_op jit(solution)/shard_map/ppermute | solution.py:615
  5.0 9.4 %collective-permute-start.2 = (bf16[128,768]{1,0:T(8,128)(2,1)S(1)}, bf16[128,768]{1,0:T(8,128)(2,1)S(1)}, u32[]{:S(2)}, u32[]{:S(2)}) collective-permute-start(bf16[128,768]{1,0:T(8,128)(2,1)S(1)} %get-tuple-element.244), channel_id=1, source_target_pairs={{0,3},{1,2},{2,1},{3,0},{4,7},{5,6},{6,5},{7,4},{8,11},{9,10},{10,... | collective-permute-start | bytes 589832 | tf_op jit(solution)/shard_map/ppermute | solution.py:615
  5.2 20.5 %slice-start = ((s8[4718592]{0:T(1024)(128)(4,1)}), s8[4194304]{0:T(1024)(128)(4,1)S(1)}, s32[]{:S(2)}) async-start(s8[4718592]{0:T(1024)(128)(4,1)} %bitcast.39), calls=%async_computation | async-start | bytes 8388608
  5.2 20.5 %slice-start.2 = ((s8[4718592]{0:T(1024)(128)(4,1)}), s8[4194304]{0:T(1024)(128)(4,1)S(1)}, s32[]{:S(2)}) async-start(s8[4718592]{0:T(1024)(128)(4,1)} %bitcast.41), calls=%async_computation.2 | async-start | bytes 8388608
  9.3 16.4 %slice-start.1 = ((s8[4718592]{0:T(1024)(128)(4,1)}), s8[524288]{0:T(1024)(128)(4,1)S(1)}, s32[]{:S(2)}) async-start(s8[4718592]{0:T(1024)(128)(4,1)} %bitcast.39), calls=%async_computation.1 | async-start | bytes 1048576
  9.3 16.4 %slice-start.3 = ((s8[4718592]{0:T(1024)(128)(4,1)}), s8[524288]{0:T(1024)(128)(4,1)S(1)}, s32[]{:S(2)}) async-start(s8[4718592]{0:T(1024)(128)(4,1)} %bitcast.41), calls=%async_computation.3 | async-start | bytes 1048576
  9.4 16.3 %collective-permute-start.3 = (bf16[128,768]{1,0:T(8,128)(2,1)S(1)}, bf16[128,768]{1,0:T(8,128)(2,1)S(1)}, u32[]{:S(2)}, u32[]{:S(2)}) collective-permute-start(bf16[128,768]{1,0:T(8,128)(2,1)S(1)} %get-tuple-element.242), channel_id=1, source_target_pairs={{0,1},{1,0},{2,3},{3,2},{4,5},{5,4},{6,7},{7,6},{8,9},{9,8},{10,11... | collective-permute-start | bytes 589832 | tf_op jit(solution)/shard_map/ppermute | solution.py:615
  9.6 16.1 %collective-permute-start.4 = (bf16[128,768]{1,0:T(8,128)(2,1)S(1)}, bf16[128,768]{1,0:T(8,128)(2,1)S(1)}, u32[]{:S(2)}, u32[]{:S(2)}) collective-permute-start(bf16[128,768]{1,0:T(8,128)(2,1)S(1)} %get-tuple-element.241), channel_id=1, source_target_pairs={{0,2},{1,3},{2,0},{3,1},{4,6},{5,7},{6,4},{7,5},{8,10},{9,11},{10,... | collective-permute-start | bytes 589832 | tf_op jit(solution)/shard_map/ppermute | solution.py:615
  11.5 14.1 %collective-permute-start.5 = (bf16[128,768]{1,0:T(8,128)(2,1)S(1)}, bf16[128,768]{1,0:T(8,128)(2,1)S(1)}, u32[]{:S(2)}, u32[]{:S(2)}) collective-permute-start(bf16[128,768]{1,0:T(8,128)(2,1)S(1)} %get-tuple-element.240), channel_id=1, source_target_pairs={{0,3},{1,2},{2,1},{3,0},{4,7},{5,6},{6,5},{7,4},{8,11},{9,10},{10,... | collective-permute-start | bytes 589832 | tf_op jit(solution)/shard_map/ppermute | solution.py:615
  34.6 12.8 %collective-permute-start.6 = (bf16[2,8,96,512]{3,2,1,0:T(8,128)(2,1)S(1)}, bf16[2,8,96,512]{3,2,1,0:T(8,128)(2,1)S(1)}, u32[]{:S(2)}, u32[]{:S(2)}) collective-permute-start(bf16[2,8,96,512]{3,2,1,0:T(8,128)(2,1)S(1)} %get-tuple-element.134), channel_id=1, source_target_pairs={{0,1},{1,0},{2,3},{3,2},{4,5},{5,4},{6,7},{7,6},{8,9},{9,8},{10,11... | collective-permute-start | bytes 4718600 | tf_op jit(solution)/shard_map/ppermute | solution.py:615
  34.9 12.5 %collective-permute-start.7 = (bf16[512,768]{1,0:T(8,128)(2,1)S(1)}, bf16[512,768]{1,0:T(8,128)(2,1)S(1)}, u32[]{:S(2)}, u32[]{:S(2)}) collective-permute-start(bf16[512,768]{1,0:T(8,128)(2,1)S(1)} %get-tuple-element.135.refs_1_.refs_3_), channel_id=1, source_target_pairs={{0,1},{1,0},{2,3},{3,2},{4,5},{5,4},{6,7},{7,6},{8,9},{9,8},{10,11... | collective-permute-start | bytes 2359304 | tf_op jit(solution)/shard_map/ppermute | solution.py:615
  35.1 12.1 %collective-permute-start.10 = (bf16[128,768]{1,0:T(8,128)(2,1)S(1)}, bf16[128,768]{1,0:T(8,128)(2,1)S(1)}, u32[]{:S(2)}, u32[]{:S(2)}) collective-permute-start(bf16[128,768]{1,0:T(8,128)(2,1)S(1)} %get-tuple-element.139), channel_id=1, source_target_pairs={{0,3},{1,2},{2,1},{3,0},{4,7},{5,6},{6,5},{7,4},{8,11},{9,10},{10,... | collective-permute-start | bytes 589832 | tf_op jit(solution)/shard_map/ppermute | solution.py:615
  37.0 10.4 %collective-permute-start.8 = (bf16[128,768]{1,0:T(8,128)(2,1)S(1)}, bf16[128,768]{1,0:T(8,128)(2,1)S(1)}, u32[]{:S(2)}, u32[]{:S(2)}) collective-permute-start(bf16[128,768]{1,0:T(8,128)(2,1)S(1)} %get-tuple-element.137), channel_id=1, source_target_pairs={{0,1},{1,0},{2,3},{3,2},{4,5},{5,4},{6,7},{7,6},{8,9},{9,8},{10,11... | collective-permute-start | bytes 589832 | tf_op jit(solution)/shard_map/ppermute | solution.py:615
  37.0 10.4 %collective-permute-start.9 = (bf16[128,768]{1,0:T(8,128)(2,1)S(1)}, bf16[128,768]{1,0:T(8,128)(2,1)S(1)}, u32[]{:S(2)}, u32[]{:S(2)}) collective-permute-start(bf16[128,768]{1,0:T(8,128)(2,1)S(1)} %get-tuple-element.138), channel_id=1, source_target_pairs={{0,2},{1,3},{2,0},{3,1},{4,6},{5,7},{6,4},{7,5},{8,10},{9,11},{10,... | collective-permute-start | bytes 589832 | tf_op jit(solution)/shard_map/ppermute | solution.py:615
  47.2 4.6 %collective-permute-start.11 = (bf16[2,768,768]{2,1,0:T(8,128)(2,1)S(1)}, bf16[2,768,768]{2,1,0:T(8,128)(2,1)S(1)}, u32[]{:S(2)}, u32[]{:S(2)}) collective-permute-start(bf16[2,768,768]{2,1,0:T(8,128)(2,1)S(1)} %get-tuple-element.148), channel_id=1, source_target_pairs={{0,1},{1,0},{2,3},{3,2},{4,5},{5,4},{6,7},{7,6},{8,9},{9,8},{10,11... | collective-permute-start | bytes 7077896 | tf_op jit(solution)/shard_map/ppermute | solution.py:615
  52.6 20.2 %collective-permute-start.12 = (bf16[8,192,256]{2,1,0:T(8,128)(2,1)S(1)}, bf16[8,192,256]{2,1,0:T(8,128)(2,1)S(1)}, u32[]{:S(2)}, u32[]{:S(2)}) collective-permute-start(bf16[8,192,256]{2,1,0:T(8,128)(2,1)S(1)} %get-tuple-element.163), channel_id=1, source_target_pairs={{0,2},{1,3},{2,0},{3,1},{4,6},{5,7},{6,4},{7,5},{8,10},{9,11},{10,... | collective-permute-start | bytes 2359304 | tf_op jit(solution)/shard_map/ppermute | solution.py:615
  54.2 19.4 %collective-permute-start.13 = (bf16[8,192,256]{2,1,0:T(8,128)(2,1)S(1)}, bf16[8,192,256]{2,1,0:T(8,128)(2,1)S(1)}, u32[]{:S(2)}, u32[]{:S(2)}) collective-permute-start(bf16[8,192,256]{2,1,0:T(8,128)(2,1)S(1)} %get-tuple-element.165), channel_id=1, source_target_pairs={{0,4},{4,0},{8,12},{12,8},{16,20},{20,16},{24,28},{28,24},{1,5},{5... | collective-permute-start | bytes 2359304 | tf_op jit(solution)/shard_map/ppermute | solution.py:615
  55.8 19.1 %collective-permute-start.14 = (bf16[8,192,256]{2,1,0:T(8,128)(2,1)S(1)}, bf16[8,192,256]{2,1,0:T(8,128)(2,1)S(1)}, u32[]{:S(2)}, u32[]{:S(2)}) collective-permute-start(bf16[8,192,256]{2,1,0:T(8,128)(2,1)S(1)} %get-tuple-element.167), channel_id=1, source_target_pairs={{0,8},{4,12},{8,0},{12,4},{16,24},{20,28},{24,16},{28,20},{1,9},{5... | collective-permute-start | bytes 2359304 | tf_op jit(solution)/shard_map/ppermute | solution.py:615
  72.2 6.5 %collective-permute-start.18 = (bf16[2,8,112,256]{3,2,1,0:T(8,128)(2,1)S(1)}, bf16[2,8,112,256]{3,2,1,0:T(8,128)(2,1)S(1)}, u32[]{:S(2)}, u32[]{:S(2)}) collective-permute-start(bf16[2,8,112,256]{3,2,1,0:T(8,128)(2,1)S(1)} %get-tuple-element.176), channel_id=1, source_target_pairs={{0,1},{1,0},{2,3},{3,2},{4,5},{5,4},{6,7},{7,6},{8,9},{9,8},{10,11... | collective-permute-start | bytes 2752520 | tf_op jit(solution)/shard_map/ppermute | solution.py:615
  72.2 5.6 %collective-permute-start.19 = (bf16[2,768,256]{2,1,0:T(8,128)(2,1)S(1)}, bf16[2,768,256]{2,1,0:T(8,128)(2,1)S(1)}, u32[]{:S(2)}, u32[]{:S(2)}) collective-permute-start(bf16[2,768,256]{2,1,0:T(8,128)(2,1)S(1)} %get-tuple-element.178), channel_id=1, source_target_pairs={{0,1},{1,0},{2,3},{3,2},{4,5},{5,4},{6,7},{7,6},{8,9},{9,8},{10,11... | collective-permute-start | bytes 2359304 | tf_op jit(solution)/shard_map/ppermute | solution.py:615
  72.7 6.0 %collective-permute-start.20 = (bf16[2,768,256]{2,1,0:T(8,128)(2,1)S(1)}, bf16[2,768,256]{2,1,0:T(8,128)(2,1)S(1)}, u32[]{:S(2)}, u32[]{:S(2)}) collective-permute-start(bf16[2,768,256]{2,1,0:T(8,128)(2,1)S(1)} %get-tuple-element.180), channel_id=1, source_target_pairs={{0,1},{1,0},{2,3},{3,2},{4,5},{5,4},{6,7},{7,6},{8,9},{9,8},{10,11... | collective-permute-start | bytes 2359304 | tf_op jit(solution)/shard_map/ppermute | solution.py:615
  75.7 12.1 %collective-permute-start.15 = (bf16[4,192,256]{2,1,0:T(8,128)(2,1)S(1)}, bf16[4,192,256]{2,1,0:T(8,128)(2,1)S(1)}, u32[]{:S(2)}, u32[]{:S(2)}) collective-permute-start(bf16[4,192,256]{2,1,0:T(8,128)(2,1)S(1)} %get-tuple-element.170), channel_id=1, source_target_pairs={{0,4},{4,0},{8,12},{12,8},{16,20},{20,16},{24,28},{28,24},{1,5},{5... | collective-permute-start | bytes 1179656 | tf_op jit(solution)/shard_map/ppermute | solution.py:615
  76.3 15.9 %collective-permute-start.16 = (bf16[4,192,256]{2,1,0:T(8,128)(2,1)S(1)}, bf16[4,192,256]{2,1,0:T(8,128)(2,1)S(1)}, u32[]{:S(2)}, u32[]{:S(2)}) collective-permute-start(bf16[4,192,256]{2,1,0:T(8,128)(2,1)S(1)} %get-tuple-element.172), channel_id=1, source_target_pairs={{0,8},{4,12},{8,0},{12,4},{16,24},{20,28},{24,16},{28,20},{1,9},{5... | collective-permute-start | bytes 1179656 | tf_op jit(solution)/shard_map/ppermute | solution.py:615
  77.9 14.3 %collective-permute-start.17 = (bf16[4,192,256]{2,1,0:T(8,128)(2,1)S(1)}, bf16[4,192,256]{2,1,0:T(8,128)(2,1)S(1)}, u32[]{:S(2)}, u32[]{:S(2)}) collective-permute-start(bf16[4,192,256]{2,1,0:T(8,128)(2,1)S(1)} %get-tuple-element.174), channel_id=1, source_target_pairs={{0,2},{1,3},{2,0},{3,1},{4,6},{5,7},{6,4},{7,5},{8,10},{9,11},{10,... | collective-permute-start | bytes 1179656 | tf_op jit(solution)/shard_map/ppermute | solution.py:615
  79.4 20.3 %collective-permute-start.24 = (bf16[8,112,256]{2,1,0:T(8,128)(2,1)S(1)}, bf16[8,112,256]{2,1,0:T(8,128)(2,1)S(1)}, u32[]{:S(2)}, u32[]{:S(2)}) collective-permute-start(bf16[8,112,256]{2,1,0:T(8,128)(2,1)S(1)} %get-tuple-element.194), channel_id=1, source_target_pairs={{0,2},{1,3},{2,0},{3,1},{4,6},{5,7},{6,4},{7,5},{8,10},{9,11},{10,... | collective-permute-start | bytes 1376264 | tf_op jit(solution)/shard_map/ppermute | solution.py:615
  80.7 13.7 %collective-permute-start.25 = (bf16[8,96,256]{2,1,0:T(8,128)(2,1)S(1)}, bf16[8,96,256]{2,1,0:T(8,128)(2,1)S(1)}, u32[]{:S(2)}, u32[]{:S(2)}) collective-permute-start(bf16[8,96,256]{2,1,0:T(8,128)(2,1)S(1)} %get-tuple-element.196), channel_id=1, source_target_pairs={{0,4},{4,0},{8,12},{12,8},{16,20},{20,16},{24,28},{28,24},{1,5},{5... | collective-permute-start | bytes 1179656 | tf_op jit(solution)/shard_map/ppermute | solution.py:615
  87.8 9.6 %collective-permute-start.26 = (bf16[8,96,256]{2,1,0:T(8,128)(2,1)S(1)}, bf16[8,96,256]{2,1,0:T(8,128)(2,1)S(1)}, u32[]{:S(2)}, u32[]{:S(2)}) collective-permute-start(bf16[8,96,256]{2,1,0:T(8,128)(2,1)S(1)} %get-tuple-element.198), channel_id=1, source_target_pairs={{0,8},{4,12},{8,0},{12,4},{16,24},{20,28},{24,16},{28,20},{1,9},{5... | collective-permute-start | bytes 1179656 | tf_op jit(solution)/shard_map/ppermute | solution.py:615
  92.9 9.3 %collective-permute-start.21 = (bf16[2,192,256]{2,1,0:T(8,128)(2,1)S(1)}, bf16[2,192,256]{2,1,0:T(8,128)(2,1)S(1)}, u32[]{:S(2)}, u32[]{:S(2)}) collective-permute-start(bf16[2,192,256]{2,1,0:T(8,128)(2,1)S(1)} %get-tuple-element.188), channel_id=1, source_target_pairs={{0,8},{4,12},{8,0},{12,4},{16,24},{20,28},{24,16},{28,20},{1,9},{5... | collective-permute-start | bytes 589832 | tf_op jit(solution)/shard_map/ppermute | solution.py:615
  93.4 10.6 %collective-permute-start.22 = (bf16[2,192,256]{2,1,0:T(8,128)(2,1)S(1)}, bf16[2,192,256]{2,1,0:T(8,128)(2,1)S(1)}, u32[]{:S(2)}, u32[]{:S(2)}) collective-permute-start(bf16[2,192,256]{2,1,0:T(8,128)(2,1)S(1)} %get-tuple-element.190), channel_id=1, source_target_pairs={{0,2},{1,3},{2,0},{3,1},{4,6},{5,7},{6,4},{7,5},{8,10},{9,11},{10,... | collective-permute-start | bytes 589832 | tf_op jit(solution)/shard_map/ppermute | solution.py:615
  94.4 9.6 %collective-permute-start.23 = (bf16[2,192,256]{2,1,0:T(8,128)(2,1)S(1)}, bf16[2,192,256]{2,1,0:T(8,128)(2,1)S(1)}, u32[]{:S(2)}, u32[]{:S(2)}) collective-permute-start(bf16[2,192,256]{2,1,0:T(8,128)(2,1)S(1)} %get-tuple-element.192), channel_id=1, source_target_pairs={{0,4},{4,0},{8,12},{12,8},{16,20},{20,16},{24,28},{28,24},{1,5},{5... | collective-permute-start | bytes 589832 | tf_op jit(solution)/shard_map/ppermute | solution.py:615
  100.4 7.4 %collective-permute-start.28 = (bf16[4,112,256]{2,1,0:T(8,128)(2,1)S(1)}, bf16[4,112,256]{2,1,0:T(8,128)(2,1)S(1)}, u32[]{:S(2)}, u32[]{:S(2)}) collective-permute-start(bf16[4,112,256]{2,1,0:T(8,128)(2,1)S(1)} %get-tuple-element.204), channel_id=1, source_target_pairs={{0,4},{4,0},{8,12},{12,8},{16,20},{20,16},{24,28},{28,24},{1,5},{5... | collective-permute-start | bytes 688136 | tf_op jit(solution)/shard_map/ppermute | solution.py:615
  101.4 5.9 %collective-permute-start.29 = (bf16[4,96,256]{2,1,0:T(8,128)(2,1)S(1)}, bf16[4,96,256]{2,1,0:T(8,128)(2,1)S(1)}, u32[]{:S(2)}, u32[]{:S(2)}) collective-permute-start(bf16[4,96,256]{2,1,0:T(8,128)(2,1)S(1)} %get-tuple-element.206), channel_id=1, source_target_pairs={{0,8},{4,12},{8,0},{12,4},{16,24},{20,28},{24,16},{28,20},{1,9},{5... | collective-permute-start | bytes 589832 | tf_op jit(solution)/shard_map/ppermute | solution.py:615
  102.1 5.7 %collective-permute-start.30 = (bf16[4,96,256]{2,1,0:T(8,128)(2,1)S(1)}, bf16[4,96,256]{2,1,0:T(8,128)(2,1)S(1)}, u32[]{:S(2)}, u32[]{:S(2)}) collective-permute-start(bf16[4,96,256]{2,1,0:T(8,128)(2,1)S(1)} %get-tuple-element.208), channel_id=1, source_target_pairs={{0,2},{1,3},{2,0},{3,1},{4,6},{5,7},{6,4},{7,5},{8,10},{9,11},{10,... | collective-permute-start | bytes 589832 | tf_op jit(solution)/shard_map/ppermute | solution.py:615
  104.6 15.8 %collective-permute-start.27 = (bf16[1,576,256]{2,1,0:T(8,128)(2,1)S(1)}, bf16[1,576,256]{2,1,0:T(8,128)(2,1)S(1)}, u32[]{:S(2)}, u32[]{:S(2)}) collective-permute-start(bf16[1,576,256]{2,1,0:T(8,128)(2,1)S(1)} %get-tuple-element.202), channel_id=1, source_target_pairs={{0,16},{4,20},{8,24},{12,28},{16,0},{20,4},{24,8},{28,12},{1,17},{... | collective-permute-start | bytes 884744 | tf_op jit(solution)/shard_map/ppermute | solution.py:615
  108.4 7.2 %collective-permute-start.31 = (bf16[2,112,256]{2,1,0:T(8,128)(2,1)S(1)}, bf16[2,112,256]{2,1,0:T(8,128)(2,1)S(1)}, u32[]{:S(2)}, u32[]{:S(2)}) collective-permute-start(bf16[2,112,256]{2,1,0:T(8,128)(2,1)S(1)} %get-tuple-element.211), channel_id=1, source_target_pairs={{0,8},{4,12},{8,0},{12,4},{16,24},{20,28},{24,16},{28,20},{1,9},{5... | collective-permute-start | bytes 344072 | tf_op jit(solution)/shard_map/ppermute | solution.py:615
  109.9 5.7 %collective-permute-start.32 = (bf16[2,96,256]{2,1,0:T(8,128)(2,1)S(1)}, bf16[2,96,256]{2,1,0:T(8,128)(2,1)S(1)}, u32[]{:S(2)}, u32[]{:S(2)}) collective-permute-start(bf16[2,96,256]{2,1,0:T(8,128)(2,1)S(1)} %get-tuple-element.213), channel_id=1, source_target_pairs={{0,2},{1,3},{2,0},{3,1},{4,6},{5,7},{6,4},{7,5},{8,10},{9,11},{10,... | collective-permute-start | bytes 294920 | tf_op jit(solution)/shard_map/ppermute | solution.py:615
  111.0 4.7 %collective-permute-start.33 = (bf16[2,96,256]{2,1,0:T(8,128)(2,1)S(1)}, bf16[2,96,256]{2,1,0:T(8,128)(2,1)S(1)}, u32[]{:S(2)}, u32[]{:S(2)}) collective-permute-start(bf16[2,96,256]{2,1,0:T(8,128)(2,1)S(1)} %get-tuple-element.215), channel_id=1, source_target_pairs={{0,4},{4,0},{8,12},{12,8},{16,20},{20,16},{24,28},{28,24},{1,5},{5... | collective-permute-start | bytes 294920 | tf_op jit(solution)/shard_map/ppermute | solution.py:615
  112.5 10.2 %collective-permute-start.42 = (bf16[2,128,768]{2,1,0:T(8,128)(2,1)S(1)}, bf16[2,128,768]{2,1,0:T(8,128)(2,1)S(1)}, u32[]{:S(2)}, u32[]{:S(2)}) collective-permute-start(bf16[2,128,768]{2,1,0:T(8,128)(2,1)S(1)} %get-tuple-element.225), channel_id=1, source_target_pairs={{0,2},{1,3},{2,0},{3,1},{4,6},{5,7},{6,4},{7,5},{8,10},{9,11},{10,... | collective-permute-start | bytes 1179656 | tf_op jit(solution)/shard_map/ppermute | solution.py:615
  116.2 8.5 %collective-permute-start.37 = (bf16[1,304,256]{2,1,0:T(8,128)(2,1)S(1)}, bf16[1,304,256]{2,1,0:T(8,128)(2,1)S(1)}, u32[]{:S(2)}, u32[]{:S(2)}) collective-permute-start(bf16[1,304,256]{2,1,0:T(8,128)(2,1)S(1)} %get-tuple-element.220), channel_id=1, source_target_pairs={{0,16},{4,20},{8,24},{12,28},{16,0},{20,4},{24,8},{28,12},{1,17},{... | collective-permute-start | bytes 466952 | tf_op jit(solution)/shard_map/ppermute | solution.py:615
  121.0 8.0 %collective-permute-start.35 = (bf16[1,576,256]{2,1,0:T(8,128)(2,1)S(1)}, bf16[1,576,256]{2,1,0:T(8,128)(2,1)S(1)}, u32[]{:S(2)}, u32[]{:S(2)}) collective-permute-start(bf16[1,576,256]{2,1,0:T(8,128)(2,1)S(1)} %get-tuple-element.218.refs_1_), channel_id=1, source_target_pairs={{0,2},{1,3},{2,0},{3,1},{4,6},{5,7},{6,4},{7,5},{8,10},{9,11},{10,... | collective-permute-start | bytes 884744 | tf_op jit(solution)/shard_map/ppermute | solution.py:615
  122.7 6.2 %collective-permute-start.41 = (bf16[128,768]{1,0:T(8,128)(2,1)S(1)}, bf16[128,768]{1,0:T(8,128)(2,1)S(1)}, u32[]{:S(2)}, u32[]{:S(2)}) collective-permute-start(bf16[128,768]{1,0:T(8,128)(2,1)S(1)} %get-tuple-element.224), channel_id=1, source_target_pairs={{0,1},{1,0},{2,3},{3,2},{4,5},{5,4},{6,7},{7,6},{8,9},{9,8},{10,11... | collective-permute-start | bytes 589832 | tf_op jit(solution)/shard_map/ppermute | solution.py:615
  122.7 8.4 %collective-permute-start.43 = (bf16[2,128,768]{2,1,0:T(8,128)(2,1)S(1)}, bf16[2,128,768]{2,1,0:T(8,128)(2,1)S(1)}, u32[]{:S(2)}, u32[]{:S(2)}) collective-permute-start(bf16[2,128,768]{2,1,0:T(8,128)(2,1)S(1)} %collective-permute-done.42.refs_11_), channel_id=1, source_target_pairs={{0,1},{1,0},{2,3},{3,2},{4,5},{5,4},{6,7},{7,6},{8,9},{9,8},{10,11... | collective-permute-start | bytes 1179656 | tf_op jit(solution)/shard_map/ppermute | solution.py:615
  125.3 5.8 %collective-permute-start.39 = (bf16[1,304,256]{2,1,0:T(8,128)(2,1)S(1)}, bf16[1,304,256]{2,1,0:T(8,128)(2,1)S(1)}, u32[]{:S(2)}, u32[]{:S(2)}) collective-permute-start(bf16[1,304,256]{2,1,0:T(8,128)(2,1)S(1)} %get-tuple-element.222.refs_5_), channel_id=1, source_target_pairs={{0,2},{1,3},{2,0},{3,1},{4,6},{5,7},{6,4},{7,5},{8,10},{9,11},{10,... | collective-permute-start | bytes 466952 | tf_op jit(solution)/shard_map/ppermute | solution.py:615
  126.8 4.3 %collective-permute-start.34 = (bf16[1,576,256]{2,1,0:T(8,128)(2,1)S(1)}, bf16[1,576,256]{2,1,0:T(8,128)(2,1)S(1)}, u32[]{:S(2)}, u32[]{:S(2)}) collective-permute-start(bf16[1,576,256]{2,1,0:T(8,128)(2,1)S(1)} %get-tuple-element.218.refs_1_), channel_id=1, source_target_pairs={{0,1},{1,0},{2,3},{3,2},{4,5},{5,4},{6,7},{7,6},{8,9},{9,8},{10,11... | collective-permute-start | bytes 884744 | tf_op jit(solution)/shard_map/ppermute | solution.py:615
  128.9 3.5 %collective-permute-start.36 = (bf16[1,576,256]{2,1,0:T(8,128)(2,1)S(1)}, bf16[1,576,256]{2,1,0:T(8,128)(2,1)S(1)}, u32[]{:S(2)}, u32[]{:S(2)}) collective-permute-start(bf16[1,576,256]{2,1,0:T(8,128)(2,1)S(1)} %collective-permute-done.35.refs_3_), channel_id=1, source_target_pairs={{0,1},{1,0},{2,3},{3,2},{4,5},{5,4},{6,7},{7,6},{8,9},{9,8},{10,11... | collective-permute-start | bytes 884744 | tf_op jit(solution)/shard_map/ppermute | solution.py:615
  129.0 2.1 %collective-permute-start.38 = (bf16[1,304,256]{2,1,0:T(8,128)(2,1)S(1)}, bf16[1,304,256]{2,1,0:T(8,128)(2,1)S(1)}, u32[]{:S(2)}, u32[]{:S(2)}) collective-permute-start(bf16[1,304,256]{2,1,0:T(8,128)(2,1)S(1)} %get-tuple-element.222.refs_5_), channel_id=1, source_target_pairs={{0,1},{1,0},{2,3},{3,2},{4,5},{5,4},{6,7},{7,6},{8,9},{9,8},{10,11... | collective-permute-start | bytes 466952 | tf_op jit(solution)/shard_map/ppermute | solution.py:615
  131.1 1.4 %collective-permute-start.40 = (bf16[1,304,256]{2,1,0:T(8,128)(2,1)S(1)}, bf16[1,304,256]{2,1,0:T(8,128)(2,1)S(1)}, u32[]{:S(2)}, u32[]{:S(2)}) collective-permute-start(bf16[1,304,256]{2,1,0:T(8,128)(2,1)S(1)} %collective-permute-done.39.refs_7_), channel_id=1, source_target_pairs={{0,1},{1,0},{2,3},{3,2},{4,5},{5,4},{6,7},{7,6},{8,9},{9,8},{10,11... | collective-permute-start | bytes 466952 | tf_op jit(solution)/shard_map/ppermute | solution.py:615
  (4 other events, 22.6 us)
